TPU v7x, 32 devices: a whole 2x2x4 slice. The times are simulated.
32 devices in a mesh: vel: 8 (over z, y), space: 4 (over x, core).
Axes of the slice: x: 2, y: 2, z: 4, core: 2. Of those that a mesh axis runs over, the one named last changes fastest.
Arguments:
- dist: float32 [4096, 32, 1024], P('vel', 'space'), may hold values from -6 to 6
- vel_index: int32 [3, 4096], P(None, 'vel'), may hold values from 0 to 15, as said below
- relax: float32 [32, 1024], P('space'), may hold values from 0.05 to 0.9
- wall_mask: int32 [32, 1024], P('space'), may hold values 0 or 1
- macro_inverse: float32 [13, 13], replicated, may hold values from -1.5 to 1.5
Outputs:
- dist_out: float32 [4096, 32, 1024], P('vel', 'space')
- macro_fields: float32 [13, 32, 1024], P(None, 'space', 'vel')
- change_norm: float32 [2], replicated
Inputs may be any that keep to these rules, and one draw needn't show every extreme that they name: `vel_index`: each point of the velocity grid of 4096 points appears in exactly one column.
All inputs are finite; a program needn't handle non-finite values. No bound on the sum of `wall_mask` on one device may be relied on, other than what follows from the above.
Results may differ from a plain program's by a relative error of at most 0.0003.
Values sent between devices are 32-bit elements; how exact they have to be, the bound alone decides.
No kernel may reach another device: no remote copies, remote signals or barrier semaphores. Data moves between devices by JAX's collectives and lax.ppermute only.
A program may use at most 256 MiB of HBM per device.

v0:
```python
import math

import jax
import jax.numpy as jnp
from jax import lax
from jax.sharding import PartitionSpec as P

NVX = 16
NY = 64
NZ = 16
MOM = 13
SWEEPS = 3
ITERS = 2


speed_range = 4.0
time_step = 0.08
coupling = 0.5


def with_halo(shard, sides, width):
    for axis, dim in sides:
        peers, length = (lax.axis_size(axis), shard.shape[dim])
        up = [(i, (i + 1) % peers) for i in range(peers)]
        down = [(j, i) for i, j in up]
        last = lax.slice_in_dim(shard, length - width, length, axis=dim)
        first = lax.slice_in_dim(shard, 0, width, axis=dim)
        before = lax.ppermute(last, axis, up)
        after = lax.ppermute(first, axis, down)
        shard = jnp.concatenate([before, shard, after], axis=dim)
    return shard


def velocities(vel_index):
    return speed_range * (2.0 * vel_index.astype(jnp.float32) + 1.0 - NVX) / NVX


def bases(velocity):
    cxv, cyv, czv = (velocity[0], velocity[1], velocity[2])
    square = cxv * cxv + cyv * cyv + czv * czv
    weights = (2.0 * speed_range / NVX) ** 3 * math.pi ** (-1.5) * jnp.exp(-square)
    heat = square - 2.5
    functions = jnp.stack(
        [
            jnp.ones_like(cxv),
            cxv,
            cyv,
            czv,
            2.0 * square / 3.0 - 1.0,
            2.0 * cxv * cyv,
            2.0 * cxv * czv,
            2.0 * cyv * czv,
            cxv * cxv - cyv * cyv,
            cyv * cyv - czv * czv,
            cxv * heat,
            cyv * heat,
            czv * heat,
        ],
        0,
    )
    moment_rows = functions * weights[None, :]
    factor = 4.0 / 15.0
    shakhov = jnp.stack(
        [
            jnp.ones_like(cxv),
            2.0 * cxv,
            2.0 * cyv,
            2.0 * czv,
            square - 1.5,
            factor * cxv * heat,
            factor * cyv * heat,
            factor * czv * heat,
        ],
        1,
    )
    walls = jnp.stack([jnp.ones_like(cxv), square - 1.5], 1)
    return (moment_rows, shakhov, walls)


def upwind_local(block, speed, axis):
    lower = jnp.roll(block, 1, axis)
    higher = jnp.roll(block, -1, axis)
    return jnp.where(speed > 0, block - lower, higher - block)


def stream(dist, velocity):
    count, width, cells = dist.shape
    padded = with_halo(dist, (("space", 1),), 1)
    lower_x = padded[:, :-2]
    higher_x = padded[:, 2:]
    cxv = velocity[0][:, None, None]
    cyv = velocity[1][:, None, None, None]
    czv = velocity[2][:, None, None, None]
    along_x = jnp.where(cxv > 0, dist - lower_x, higher_x - dist)
    grid = dist.reshape(count, width, NY, NZ)
    across = cyv * upwind_local(grid, cyv, 2) + czv * upwind_local(grid, czv, 3)
    total = cxv * along_x + across.reshape(count, width, cells)
    return dist - time_step * total


def slab_sweep(field):
    padded = with_halo(field, (("space", 1),), 1)
    beside_all = padded[:, :-2] + padded[:, 2:]
    for axis in (2, 3):
        beside_all = beside_all + jnp.roll(field, 1, axis) + jnp.roll(field, -1, axis)
    return beside_all


def smooth(local, neighbours):
    rows, width, cells = local.shape
    source = local[1:5].reshape(4, width, cells // NZ, NZ)
    field = source
    for sweep in range(SWEEPS):
        field = (source + coupling * neighbours(field)) / (1.0 + 6.0 * coupling)
    return jnp.concatenate([local[0:1], field.reshape(4, width, cells), local[5:]], 0)


def shards(dist, vel_index, relax, wall_mask, macro_inverse):
    highest = lax.Precision.HIGHEST
    count, width, cells = dist.shape
    share = cells // lax.axis_size("vel")
    velocity = velocities(vel_index)
    moment_rows, shakhov, walls = bases(velocity)
    norms = []
    owned_block = None
    for step in range(ITERS):
        read = stream(dist, velocity)
        partial_moments = jnp.dot(
            moment_rows, read.reshape(count, width * cells), precision=highest
        ).reshape(MOM, width, cells)
        totals = lax.psum(partial_moments, "vel")
        local = jnp.einsum("kj,jxc->kxc", macro_inverse, totals, precision=highest)
        updated = smooth(local, slab_sweep)
        change = lax.psum(jnp.sum((updated - totals) ** 2), "space")
        fields = jnp.concatenate([updated[0:5], updated[10:13]], 0)
        owned_block = lax.dynamic_slice_in_dim(updated, lax.axis_index("vel") * share, share, 2)
        norms.append(jnp.sqrt(change))
        flat_fields = fields.reshape(8, width * cells)
        target = jnp.dot(shakhov, flat_fields, precision=highest).reshape(count, width, cells)
        wall_fields = jnp.stack([flat_fields[0], flat_fields[4]], 0)
        wall_value = jnp.dot(walls, wall_fields, precision=highest).reshape(count, width, cells)
        dist = jnp.where(wall_mask[None] > 0, wall_value, read + relax[None] * (target - read))
    return (dist, owned_block, jnp.stack(norms))


def solution(mesh):
    return jax.shard_map(
        shards,
        mesh=mesh,
        in_specs=(P("vel", "space", None), P(None, "vel"), P("space", None), P("space", None), P()),
        out_specs=(P("vel", "space", None), P(None, "space", "vel"), P()),
        check_vma=False,
    )
```

profile of v0, /device:TPU:0, one launch (start us, length us, event | category | flops | bytes accessed | tf_op | source)
XLA Modules:
  0.0 875.6 jit_solution(10346973159171540213)
XLA Ops:
  7.2 15.2 %copy.217 = f32[512,8,1024]{2,0,1:T(8,128)S(1)} copy(f32[512,8,1024]{2,1,0:T(8,128)} %param.5) | data formatting | bytes 33554432 | tf_op args[0]
  22.4 6.2 copy-done.3
  28.6 2.3 fusion.107
  31.4 2.4 collective-permute-start.1
  33.7 17.4 %copy.208 = f32[512,8,1024]{0,2,1:T(8,128)} copy(f32[512,8,1024]{2,1,0:T(8,128)} %param.5) | data formatting | bytes 33554432 | tf_op args[0]
  51.2 24.8 %fusion.104 = (f32[512,8,63,16]{0,3,2,1:T(8,128)}, f32[512,8,63,16]{0,3,2,1:T(8,128)}) fusion(f32[512,8,64,16]{0,3,2,1:T(8,128)} %bitcast.97), kind=kLoop, calls=%fused_computation.158 | loop fusion | bytes 66060288 | tf_op jit(solution)/shard_map/jit(_roll_static)/slice | solution.py:81
  77.9 12.1 %fusion.106 = (f32[512,8,64,15]{0,3,2,1:T(8,128)}, f32[512,8,64,15]{0,3,2,1:T(8,128)}) fusion(f32[512,8,64,16]{0,3,2,1:T(8,128)S(1)} %bitcast.100), kind=kLoop, calls=%fused_computation.160 | loop fusion | bytes 62914560 | tf_op jit(solution)/shard_map/jit(_roll_static)/slice | solution.py:81
  90.0 8.0 fusion.105
  98.1 22.2 %pad_maximum_fusion.4 = (f32[512,8,64,16]{0,3,2,1:T(8,128)}, f32[512,8,64,16]{0,3,2,1:T(8,128)}) fusion(f32[512,8,63,16]{0,3,2,1:T(8,128)} %get-tuple-element.31, f32[512,8,1,16]{0,3,2,1:T(8,128)S(1)} %get-tuple-element.29, f32[512,8,1,16]{0,3,2,1:T(8,128)S(1)} %get-tuple-element.30, f32[512,8,63,16]{0,3,2,1:T(8,128)} %get-tuple-element.32), kind=kLoop, calls=%fused_computation.19 | loop fusion | flops 8388608 | bytes 67108864 | tf_op jit(solution)/shard_map/jit(_roll_static)/concatenate | solution.py:81
  120.2 16.5 %copy.210 = f32[512,8,1024]{2,0,1:T(8,128)} copy(f32[512,8,1024]{0,2,1:T(8,128)} %bitcast.109) | data formatting | bytes 33554432 | tf_op jit(solution)/shard_map/jit(_roll_static)/concatenate | solution.py:81
  136.7 16.4 %copy.211 = f32[512,8,1024]{2,0,1:T(8,128)} copy(f32[512,8,1024]{0,2,1:T(8,128)} %bitcast.107) | data formatting | bytes 33554432 | tf_op jit(solution)/shard_map/jit(_roll_static)/concatenate | solution.py:82
  153.1 22.7 %pad_maximum_fusion.6 = (f32[512,8,64,16]{0,3,2,1:T(8,128)}, f32[512,8,64,16]{0,3,2,1:T(8,128)}) fusion(f32[512,8,64,15]{0,3,2,1:T(8,128)} %get-tuple-element.35, f32[512,8,64,1]{0,3,2,1:T(1,128)S(1)} %get-tuple-element.33, f32[512,8,64,1]{0,3,2,1:T(1,128)S(1)} %get-tuple-element.34, f32[512,8,64,15]{0,3,2,1:T(8,128)} %get-tuple-element.36), kind=kLoop, calls=%fused_computation.21 | loop fusion | flops 8388608 | bytes 67108864 | tf_op jit(solution)/shard_map/jit(_roll_static)/concatenate | solution.py:81
  175.8 16.4 %copy.214 = f32[512,8,1024]{2,0,1:T(8,128)} copy(f32[512,8,1024]{0,2,1:T(8,128)} %bitcast.110) | data formatting | bytes 33554432 | tf_op jit(solution)/shard_map/jit(_roll_static)/concatenate | solution.py:81
  192.2 16.5 %copy.215 = f32[512,8,1024]{2,0,1:T(8,128)} copy(f32[512,8,1024]{0,2,1:T(8,128)} %bitcast.108) | data formatting | bytes 33554432 | tf_op jit(solution)/shard_map/jit(_roll_static)/concatenate | solution.py:82
  208.9 45.0 %fusion.12 = f32[512,8,1024]{2,0,1:T(8,128)} fusion(f32[512,8,1024]{2,0,1:T(8,128)} %copy-done.3, f32[512,1,1024]{2,0,1:T(8,128)} %collective-permute-done.1, f32[512,1,1024]{2,0,1:T(8,128)} %collective-permute-done, f32[512,8,1024]{2,0,1:T(8,128)} %copy.215, f32[512,8,1024]{2,0,1:T(8,128)} %copy.214, f32[512,8,1024]{2,0,1:T(8,128)} %copy.211, ...), kind=kLoop, calls=%fused_computation.16 | loop fusion | flops 75497472 | bytes 104865280 | tf_op jit(solution)/shard_map/sub | solution.py:98
  254.1 16.4 %copy.218 = f32[512,8,1024]{0,2,1:T(8,128)} copy(f32[512,8,1024]{2,0,1:T(8,128)} %fusion.12) | data formatting | bytes 33554432 | tf_op jit(solution)/shard_map/sub | solution.py:98
  270.5 18.1 %fusion.16 = f32[13,8,1024]{2,0,1:T(8,128)} fusion(f32[512,8,1024]{0,2,1:T(8,128)} %copy.218, f32[13,512]{1,0:T(8,128)S(1)} %stack.18, f32[512]{0:T(512)S(1)} %bitcast.130), kind=kOutput, calls=%fused_computation.29 | convolution fusion | flops 654318080 | bytes 17231872 | tf_op jit(solution)/shard_map/dot_general | solution.py:128
  288.7 74.4 %all-reduce.5.cloned.1.call-done = f32[13,8,1024]{2,0,1:T(8,128)} async-done(((f32[13,8,1024]{2,0,1:T(8,128)}), f32[13,8,1024]{2,0,1:T(8,128)}) %all-reduce.5.cloned.1.call-update) | async-done | bytes 426000 | tf_op jit(solution)/shard_map/psum | solution.py:131
  368.1 2.5 collective-permute-done.2
  375.1 2.6 collective-permute-done.4
  382.6 2.2 collective-permute-done.6
  386.8 16.0 %fusion.68 = f32[512,8192]{1,0:T(8,128)} fusion(f32[1,8192]{1,0:T(1,128)S(1)} %slice.445, f32[1,8192]{1,0:T(1,128)S(1)} %bitcast.115, f32[512,1]{0,1:T(1,128)S(1)} %get-tuple-element.119), kind=kOutput, calls=%fused_computation.101 | convolution fusion | flops 100679680 | bytes 16844800 | tf_op jit(solution)/shard_map/dot_general | solution.py:141
  403.0 22.5 %bitcast_select_fusion = f32[512,8,1024]{2,0,1:T(8,128)} fusion(f32[64,8,8,1024]{3,2,1,0:T(8,128)} %bitcast.103, f32[512,8,1024]{2,0,1:T(8,128)} %fusion.12, f32[8,1024,8]{1,2,0:T(8,128)S(1)} %bitcast.114, f32[8,1024]{1,0:T(8,128)S(1)} %copy-done.16, pred[8,1024]{1,0:T(8,128)(4,1)S(1)} %broadcast_compare_fusion, f32[512,8]{0,1:T(8,128)S(1)} %stack.20), kind=kOutput, calls=%fused_computation | convolution fusion | flops 419430400 | bytes 50651136 | tf_op jit(solution)/shard_map/dot_general | solution.py:139
  425.5 16.4 %copy.221 = f32[512,8,1024]{0,2,1:T(8,128)} copy(f32[512,8,1024]{2,0,1:T(8,128)} %bitcast_select_fusion) | data formatting | bytes 33554432 | tf_op jit(solution)/shard_map/jit(_where)/select_n | solution.py:142
  441.9 24.7 %fusion.99 = (f32[512,8,63,16]{0,3,2,1:T(8,128)}, f32[512,8,63,16]{0,3,2,1:T(8,128)}) fusion(f32[512,8,64,16]{0,3,2,1:T(8,128)} %bitcast.93), kind=kLoop, calls=%fused_computation.153 | loop fusion | bytes 66060288 | tf_op jit(solution)/shard_map/jit(_roll_static)/slice | solution.py:81
  468.6 12.1 %fusion.101 = (f32[512,8,64,15]{0,3,2,1:T(8,128)}, f32[512,8,64,15]{0,3,2,1:T(8,128)}) fusion(f32[512,8,64,16]{0,3,2,1:T(8,128)S(1)} %bitcast.96), kind=kLoop, calls=%fused_computation.155 | loop fusion | bytes 62914560 | tf_op jit(solution)/shard_map/jit(_roll_static)/slice | solution.py:81
  480.7 5.0 fusion.102
  487.8 14.1 %pad_maximum_fusion.8 = f32[512,8,64,16]{0,3,2,1:T(8,128)} fusion(f32[512,8,63,16]{0,3,2,1:T(8,128)} %get-tuple-element.21, f32[512,8,1,16]{0,3,2,1:T(8,128)S(1)} %get-tuple-element.19), kind=kLoop, calls=%fused_computation.23 | loop fusion | flops 4194304 | bytes 33554432 | tf_op jit(solution)/shard_map/jit(_roll_static)/concatenate | solution.py:81
  502.9 6.3 pad_maximum_fusion.9
  509.3 8.0 fusion.100
  517.3 16.5 %copy.222 = f32[512,8,1024]{2,0,1:T(8,128)} copy(f32[512,8,1024]{0,2,1:T(8,128)} %bitcast.101) | data formatting | bytes 33554432 | tf_op jit(solution)/shard_map/jit(_roll_static)/concatenate | solution.py:81
  533.8 16.4 %copy.223 = f32[512,8,1024]{2,0,1:T(8,128)} copy(f32[512,8,1024]{0,2,1:T(8,128)} %bitcast.102) | data formatting | bytes 33554432 | tf_op jit(solution)/shard_map/jit(_roll_static)/concatenate | solution.py:82
  550.2 12.7 %pad_maximum_fusion.10 = f32[512,8,64,16]{0,3,2,1:T(8,128)} fusion(f32[512,8,64,15]{0,3,2,1:T(8,128)} %get-tuple-element.25, f32[512,8,64,1]{0,3,2,1:T(1,128)S(1)} %get-tuple-element.23), kind=kLoop, calls=%fused_computation.25 | loop fusion | flops 4194304 | bytes 33554432 | tf_op jit(solution)/shard_map/jit(_roll_static)/concatenate | solution.py:81
  562.9 16.4 %copy.224 = f32[512,8,1024]{2,0,1:T(8,128)} copy(f32[512,8,1024]{0,2,1:T(8,128)} %bitcast.104) | data formatting | bytes 33554432 | tf_op jit(solution)/shard_map/jit(_roll_static)/concatenate | solution.py:81
  579.3 12.8 %pad_maximum_fusion.11 = f32[512,8,64,16]{0,3,2,1:T(8,128)} fusion(f32[512,8,64,1]{0,3,2,1:T(1,128)S(1)} %get-tuple-element.24, f32[512,8,64,15]{0,3,2,1:T(8,128)} %get-tuple-element.26), kind=kLoop, calls=%fused_computation.26 | loop fusion | flops 4194304 | bytes 33554432 | tf_op jit(solution)/shard_map/jit(_roll_static)/concatenate | solution.py:82
  592.1 16.5 %copy.225 = f32[512,8,1024]{2,0,1:T(8,128)} copy(f32[512,8,1024]{0,2,1:T(8,128)} %bitcast.105) | data formatting | bytes 33554432 | tf_op jit(solution)/shard_map/jit(_roll_static)/concatenate | solution.py:82
  608.6 44.9 %fusion.5 = f32[512,8,1024]{2,0,1:T(8,128)} fusion(f32[512,8,1024]{2,0,1:T(8,128)} %bitcast_select_fusion, f32[512,1,1024]{2,0,1:T(8,128)} %collective-permute-done.9, f32[512,1,1024]{2,0,1:T(8,128)} %collective-permute-done.8, f32[512,8,1024]{2,0,1:T(8,128)} %copy.225, f32[512,8,1024]{2,0,1:T(8,128)} %copy.224, f32[512,8,1024]{2,0,1:T(8,128)} %copy.223, ...), kind=kLoop, calls=%fused_computation.7 | loop fusion | flops 75497472 | bytes 104865280 | tf_op jit(solution)/shard_map/sub | solution.py:98
  653.5 16.4 %copy.226 = f32[512,8,1024]{0,2,1:T(8,128)} copy(f32[512,8,1024]{2,0,1:T(8,128)} %fusion.5) | data formatting | bytes 33554432 | tf_op jit(solution)/shard_map/sub | solution.py:98
  670.0 18.5 %fusion.14 = f32[13,8,1024]{2,0,1:T(8,128)} fusion(f32[512,8,1024]{0,2,1:T(8,128)} %copy.226, f32[13,512]{1,0:T(8,128)S(1)} %copy-done.13, f32[512]{0:T(512)S(1)} %bitcast.131), kind=kOutput, calls=%fused_computation.27 | convolution fusion | flops 654318080 | bytes 17231872 | tf_op jit(solution)/shard_map/dot_general | solution.py:128
  690.1 70.0 %all-reduce.7.cloned.1.call-done = f32[13,8,1024]{2,0,1:T(8,128)} async-done(((f32[13,8,1024]{2,0,1:T(8,128)}), f32[13,8,1024]{2,0,1:T(8,128)}) %all-reduce.7.cloned.1.call-update) | async-done | bytes 426000 | tf_op jit(solution)/shard_map/psum | solution.py:131
  765.1 2.5 collective-permute-done.10
  772.2 2.4 collective-permute-done.12
  779.1 2.6 collective-permute-done.14
  784.9 8.2 all-reduce.1
  795.3 15.9 %fusion.72 = f32[512,8192]{0,1:T(8,128)} fusion(f32[1,8192]{1,0:T(1,128)S(1)} %slice.499, f32[1,8192]{1,0:T(1,128)S(1)} %bitcast.117, f32[512,1]{0,1:T(1,128)S(1)} %copy-done.21), kind=kOutput, calls=%fused_computation.105 | convolution fusion | flops 100679680 | bytes 16844800 | tf_op jit(solution)/shard_map/dot_general | solution.py:141
  811.2 16.5 %copy.229 = f32[512,8,1024]{2,0,1:T(8,128)} copy(f32[512,8,1024]{0,2,1:T(8,128)} %bitcast.106) | data formatting | bytes 33554432 | tf_op jit(solution)/shard_map/reshape | solution.py:141
  827.8 22.5 %add_select_fusion = f32[512,8,1024]{2,0,1:T(8,128)} fusion(f32[512,8,1024]{2,0,1:T(8,128)} %copy.229, f32[512,8,1024]{2,0,1:T(8,128)} %fusion.5, f32[8,1024,8]{1,2,0:T(8,128)S(1)} %bitcast.113, f32[8,1024]{1,0:T(8,128)S(1)} %copy-done.17, pred[8,1024]{1,0:T(8,128)(4,1)S(1)} %copy-done.19, f32[512,8]{0,1:T(8,128)S(1)} %copy-done.15), kind=kOutput, calls=%fused_computation.31 | convolution fusion | flops 419430400 | bytes 50651136 | tf_op jit(solution)/shard_map/dot_general | solution.py:139
  850.3 17.8 %copy.232 = f32[512,8,1024]{2,1,0:T(8,128)} copy(f32[512,8,1024]{2,0,1:T(8,128)} %add_select_fusion) | data formatting | bytes 33554432
  (192 shorter events, 44.5 us)
Async XLA Ops:
  7.2 355.9 %copy-start = (f32[13,13]{1,0:T(8,128)S(1)}, f32[13,13]{1,0:T(8,128)}, u32[]{:S(2)}) copy-start(f32[13,13]{1,0:T(8,128)} %param.9) | copy-start | bytes 2032
  7.2 355.9 %all-reduce.5.cloned.1.call-start = ((), (), s32[]{:S(2)}) async-start(), calls=%async_computation | async-start | bytes 1048576 | tf_op jit(solution)/shard_map/psum | solution.py:131
  30.9 178.0 %collective-permute-start = (f32[512,1,1024]{2,0,1:T(8,128)}, f32[512,1,1024]{2,0,1:T(8,128)}, u32[]{:S(2)}, u32[]{:S(2)}) collective-permute-start(f32[512,1,1024]{2,0,1:T(8,128)} %get-tuple-element.37), channel_id=1, source_target_pairs={{0,1},{1,2},{2,3},{3,0},{4,5},{5,6},{6,7},{7,4},{8,9},{9,10},{10,1... | collective-permute-start | bytes 6291464 | tf_op jit(solution)/shard_map/ppermute | solution.py:28
  31.4 177.6 %collective-permute-start.1 = (f32[512,1,1024]{2,0,1:T(8,128)}, f32[512,1,1024]{2,0,1:T(8,128)}, u32[]{:S(2)}, u32[]{:S(2)}) collective-permute-start(f32[512,1,1024]{2,0,1:T(8,128)} %get-tuple-element.38), channel_id=1, source_target_pairs={{1,0},{2,1},{3,2},{0,3},{5,4},{6,5},{7,6},{4,7},{9,8},{10,9},{11,1... | collective-permute-start | bytes 6291464 | tf_op jit(solution)/shard_map/ppermute | solution.py:29
  51.2 26.7 %copy-start.2 = (f32[512,8,1024]{0,2,1:T(8,128)S(1)}, f32[512,8,1024]{0,2,1:T(8,128)}, u32[]{:S(2)}) copy-start(f32[512,8,1024]{0,2,1:T(8,128)} %copy.208) | copy-start | bytes 50331652
  208.7 45.3 %copy-start.22 = (f32[1,512]{1,0:T(1,128)}, f32[1,512]{1,0:T(1,128)S(1)}, u32[]{:S(2)}) copy-start(f32[1,512]{1,0:T(1,128)S(1)} %get-tuple-element.116) | copy-start | bytes 6148
  208.7 45.3 %copy-start.24 = (f32[1,512]{1,0:T(1,128)}, f32[1,512]{1,0:T(1,128)S(1)}, u32[]{:S(2)}) copy-start(f32[1,512]{1,0:T(1,128)S(1)} %get-tuple-element.114) | copy-start | bytes 6148
  208.7 45.3 %copy-start.26 = (f32[1,512]{1,0:T(1,128)}, f32[1,512]{1,0:T(1,128)S(1)}, u32[]{:S(2)}) copy-start(f32[1,512]{1,0:T(1,128)S(1)} %get-tuple-element.115) | copy-start | bytes 6148
  208.8 61.7 %copy-start.29 = (f32[1,512]{1,0:T(1,128)}, f32[1,512]{1,0:T(1,128)S(1)}, u32[]{:S(2)}) copy-start(f32[1,512]{1,0:T(1,128)S(1)} %get-tuple-element.117) | copy-start | bytes 6148
  208.8 178.0 %copy-start.20 = (f32[512,1]{0,1:T(1,128)}, f32[512,1]{0,1:T(1,128)S(1)}, u32[]{:S(2)}) copy-start(f32[512,1]{0,1:T(1,128)S(1)} %get-tuple-element.119) | copy-start | bytes 6148
  208.9 61.6 %copy-start.12 = (f32[13,512]{1,0:T(8,128)}, f32[13,512]{1,0:T(8,128)S(1)}, u32[]{:S(2)}) copy-start(f32[13,512]{1,0:T(8,128)S(1)} %stack.18) | copy-start | bytes 79876
  208.9 45.1 %copy-start.32 = (pred[512]{0:T(512)(128)(4,1)}, pred[512]{0:T(512)(128)(4,1)S(1)}, u32[]{:S(2)}) copy-start(pred[512]{0:T(512)(128)(4,1)S(1)} %broadcast_compare_fusion.3) | copy-start | bytes 1540
  208.9 45.1 %copy-start.34 = (pred[512]{0:T(512)(128)(4,1)}, pred[512]{0:T(512)(128)(4,1)S(1)}, u32[]{:S(2)}) copy-start(pred[512]{0:T(512)(128)(4,1)S(1)} %get-tuple-element.124) | copy-start | bytes 1540
  208.9 45.1 %copy-start.36 = (pred[512]{0:T(512)(128)(4,1)}, pred[512]{0:T(512)(128)(4,1)S(1)}, u32[]{:S(2)}) copy-start(pred[512]{0:T(512)(128)(4,1)S(1)} %get-tuple-element.125) | copy-start | bytes 1540
  270.5 18.2 %copy-start.28 = (s32[8,1024]{1,0:T(8,128)S(1)}, s32[8,1024]{1,0:T(8,128)}, u32[]{:S(2)}) copy-start(s32[8,1024]{1,0:T(8,128)} %param.8) | copy-start | bytes 98308
  288.6 471.5 %all-reduce.7.cloned.1.call-start = ((), (), s32[]{:S(2)}) async-start(), calls=%async_computation.1 | async-start | bytes 1048576 | tf_op jit(solution)/shard_map/psum | solution.py:131
  288.7 114.3 %copy-start.14 = (f32[512,8]{0,1:T(8,128)}, f32[512,8]{0,1:T(8,128)S(1)}, u32[]{:S(2)}) copy-start(f32[512,8]{0,1:T(8,128)S(1)} %stack.20) | copy-start | bytes 49156
  288.7 114.2 %copy-start.18 = (pred[8,1024]{1,0:T(8,128)(4,1)}, pred[8,1024]{1,0:T(8,128)(4,1)S(1)}, u32[]{:S(2)}) copy-start(pred[8,1024]{1,0:T(8,128)(4,1)S(1)} %broadcast_compare_fusion) | copy-start | bytes 24580
  366.2 4.4 collective-permute-start.2
  366.3 4.8 collective-permute-start.3
  368.1 34.7 %copy-start.10 = (f32[1,8,1024]{2,0,1:T(1,128)}, f32[1,8,1024]{2,0,1:T(1,128)S(1)}, u32[]{:S(2)}) copy-start(f32[1,8,1024]{2,0,1:T(1,128)S(1)} %slice.516) | copy-start | bytes 98308
  373.1 4.6 collective-permute-start.4
  374.3 3.8 collective-permute-start.5
  379.8 23.1 %copy-start.16 = (f32[8,1024]{1,0:T(8,128)S(1)}, f32[8,1024]{1,0:T(8,128)}, u32[]{:S(2)}) copy-start(f32[8,1024]{1,0:T(8,128)} %param.7) | copy-start | bytes 98308
  380.1 4.6 collective-permute-start.6
  381.4 3.7 collective-permute-start.7
  386.1 39.4 %copy-start.4 = (f32[4,8,64,16]{3,2,1,0:T(8,128)}, f32[4,8,64,16]{3,2,1,0:T(8,128)S(1)}, u32[]{:S(2)}) copy-start(f32[4,8,64,16]{3,2,1,0:T(8,128)S(1)} %fusion.49) | copy-start | bytes 393220
  441.9 26.7 %copy-start.1 = (f32[512,8,1024]{0,2,1:T(8,128)S(1)}, f32[512,8,1024]{0,2,1:T(8,128)}, u32[]{:S(2)}) copy-start(f32[512,8,1024]{0,2,1:T(8,128)} %copy.221) | copy-start | bytes 50331652
  480.7 21.2 %slice-start = ((s8[16515072]{0:T(1024)(128)(4,1)}), s8[4194304]{0:T(1024)(128)(4,1)S(1)}, s32[]{:S(2)}) async-start(s8[16515072]{0:T(1024)(128)(4,1)} %bitcast.111), calls=%async_computation.2 | async-start | bytes 8388608
  485.7 122.9 %collective-permute-start.8 = (f32[512,1,1024]{2,0,1:T(8,128)}, f32[512,1,1024]{2,0,1:T(8,128)}, u32[]{:S(2)}, u32[]{:S(2)}) collective-permute-start(f32[512,1,1024]{2,0,1:T(8,128)} %get-tuple-element.27), channel_id=1, source_target_pairs={{0,1},{1,2},{2,3},{3,0},{4,5},{5,6},{6,7},{7,4},{8,9},{9,10},{10,1... | collective-permute-start | bytes 6291464 | tf_op jit(solution)/shard_map/ppermute | solution.py:28
  487.3 121.3 %collective-permute-start.9 = (f32[512,1,1024]{2,0,1:T(8,128)}, f32[512,1,1024]{2,0,1:T(8,128)}, u32[]{:S(2)}, u32[]{:S(2)}) collective-permute-start(f32[512,1,1024]{2,0,1:T(8,128)} %get-tuple-element.28), channel_id=1, source_target_pairs={{1,0},{2,1},{3,2},{0,3},{5,4},{6,5},{7,6},{4,7},{9,8},{10,9},{11,1... | collective-permute-start | bytes 6291464 | tf_op jit(solution)/shard_map/ppermute | solution.py:29
  592.1 16.5 %copy-start.33 = (pred[512]{0:T(512)(128)(4,1)S(1)}, pred[512]{0:T(512)(128)(4,1)}, u32[]{:S(2)}) copy-start(pred[512]{0:T(512)(128)(4,1)} %copy-done.32) | copy-start | bytes 1540
  592.1 16.5 %copy-start.35 = (pred[512]{0:T(512)(128)(4,1)S(1)}, pred[512]{0:T(512)(128)(4,1)}, u32[]{:S(2)}) copy-start(pred[512]{0:T(512)(128)(4,1)} %copy-done.34) | copy-start | bytes 1540
  592.1 16.5 %copy-start.37 = (pred[512]{0:T(512)(128)(4,1)S(1)}, pred[512]{0:T(512)(128)(4,1)}, u32[]{:S(2)}) copy-start(pred[512]{0:T(512)(128)(4,1)} %copy-done.36) | copy-start | bytes 1540
  670.0 18.5 %copy-start.7 = (f32[13,8,1024]{2,0,1:T(8,128)S(1)}, f32[13,8,1024]{2,0,1:T(8,128)}, u32[]{:S(2)}) copy-start(f32[13,8,1024]{2,0,1:T(8,128)} %copy-done.6) | copy-start | bytes 1277956
  670.0 18.6 %copy-start.5 = (f32[4,8,64,16]{3,2,1,0:T(8,128)S(1)}, f32[4,8,64,16]{3,2,1,0:T(8,128)}, u32[]{:S(2)}) copy-start(f32[4,8,64,16]{3,2,1,0:T(8,128)} %copy-done.4) | copy-start | bytes 393220
  670.0 19.3 %copy-start.8 = (f32[13,8,1024]{2,0,1:T(8,128)S(1)}, f32[13,8,1024]{2,0,1:T(8,128)}, u32[]{:S(2)}) copy-start(f32[13,8,1024]{2,0,1:T(8,128)} %all-reduce.5.cloned.1.call-done) | copy-start | bytes 1277956
  670.0 19.3 %copy-start.11 = (f32[1,8,1024]{2,0,1:T(1,128)S(1)}, f32[1,8,1024]{2,0,1:T(1,128)}, u32[]{:S(2)}) copy-start(f32[1,8,1024]{2,0,1:T(1,128)} %copy-done.10) | copy-start | bytes 98308
  763.2 4.4 collective-permute-start.10
  763.3 4.8 collective-permute-start.11
  770.0 4.6 collective-permute-start.12
  771.3 3.8 collective-permute-start.13
  775.1 20.2 %copy-start.21 = (f32[512,1]{0,1:T(1,128)S(1)}, f32[512,1]{0,1:T(1,128)}, u32[]{:S(2)}) copy-start(f32[512,1]{0,1:T(1,128)} %copy-done.20) | copy-start | bytes 6148
  777.1 4.6 collective-permute-start.14
  778.5 3.4 collective-permute-start.15
  811.1 16.6 %copy-start.15 = (f32[512,8]{0,1:T(8,128)S(1)}, f32[512,8]{0,1:T(8,128)}, u32[]{:S(2)}) copy-start(f32[512,8]{0,1:T(8,128)} %copy-done.14) | copy-start | bytes 49156
  811.2 16.6 %copy-start.17 = (f32[8,1024]{1,0:T(8,128)S(1)}, f32[8,1024]{1,0:T(8,128)}, u32[]{:S(2)}) copy-start(f32[8,1024]{1,0:T(8,128)} %param.7) | copy-start | bytes 98308
  811.2 16.6 %copy-start.19 = (pred[8,1024]{1,0:T(8,128)(4,1)S(1)}, pred[8,1024]{1,0:T(8,128)(4,1)}, u32[]{:S(2)}) copy-start(pred[8,1024]{1,0:T(8,128)(4,1)} %copy-done.18) | copy-start | bytes 24580
  (12 other events, 165.8 us)
Sparse Core Ops, SparseCore 0:
  288.7 74.3 all-reduce.4
  688.6 71.4 all-reduce.6
where the time goes:
time: 883 us; the launch traced here: 876 us
  local copies, waits for them, and re-layouts  367 us (42%)
  other arithmetic  189 us (21%)
  waiting for transfers between devices  161 us (18%)
  matrix products  117 us (13%)
  starting transfers between devices  17.2 us (2%)
  between operations  16.6 us (2%)
    psum x2, waiting for transfers between devices, shards(): totals = lax.psum(partial_moments, 'vel')  144 us
    sub x2, other arithmetic, stream(): return dist - time_step * total  90 us
    slice x8, local copies, waits for them, and re-layouts, upwind_local(): lower = jnp.roll(block, 1, axis)  89.9 us
    concatenate x4, other arithmetic, upwind_local(): lower = jnp.roll(block, 1, axis)  71.6 us
    concatenate x4, local copies, waits for them, and re-layouts, upwind_local(): lower = jnp.roll(block, 1, axis)  65.8 us
    concatenate x4, local copies, waits for them, and re-layouts, upwind_local(): higher = jnp.roll(block, -1, axis)  65.8 us
    unnamed x88, local copies, waits for them, and re-layouts  62.3 us
    dot_general x2, matrix products, shards(): jnp.dot(shakhov, flat_fields, precision=highest)  45 us
  transfers between devices with their start and end apart: 18, of which 14 were waited for; matrix products, arithmetic and copies ran while one was open for 34% of the time, Pallas kernels for 0%

commit v1 on v0

v1 whole, which is shorter than its diff:
```python
import functools
import math

import jax
import jax.numpy as jnp
import numpy as np
from jax import lax
from jax.experimental import pallas as pl
from jax.experimental.pallas import tpu as pltpu
from jax.sharding import PartitionSpec as P

NVX = 16
NZ = 16
MOM = 13
SWEEPS = 3
LANES = 128
SUB = 8
SETS = 7
PICK = (0, 1, 2, 3, 4, 10, 11, 12)

speed_range = 4.0
time_step = 0.08
coupling = 0.5
MIB = 2**20

UP, M1, DOWN, AA, PAY = 0, 40, 144, 184, 288


def functions_of(cx, cy, cz):
    square = cx * cx + cy * cy + cz * cz
    heat = square - 2.5
    one = cx * 0.0 + 1.0
    rows = [
        one, cx, cy, cz, 2.0 * square / 3.0 - 1.0, 2.0 * cx * cy, 2.0 * cx * cz, 2.0 * cy * cz,
        cx * cx - cy * cy, cy * cy - cz * cz, cx * heat, cy * heat, cz * heat,
    ]
    factor = 4.0 / 15.0
    shakhov = [
        one, 2.0 * cx, 2.0 * cy, 2.0 * cz, square - 1.5,
        factor * cx * heat, factor * cy * heat, factor * cz * heat,
    ]
    return rows, shakhov, square


def half_speeds(cx, cy, cz):
    out = []
    for c in (cx, cy, cz):
        out.append(time_step * c * (c > 0))
        out.append(-time_step * c * (c < 0))
    return out


@functools.lru_cache(None)
def stream_matrices():
    line = speed_range * (2.0 * np.arange(NVX) + 1.0 - NVX) / NVX
    cx, cy, cz = (g.reshape(-1) for g in np.meshgrid(line, line, line, indexing="ij"))
    rows, shakhov, square = functions_of(cx, cy, cz)
    weight = (2.0 * speed_range / NVX) ** 3 * math.pi ** (-1.5) * np.exp(-square)
    rows = np.stack(rows) * weight
    shakhov = np.stack(shakhov)
    speeds = half_speeds(cx, cy, cz)
    stay = 1.0 - sum(speeds)
    out = np.stack([(rows * s) @ shakhov.T for s in [stay] + speeds])
    out[np.abs(out) < 1e-13] = 0.0
    return out


def split(value):
    high = value.astype(jnp.bfloat16)
    low = (value - high.astype(jnp.float32)).astype(jnp.bfloat16)
    return high, low


class Group:
    def __init__(self, tx, ty, tz):
        self.ax, self.ay, self.az = jnp.abs(tx), jnp.abs(ty), jnp.abs(tz)
        self.stay = 1.0 - self.ax - self.ay - self.az
        self.px = tx > 0
        py, pz = ty > 0, tz > 0
        lane = lax.broadcasted_iota(jnp.int32, tx.shape, 1)
        zl = lane & (NZ - 1)
        self.zfrom = jnp.where(
            pz,
            jnp.where(zl == 0, lane + (NZ - 1), lane - 1),
            jnp.where(zl == NZ - 1, lane - (NZ - 1), lane + 1),
        )
        self.yfrom = jnp.where(py, (lane - NZ) & (LANES - 1), (lane + NZ) & (LANES - 1))
        self.lower = py & (lane >= LANES - NZ)
        self.higher = jnp.logical_not(py) & (lane < NZ)

    def across(self, row):
        count = len(row)
        out = []
        for k in range(count):
            beside = jnp.where(
                self.lower, row[(k - 1) % count], jnp.where(self.higher, row[(k + 1) % count], row[k])
            )
            in_y = jnp.take_along_axis(beside, self.yfrom, axis=1)
            in_z = jnp.take_along_axis(row[k], self.zfrom, axis=1)
            out.append(self.stay * row[k] + self.ay * in_y + self.az * in_z)
        return out

    def stream(self, planes, width, put):
        before, now, after = None, planes(0), None
        for x in range(width):
            after = planes(x + 1) if x + 1 < width else None
            mid = self.across(now)
            out = []
            for k in range(len(now)):
                lo = before[k] if before is not None else jnp.zeros_like(now[k])
                hi = after[k] if after is not None else jnp.zeros_like(now[k])
                out.append(mid[k] + self.ax * jnp.where(self.px, lo, hi))
            put(x, out, now)
            before, now = now, after


def group_at(dtc_ref, rows):
    return Group(dtc_ref[0, rows, :], dtc_ref[1, rows, :], dtc_ref[2, rows, :])


def lane_blocks(value):
    return [value[:, k * LANES : (k + 1) * LANES] for k in range(value.shape[1] // LANES)]


def roll_y(value, sign):
    cells = value.shape[1]
    return pltpu.roll(value, NZ if sign > 0 else cells - NZ, axis=1)


def roll_z(value, sign):
    cells = value.shape[1]
    zl = lax.broadcasted_iota(jnp.int32, value.shape, 1) & (NZ - 1)
    if sign > 0:
        return jnp.where(zl == 0, pltpu.roll(value, cells - (NZ - 1), axis=1), pltpu.roll(value, 1, axis=1))
    return jnp.where(zl == NZ - 1, pltpu.roll(value, NZ - 1, axis=1), pltpu.roll(value, cells - 1, axis=1))


def outflow_kernel(dist_ref, dtc_ref, out_ref, *, count, blocks):
    px = dtc_ref[0] > 0
    stride = blocks * SUB
    for k in range(blocks):
        at = slice(k * LANES, (k + 1) * LANES)
        plane = [dist_ref[pl.ds(k * SUB + x, count, stride=stride), :] for x in (0, 1, SUB - 2, SUB - 1)]
        out_ref[0, :, at] = jnp.where(px, plane[3], plane[0])
        out_ref[1, :, at] = jnp.where(px, plane[2], plane[1])


def outflow(flat, dtc, vels, blocks):
    count = min(64, vels)
    rows = count * blocks * SUB
    cells = blocks * LANES
    return pl.pallas_call(
        functools.partial(outflow_kernel, count=count, blocks=blocks),
        grid=(vels // count,),
        in_specs=[
            pl.BlockSpec((rows, LANES), lambda i: (i, 0)),
            pl.BlockSpec((1, count, LANES), lambda i: (0, i, 0)),
        ],
        out_specs=pl.BlockSpec((2, count, cells), lambda i: (0, i, 0)),
        out_shape=jax.ShapeDtypeStruct((2, vels, cells), jnp.float32),
        compiler_params=pltpu.CompilerParams(vmem_limit_bytes=24 * MIB),
        cost_estimate=pl.CostEstimate(flops=0, bytes_accessed=20 * vels * blocks * SUB * LANES // 4, transcendentals=0),
        name="outflow_planes",
    )(flat, dtc)


def moments_kernel(me_ref, dist_ref, dtc_ref, index_ref, cst_ref, *refs, vels, blocks):
    outs = refs[:blocks]
    held, rhi, rlo, table, wst, acc, gacc, pay, sems = refs[blocks:]
    stride = blocks * SUB
    chunk = min(64, vels)
    chunks = vels // chunk
    copies = [
        pltpu.make_async_copy(
            dist_ref.at[pl.ds(c * chunk * stride, chunk * stride)],
            held.at[pl.ds(c * chunk * stride, chunk * stride)],
            sems.at[c],
        )
        for c in range(chunks)
    ]
    for copy in copies:
        copy.start()

    speed = [speed_range * (2.0 * index_ref[a : a + 1, :].astype(jnp.float32) + 1.0 - NVX) / NVX for a in range(3)]
    rows, _, square = functions_of(*speed)
    weight = (2.0 * speed_range / NVX) ** 3 * math.pi ** (-1.5) * jnp.exp(-square)
    table[...] = jnp.zeros_like(table)
    for m, row in enumerate(rows):
        table[m : m + 1, :] = row * weight
    base = table[...]
    speeds = []
    for c in speed:
        speeds.append(jnp.where(c > 0, time_step * c, 0.0))
        speeds.append(jnp.where(c < 0, -time_step * c, 0.0))
    full = jnp.concatenate([base] + [base * s for s in speeds], axis=0)
    span = SETS * 16
    for variant, factor in enumerate([None, speeds[0], speeds[1]]):
        high, low = split(full if factor is None else full * factor)
        wst[variant, 0:span, :] = high
        wst[variant, span : 2 * span, :] = low

    for c in range(chunks):
        copies[c].wait()

        @pl.loop(0, chunk // 16)
        def _(i, c=c):
            first = pl.multiple_of(c * chunk + i * 16, 16)
            here = pl.ds(first, 16)
            group = group_at(dtc_ref, here)
            origin = first * stride

            def planes(x):
                return [held[pl.ds(origin + k * SUB + x, 16, stride=stride), :] for k in range(blocks)]

            def put(x, blocks_out, now):
                for k, value in enumerate(blocks_out):
                    at = slice(k * LANES, (k + 1) * LANES)
                    high, low = split(value)
                    rhi[x, here, at] = high
                    rlo[x, here, at] = low
                if x in (0, SUB - 1):
                    slot = SUB if x == SUB - 1 else SUB + 1
                    for k, value in enumerate(now):
                        at = slice(k * LANES, (k + 1) * LANES)
                        high, low = split(value)
                        rhi[slot, here, at] = high
                        rlo[slot, here, at] = low

            group.stream(planes, SUB, put)

    wide = 2 * LANES

    @pl.loop(0, blocks // 2)
    def _(b):
        at = pl.ds(pl.multiple_of(b * wide, wide), wide)
        for slot in range(SUB + 2):
            variant = max(0, slot - SUB + 1)
            first = jnp.dot(wst[variant], rhi[slot, :, at], preferred_element_type=jnp.float32)
            second = jnp.dot(wst[variant, 0:span, :], rlo[slot, :, at], preferred_element_type=jnp.float32)
            total = first[0:span] + first[span:] + second
            if slot < SUB:
                for j in range(2):
                    acc[2 * b + j, pl.ds(slot, span, stride=SUB), :] = total[:, j * LANES : (j + 1) * LANES]
            else:
                gacc[slot - SUB, :, at] = total

    al = cst_ref[0, 0:SUB, :]
    beyond = cst_ref[0, SUB : SUB + 1, :]
    below = cst_ref[0, 2 * SUB - 1 : 2 * SUB, :]
    plane = lax.broadcasted_iota(jnp.int32, al.shape, 0)

    def own(i, m):
        first = (i * 16 + m) * SUB
        return jnp.concatenate([acc[k, first : first + SUB, :] for k in range(blocks)], axis=1)

    for m in range(MOM):
        sets = [own(i, m) for i in range(SETS)]
        value = al * (sets[0] - sum(sets[1:]))
        value = value + jnp.where(plane == 0, 0.0, pltpu.roll(al * sets[1], 1, axis=0))
        value = value + jnp.where(plane == SUB - 1, 0.0, pltpu.roll(al * sets[2], SUB - 1, axis=0))
        value = value + roll_y(al * sets[3], 1) + roll_y(al * sets[4], -1)
        value = value + roll_z(al * sets[5], 1) + roll_z(al * sets[6], -1)
        for k in range(blocks):
            at = slice(k * LANES, (k + 1) * LANES)
            pay[k, M1 + m * SUB : M1 + (m + 1) * SUB, :] = sets[0][:, at]
            pay[k, AA + m * SUB : AA + (m + 1) * SUB, :] = value[:, at]

    for side, (scale, edge, toward, start) in enumerate([(beyond, SUB - 1, 1, UP), (below, 0, 2, DOWN)]):
        sets = [gacc[side, i * 16 : (i + 1) * 16, :] for i in range(SETS)]
        near = scale * (sets[0] - sum(sets[1:]))
        near = near + roll_y(scale * sets[3], 1) + roll_y(scale * sets[4], -1)
        near = near + roll_z(scale * sets[5], 1) + roll_z(scale * sets[6], -1)
        out_of = jnp.concatenate(
            [acc[k, pl.ds(toward * 16 * SUB + edge, 16, stride=SUB), :] for k in range(blocks)], axis=1
        )
        near = near + al[edge : edge + 1, :] * out_of
        far = scale * sets[toward]
        for k in range(blocks):
            at = slice(k * LANES, (k + 1) * LANES)
            for j, value in enumerate((sets[0], near, far)):
                pay[k, start + j * MOM : start + (j + 1) * MOM, :] = value[0:MOM, at]
            pay[k, start + 3 * MOM : start + 3 * MOM + 1, :] = jnp.zeros((1, LANES), jnp.float32)

    mine = me_ref[0]
    for k in range(blocks):
        outs[k][...] = pay[lax.rem(mine + k, blocks)]


def both_moments(place, flat, dtc, vel_index, cst, vels, blocks):
    cells = blocks * LANES
    vmem = pl.BlockSpec(memory_space=pltpu.VMEM)
    span = SETS * 16
    chunks = vels // min(64, vels)
    return pl.pallas_call(
        functools.partial(moments_kernel, vels=vels, blocks=blocks),
        in_specs=[pl.BlockSpec(memory_space=pltpu.SMEM), pl.BlockSpec(memory_space=pl.ANY), vmem, vmem, vmem],
        out_specs=[vmem] * blocks,
        out_shape=[jax.ShapeDtypeStruct((PAY, LANES), jnp.float32)] * blocks,
        scratch_shapes=[
            pltpu.VMEM((vels * blocks * SUB, LANES), jnp.float32),
            pltpu.VMEM((SUB + 2, vels, cells), jnp.bfloat16),
            pltpu.VMEM((SUB + 2, vels, cells), jnp.bfloat16),
            pltpu.VMEM((16, vels), jnp.float32),
            pltpu.VMEM((3, 2 * span, vels), jnp.bfloat16),
            pltpu.VMEM((blocks, span * SUB, LANES), jnp.float32),
            pltpu.VMEM((2, span, cells), jnp.float32),
            pltpu.VMEM((blocks, PAY, LANES), jnp.float32),
            pltpu.SemaphoreType.DMA((chunks,)),
        ],
        compiler_params=pltpu.CompilerParams(vmem_limit_bytes=54 * MIB),
        cost_estimate=pl.CostEstimate(
            flops=2 * 336 * vels * 10 * cells, bytes_accessed=4 * vels * SUB * cells, transcendentals=0
        ),
        name="moments_of_both",
    )(place, flat, dtc, vel_index, cst)


def carried_kernel(dist_ref, dtc_ref, al_ref, out_ref, mid, *, count, blocks):
    stride = blocks * SUB

    @pl.loop(0, count // SUB)
    def _(i):
        first = pl.multiple_of(i * SUB, SUB)
        here = pl.ds(first, SUB)
        group = group_at(dtc_ref, here)
        origin = first * stride

        def planes(x):
            return [dist_ref[pl.ds(origin + k * SUB + x, SUB, stride=stride), :] for k in range(blocks)]

        def scaled(x, k):
            return al_ref[x : x + 1, k * LANES : (k + 1) * LANES]

        def put_mid(x, values, now):
            for k, value in enumerate(values):
                mid[x, k] = scaled(x, k) * value

        def put_out(x, values, now):
            for k, value in enumerate(values):
                out_ref[k, x, here, :] = scaled(x, k) * value

        group.stream(planes, SUB, put_mid)
        group.stream(lambda x: [mid[x, k] for k in range(blocks)], SUB, put_out)


def carried(flat, dtc, al, vels, blocks):
    count = min(64, vels)
    rows = count * blocks * SUB
    return pl.pallas_call(
        functools.partial(carried_kernel, count=count, blocks=blocks),
        grid=(vels // count,),
        in_specs=[
            pl.BlockSpec((rows, LANES), lambda i: (i, 0)),
            pl.BlockSpec((3, count, LANES), lambda i: (0, i, 0)),
            pl.BlockSpec((SUB, blocks * LANES), lambda i: (0, 0)),
        ],
        out_specs=pl.BlockSpec((blocks, SUB, count, LANES), lambda i: (0, 0, i, 0)),
        out_shape=jax.ShapeDtypeStruct((blocks, SUB, vels, LANES), jnp.float32),
        scratch_shapes=[pltpu.VMEM((SUB, blocks, SUB, LANES), jnp.float32)],
        compiler_params=pltpu.CompilerParams(vmem_limit_bytes=24 * MIB),
        cost_estimate=pl.CostEstimate(
            flops=40 * vels * blocks * SUB * LANES, bytes_accessed=8 * vels * blocks * SUB * LANES, transcendentals=0
        ),
        name="carried_part",
    )(flat, dtc, al)


def inflow_kernel(core_ref, swap_ref, first_ref, second_ref, dtc_ref, al_ref, out_ref, *, count, blocks, half):
    core = core_ref[0]
    mine = (pl.program_id(0) // half) == core

    @pl.loop(0, count // SUB)
    def _(i):
        here = pl.ds(pl.multiple_of(i * SUB, SUB), SUB)
        group = group_at(dtc_ref, here)
        from_far = group.px == (core == 0)

        def halo(depth):
            far = jnp.where(mine, first_ref[depth, here, :], second_ref[depth, here, :])
            near = swap_ref[depth, here, :]
            return [jnp.where(from_far, a, b) for a, b in zip(lane_blocks(far), lane_blocks(near))]

        def scale(k, when_up, when_down):
            at = slice(k * LANES, (k + 1) * LANES)
            return jnp.where(group.px, al_ref[when_up : when_up + 1, at], al_ref[when_down : when_down + 1, at])

        near, far = halo(0), halo(1)
        edge = [scale(k, 0, SUB - 1) * group.ax * near[k] for k in range(blocks)]
        beyond = group.across(near)
        inside = group.across(edge)
        for k in range(blocks):
            streamed = beyond[k] + group.ax * far[k]
            value = inside[k] + group.ax * scale(k, 2 * SUB - 1, SUB) * streamed
            out_ref[k, 0, here, :] = scale(k, 0, SUB - 1) * value
            out_ref[k, 1, here, :] = scale(k, 1, SUB - 2) * group.ax * edge[k]


def inflow(core, swap, first, second, dtc, al16, vels, blocks):
    halves = vels // first.shape[1]
    count = min(64, first.shape[1])
    half = first.shape[1] // count
    cells = blocks * LANES
    narrow = pl.BlockSpec((2, count, cells), lambda i: (0, i % half, 0))
    return pl.pallas_call(
        functools.partial(inflow_kernel, count=count, blocks=blocks, half=half),
        grid=(vels // count,),
        in_specs=[
            pl.BlockSpec(memory_space=pltpu.SMEM),
            pl.BlockSpec((2, count, cells), lambda i: (0, i, 0)),
            narrow,
            narrow,
            pl.BlockSpec((3, count, LANES), lambda i: (0, i, 0)),
            pl.BlockSpec((2 * SUB, cells), lambda i: (0, 0)),
        ],
        out_specs=pl.BlockSpec((blocks, 2, count, LANES), lambda i: (0, 0, i, 0)),
        out_shape=jax.ShapeDtypeStruct((blocks, 2, vels, LANES), jnp.float32),
        compiler_params=pltpu.CompilerParams(vmem_limit_bytes=24 * MIB),
        cost_estimate=pl.CostEstimate(flops=60 * vels * cells, bytes_accessed=24 * vels * cells, transcendentals=0),
        name="inflow_part",
    )(core, swap, first, second, dtc, al16)


def small_call(kernel, outs, name, specs, args, scratch=(), limit=16):
    vmem = pl.BlockSpec(memory_space=pltpu.VMEM)
    smem = pl.BlockSpec(memory_space=pltpu.SMEM)
    return pl.pallas_call(
        kernel,
        in_specs=[smem if s == "s" else vmem for s in specs],
        out_specs=[vmem] * len(outs),
        out_shape=[jax.ShapeDtypeStruct(o, jnp.float32) for o in outs],
        scratch_shapes=list(scratch),
        compiler_params=pltpu.CompilerParams(vmem_limit_bytes=limit * MIB),
        name=name,
    )(*args)


def total_kernel(*refs):
    parts, (all_ref, up_ref, down_ref) = refs[:-3], refs[-3:]
    value = parts[0][...]
    for part in parts[1:]:
        value = value + part[...]
    all_ref[...] = value
    up_ref[...] = value[UP:DOWN]
    down_ref[...] = value[M1:AA]


def mix(inverse, values):
    return [sum(inverse[k, j] * values[j] for j in range(MOM)) for k in range(MOM)]


def chunk_kernel(inv_ref, own_ref, low_ref, high_ref, send_ref, keep_ref):
    plane = lax.broadcasted_iota(jnp.int32, (SUB, LANES), 0)
    inverse = {(k, j): inv_ref[k, j] for k in range(MOM) for j in range(MOM)}
    inner, outer, later = [], [], []
    for m in range(MOM):

        def row(ref, at):
            return ref[at : at + 1, :]

        first = own_ref[M1 + m * SUB : M1 + (m + 1) * SUB, :]
        second = own_ref[AA + m * SUB : AA + (m + 1) * SUB, :]
        low = low_ref[M1 + m * SUB : M1 + (m + 1) * SUB, :]
        high = high_ref[m * SUB : (m + 1) * SUB, :]
        below = DOWN - M1 + m
        inner.append(
            first + jnp.where(plane == 0, row(low_ref, m), 0.0) + jnp.where(plane == SUB - 1, row(high_ref, below), 0.0)
        )
        outer.append(
            jnp.where(plane < SUB // 2, high, low)
            + jnp.where(plane == 0, row(own_ref, UP + m), 0.0)
            + jnp.where(plane == SUB - 1, row(own_ref, DOWN + m), 0.0)
        )
        later.append(
            second
            + jnp.where(plane == 0, row(low_ref, MOM + m), 0.0)
            + jnp.where(plane == 1, row(low_ref, 2 * MOM + m), 0.0)
            + jnp.where(plane == SUB - 1, row(high_ref, below + MOM), 0.0)
            + jnp.where(plane == SUB - 2, row(high_ref, below + 2 * MOM), 0.0)
        )
    local, around, ahead = (mix(inverse, v) for v in (inner, outer, later))
    for n, k in enumerate(PICK):
        send_ref[n * 16 : n * 16 + SUB, :] = local[k]
        send_ref[n * 16 + SUB : (n + 1) * 16, :] = around[k]
        send_ref[128 + n * SUB : 128 + (n + 1) * SUB, :] = ahead[k]
    for m in range(MOM):
        for n, values in enumerate((inner, local, later, ahead)):
            keep_ref[(n * MOM + m) * SUB : (n * MOM + m + 1) * SUB, :] = values[m]


def sweeps(source):
    rows = source.shape[0]
    field = source
    for _ in range(SWEEPS):
        beside = pltpu.roll(field, 1, axis=0) + pltpu.roll(field, rows - 1, axis=0)
        beside = beside + roll_y(field, 1) + roll_y(field, -1) + roll_z(field, 1) + roll_z(field, -1)
        field = (source + coupling * beside) * (1.0 / (1.0 + 6.0 * coupling))
    return field


def fields_kernel(place_ref, inv_ref, cst_ref, keep_ref, *refs, blocks):
    parts = refs[:blocks]
    h1_ref, next_ref, up_ref, down_ref, own_ref, norm_ref, whole, wide = refs[blocks:]
    mine = place_ref[0]
    for k in range(blocks):
        whole[lax.rem(mine + (blocks - k), blocks)] = parts[k][...]

    def rows(first, count):
        return jnp.concatenate([whole[k, first : first + count, :] for k in range(blocks)], axis=1)

    al = cst_ref[0, 0:SUB, :]
    updated, moved = [], []
    for n in range(8):
        value = rows(n * 16, 16)
        if 1 <= n <= 4:
            value = sweeps(value)
        updated.append(value[0:SUB])
        given = cst_ref[1 if n in (0, 4) else 2] * value
        inside = given[0:SUB]
        shifted = [
            inside,
            pltpu.roll(given, 1, axis=0)[0:SUB],
            pltpu.roll(given, 2 * SUB - 1, axis=0)[0:SUB],
            roll_y(inside, 1),
            roll_y(inside, -1),
            roll_z(inside, 1),
            roll_z(inside, -1),
        ]
        for s in range(SETS):
            value = al * shifted[s]
            for k in range(blocks):
                first = (s * 8 + n) * SUB
                h1_ref[k, first : first + SUB, :] = value[:, k * LANES : (k + 1) * LANES]
        moved.append(shifted)

    matrices = stream_matrices()
    added = []
    for m in range(MOM):
        value = None
        for s in range(SETS):
            for n in range(8):
                factor = float(matrices[s, m, n])
                if factor != 0.0:
                    term = factor * moved[n][s]
                    value = term if value is None else value + term
        added.append(value)
    inverse = {(k, j): inv_ref[k, j] for k in range(MOM) for j in range(MOM)}
    mixed = mix(inverse, added)

    for n, k in enumerate(PICK):
        value = rows(128 + n * SUB, SUB) + mixed[k]
        next_ref[n * SUB : (n + 1) * SUB, :] = value
        if 1 <= n <= 4:
            up_ref[(n - 1) * 4 : n * 4, :] = value[SUB // 2 :]
            down_ref[(n - 1) * 4 : n * 4, :] = value[: SUB // 2]

    def keep(n, m):
        return keep_ref[(n * MOM + m) * SUB : (n * MOM + m + 1) * SUB, :]

    def owned(value):
        for k in range(blocks):
            wide[k] = value[:, k * LANES : (k + 1) * LANES]
        return wide[mine]

    square = jnp.zeros((SUB, LANES), jnp.float32)
    for m in range(MOM):
        mine_now = owned(updated[m]) if 1 <= m <= 4 else keep(1, m)
        square = square + (mine_now - keep(0, m)) ** 2
        own_ref[m * SUB : (m + 1) * SUB, :] = keep(2, m) + owned(added[m])
        own_ref[(MOM + m) * SUB : (MOM + m + 1) * SUB, :] = keep(3, m) + owned(mixed[m])
    norm_ref[...] = square


def last_kernel(place_ref, cst_ref, next_ref, low_ref, high_ref, own_ref, h2_ref, out_ref, norm_ref, wide, *, blocks):
    mine = place_ref[0]
    square = jnp.zeros((SUB, LANES), jnp.float32)
    for n in range(8):
        value = next_ref[n * SUB : (n + 1) * SUB, :]
        if 1 <= n <= 4:
            at = slice((n - 1) * 4, n * 4)
            value = sweeps(jnp.concatenate([value, high_ref[at, :], low_ref[at, :]], axis=0))[0:SUB]
            for k in range(blocks):
                wide[n - 1, k] = value[:, k * LANES : (k + 1) * LANES]
        given = cst_ref[1 if n in (0, 4) else 2, 0:SUB, :] * value
        for k in range(blocks):
            h2_ref[k, n * SUB : (n + 1) * SUB, :] = given[:, k * LANES : (k + 1) * LANES]
    for m in range(MOM):
        moments = own_ref[m * SUB : (m + 1) * SUB, :]
        if 1 <= m <= 4:
            value = wide[m - 1, mine]
        else:
            value = own_ref[(MOM + m) * SUB : (MOM + m + 1) * SUB, :]
        out_ref[m] = value
        square = square + (value - moments) ** 2
    norm_ref[...] = square


def finish_kernel(carried_ref, inflow_ref, h1_ref, h2_ref, rows_ref, dtc_ref, out_ref, *, vels):
    out = out_ref.reshape(vels * SUB, LANES)
    px = dtc_ref[0] > 0
    for x in range(0, SUB, 2):
        field = jnp.concatenate(
            [
                jnp.concatenate(
                    [h1_ref[0, pl.ds(x + j, SETS * 8, stride=SUB), :], h2_ref[0, pl.ds(x + j, 8, stride=SUB), :]], axis=0
                )
                for j in range(2)
            ],
            axis=1,
        )
        high, low = split(field)
        term = jnp.dot(
            rows_ref[...], jnp.concatenate([high, low, high], axis=0), preferred_element_type=jnp.float32
        )
        for j in range(2):
            value = carried_ref[0, x + j] + term[:, j * LANES : (j + 1) * LANES]
            if x + j in (0, 1):
                value = value + jnp.where(px, inflow_ref[0, x + j], 0.0)
            elif x + j in (SUB - 2, SUB - 1):
                value = value + jnp.where(px, 0.0, inflow_ref[0, SUB - 1 - x - j])
            out[pl.ds(x + j, vels, stride=SUB), :] = value


def finish(carried_part, inflow_part, h1, h2, rows, dtc, vels, blocks):
    return pl.pallas_call(
        functools.partial(finish_kernel, vels=vels),
        grid=(blocks,),
        in_specs=[
            pl.BlockSpec((1, SUB, vels, LANES), lambda k: (k, 0, 0, 0)),
            pl.BlockSpec((1, 2, vels, LANES), lambda k: (k, 0, 0, 0)),
            pl.BlockSpec((1, SETS * 8 * SUB, LANES), lambda k: (k, 0, 0)),
            pl.BlockSpec((1, 8 * SUB, LANES), lambda k: (k, 0, 0)),
            pl.BlockSpec((vels, 3 * 64), lambda k: (0, 0)),
            pl.BlockSpec((1, vels, LANES), lambda k: (0, 0, 0)),
        ],
        out_specs=pl.BlockSpec((vels, 1, SUB, LANES), lambda k: (0, k, 0, 0)),
        out_shape=jax.ShapeDtypeStruct((vels, blocks, SUB, LANES), jnp.float32),
        compiler_params=pltpu.CompilerParams(vmem_limit_bytes=32 * MIB),
        cost_estimate=pl.CostEstimate(
            flops=2 * 192 * vels * blocks * SUB * LANES, bytes_accessed=8 * vels * blocks * SUB * LANES, transcendentals=0
        ),
        name="finish_dist",
    )(carried_part, inflow_part, h1, h2, rows, dtc)


def ring(axis, step):
    size = lax.axis_size(axis)
    return [(i, (i + step) % size) for i in range(size)]


def shards(dist, vel_index, relax, wall_mask, macro_inverse):
    vels, width, cells = dist.shape
    blocks = cells // LANES
    peers, slabs = lax.axis_size("vel"), lax.axis_size("space")
    assert width == SUB and peers % blocks == 0 and slabs == 4 and blocks % 2 == 0
    sub = peers // blocks
    me = lax.axis_index("vel")
    place = (me // sub).astype(jnp.int32).reshape(1)
    core = (lax.axis_index("space") % 2).astype(jnp.int32).reshape(1)

    flat = dist.reshape(vels, width, blocks, LANES).transpose(0, 2, 1, 3).reshape(vels * blocks * width, LANES)
    speed = speed_range * (2.0 * vel_index.astype(jnp.float32) + 1.0 - NVX) / NVX
    dtc = jnp.broadcast_to((time_step * speed)[:, :, None], (3, vels, LANES))

    leaving = outflow(flat, dtc, vels, blocks)
    swap = lax.ppermute(leaving, "space", [(i, i ^ 1) for i in range(slabs)])

    wall = wall_mask > 0
    coefficients = jnp.stack(
        [
            jnp.where(wall, 0.0, 1.0 - relax),
            jnp.where(wall, 1.0, relax),
            jnp.where(wall, 0.0, relax),
        ],
        0,
    )
    from_low = lax.ppermute(coefficients[:, SUB - 1 :], "space", ring("space", 1))
    from_high = lax.ppermute(coefficients[:, :1], "space", ring("space", -1))
    cst = jnp.concatenate(
        [coefficients, from_high, jnp.zeros((3, SUB - 2, cells), jnp.float32), from_low], 1
    )

    half = vels // 2
    start = core[0] * half
    mine = lax.dynamic_slice_in_dim(leaving, start, half, 1)
    other = lax.dynamic_slice_in_dim(swap, start, half, 1)
    plus = lax.dynamic_slice_in_dim(speed[0], start, half, 0) > 0
    across = jnp.where((plus == (core[0] == 1))[None, :, None], mine, other)
    first = lax.ppermute(across, "space", [(i, i ^ 2) for i in range(slabs)])
    second = lax.ppermute(first, "space", [(i, i ^ 1) for i in range(slabs)])

    parts = both_moments(place, flat, dtc, vel_index, cst, vels, blocks)
    got = [parts[0]] + [lax.ppermute(parts[k], "vel", ring("vel", k * sub)) for k in range(1, blocks)]
    if sub > 1:
        part = sum(got)
        got = [part]
        for k in range(1, sub):
            pairs = [(i, i // sub * sub + (i % sub + k) % sub) for i in range(peers)]
            got.append(lax.ppermute(part, "vel", pairs))
    chunk, up, down = small_call(
        total_kernel, [(PAY, LANES), (DOWN - UP, LANES), (AA - M1, LANES)], "sum_moments", "v" * len(got), got
    )
    low = lax.ppermute(up, "space", ring("space", 1))
    high = lax.ppermute(down, "space", ring("space", -1))
    send, keep = small_call(
        chunk_kernel, [(192, LANES), (4 * MOM * SUB, LANES)], "local_fields", "svvv", (macro_inverse, chunk, low, high)
    )
    pieces = [send] + [lax.ppermute(send, "vel", ring("vel", k * sub)) for k in range(1, blocks)]

    carried_part = carried(flat, dtc, coefficients[0], vels, blocks)

    h1, following, up2, down2, own, norm1 = small_call(
        functools.partial(fields_kernel, blocks=blocks),
        [
            (blocks, SETS * 8 * SUB, LANES),
            (8 * SUB, cells),
            (16, cells),
            (16, cells),
            (2 * MOM * SUB, LANES),
            (SUB, LANES),
        ],
        "first_fields",
        "ssvv" + "v" * blocks,
        (place, macro_inverse, cst, keep, *pieces),
        [pltpu.VMEM((blocks, 192, LANES), jnp.float32), pltpu.VMEM((blocks, SUB, LANES), jnp.float32)],
        32,
    )
    low2 = lax.ppermute(up2, "space", ring("space", 1))
    high2 = lax.ppermute(down2, "space", ring("space", -1))
    h2, owned, norm2 = small_call(
        functools.partial(last_kernel, blocks=blocks),
        [(blocks, 8 * SUB, LANES), (MOM, SUB, LANES), (SUB, LANES)],
        "last_fields",
        "svvvvv",
        (place, cst, following, low2, high2, own),
        [pltpu.VMEM((4, blocks, SUB, LANES), jnp.float32)],
        32,
    )
    squares = jnp.stack([jnp.sum(norm1), jnp.sum(norm2)]) / sub
    norms = jnp.sqrt(lax.psum(squares, ("vel", "space")))
    if sub > 1:
        owned = lax.dynamic_slice_in_dim(owned, (me % sub) * (LANES // sub), LANES // sub, 2)

    speeds = half_speeds(*[speed[a][:, None] for a in range(3)])
    basis = jnp.stack(functions_of(*speed)[1], 1)
    stay = 1.0 - sum(speeds)
    rows = jnp.concatenate([basis * s for s in [stay] + speeds] + [basis], 1)
    rows_high = lax.reduce_precision(rows, 8, 7)
    rows = jnp.concatenate([rows_high, rows_high, rows - rows_high], 1).astype(jnp.bfloat16)

    inflow_part = inflow(core, swap, first, second, dtc, cst[0], vels, blocks)
    out = finish(carried_part, inflow_part, h1, h2, rows, dtc, vels, blocks)
    out = out.transpose(0, 2, 1, 3).reshape(vels, width, cells)
    return (out, owned, norms)


def solution(mesh):
    return jax.shard_map(
        shards,
        mesh=mesh,
        in_specs=(P("vel", "space", None), P(None, "vel"), P("space", None), P("space", None), P()),
        out_specs=(P("vel", "space", None), P(None, "space", "vel"), P()),
        check_vma=False,
    )
```

time: 883 us -> 313 us (0.35)
  local copies, waits for them, and re-layouts: 367 us -> 33.9 us
  other arithmetic: 189 us -> 7.77 us
  matrix products: 117 us -> 0 us
  Pallas kernels: 0 us -> 113 us
  waiting for transfers between devices: 161 us -> 83.3 us
  blocking collectives: 8.17 us -> 37.5 us
  starting transfers between devices: 17.2 us -> 36.3 us
  between operations: 16.6 us -> 0.84 us
    psum x2 -> x0, waiting for transfers between devices: 144 us -> none  [shards(): totals = lax.psum(partial_moments, 'vel')]
    concatenate x10 -> x2, local copies, waits for them, and re-layouts: 133 us -> 3.42 us  [the longest x1 3.35 us: shards(): rows = jnp.concatenate([basis * s for s in [stay] + speeds] + [basis], 1)]
    dot_general x8 -> x0, matrix products: 117 us -> none  [the longest x2 45 us: shards(): jnp.dot(shakhov, flat_fields, precision=highest)]
    pallas_call x0 -> x9, Pallas kernels: none -> 113 us  [the longest x1 40.2 us: both_moments(): pl.pallas_call(functools.partial(moments_kernel, vels=vels, blocks=blocks...]
    slice x54 -> x0, local copies, waits for them, and re-layouts: 104 us -> none  [the longest x8 89.9 us: upwind_local(): lower = jnp.roll(block, 1, axis)]
    sub x2 -> x1, other arithmetic: 90 us -> 0.01 us  [shards(): stay = 1.0 - sum(speeds)]
    concatenate x8 -> x2, other arithmetic: 90.9 us -> 0.91 us  [the longest x1 0.76 us: shards(): jnp.concatenate([coefficients, from_high, jnp.zeros((3, SUB - 2, cells),...]
    ppermute x16 -> x23, waiting for transfers between devices: 16.9 us -> 83.3 us  [the longest x1 45.9 us: shards(): first = lax.ppermute(across, 'space', [(i, i ^ 2) for i in range(slabs)])]
  transfers between devices with their start and end apart: 18 -> 23, of which waited for: 14 -> 11; matrix products, arithmetic and copies ran while one was open for 34% -> 7% of each run, Pallas kernels for 0% -> 26%
where the time goes in v1:
time: 313 us; the launch traced here: 312 us
  Pallas kernels  113 us (36%)
  waiting for transfers between devices  83.3 us (27%)
  blocking collectives  37.5 us (12%)
  starting transfers between devices  36.3 us (12%)
  local copies, waits for them, and re-layouts  33.9 us (11%)
  other arithmetic  7.77 us (2%)
    ppermute x1, waiting for transfers between devices, shards(): first = lax.ppermute(across, 'space', [(i, i ^ 2) for i in range(slabs)])  45.9 us
    pallas_call x1, Pallas kernels, both_moments(): pl.pallas_call(functools.partial(moments_kernel, vels=vels, blocks=blocks...  40.2 us
    psum x1, blocking collectives, shards(): norms = jnp.sqrt(lax.psum(squares, ('vel', 'space')))  37.5 us
    pallas_call x1, Pallas kernels, carried(): pl.pallas_call(functools.partial(carried_kernel, count=count, blocks=bloc...  31.8 us
    unnamed x34, local copies, waits for them, and re-layouts  16.9 us
    ppermute x7, starting transfers between devices, shards(): lax.ppermute(parts[k], 'vel', ring('vel', k * sub))  15.9 us
    pallas_call x1, Pallas kernels, finish(): pl.pallas_call(functools.partial(finish_kernel, vels=vels), grid=(blocks,...  15.3 us
    ppermute x7, waiting for transfers between devices, shards(): lax.ppermute(parts[k], 'vel', ring('vel', k * sub))  14.9 us
  transfers between devices with their start and end apart: 23, of which 11 were waited for; matrix products, arithmetic and copies ran while one was open for 7% of the time, Pallas kernels for 26%

profile of v1, /device:TPU:0, one launch (start us, length us, event | category | flops | bytes accessed | tf_op | source)
XLA Modules:
  0.0 312.3 jit_solution(5302862549573456185)
XLA Ops:
  1.6 5.8 %copy-done = f32[512,8,1024]{2,1,0:T(8,128)S(1)} copy-done((f32[512,8,1024]{2,1,0:T(8,128)S(1)}, f32[512,8,1024]{2,1,0:T(8,128)}, u32[]{:S(2)}) %copy-start) | copy-done | bytes 16777240
  7.4 6.1 %outflow_planes.1 = f32[2,512,1024]{2,1,0:T(8,128)} custom-call(f32[32768,128]{1,0:T(8,128)S(1)} %bitcast.43, f32[3,512,128]{2,1,0:T(8,128)S(1)} %broadcast_in_dim.24.dtc_ref), custom_call_target="tpu_custom_call" | custom-call | bytes 20971520 | tf_op jit(solution)/shard_map/outflow_planes/pallas_call | solution.py:152
  14.0 7.0 %collective-permute-done.swap_ref = f32[2,512,1024]{2,1,0:T(8,128)} collective-permute-done((f32[2,512,1024]{2,1,0:T(8,128)}, f32[2,512,1024]{2,1,0:T(8,128)}, u32[]{:S(2)}, u32[]{:S(2)}) %collective-permute-start) | collective-permute-done | bytes 4194336 | tf_op jit(solution)/shard_map/ppermute | solution.py:665
  21.1 2.5 dynamic-slice_select_fusion
  23.5 2.9 collective-permute-start.1
  26.5 45.9 %collective-permute-done.1.first_ref = f32[2,256,1024]{2,1,0:T(8,128)S(1)} collective-permute-done((f32[2,256,1024]{2,1,0:T(8,128)S(1)}, f32[2,256,1024]{2,1,0:T(8,128)S(1)}, u32[]{:S(2)}, u32[]{:S(2)}) %collective-permute-start.1) | collective-permute-done | bytes 2097184 | tf_op jit(solution)/shard_map/ppermute | solution.py:688
  72.4 1.9 collective-permute-start.3
  74.4 1.3 collective-permute-done.3
  75.7 1.7 collective-permute-done.4
  78.2 40.2 %moments_of_both.1 = (f32[288,128]{1,0:T(8,128)}, f32[288,128]{1,0:T(8,128)}, f32[288,128]{1,0:T(8,128)}, f32[288,128]{1,0:T(8,128)}, f32[288,128]{1,0:T(8,128)}...) custom-call(s32[1]{0:T(128)} %bitcast.10.me_ref.place_ref, f32[32768,128]{1,0:T(8,128)} %bitcast.41, ...), custom_call_target="tpu_custom_call" | custom-call | flops 3523215360 | bytes 16777216 | tf_op jit(solution)/shard_map/moments_of_both/pallas_call | solution.py:294
  118.4 1.6 collective-permute-start.5
  119.9 1.6 collective-permute-start.6
  121.5 2.5 collective-permute-start.7
  124.1 1.2 collective-permute-start.8
  125.3 2.9 collective-permute-done.5.refs_1_
  128.5 2.1 collective-permute-start.10
  130.6 8.7 %collective-permute-done.7.refs_3_ = f32[288,128]{1,0:T(8,128)S(1)} collective-permute-done((f32[288,128]{1,0:T(8,128)}, f32[288,128]{1,0:T(8,128)S(1)}, u32[]{:S(2)}, u32[]{:S(2)}) %collective-permute-start.7) | collective-permute-done | bytes 147488 | tf_op jit(solution)/shard_map/ppermute | solution.py:692
  139.3 6.9 %collective-permute-start.11 = (f32[288,128]{1,0:T(8,128)}, f32[288,128]{1,0:T(8,128)S(1)}, u32[]{:S(2)}, u32[]{:S(2)}) collective-permute-start(f32[288,128]{1,0:T(8,128)} %get-tuple-element.32), channel_id=1, source_target_pairs={{0,28},{4,0},{8,4},{12,8},{16,12},{20,16},{24,20},{28,24},{1,29},{... | collective-permute-start | bytes 442376 | tf_op jit(solution)/shard_map/ppermute | solution.py:692
  146.2 3.0 collective-permute-done.11.refs_7_
  149.2 0.9 copy-done.11
  150.2 1.7 collective-permute-start.13
  152.0 2.0 collective-permute-done.12.low_ref
  154.0 0.9 local_fields.1
  154.8 5.1 %collective-permute-start.20 = (f32[192,128]{1,0:T(8,128)S(1)}, f32[192,128]{1,0:T(8,128)}, u32[]{:S(2)}, u32[]{:S(2)}) collective-permute-start(f32[192,128]{1,0:T(8,128)S(1)} %get-tuple-element.37.refs_0_), channel_id=1, source_target_pairs={{0,28},{4,0},{8,4},{12,8},{16,12},{20,16},{24,20},{28,24},{1,29},{... | collective-permute-start | bytes 294920 | tf_op jit(solution)/shard_map/ppermute | solution.py:707
  160.8 0.9 copy.60
  161.7 0.9 copy.59
  164.2 0.9 copy.56
  165.9 0.9 copy.54
  166.8 0.9 copy.53
  173.5 3.3 %concatenate.12 = f32[512,64]{1,0:T(8,128)} concatenate(f32[512,8]{1,0:T(8,128)} %copy.46, f32[512,8]{1,0:T(8,128)} %copy.47, f32[512,8]{1,0:T(8,128)} %copy.48, f32[512,8]{1,0:T(8,128)} %copy.49, f32[512,8]{1,0:T(8,128)} %copy.50, f32[512,8]{1,0:T(8,128)} %copy.51, f32[512,8]{1,0:T(8,128)} %copy.52, f32[512,1]{1,0:T(8,128)} %copy.53, f32[512,1]{1,0:T(8,128)} %copy.54, ...), dimensions={1} | concatenate | bytes 262144 | tf_op jit(solution)/shard_map/concatenate | solution.py:746
  176.9 3.5 %collective-permute-start.17 = (f32[192,128]{1,0:T(8,128)S(1)}, f32[192,128]{1,0:T(8,128)S(1)}, u32[]{:S(2)}, u32[]{:S(2)}) collective-permute-start(f32[192,128]{1,0:T(8,128)S(1)} %get-tuple-element.37.refs_0_), channel_id=1, source_target_pairs={{0,16},{4,20},{8,24},{12,28},{16,0},{20,4},{24,8},{28,12},{1,17},{... | collective-permute-start | bytes 294920 | tf_op jit(solution)/shard_map/ppermute | solution.py:707
  180.4 1.0 collective-permute-start.15
  181.4 1.1 collective-permute-start.14
  182.5 1.0 reduce-precision_convert_fusion
  183.5 5.9 %collective-permute-done.17.refs_4_ = f32[192,128]{1,0:T(8,128)S(1)} collective-permute-done((f32[192,128]{1,0:T(8,128)S(1)}, f32[192,128]{1,0:T(8,128)S(1)}, u32[]{:S(2)}, u32[]{:S(2)}) %collective-permute-start.17) | collective-permute-done | bytes 98336 | tf_op jit(solution)/shard_map/ppermute | solution.py:707
  189.5 4.5 %collective-permute-done.16.refs_3_ = f32[192,128]{1,0:T(8,128)S(1)} collective-permute-done((f32[192,128]{1,0:T(8,128)S(1)}, f32[192,128]{1,0:T(8,128)S(1)}, u32[]{:S(2)}, u32[]{:S(2)}) %collective-permute-start.16) | collective-permute-done | bytes 98336 | tf_op jit(solution)/shard_map/ppermute | solution.py:707
  194.0 0.9 copy-done.13
  194.9 4.9 %first_fields.1 = (f32[8,448,128]{2,1,0:T(8,128)S(1)}, f32[64,1024]{1,0:T(8,128)S(1)}, f32[16,1024]{1,0:T(8,128)}, f32[16,1024]{1,0:T(8,128)}, f32[208,128]{1,0:T(8,128)S(1)}, /*index=5*/f32[8,128]{1,0:T(8,128)S(1)}) custom-call(s32[1]{0:T(128)} %bitcast.10.me_ref.place_ref, f32[13,13]{1,0:T(8,128)S(1)} %copy-done.14, f32[3,16,1024]{2,1,0:T(8,128)S(1)} %copy-done.4, ...), custom_call_target="tpu_custom_call" | custom-call | tf_op jit(solution)/shard_map/first_fields/pallas_call | solution.py:426
  199.8 1.2 copy-done.5
  201.7 1.7 collective-permute-start.22
  203.6 31.8 %carried_part.1.carried_ref = f32[8,8,512,128]{3,2,1,0:T(8,128)S(1)} custom-call(f32[32768,128]{1,0:T(8,128)} %bitcast.42, f32[3,512,128]{2,1,0:T(8,128)S(1)} %copy-done.3, f32[8,1024]{1,0:T(8,128)S(1)} %get-tuple-element.56.al_ref), custom_call_target="tpu_custom_call" | custom-call | flops 167772160 | bytes 33554432 | tf_op jit(solution)/shard_map/carried_part/pallas_call | solution.py:349
  235.5 5.7 %copy-done.1 = f32[8,8,512,128]{3,2,1,0:T(8,128)} copy-done((f32[8,8,512,128]{3,2,1,0:T(8,128)}, f32[8,8,512,128]{3,2,1,0:T(8,128)S(1)}, u32[]{:S(2)}) %copy-start.1) | copy-done | bytes 16777240
  241.8 0.9 copy-done.10
  242.8 3.1 last_fields.1
  247.2 1.3 pad_maximum_fusion.5
  248.5 37.5 %psum.7 = f32[2]{0:T(128)S(1)} all-reduce(f32[2]{0:T(128)S(1)} %pad_maximum_fusion.5), channel_id=1, replica_groups=mesh['vel'=8,'space'=4] {'vel','space'}, use_global_device_ids=true, to_apply=%region_2.3 | all-reduce | flops 2 | bytes 16 | tf_op jit(solution)/shard_map/psum | solution.py:739
  286.5 10.5 %inflow_part.1.inflow_ref = f32[8,2,512,128]{3,2,1,0:T(8,128)S(1)} custom-call(s32[1]{0:T(128)} %bitcast.3.core_ref, f32[2,512,1024]{2,1,0:T(8,128)} %collective-permute-done.swap_ref, f32[2,256,1024]{2,1,0:T(8,128)S(1)} %collective-permute-done.1.first_ref, f32[2,256,1024]{2,1,0:T(8,128)} %collective-permute-done.2.second_ref, ...), custom_call_target="tpu_custom_call" | custom-call | flops 31457280 | bytes 12582912 | tf_op jit(solution)/shard_map/inflow_part/pallas_call | solution.py:404
  297.0 15.3 %finish_dist.1 = f32[512,8,8,128]{3,2,1,0:T(8,128)} custom-call(f32[8,8,512,128]{3,2,1,0:T(8,128)} %copy-done.1, f32[8,2,512,128]{3,2,1,0:T(8,128)S(1)} %inflow_part.1.inflow_ref, f32[8,448,128]{2,1,0:T(8,128)S(1)} %copy-done.6, f32[8,64,128]{2,1,0:T(8,128)S(1)} %copy-done.8, bf16[512,192]{1,0:T(8,128)(2,1)S(1)} %pad_maximum_fusion.rows_ref, ...), custom_call_target="tpu_custom_call" | custom-call | flops 1610612736 | bytes 33554432 | tf_op jit(solution)/shard_map/finish_dist/pallas_call | solution.py:624
  (80 shorter events, 15.4 us)
Async XLA Ops:
  1.6 5.8 %copy-start = (f32[512,8,1024]{2,1,0:T(8,128)S(1)}, f32[512,8,1024]{2,1,0:T(8,128)}, u32[]{:S(2)}) copy-start(f32[512,8,1024]{2,1,0:T(8,128)} %param.5) | copy-start | bytes 50331652
  7.4 6.1 %copy-start.2 = (f32[3,512,128]{2,1,0:T(8,128)}, f32[3,512,128]{2,1,0:T(8,128)S(1)}, u32[]{:S(2)}) copy-start(f32[3,512,128]{2,1,0:T(8,128)S(1)} %broadcast_in_dim.24.dtc_ref) | copy-start | bytes 2359300
  13.5 13.0 %copy-start.15 = (f32[8,1024]{1,0:T(8,128)S(1)}, f32[8,1024]{1,0:T(8,128)}, u32[]{:S(2)}) copy-start(f32[8,1024]{1,0:T(8,128)} %param.7) | copy-start | bytes 98308
  13.5 13.0 %copy-start.16 = (s32[8,1024]{1,0:T(8,128)S(1)}, s32[8,1024]{1,0:T(8,128)}, u32[]{:S(2)}) copy-start(s32[8,1024]{1,0:T(8,128)} %param.8) | copy-start | bytes 98308
  13.5 7.6 %collective-permute-start = (f32[2,512,1024]{2,1,0:T(8,128)}, f32[2,512,1024]{2,1,0:T(8,128)}, u32[]{:S(2)}, u32[]{:S(2)}) collective-permute-start(f32[2,512,1024]{2,1,0:T(8,128)} %outflow_planes.1), channel_id=1, source_target_pairs={{0,1},{1,0},{2,3},{3,2},{4,5},{5,4},{6,7},{7,6},{8,9},{9,8},{10,11... | collective-permute-start | bytes 12582920 | tf_op jit(solution)/shard_map/ppermute | solution.py:665
  23.5 48.9 %collective-permute-start.1 = (f32[2,256,1024]{2,1,0:T(8,128)S(1)}, f32[2,256,1024]{2,1,0:T(8,128)S(1)}, u32[]{:S(2)}, u32[]{:S(2)}) collective-permute-start(f32[2,256,1024]{2,1,0:T(8,128)S(1)} %dynamic-slice_select_fusion), channel_id=1, source_target_pairs={{0,2},{1,3},{2,0},{3,1},{4,6},{5,7},{6,4},{7,5},{8,10},{9,11},{10,... | collective-permute-start | bytes 6291464 | tf_op jit(solution)/shard_map/ppermute | solution.py:688
  72.4 214.1 %collective-permute-start.2 = (f32[2,256,1024]{2,1,0:T(8,128)S(1)}, f32[2,256,1024]{2,1,0:T(8,128)}, u32[]{:S(2)}, u32[]{:S(2)}) collective-permute-start(f32[2,256,1024]{2,1,0:T(8,128)S(1)} %collective-permute-done.1.first_ref), channel_id=1, source_target_pairs={{0,1},{1,0},{2,3},{3,2},{4,5},{5,4},{6,7},{7,6},{8,9},{9,8},{10,11... | collective-permute-start | bytes 6291464 | tf_op jit(solution)/shard_map/ppermute | solution.py:689
  72.4 3.3 %collective-permute-start.3 = (f32[3,1,1024]{2,1,0:T(1,128)S(1)}, f32[3,1,1024]{2,1,0:T(1,128)S(1)}, u32[]{:S(2)}, u32[]{:S(2)}) collective-permute-start(f32[3,1,1024]{2,1,0:T(1,128)S(1)} %get-tuple-element.53), channel_id=1, source_target_pairs={{0,3},{1,0},{2,1},{3,2},{4,7},{5,4},{6,5},{7,6},{8,11},{9,8},{10,9... | collective-permute-start | bytes 36872 | tf_op jit(solution)/shard_map/ppermute | solution.py:677
  74.3 3.1 collective-permute-start.4
  78.2 75.8 %copy-start.14 = (f32[13,13]{1,0:T(8,128)S(1)}, f32[13,13]{1,0:T(8,128)}, u32[]{:S(2)}) copy-start(f32[13,13]{1,0:T(8,128)} %inv_ref.3) | copy-start | bytes 2032
  118.4 9.8 %collective-permute-start.5 = (f32[288,128]{1,0:T(8,128)}, f32[288,128]{1,0:T(8,128)S(1)}, u32[]{:S(2)}, u32[]{:S(2)}) collective-permute-start(f32[288,128]{1,0:T(8,128)} %get-tuple-element.26), channel_id=1, source_target_pairs={{0,4},{4,8},{8,12},{12,16},{16,20},{20,24},{24,28},{28,0},{1,5},{5... | collective-permute-start | bytes 442376 | tf_op jit(solution)/shard_map/ppermute | solution.py:692
  119.9 8.5 %collective-permute-start.6 = (f32[288,128]{1,0:T(8,128)}, f32[288,128]{1,0:T(8,128)S(1)}, u32[]{:S(2)}, u32[]{:S(2)}) collective-permute-start(f32[288,128]{1,0:T(8,128)} %get-tuple-element.27), channel_id=1, source_target_pairs={{0,8},{4,12},{8,16},{12,20},{16,24},{20,28},{24,0},{28,4},{1,9},{5... | collective-permute-start | bytes 442376 | tf_op jit(solution)/shard_map/ppermute | solution.py:692
  121.5 17.8 %collective-permute-start.7 = (f32[288,128]{1,0:T(8,128)}, f32[288,128]{1,0:T(8,128)S(1)}, u32[]{:S(2)}, u32[]{:S(2)}) collective-permute-start(f32[288,128]{1,0:T(8,128)} %get-tuple-element.28), channel_id=1, source_target_pairs={{0,12},{4,16},{8,20},{12,24},{16,28},{20,0},{24,4},{28,8},{1,13},{... | collective-permute-start | bytes 442376 | tf_op jit(solution)/shard_map/ppermute | solution.py:692
  124.1 22.1 %collective-permute-start.8 = (f32[288,128]{1,0:T(8,128)}, f32[288,128]{1,0:T(8,128)S(1)}, u32[]{:S(2)}, u32[]{:S(2)}) collective-permute-start(f32[288,128]{1,0:T(8,128)} %get-tuple-element.29), channel_id=1, source_target_pairs={{0,16},{4,20},{8,24},{12,28},{16,0},{20,4},{24,8},{28,12},{1,17},{... | collective-permute-start | bytes 442376 | tf_op jit(solution)/shard_map/ppermute | solution.py:692
  128.2 18.0 %collective-permute-start.9 = (f32[288,128]{1,0:T(8,128)}, f32[288,128]{1,0:T(8,128)S(1)}, u32[]{:S(2)}, u32[]{:S(2)}) collective-permute-start(f32[288,128]{1,0:T(8,128)} %get-tuple-element.30), channel_id=1, source_target_pairs={{0,20},{4,24},{8,28},{12,0},{16,4},{20,8},{24,12},{28,16},{1,21},{... | collective-permute-start | bytes 442376 | tf_op jit(solution)/shard_map/ppermute | solution.py:692
  128.5 17.7 %collective-permute-start.10 = (f32[288,128]{1,0:T(8,128)}, f32[288,128]{1,0:T(8,128)S(1)}, u32[]{:S(2)}, u32[]{:S(2)}) collective-permute-start(f32[288,128]{1,0:T(8,128)} %get-tuple-element.31), channel_id=1, source_target_pairs={{0,24},{4,28},{8,0},{12,4},{16,8},{20,12},{24,16},{28,20},{1,25},{... | collective-permute-start | bytes 442376 | tf_op jit(solution)/shard_map/ppermute | solution.py:692
  139.3 9.8 %collective-permute-start.11 = (f32[288,128]{1,0:T(8,128)}, f32[288,128]{1,0:T(8,128)S(1)}, u32[]{:S(2)}, u32[]{:S(2)}) collective-permute-start(f32[288,128]{1,0:T(8,128)} %get-tuple-element.32), channel_id=1, source_target_pairs={{0,28},{4,0},{8,4},{12,8},{16,12},{20,16},{24,20},{28,24},{1,29},{... | collective-permute-start | bytes 442376 | tf_op jit(solution)/shard_map/ppermute | solution.py:692
  149.2 0.9 copy-start.11
  150.1 3.8 %collective-permute-start.12 = (f32[144,128]{1,0:T(8,128)S(1)}, f32[144,128]{1,0:T(8,128)S(1)}, u32[]{:S(2)}, u32[]{:S(2)}) collective-permute-start(f32[144,128]{1,0:T(8,128)S(1)} %get-tuple-element.34), channel_id=1, source_target_pairs={{0,1},{1,2},{2,3},{3,0},{4,5},{5,6},{6,7},{7,4},{8,9},{9,10},{10,1... | collective-permute-start | bytes 221192 | tf_op jit(solution)/shard_map/ppermute | solution.py:702
  150.2 3.8 %collective-permute-start.13 = (f32[144,128]{1,0:T(8,128)S(1)}, f32[144,128]{1,0:T(8,128)S(1)}, u32[]{:S(2)}, u32[]{:S(2)}) collective-permute-start(f32[144,128]{1,0:T(8,128)S(1)} %get-tuple-element.35), channel_id=1, source_target_pairs={{0,3},{1,0},{2,1},{3,2},{4,7},{5,4},{6,5},{7,6},{8,11},{9,8},{10,9... | collective-permute-start | bytes 221192 | tf_op jit(solution)/shard_map/ppermute | solution.py:703
  154.8 26.6 %copy-start.12 = (f32[192,128]{1,0:T(8,128)}, f32[192,128]{1,0:T(8,128)S(1)}, u32[]{:S(2)}) copy-start(f32[192,128]{1,0:T(8,128)S(1)} %get-tuple-element.37.refs_0_) | copy-start | bytes 294916
  154.8 25.6 %collective-permute-start.20 = (f32[192,128]{1,0:T(8,128)S(1)}, f32[192,128]{1,0:T(8,128)}, u32[]{:S(2)}, u32[]{:S(2)}) collective-permute-start(f32[192,128]{1,0:T(8,128)S(1)} %get-tuple-element.37.refs_0_), channel_id=1, source_target_pairs={{0,28},{4,0},{8,4},{12,8},{16,12},{20,16},{24,20},{28,24},{1,29},{... | collective-permute-start | bytes 294920 | tf_op jit(solution)/shard_map/ppermute | solution.py:707
  159.9 20.5 %collective-permute-start.19 = (f32[192,128]{1,0:T(8,128)S(1)}, f32[192,128]{1,0:T(8,128)}, u32[]{:S(2)}, u32[]{:S(2)}) collective-permute-start(f32[192,128]{1,0:T(8,128)S(1)} %get-tuple-element.37.refs_0_), channel_id=1, source_target_pairs={{0,24},{4,28},{8,0},{12,4},{16,8},{20,12},{24,16},{28,20},{1,25},{... | collective-permute-start | bytes 294920 | tf_op jit(solution)/shard_map/ppermute | solution.py:707
  160.8 20.6 %collective-permute-start.18 = (f32[192,128]{1,0:T(8,128)S(1)}, f32[192,128]{1,0:T(8,128)}, u32[]{:S(2)}, u32[]{:S(2)}) collective-permute-start(f32[192,128]{1,0:T(8,128)S(1)} %get-tuple-element.37.refs_0_), channel_id=1, source_target_pairs={{0,20},{4,24},{8,28},{12,0},{16,4},{20,8},{24,12},{28,16},{1,21},{... | collective-permute-start | bytes 294920 | tf_op jit(solution)/shard_map/ppermute | solution.py:707
  162.5 31.5 %copy-start.4 = (f32[3,16,1024]{2,1,0:T(8,128)S(1)}, f32[3,16,1024]{2,1,0:T(8,128)}, u32[]{:S(2)}) copy-start(f32[3,16,1024]{2,1,0:T(8,128)} %pad_maximum_fusion.1.cst_ref) | copy-start | bytes 589828
  167.7 35.9 %copy-start.3 = (f32[3,512,128]{2,1,0:T(8,128)S(1)}, f32[3,512,128]{2,1,0:T(8,128)}, u32[]{:S(2)}) copy-start(f32[3,512,128]{2,1,0:T(8,128)} %copy-done.2) | copy-start | bytes 2359300
  176.9 12.6 %collective-permute-start.17 = (f32[192,128]{1,0:T(8,128)S(1)}, f32[192,128]{1,0:T(8,128)S(1)}, u32[]{:S(2)}, u32[]{:S(2)}) collective-permute-start(f32[192,128]{1,0:T(8,128)S(1)} %get-tuple-element.37.refs_0_), channel_id=1, source_target_pairs={{0,16},{4,20},{8,24},{12,28},{16,0},{20,4},{24,8},{28,12},{1,17},{... | collective-permute-start | bytes 294920 | tf_op jit(solution)/shard_map/ppermute | solution.py:707
  180.4 13.6 %collective-permute-start.16 = (f32[192,128]{1,0:T(8,128)S(1)}, f32[192,128]{1,0:T(8,128)S(1)}, u32[]{:S(2)}, u32[]{:S(2)}) collective-permute-start(f32[192,128]{1,0:T(8,128)S(1)} %get-tuple-element.37.refs_0_), channel_id=1, source_target_pairs={{0,12},{4,16},{8,20},{12,24},{16,28},{20,0},{24,4},{28,8},{1,13},{... | collective-permute-start | bytes 294920 | tf_op jit(solution)/shard_map/ppermute | solution.py:707
  180.4 13.6 %collective-permute-start.15 = (f32[192,128]{1,0:T(8,128)S(1)}, f32[192,128]{1,0:T(8,128)S(1)}, u32[]{:S(2)}, u32[]{:S(2)}) collective-permute-start(f32[192,128]{1,0:T(8,128)S(1)} %get-tuple-element.37.refs_0_), channel_id=1, source_target_pairs={{0,8},{4,12},{8,16},{12,20},{16,24},{20,28},{24,0},{28,4},{1,9},{5... | collective-permute-start | bytes 294920 | tf_op jit(solution)/shard_map/ppermute | solution.py:707
  181.4 12.6 %collective-permute-start.14 = (f32[192,128]{1,0:T(8,128)S(1)}, f32[192,128]{1,0:T(8,128)S(1)}, u32[]{:S(2)}, u32[]{:S(2)}) collective-permute-start(f32[192,128]{1,0:T(8,128)S(1)} %get-tuple-element.37.refs_0_), channel_id=1, source_target_pairs={{0,4},{4,8},{8,12},{12,16},{16,20},{20,24},{24,28},{28,0},{1,5},{5... | collective-permute-start | bytes 294920 | tf_op jit(solution)/shard_map/ppermute | solution.py:707
  194.0 0.9 copy-start.13
  199.8 1.2 copy-start.5
  201.0 0.7 copy-start.9
  201.7 40.1 %collective-permute-start.21 = (f32[16,1024]{1,0:T(8,128)}, f32[16,1024]{1,0:T(8,128)S(1)}, u32[]{:S(2)}, u32[]{:S(2)}) collective-permute-start(f32[16,1024]{1,0:T(8,128)} %get-tuple-element.40), channel_id=1, source_target_pairs={{0,1},{1,2},{2,3},{3,0},{4,5},{5,6},{6,7},{7,4},{8,9},{9,10},{10,1... | collective-permute-start | bytes 196616 | tf_op jit(solution)/shard_map/ppermute | solution.py:727
  201.7 40.1 %collective-permute-start.22 = (f32[16,1024]{1,0:T(8,128)}, f32[16,1024]{1,0:T(8,128)}, u32[]{:S(2)}, u32[]{:S(2)}) collective-permute-start(f32[16,1024]{1,0:T(8,128)} %get-tuple-element.41), channel_id=1, source_target_pairs={{0,3},{1,0},{2,1},{3,2},{4,7},{5,4},{6,5},{7,6},{8,11},{9,8},{10,9... | collective-permute-start | bytes 196616 | tf_op jit(solution)/shard_map/ppermute | solution.py:728
  235.5 5.8 %copy-start.1 = (f32[8,8,512,128]{3,2,1,0:T(8,128)}, f32[8,8,512,128]{3,2,1,0:T(8,128)S(1)}, u32[]{:S(2)}) copy-start(f32[8,8,512,128]{3,2,1,0:T(8,128)S(1)} %carried_part.1.carried_ref) | copy-start | bytes 50331652
  241.8 1.0 copy-start.10
  245.9 0.7 copy-start.7
  286.5 10.5 %copy-start.6 = (f32[8,448,128]{2,1,0:T(8,128)S(1)}, f32[8,448,128]{2,1,0:T(8,128)}, u32[]{:S(2)}) copy-start(f32[8,448,128]{2,1,0:T(8,128)} %copy-done.5) | copy-start | bytes 5505028
  286.5 10.5 %copy-start.8 = (f32[8,64,128]{2,1,0:T(8,128)S(1)}, f32[8,64,128]{2,1,0:T(8,128)}, u32[]{:S(2)}) copy-start(f32[8,64,128]{2,1,0:T(8,128)} %copy-done.7) | copy-start | bytes 786436

commit v2 on v1

v2 whole, which is shorter than its diff:
```python
import functools
import math

import jax
import jax.numpy as jnp
import numpy as np
from jax import lax
from jax.experimental import pallas as pl
from jax.experimental.pallas import tpu as pltpu
from jax.sharding import PartitionSpec as P

NVX = 16
NZ = 16
MOM = 13
SWEEPS = 3
LANES = 128
SUB = 8
SETS = 7
PICK = (0, 1, 2, 3, 4, 10, 11, 12)

speed_range = 4.0
time_step = 0.08
coupling = 0.5
MIB = 2**20
PIECES = 8

UP, M1, DOWN, AA, PAY = 0, 40, 144, 184, 288
STILL = (0, 10, 11, 12)
MOVED, FIXED, EDGE, LATER, SQUARE, SENT = 64, 96, 128, 136, 240, 248


def functions_of(cx, cy, cz):
    square = cx * cx + cy * cy + cz * cz
    heat = square - 2.5
    one = cx * 0.0 + 1.0
    rows = [
        one, cx, cy, cz, 2.0 * square / 3.0 - 1.0, 2.0 * cx * cy, 2.0 * cx * cz, 2.0 * cy * cz,
        cx * cx - cy * cy, cy * cy - cz * cz, cx * heat, cy * heat, cz * heat,
    ]
    factor = 4.0 / 15.0
    shakhov = [
        one, 2.0 * cx, 2.0 * cy, 2.0 * cz, square - 1.5,
        factor * cx * heat, factor * cy * heat, factor * cz * heat,
    ]
    return rows, shakhov, square


def half_speeds(cx, cy, cz):
    out = []
    for c in (cx, cy, cz):
        out.append(time_step * c * (c > 0))
        out.append(-time_step * c * (c < 0))
    return out


@functools.lru_cache(None)
def stream_matrices():
    line = speed_range * (2.0 * np.arange(NVX) + 1.0 - NVX) / NVX
    cx, cy, cz = (g.reshape(-1) for g in np.meshgrid(line, line, line, indexing="ij"))
    rows, shakhov, square = functions_of(cx, cy, cz)
    weight = (2.0 * speed_range / NVX) ** 3 * math.pi ** (-1.5) * np.exp(-square)
    rows = np.stack(rows) * weight
    shakhov = np.stack(shakhov)
    speeds = half_speeds(cx, cy, cz)
    stay = 1.0 - sum(speeds)
    out = np.stack([(rows * s) @ shakhov.T for s in [stay] + speeds])
    out[np.abs(out) < 1e-13] = 0.0
    return out


def split(value):
    high = value.astype(jnp.bfloat16)
    low = (value - high.astype(jnp.float32)).astype(jnp.bfloat16)
    return high, low


def speeds_at(index):
    speed = speed_range * (2.0 * index.astype(jnp.float32) + 1.0 - NVX) / NVX
    return [time_step * speed[a : a + 1] for a in range(3)]


class Upwind:
    def __init__(self, index):
        tx, ty, tz = speeds_at(index)
        shape = (NZ, LANES)
        self.ax, self.ay, self.az = (jnp.broadcast_to(jnp.abs(t), shape) for t in (tx, ty, tz))
        self.stay = 1.0 - self.ax - self.ay - self.az
        self.px, self.py, self.pz = (jnp.broadcast_to(t, shape) > 0 for t in (tx, ty, tz))

    def across(self, read, y, count):
        here = read(y)
        in_y = jnp.where(self.py, read(lax.rem(y + count - 1, count)), read(lax.rem(y + 1, count)))
        in_z = jnp.where(self.pz, pltpu.roll(here, 1, axis=0), pltpu.roll(here, NZ - 1, axis=0))
        return self.stay * here + self.ay * in_y + self.az * in_z

    def stream(self, ref, x, y, count):
        mid = self.across(lambda j: ref[x + 1, rows_of(j), :], y, count)
        return mid + self.ax * jnp.where(self.px, ref[x, rows_of(y), :], ref[x + 2, rows_of(y), :])


def rows_of(y):
    return pl.ds(pl.multiple_of(y * NZ, NZ), NZ)


def each_y(count, body, step=16):
    @pl.loop(0, count // step)
    def _(i):
        for j in range(step):
            body(i * step + j)


def lane_copies(ref_row, target, blocks):
    for k in range(blocks):
        at = slice(k * LANES, (k + 1) * LANES)
        target[at, :] = jnp.broadcast_to(ref_row[:, at], (LANES, LANES)).T


def roll_y(value, sign):
    cells = value.shape[1]
    return pltpu.roll(value, NZ if sign > 0 else cells - NZ, axis=1)


def roll_z(value, sign):
    cells = value.shape[1]
    zl = lax.broadcasted_iota(jnp.int32, value.shape, 1) & (NZ - 1)
    if sign > 0:
        return jnp.where(zl == 0, pltpu.roll(value, cells - (NZ - 1), axis=1), pltpu.roll(value, 1, axis=1))
    return jnp.where(zl == NZ - 1, pltpu.roll(value, NZ - 1, axis=1), pltpu.roll(value, cells - 1, axis=1))


def outflow_kernel(dist_ref, dtc_ref, out_ref, *, count, blocks):
    px = dtc_ref[...] > 0
    stride = blocks * SUB
    for k in range(blocks):
        at = slice(k * LANES, (k + 1) * LANES)
        plane = [dist_ref[pl.ds(k * SUB + x, count, stride=stride), :] for x in (0, 1, SUB - 2, SUB - 1)]
        out_ref[0, :, at] = jnp.where(px, plane[3], plane[0])
        out_ref[1, :, at] = jnp.where(px, plane[2], plane[1])


def outflow(flat, dtc, vels, blocks):
    count = min(64, vels)
    rows = count * blocks * SUB
    cells = blocks * LANES
    return pl.pallas_call(
        functools.partial(outflow_kernel, count=count, blocks=blocks),
        grid=(vels // count,),
        in_specs=[
            pl.BlockSpec((rows, LANES), lambda i: (i, 0)),
            pl.BlockSpec((count, LANES), lambda i: (i, 0)),
        ],
        out_specs=pl.BlockSpec((2, count, cells), lambda i: (0, i, 0)),
        out_shape=jax.ShapeDtypeStruct((2, vels, cells), jnp.float32),
        compiler_params=pltpu.CompilerParams(vmem_limit_bytes=54 * MIB),
        cost_estimate=pl.CostEstimate(flops=0, bytes_accessed=20 * vels * blocks * SUB * LANES // 4, transcendentals=0),
        name="outflow_planes",
    )(flat, dtc)


def moments_kernel(me_ref, dist_ref, index_ref, cst_ref, high_ref, low_ref, *refs, vels, blocks):
    half = blocks // 2
    outs = refs[:half]
    held, turned, rhi, rlo, table, wst, acc, gacc, pay, sems, out_sems = refs[half:]
    stride = blocks * SUB
    chunks = vels // LANES
    part = LANES * stride
    span = SETS * 16
    ys = blocks * LANES // NZ

    piece = part // PIECES

    def fetch(c):
        return [
            pltpu.make_async_copy(
                dist_ref.at[pl.ds(c * part + p * piece, piece)],
                held.at[c % 2, pl.ds(p * piece, piece)],
                sems.at[c % 2, p],
            )
            for p in range(PIECES)
        ]

    for c in range(min(2, chunks)):
        for copy in fetch(c):
            copy.start()

    speed = [speed_range * (2.0 * index_ref[a : a + 1, :].astype(jnp.float32) + 1.0 - NVX) / NVX for a in range(3)]
    rows, _, square = functions_of(*speed)
    weight = (2.0 * speed_range / NVX) ** 3 * math.pi ** (-1.5) * jnp.exp(-square)
    table[...] = jnp.zeros_like(table)
    for m, row in enumerate(rows):
        table[m : m + 1, :] = row * weight
    base = table[...]
    speeds = []
    for c in speed:
        speeds.append(jnp.where(c > 0, time_step * c, 0.0))
        speeds.append(jnp.where(c < 0, -time_step * c, 0.0))
    full = jnp.concatenate([base] + [base * s for s in speeds] + [jnp.zeros_like(base)], axis=0)
    for variant, factor in enumerate([None, speeds[0], speeds[1]]):
        high, low = split((full if factor is None else full * factor).T)
        wst[variant, :, 0:LANES] = high
        wst[variant, :, LANES:] = low

    empty = jnp.zeros((ys * NZ, LANES), jnp.float32)
    turned[0] = empty
    turned[SUB + 1] = empty
    for c in range(chunks):
        for copy in fetch(c):
            copy.wait()
        lanes = slice(c * LANES, (c + 1) * LANES)

        @pl.loop(0, blocks)
        def _(k, c=c):
            for x in range(SUB):
                value = held[c % 2, pl.ds(k * SUB + x, LANES, stride=stride), :]
                turned[x + 1, pl.ds(pl.multiple_of(k * LANES, LANES), LANES), :] = value.T

        if c + 2 < chunks:
            for copy in fetch(c + 2):
                copy.start()
        upwind = Upwind(index_ref[:, lanes])

        @pl.loop(0, SUB)
        def _(x, upwind=upwind, lanes=lanes):
            def one(y):
                high, low = split(upwind.stream(turned, x, y, ys))
                rhi[x, rows_of(y), lanes] = high
                rlo[x, rows_of(y), lanes] = low

            each_y(ys, one)

        def edges(y, lanes=lanes):
            for slot, x in ((SUB, SUB - 1), (SUB + 1, 0)):
                high, low = split(turned[x + 1, rows_of(y), :])
                rhi[slot, rows_of(y), lanes] = high
                rlo[slot, rows_of(y), lanes] = low

        each_y(ys, edges)

    away = [
        pltpu.make_async_copy(rhi.at[pl.ds(0, SUB)], high_ref, out_sems.at[0]),
        pltpu.make_async_copy(rlo.at[pl.ds(0, SUB)], low_ref, out_sems.at[1]),
    ]
    for copy in away:
        copy.start()
    wide = 2 * LANES

    @pl.loop(0, blocks // 2)
    def _(b):
        at = pl.ds(pl.multiple_of(b * wide, wide), wide)
        for slot in range(SUB + 2):
            variant = max(0, slot - SUB + 1)
            first = jnp.dot(rhi[slot, at, :], wst[variant], preferred_element_type=jnp.float32)
            second = jnp.dot(rlo[slot, at, :], wst[variant, :, 0:LANES], preferred_element_type=jnp.float32)
            total = (first[:, 0:LANES] + first[:, LANES:] + second).T[0:span]
            if slot < SUB:
                for j in range(2):
                    acc[2 * b + j, pl.ds(slot, span, stride=SUB), :] = total[:, j * LANES : (j + 1) * LANES]
            else:
                gacc[slot - SUB, :, at] = total

    al = cst_ref[0, 0:SUB, :]
    beyond = cst_ref[0, SUB : SUB + 1, :]
    below = cst_ref[0, 2 * SUB - 1 : 2 * SUB, :]
    plane = lax.broadcasted_iota(jnp.int32, al.shape, 0)

    def own(i, m):
        first = (i * 16 + m) * SUB
        return jnp.concatenate([acc[k, first : first + SUB, :] for k in range(blocks)], axis=1)

    for m in range(MOM):
        sets = [own(i, m) for i in range(SETS)]
        value = al * (sets[0] - sum(sets[1:]))
        value = value + jnp.where(plane == 0, 0.0, pltpu.roll(al * sets[1], 1, axis=0))
        value = value + jnp.where(plane == SUB - 1, 0.0, pltpu.roll(al * sets[2], SUB - 1, axis=0))
        value = value + roll_y(al * sets[3], 1) + roll_y(al * sets[4], -1)
        value = value + roll_z(al * sets[5], 1) + roll_z(al * sets[6], -1)
        for k in range(blocks):
            at = slice(k * LANES, (k + 1) * LANES)
            pay[k, M1 + m * SUB : M1 + (m + 1) * SUB, :] = sets[0][:, at]
            pay[k, AA + m * SUB : AA + (m + 1) * SUB, :] = value[:, at]

    for side, (scale, edge, toward, start) in enumerate([(beyond, SUB - 1, 1, UP), (below, 0, 2, DOWN)]):
        sets = [gacc[side, i * 16 : (i + 1) * 16, :] for i in range(SETS)]
        near = scale * (sets[0] - sum(sets[1:]))
        near = near + roll_y(scale * sets[3], 1) + roll_y(scale * sets[4], -1)
        near = near + roll_z(scale * sets[5], 1) + roll_z(scale * sets[6], -1)
        out_of = jnp.concatenate(
            [acc[k, pl.ds(toward * 16 * SUB + edge, 16, stride=SUB), :] for k in range(blocks)], axis=1
        )
        near = near + al[edge : edge + 1, :] * out_of
        far = scale * sets[toward]
        for k in range(blocks):
            at = slice(k * LANES, (k + 1) * LANES)
            for j, value in enumerate((sets[0], near, far)):
                pay[k, start + j * MOM : start + (j + 1) * MOM, :] = value[0:MOM, at]
            pay[k, start + 3 * MOM : start + 3 * MOM + 1, :] = jnp.zeros((1, LANES), jnp.float32)

    mine = me_ref[0]
    for k in range(half):
        near = jnp.bitwise_xor(mine, k)
        outs[k][0:PAY, :] = pay[near]
        outs[k][PAY:, :] = pay[jnp.bitwise_xor(near, half)]
    for copy in away:
        copy.wait()


def both_moments(place, flat, vel_index, cst, vels, blocks):
    cells = blocks * LANES
    vmem = pl.BlockSpec(memory_space=pltpu.VMEM)
    span = SETS * 16
    anywhere = pl.BlockSpec(memory_space=pl.ANY)
    streamed = jax.ShapeDtypeStruct((SUB, cells, vels), jnp.bfloat16)
    return pl.pallas_call(
        functools.partial(moments_kernel, vels=vels, blocks=blocks),
        in_specs=[pl.BlockSpec(memory_space=pltpu.SMEM), anywhere, vmem, vmem],
        out_specs=[anywhere, anywhere] + [vmem] * (blocks // 2),
        out_shape=[streamed, streamed] + [jax.ShapeDtypeStruct((2 * PAY, LANES), jnp.float32)] * (blocks // 2),
        scratch_shapes=[
            pltpu.VMEM((2, LANES * blocks * SUB, LANES), jnp.float32),
            pltpu.VMEM((SUB + 2, cells, LANES), jnp.float32),
            pltpu.VMEM((SUB + 2, cells, vels), jnp.bfloat16),
            pltpu.VMEM((SUB + 2, cells, vels), jnp.bfloat16),
            pltpu.VMEM((16, vels), jnp.float32),
            pltpu.VMEM((3, vels, 2 * LANES), jnp.bfloat16),
            pltpu.VMEM((blocks, span * SUB, LANES), jnp.float32),
            pltpu.VMEM((2, span, cells), jnp.float32),
            pltpu.VMEM((blocks, PAY, LANES), jnp.float32),
            pltpu.SemaphoreType.DMA((2, PIECES)),
            pltpu.SemaphoreType.DMA((2,)),
        ],
        compiler_params=pltpu.CompilerParams(vmem_limit_bytes=54 * MIB),
        cost_estimate=pl.CostEstimate(
            flops=2 * 336 * vels * 10 * cells, bytes_accessed=8 * vels * SUB * cells, transcendentals=0
        ),
        name="moments_of_both",
    )(place, flat, vel_index, cst)


def carried_kernel(high_ref, low_ref, index_ref, al_ref, out_ref, mid, scale, *, blocks):
    ys = blocks * LANES // NZ

    @pl.when(pl.program_id(0) == 0)
    def _():
        for x in range(SUB):
            lane_copies(al_ref[x : x + 1, :], scale.at[x], blocks)
        empty = jnp.zeros((ys * NZ, LANES), jnp.float32)
        mid[0] = empty
        mid[SUB + 1] = empty

    upwind = Upwind(index_ref[...])

    @pl.loop(0, SUB)
    def _(x):
        def one(y):
            at = rows_of(y)
            value = high_ref[x, at, :].astype(jnp.float32) + low_ref[x, at, :].astype(jnp.float32)
            mid[x + 1, at, :] = scale[x, at, :] * value

        each_y(ys, one)

    @pl.loop(0, SUB)
    def _(x):
        def one(y):
            out_ref[x, rows_of(y), :] = scale[x, rows_of(y), :] * upwind.stream(mid, x, y, ys)

        each_y(ys, one)


def carried(high, low, vel_index, al, first, count, blocks):
    cells = blocks * LANES
    start = first // LANES
    block = pl.BlockSpec((SUB, cells, LANES), lambda i: (0, 0, i + start))
    return pl.pallas_call(
        functools.partial(carried_kernel, blocks=blocks),
        grid=(count // LANES,),
        in_specs=[
            block,
            block,
            pl.BlockSpec((3, LANES), lambda i: (0, i + start)),
            pl.BlockSpec((SUB, cells), lambda i: (0, 0)),
        ],
        out_specs=pl.BlockSpec((SUB, cells, LANES), lambda i: (0, 0, i)),
        out_shape=jax.ShapeDtypeStruct((SUB, cells, count), jnp.float32),
        scratch_shapes=[
            pltpu.VMEM((SUB + 2, cells, LANES), jnp.float32),
            pltpu.VMEM((SUB, cells, LANES), jnp.float32),
        ],
        compiler_params=pltpu.CompilerParams(vmem_limit_bytes=56 * MIB),
        cost_estimate=pl.CostEstimate(
            flops=40 * count * cells * SUB, bytes_accessed=8 * count * cells * SUB, transcendentals=0
        ),
        name="carried_part",
    )(high, low, vel_index, al)


def inflow_kernel(
    core_ref, swap_ref, first_ref, second_ref, sign_ref, index_ref, al_ref, out_ref, halo, edge, scale, *, blocks, half
):
    core = core_ref[0]
    ys = blocks * LANES // NZ

    @pl.when(pl.program_id(0) == 0)
    def _():
        for j, x in enumerate((0, SUB - 1, 1, SUB - 2, 2 * SUB - 1, SUB)):
            lane_copies(al_ref[x : x + 1, :], scale.at[j], blocks)

    from_far = (sign_ref[...] > 0) == (core == 0)
    if half >= LANES:
        mine = (pl.program_id(0) // (half // LANES)) == core
    for depth in range(2):
        for k in range(blocks):
            at = slice(k * LANES, (k + 1) * LANES)
            one, two = first_ref[depth, :, at], second_ref[depth, :, at]
            if half >= LANES:
                far = jnp.where(mine, one, two)
            else:
                far = jnp.where(core == 0, jnp.concatenate([one, two], axis=0), jnp.concatenate([two, one], axis=0))
            halo[depth, at, :] = jnp.where(from_far, far, swap_ref[depth, :, at]).T

    upwind = Upwind(index_ref[...])

    def scaled(pair, at):
        return jnp.where(upwind.px, scale[2 * pair, at, :], scale[2 * pair + 1, at, :])

    def start(y):
        at = rows_of(y)
        value = scaled(0, at) * upwind.ax * halo[0, at, :]
        edge[at, :] = value
        out_ref[1, at, :] = scaled(1, at) * upwind.ax * value

    each_y(ys, start)

    def finish_one(y):
        at = rows_of(y)
        inside = upwind.across(lambda j: edge[rows_of(j), :], y, ys)
        beyond = upwind.across(lambda j: halo[0, rows_of(j), :], y, ys) + upwind.ax * halo[1, at, :]
        out_ref[0, at, :] = scaled(0, at) * (inside + upwind.ax * scaled(2, at) * beyond)

    each_y(ys, finish_one)


def inflow(core, swap, first, second, sign, vel_index, al16, vels, blocks):
    half = first.shape[1]
    cells = blocks * LANES
    count = min(LANES, half)
    narrow = pl.BlockSpec((2, count, cells), lambda i: (0, i % (half // count), 0))
    return pl.pallas_call(
        functools.partial(inflow_kernel, blocks=blocks, half=half),
        grid=(vels // LANES,),
        in_specs=[
            pl.BlockSpec(memory_space=pltpu.SMEM),
            pl.BlockSpec((2, LANES, cells), lambda i: (0, i, 0)),
            narrow,
            narrow,
            pl.BlockSpec((LANES, LANES), lambda i: (i, 0)),
            pl.BlockSpec((3, LANES), lambda i: (0, i)),
            pl.BlockSpec((2 * SUB, cells), lambda i: (0, 0)),
        ],
        out_specs=pl.BlockSpec((2, cells, LANES), lambda i: (0, 0, i)),
        out_shape=jax.ShapeDtypeStruct((2, cells, vels), jnp.float32),
        scratch_shapes=[
            pltpu.VMEM((2, cells, LANES), jnp.float32),
            pltpu.VMEM((cells, LANES), jnp.float32),
            pltpu.VMEM((6, cells, LANES), jnp.float32),
        ],
        compiler_params=pltpu.CompilerParams(vmem_limit_bytes=24 * MIB),
        cost_estimate=pl.CostEstimate(flops=60 * vels * cells, bytes_accessed=24 * vels * cells, transcendentals=0),
        name="inflow_part",
    )(core, swap, first, second, sign, vel_index, al16)


def small_call(kernel, outs, name, specs, args, scratch=(), limit=16):
    vmem = pl.BlockSpec(memory_space=pltpu.VMEM)
    smem = pl.BlockSpec(memory_space=pltpu.SMEM)
    return pl.pallas_call(
        kernel,
        in_specs=[smem if s == "s" else vmem for s in specs],
        out_specs=[vmem] * len(outs),
        out_shape=[jax.ShapeDtypeStruct(o, jnp.float32) for o in outs],
        scratch_shapes=list(scratch),
        compiler_params=pltpu.CompilerParams(vmem_limit_bytes=limit * MIB),
        name=name,
    )(*args)


def pair_kernel(*refs):
    parts, (near_ref, far_ref) = refs[:-2], refs[-2:]
    value = parts[0][...]
    for part in parts[1:]:
        value = value + part[...]
    near_ref[...] = value[0:PAY]
    far_ref[...] = value[PAY:]


def total_kernel(*refs):
    parts, (all_ref, up_ref, down_ref) = refs[:-3], refs[-3:]
    value = parts[0][...]
    for part in parts[1:]:
        value = value + part[...]
    all_ref[...] = value
    up_ref[...] = value[UP:DOWN]
    down_ref[...] = value[M1:AA]


def mix(inverse, values):
    return [sum(inverse[k, j] * values[j] for j in range(MOM)) for k in range(MOM)]


def chunk_kernel(inv_ref, own_ref, low_ref, high_ref, send_ref):
    plane = lax.broadcasted_iota(jnp.int32, (SUB, LANES), 0)
    inverse = {(k, j): inv_ref[k, j] for k in range(MOM) for j in range(MOM)}
    inner, outer, later = [], [], []
    for m in range(MOM):

        def row(ref, at):
            return ref[at : at + 1, :]

        first = own_ref[M1 + m * SUB : M1 + (m + 1) * SUB, :]
        second = own_ref[AA + m * SUB : AA + (m + 1) * SUB, :]
        low = low_ref[M1 + m * SUB : M1 + (m + 1) * SUB, :]
        high = high_ref[m * SUB : (m + 1) * SUB, :]
        below = DOWN - M1 + m
        inner.append(
            first + jnp.where(plane == 0, row(low_ref, m), 0.0) + jnp.where(plane == SUB - 1, row(high_ref, below), 0.0)
        )
        outer.append(
            jnp.where(plane < SUB // 2, high, low)
            + jnp.where(plane == 0, row(own_ref, UP + m), 0.0)
            + jnp.where(plane == SUB - 1, row(own_ref, DOWN + m), 0.0)
        )
        later.append(
            second
            + jnp.where(plane == 0, row(low_ref, MOM + m), 0.0)
            + jnp.where(plane == 1, row(low_ref, 2 * MOM + m), 0.0)
            + jnp.where(plane == SUB - 1, row(high_ref, below + MOM), 0.0)
            + jnp.where(plane == SUB - 2, row(high_ref, below + 2 * MOM), 0.0)
        )
    local, around = mix(inverse, inner), mix(inverse, outer)
    for n in range(4):
        send_ref[n * 16 : n * 16 + SUB, :] = local[n + 1]
        send_ref[n * 16 + SUB : (n + 1) * 16, :] = around[n + 1]
        send_ref[MOVED + n * SUB : MOVED + (n + 1) * SUB, :] = inner[n + 1]
    for n, k in enumerate(STILL):
        send_ref[FIXED + n * SUB : FIXED + (n + 1) * SUB, :] = local[k]
        send_ref[EDGE + n : EDGE + n + 1, :] = around[k][0:1]
        send_ref[EDGE + 4 + n : EDGE + 5 + n, :] = around[k][SUB - 1 :]
    for m in range(MOM):
        send_ref[LATER + m * SUB : LATER + (m + 1) * SUB, :] = later[m]
    send_ref[SQUARE:SENT, :] = sum((local[m] - inner[m]) ** 2 for m in range(MOM) if not 1 <= m <= 4)


def sweeps(source):
    rows = source.shape[0]
    field = source
    for _ in range(SWEEPS):
        beside = pltpu.roll(field, 1, axis=0) + pltpu.roll(field, rows - 1, axis=0)
        beside = beside + roll_y(field, 1) + roll_y(field, -1) + roll_z(field, 1) + roll_z(field, -1)
        field = (source + coupling * beside) * (1.0 / (1.0 + 6.0 * coupling))
    return field


def fields_kernel(place_ref, inv_ref, cst_ref, *refs, blocks):
    parts = refs[:blocks]
    h1_ref, later_ref, next_ref, up_ref, down_ref, norm_ref, whole = refs[blocks:]
    mine = place_ref[0]
    for k in range(blocks):
        whole[jnp.bitwise_xor(mine, k)] = parts[k][...]

    def rows(first, count):
        return jnp.concatenate([whole[k, first : first + count, :] for k in range(blocks)], axis=1)

    def fold(value):
        return sum(value[:, k * LANES : (k + 1) * LANES] for k in range(blocks))

    square = sum(whole[k, SQUARE:SENT, :] for k in range(blocks))
    al = cst_ref[0, 0:SUB, :]
    edges = rows(EDGE, SUB)
    plane = lax.broadcasted_iota(jnp.int32, al.shape, 0)
    moved = []
    for n, m in enumerate(PICK):
        if 1 <= m <= 4:
            value = sweeps(rows((m - 1) * 16, 16))
            square = square + fold((value[0:SUB] - rows(MOVED + (m - 1) * SUB, SUB)) ** 2)
        else:
            k = STILL.index(m)
            around = jnp.where(
                plane == 0, edges[k : k + 1], jnp.where(plane == SUB - 1, edges[4 + k : 5 + k], 0.0)
            )
            value = jnp.concatenate([rows(FIXED + k * SUB, SUB), around], axis=0)
        given = cst_ref[1 if n in (0, 4) else 2] * value
        inside = given[0:SUB]
        shifted = [
            inside,
            pltpu.roll(given, 1, axis=0)[0:SUB],
            pltpu.roll(given, 2 * SUB - 1, axis=0)[0:SUB],
            roll_y(inside, 1),
            roll_y(inside, -1),
            roll_z(inside, 1),
            roll_z(inside, -1),
        ]
        for s in range(SETS):
            value = al * shifted[s]
            for k in range(blocks):
                first = (s * 8 + n) * SUB
                h1_ref[k, first : first + SUB, :] = value[:, k * LANES : (k + 1) * LANES]
        moved.append(shifted)
    norm_ref[...] = square

    matrices = stream_matrices()
    moments = []
    for m in range(MOM):
        value = rows(LATER + m * SUB, SUB)
        for s in range(SETS):
            for n in range(8):
                factor = float(matrices[s, m, n])
                if factor != 0.0:
                    value = value + factor * moved[n][s]
        later_ref[m * SUB : (m + 1) * SUB, :] = value
        moments.append(value)
    inverse = {(k, j): inv_ref[k, j] for k in range(MOM) for j in range(MOM)}
    for m, value in enumerate(mix(inverse, moments)):
        next_ref[m * SUB : (m + 1) * SUB, :] = value
        if 1 <= m <= 4:
            up_ref[(m - 1) * 4 : m * 4, :] = value[SUB // 2 :]
            down_ref[(m - 1) * 4 : m * 4, :] = value[: SUB // 2]


def last_kernel(place_ref, cst_ref, later_ref, next_ref, low_ref, high_ref, h2_ref, out_ref, norm_ref, wide, *, blocks):
    mine = place_ref[0]
    square = jnp.zeros((SUB, LANES), jnp.float32)
    for m in range(MOM):
        value = next_ref[m * SUB : (m + 1) * SUB, :]
        if 1 <= m <= 4:
            at = slice((m - 1) * 4, m * 4)
            value = sweeps(jnp.concatenate([value, high_ref[at, :], low_ref[at, :]], axis=0))[0:SUB]
        off = (value - later_ref[m * SUB : (m + 1) * SUB, :]) ** 2
        for k in range(blocks):
            wide[m, k] = value[:, k * LANES : (k + 1) * LANES]
            square = square + off[:, k * LANES : (k + 1) * LANES]
        out_ref[m] = wide[m, mine]
        if m in PICK:
            n = PICK.index(m)
            given = cst_ref[1 if n in (0, 4) else 2, 0:SUB, :] * value
            for k in range(blocks):
                h2_ref[k, n * SUB : (n + 1) * SUB, :] = given[:, k * LANES : (k + 1) * LANES]
    norm_ref[...] = square


def finish_kernel(*refs, vels, parts):
    carried_refs = refs[:parts]
    inflow_ref, h1_ref, h2_ref, index_ref, out_ref, rows, table = refs[parts:]

    @pl.when(pl.program_id(0) == 0)
    def _():
        speed = [speed_range * (2.0 * index_ref[a : a + 1, :].astype(jnp.float32) + 1.0 - NVX) / NVX for a in range(3)]
        for n, row in enumerate(functions_of(*speed)[1]):
            table[n : n + 1, :] = row
        base = table[...]
        speeds = []
        for c in speed:
            speeds.append(jnp.where(c > 0, time_step * c, 0.0))
            speeds.append(jnp.where(c < 0, -time_step * c, 0.0))
        full = jnp.concatenate([base * (1.0 - sum(speeds))] + [base * s for s in speeds] + [base], axis=0)
        high = full.astype(jnp.bfloat16).astype(jnp.float32)
        stacked = jnp.concatenate([high, high, full - high, jnp.zeros_like(full)], axis=0)
        rows[...] = stacked.T.astype(jnp.bfloat16)

    out = out_ref.reshape(vels * SUB, LANES)
    px = index_ref[0:1, :] * 2 >= NVX
    for x in range(0, SUB, 2):
        field = jnp.concatenate(
            [
                jnp.concatenate(
                    [h1_ref[0, pl.ds(x + j, SETS * 8, stride=SUB), :], h2_ref[0, pl.ds(x + j, 8, stride=SUB), :]], axis=0
                )
                for j in range(2)
            ],
            axis=1,
        )
        high, low = split(field)
        term = jnp.dot(
            rows[...],
            jnp.concatenate([high, low, high, jnp.zeros_like(high)], axis=0),
            preferred_element_type=jnp.float32,
        )
        for j in range(2):
            value = jnp.concatenate([ref[x + j] for ref in carried_refs], axis=1)
            if x + j in (0, 1):
                value = value + jnp.where(px, inflow_ref[x + j], 0.0)
            elif x + j in (SUB - 2, SUB - 1):
                value = value + jnp.where(px, 0.0, inflow_ref[SUB - 1 - x - j])
            out[pl.ds(x + j, vels, stride=SUB), :] = value.T + term[:, j * LANES : (j + 1) * LANES]


def finish(carried_parts, inflow_part, h1, h2, vel_index, vels, blocks):
    return pl.pallas_call(
        functools.partial(finish_kernel, vels=vels, parts=len(carried_parts)),
        grid=(blocks,),
        in_specs=[pl.BlockSpec((SUB, LANES, part.shape[2]), lambda k: (0, k, 0)) for part in carried_parts]
        + [
            pl.BlockSpec((2, LANES, vels), lambda k: (0, k, 0)),
            pl.BlockSpec((1, SETS * 8 * SUB, LANES), lambda k: (k, 0, 0)),
            pl.BlockSpec((1, 8 * SUB, LANES), lambda k: (k, 0, 0)),
            pl.BlockSpec((3, vels), lambda k: (0, 0)),
        ],
        out_specs=pl.BlockSpec((vels, 1, SUB, LANES), lambda k: (0, k, 0, 0)),
        out_shape=jax.ShapeDtypeStruct((vels, blocks, SUB, LANES), jnp.float32),
        scratch_shapes=[pltpu.VMEM((vels, 256), jnp.bfloat16), pltpu.VMEM((8, vels), jnp.float32)],
        compiler_params=pltpu.CompilerParams(vmem_limit_bytes=54 * MIB),
        cost_estimate=pl.CostEstimate(
            flops=2 * 256 * vels * blocks * SUB * LANES, bytes_accessed=8 * vels * blocks * SUB * LANES, transcendentals=0
        ),
        name="finish_dist",
    )(*carried_parts, inflow_part, h1, h2, vel_index)


def ring(axis, step):
    size = lax.axis_size(axis)
    return [(i, (i + step) % size) for i in range(size)]


def shards(dist, vel_index, relax, wall_mask, macro_inverse):
    vels, width, cells = dist.shape
    blocks = cells // LANES
    peers, slabs = lax.axis_size("vel"), lax.axis_size("space")
    assert width == SUB and peers % blocks == 0 and slabs == 4 and blocks % 2 == 0
    sub = peers // blocks
    me = lax.axis_index("vel")
    place = (me // sub).astype(jnp.int32).reshape(1)
    core = (lax.axis_index("space") % 2).astype(jnp.int32).reshape(1)

    flat = dist.reshape(vels, width, blocks, LANES).transpose(0, 2, 1, 3).reshape(vels * blocks * width, LANES)
    speed = speed_range * (2.0 * vel_index.astype(jnp.float32) + 1.0 - NVX) / NVX
    sign = jnp.broadcast_to(speed[0][:, None], (vels, LANES))

    wall = wall_mask > 0
    coefficients = jnp.stack(
        [
            jnp.where(wall, 0.0, 1.0 - relax),
            jnp.where(wall, 1.0, relax),
            jnp.where(wall, 0.0, relax),
        ],
        0,
    )
    from_low = lax.ppermute(coefficients[:, SUB - 1 :], "space", ring("space", 1))
    from_high = lax.ppermute(coefficients[:, :1], "space", ring("space", -1))

    leaving = outflow(flat, sign, vels, blocks)
    swap = lax.ppermute(leaving, "space", [(i, i ^ 1) for i in range(slabs)])
    cst = jnp.concatenate(
        [coefficients, from_high, jnp.zeros((3, SUB - 2, cells), jnp.float32), from_low], 1
    )

    (cst, leaving) = lax.optimization_barrier((cst, leaving))
    high_part, low_part, *parts = both_moments(place, flat, vel_index, cst, vels, blocks)
    (swap, parts) = lax.optimization_barrier((swap, parts))

    half = vels // 2
    start = core[0] * half
    mine = lax.dynamic_slice_in_dim(leaving, start, half, 1)
    other = lax.dynamic_slice_in_dim(swap, start, half, 1)
    plus = lax.dynamic_slice_in_dim(speed[0], start, half, 0) > 0
    across = jnp.where((plus == (core[0] == 1))[None, :, None], mine, other)
    (across, parts) = lax.optimization_barrier((across, parts))
    first = lax.ppermute(across, "space", [(i, i ^ 2) for i in range(slabs)])

    def beside(step):
        return [(i, (i // sub ^ step) * sub + i % sub) for i in range(peers)]

    spans = [(0, vels)] if vels < 2 * LANES else [(0, vels // 2), (vels // 2, vels - vels // 2)]

    def carry(span):
        return carried(high_part, low_part, vel_index, coefficients[0], span[0], span[1], blocks)

    got = [parts[0]] + [lax.ppermute(parts[k], "vel", beside(k)) for k in range(1, blocks // 2)]
    carried_parts = [carry(spans[0])]
    (got[1], carried_parts[0]) = lax.optimization_barrier((got[1], carried_parts[0]))
    near, far = small_call(pair_kernel, [(PAY, LANES)] * 2, "sum_near", "v" * len(got), got)
    got = [near, lax.ppermute(far, "vel", beside(blocks // 2))]
    if len(spans) > 1:
        (al, _) = lax.optimization_barrier((coefficients[0], near))
        carried_parts.append(carried(high_part, low_part, vel_index, al, *spans[1], blocks))
        (got[1], carried_parts[1]) = lax.optimization_barrier((got[1], carried_parts[1]))
    if sub > 1:
        part = sum(got)
        got = [part]
        for k in range(1, sub):
            pairs = [(i, i // sub * sub + (i % sub + k) % sub) for i in range(peers)]
            got.append(lax.ppermute(part, "vel", pairs))
    chunk, up, down = small_call(
        total_kernel, [(PAY, LANES), (DOWN - UP, LANES), (AA - M1, LANES)], "sum_moments", "v" * len(got), got
    )
    low = lax.ppermute(up, "space", ring("space", 1))
    high = lax.ppermute(down, "space", ring("space", -1))
    (send,) = small_call(
        chunk_kernel, [(SENT, LANES)], "local_fields", "svvv", (macro_inverse, chunk, low, high)
    )
    pieces = [send] + [lax.ppermute(send, "vel", beside(k)) for k in range(1, blocks // 2 + 1)]
    (first, send) = lax.optimization_barrier((first, send))
    second = lax.ppermute(first, "space", [(i, i ^ 1) for i in range(slabs)])
    pieces += [lax.ppermute(pieces[blocks // 2], "vel", beside(k)) for k in range(1, blocks // 2)]
    inflow_part = inflow(core, swap, first, second, sign, vel_index, cst[0], vels, blocks)
    (pieces[-1], inflow_part) = lax.optimization_barrier((pieces[-1], inflow_part))

    h1, later, following, up2, down2, norm1 = small_call(
        functools.partial(fields_kernel, blocks=blocks),
        [
            (blocks, SETS * 8 * SUB, LANES),
            (MOM * SUB, cells),
            (MOM * SUB, cells),
            (16, cells),
            (16, cells),
            (SUB, LANES),
        ],
        "first_fields",
        "ssv" + "v" * blocks,
        (place, macro_inverse, cst, *pieces),
        [pltpu.VMEM((blocks, SENT, LANES), jnp.float32)],
        16,
    )
    low2 = lax.ppermute(up2, "space", ring("space", 1))
    high2 = lax.ppermute(down2, "space", ring("space", -1))
    h2, owned, norm2 = small_call(
        functools.partial(last_kernel, blocks=blocks),
        [(blocks, 8 * SUB, LANES), (MOM, SUB, LANES), (SUB, LANES)],
        "last_fields",
        "svvvvv",
        (place, cst, later, following, low2, high2),
        [pltpu.VMEM((MOM, blocks, SUB, LANES), jnp.float32)],
        16,
    )

    squares = jnp.stack([jnp.sum(norm1), jnp.sum(norm2)])
    around = [lax.ppermute(squares, "space", ring("space", k)) for k in range(1, slabs)]
    if sub > 1:
        owned = lax.dynamic_slice_in_dim(owned, (me % sub) * (LANES // sub), LANES // sub, 2)

    out = finish(carried_parts, inflow_part, h1, h2, vel_index, vels, blocks)
    (around[0], out) = lax.optimization_barrier((around[0], out))
    slab = lax.axis_index("space")
    every = jnp.stack([squares] + around)
    norms = jnp.sqrt(jnp.sum(jnp.roll(every[::-1], slab + 1, axis=0), axis=0))
    out = out.transpose(0, 2, 1, 3).reshape(vels, width, cells)
    return (out, owned, norms)


def solution(mesh):
    return jax.shard_map(
        shards,
        mesh=mesh,
        in_specs=(P("vel", "space", None), P(None, "vel"), P("space", None), P("space", None), P()),
        out_specs=(P("vel", "space", None), P(None, "space", "vel"), P()),
        check_vma=False,
    )
```

time: 313 us -> 180 us (0.58)
  waiting for transfers between devices: 83.3 us -> 22.3 us
  blocking collectives: 37.5 us -> 0 us
  local copies, waits for them, and re-layouts: 33.9 us -> 5.57 us
  starting transfers between devices: 36.3 us -> 30.5 us
    ppermute x1, waiting for transfers between devices: 45.9 us -> 0.01 us  [shards(): first = lax.ppermute(across, 'space', [(i, i ^ 2) for i in range(slabs)])]
    psum x1 -> x0, blocking collectives: 37.5 us -> none  [shards(): norms = jnp.sqrt(lax.psum(squares, ('vel', 'space')))]
    ppermute x14, waiting for transfers between devices: 25.4 us -> 7.71 us  [the longest x4 6.38 us: shards(): lax.ppermute(send, 'vel', beside(k))]
    unnamed x34 -> x30, local copies, waits for them, and re-layouts: 16.9 us -> 3.99 us
    mul x13 -> x0, local copies, waits for them, and re-layouts: 11 us -> none  [the longest x7 5.83 us: shards(): rows = jnp.concatenate([basis * s for s in [stay] + speeds] + [basis], 1)]
    ppermute x1, waiting for transfers between devices: 1.98 us -> 9.38 us  [shards(): low = lax.ppermute(up, 'space', ring('space', 1))]
    ppermute x14, starting transfers between devices: 27.5 us -> 20.4 us  [the longest x4 6.32 us: shards(): lax.ppermute(send, 'vel', beside(k))]
    ppermute x1, waiting for transfers between devices: 7.05 us -> 0.01 us  [shards(): swap = lax.ppermute(leaving, 'space', [(i, i ^ 1) for i in range(slabs)])]
  transfers between devices with their start and end apart: 23 -> 23, of which waited for: 11 -> 6; matrix products, arithmetic and copies ran while one was open for 7% -> 2% of each run, Pallas kernels for 26% -> 53%
where the time goes in v2:
time: 180 us
  Pallas kernels  113 us (63%)
  starting transfers between devices  30.5 us (17%)
  waiting for transfers between devices  22.3 us (12%)
  other arithmetic  7.67 us (4%)
  local copies, waits for them, and re-layouts  5.57 us (3%)
    pallas_call x1, Pallas kernels, both_moments(): pl.pallas_call(functools.partial(moments_kernel, vels=vels, blocks=blocks...  40.5 us
    pallas_call x2, Pallas kernels, carried(): pl.pallas_call(functools.partial(carried_kernel, blocks=blocks), grid=(co...  29.6 us
    pallas_call x1, Pallas kernels, finish(): pl.pallas_call(functools.partial(finish_kernel, vels=vels, parts=len(carr...  17.2 us
    pallas_call x1, Pallas kernels, outflow(): pl.pallas_call(functools.partial(outflow_kernel, count=count, blocks=bloc...  11.5 us
    ppermute x1, waiting for transfers between devices, shards(): low = lax.ppermute(up, 'space', ring('space', 1))  9.38 us
    pallas_call x1, Pallas kernels, inflow(): pl.pallas_call(functools.partial(inflow_kernel, blocks=blocks, half=half)...  7.25 us
    pallas_call x5, Pallas kernels, small_call(): pl.pallas_call(kernel, in_specs=[smem if s == 's' else vmem for s in spec...  6.97 us
    ppermute x4, waiting for transfers between devices, shards(): lax.ppermute(send, 'vel', beside(k))  6.38 us
  transfers between devices with their start and end apart: 23, of which 6 were waited for; matrix products, arithmetic and copies ran while one was open for 2% of the time, Pallas kernels for 53%

profile of v2, /device:TPU:0, one launch (start us, length us, event | category | flops | bytes accessed | tf_op | source)
XLA Modules:
  0.0 179.8 jit_solution(11900917005149777598)
XLA Ops:
  0.6 0.7 fusion.2
  1.3 0.9 broadcast_in_dim.28.dtc_ref.sign_ref
  2.2 11.5 %outflow_planes.1 = f32[2,512,1024]{2,1,0:T(8,128)} custom-call(f32[32768,128]{1,0:T(8,128)} %bitcast.25, f32[512,128]{1,0:T(8,128)} %broadcast_in_dim.28.dtc_ref.sign_ref), custom_call_target="tpu_custom_call" | custom-call | bytes 20971520 | tf_op jit(solution)/shard_map/outflow_planes/pallas_call | solution.py:145
  13.7 0.5 collective-permute-start.2
  14.3 2.6 %collective-permute-start = (f32[3,1,1024]{2,1,0:T(1,128)S(1)}, f32[3,1,1024]{2,1,0:T(1,128)S(1)}, u32[]{:S(2)}, u32[]{:S(2)}) collective-permute-start(f32[3,1,1024]{2,1,0:T(1,128)S(1)} %get-tuple-element.89), channel_id=1, source_target_pairs={{0,3},{1,0},{2,1},{3,2},{4,7},{5,4},{6,5},{7,6},{8,11},{9,8},{10,9... | collective-permute-start | bytes 36872 | tf_op jit(solution)/shard_map/ppermute | solution.py:746
  17.0 1.2 collective-permute-done.1
  18.3 2.6 %collective-permute-done = f32[3,1,1024]{2,1,0:T(1,128)S(1)} collective-permute-done((f32[3,1,1024]{2,1,0:T(1,128)S(1)}, f32[3,1,1024]{2,1,0:T(1,128)S(1)}, u32[]{:S(2)}, u32[]{:S(2)}) %collective-permute-start) | collective-permute-done | bytes 12320 | tf_op jit(solution)/shard_map/ppermute | solution.py:746
  20.9 0.8 pad_maximum_fusion.cst_ref
  21.6 40.5 %moments_of_both.1 = (bf16[8,1024,512]{2,1,0:T(8,128)(2,1)}, bf16[8,1024,512]{2,1,0:T(8,128)(2,1)}, f32[576,128]{1,0:T(8,128)}, f32[576,128]{1,0:T(8,128)}, f32[576,128]{1,0:T(8,128)}, /*index=5*/f32[576,128]{1,0:T(8,128)}) custom-call(s32[1]{0:T(128)} %bitcast.me_ref.place_ref, f32[32768,128]{1,0:T(8,128)} %bitcast.26, s32[3,512]{1,0:T(4,128)} %refs_5_.1, ...), custom_call_target="tpu_custom_call" | custom-call | flops 3523215360 | bytes 33554432 | tf_op jit(solution)/shard_map/moments_of_both/pallas_call | solution.py:313
  62.2 1.9 %dynamic-slice_select_fusion = f32[2,256,1024]{2,1,0:T(8,128)S(1)} fusion(f32[2,512,1024]{2,1,0:T(8,128)} %collective-permute-done.2.swap_ref, s32[]{:T(128)S(6)} %select_n.44, f32[2,512,1024]{2,1,0:T(8,128)S(1)} %copy-done.8, pred[256]{0:T(512)(128)(4,1)S(1)} %compare_reduce_fusion), kind=kLoop, calls=%fused_computation | loop fusion | flops 524288 | bytes 6291716 | tf_op jit(solution)/shard_map/jit(_where)/select_n | solution.py:763
  64.1 3.0 %collective-permute-start.16 = (f32[2,256,1024]{2,1,0:T(8,128)S(1)}, f32[2,256,1024]{2,1,0:T(8,128)S(1)}, u32[]{:S(2)}, u32[]{:S(2)}) collective-permute-start(f32[2,256,1024]{2,1,0:T(8,128)S(1)} %dynamic-slice_select_fusion), channel_id=1, source_target_pairs={{0,2},{1,3},{2,0},{3,1},{4,6},{5,7},{6,4},{7,5},{8,10},{9,11},{10,... | collective-permute-start | bytes 6291464 | tf_op jit(solution)/shard_map/ppermute | solution.py:765
  67.1 1.5 collective-permute-start.3
  68.7 1.6 collective-permute-start.4
  70.2 0.4 collective-permute-start.5
  70.6 15.1 %carried_part.2.refs_0_ = f32[8,1024,256]{2,1,0:T(8,128)} custom-call(bf16[8,1024,512]{2,1,0:T(8,128)(2,1)} %get-tuple-element.58.high_ref, bf16[8,1024,512]{2,1,0:T(8,128)(2,1)} %get-tuple-element.59.low_ref, s32[3,512]{1,0:T(4,128)} %refs_5_.1, f32[8,1024]{1,0:T(8,128)} %copy-done.9), custom_call_target="tpu_custom_call" | custom-call | flops 83886080 | bytes 16777216 | tf_op jit(solution)/shard_map/carried_part/pallas_call | solution.py:373
  85.8 2.7 %collective-permute-start.6 = (f32[288,128]{1,0:T(8,128)S(1)}, f32[288,128]{1,0:T(8,128)S(1)}, u32[]{:S(2)}, u32[]{:S(2)}) collective-permute-start(f32[288,128]{1,0:T(8,128)S(1)} %get-tuple-element.64), channel_id=1, source_target_pairs={{0,16},{4,20},{8,24},{12,28},{16,0},{20,4},{24,8},{28,12},{1,17},{... | collective-permute-start | bytes 442376 | tf_op jit(solution)/shard_map/ppermute | solution.py:779
  88.5 14.5 %carried_part.3.refs_1_ = f32[8,1024,256]{2,1,0:T(8,128)} custom-call(bf16[8,1024,512]{2,1,0:T(8,128)(2,1)} %get-tuple-element.58.high_ref, bf16[8,1024,512]{2,1,0:T(8,128)(2,1)} %get-tuple-element.59.low_ref, s32[3,512]{1,0:T(4,128)} %refs_5_.1, f32[8,1024]{1,0:T(8,128)} %copy-done.9), custom_call_target="tpu_custom_call" | custom-call | flops 83886080 | bytes 16777216 | tf_op jit(solution)/shard_map/carried_part/pallas_call | solution.py:373
  103.0 1.7 collective-permute-start.8
  104.8 9.4 %collective-permute-done.7.low_ref = f32[144,128]{1,0:T(8,128)S(1)} collective-permute-done((f32[144,128]{1,0:T(8,128)S(1)}, f32[144,128]{1,0:T(8,128)S(1)}, u32[]{:S(2)}, u32[]{:S(2)}) %collective-permute-start.7) | collective-permute-done | bytes 73760 | tf_op jit(solution)/shard_map/ppermute | solution.py:793
  114.2 0.8 local_fields.1.refs_0_
  115.0 0.4 collective-permute-start.17
  115.3 2.8 %collective-permute-start.12 = (f32[248,128]{1,0:T(8,128)S(1)}, f32[248,128]{1,0:T(8,128)S(1)}, u32[]{:S(2)}, u32[]{:S(2)}) collective-permute-start(f32[248,128]{1,0:T(8,128)S(1)} %local_fields.1.refs_0_), channel_id=1, source_target_pairs={{0,16},{4,20},{8,24},{12,28},{16,0},{20,4},{24,8},{28,12},{1,17},{... | collective-permute-start | bytes 380936 | tf_op jit(solution)/shard_map/ppermute | solution.py:798
  118.2 6.4 %collective-permute-done.12.refs_4_ = f32[248,128]{1,0:T(8,128)S(1)} collective-permute-done((f32[248,128]{1,0:T(8,128)S(1)}, f32[248,128]{1,0:T(8,128)S(1)}, u32[]{:S(2)}, u32[]{:S(2)}) %collective-permute-start.12) | collective-permute-done | bytes 127008 | tf_op jit(solution)/shard_map/ppermute | solution.py:798
  124.6 1.7 collective-permute-start.15
  126.2 0.5 collective-permute-start.9
  126.7 1.3 collective-permute-start.10
  128.0 1.7 collective-permute-start.11
  129.7 1.3 collective-permute-done.15.refs_7_
  131.0 2.3 %collective-permute-start.13 = (f32[248,128]{1,0:T(8,128)S(1)}, f32[248,128]{1,0:T(8,128)S(1)}, u32[]{:S(2)}, u32[]{:S(2)}) collective-permute-start(f32[248,128]{1,0:T(8,128)S(1)} %collective-permute-done.12.refs_4_), channel_id=1, source_target_pairs={{0,4},{4,0},{8,12},{12,8},{16,20},{20,16},{24,28},{28,24},{1,5},{5... | collective-permute-start | bytes 380936 | tf_op jit(solution)/shard_map/ppermute | solution.py:801
  133.4 0.7 collective-permute-start.14
  134.0 7.2 %inflow_part.1.refs_2_ = f32[2,1024,512]{2,1,0:T(8,128)S(1)} custom-call(s32[1]{0:T(128)} %bitcast.10.core_ref, f32[2,512,1024]{2,1,0:T(8,128)} %collective-permute-done.2.swap_ref, f32[2,256,1024]{2,1,0:T(8,128)S(1)} %collective-permute-done.16.first_ref, f32[2,256,1024]{2,1,0:T(8,128)S(1)} %collective-permute-done.17.second_ref, f32[512,128]{1,0:T(8,128)S(1)} %copy-done.2, ...), custom_call_target="tpu_custom_call" | custom-call | flops 31457280 | bytes 12582912 | tf_op jit(solution)/shard_map/inflow_part/pallas_call | solution.py:447
  141.3 1.9 %copy-done = f32[2,1024,512]{2,1,0:T(8,128)} copy-done((f32[2,1024,512]{2,1,0:T(8,128)}, f32[2,1024,512]{2,1,0:T(8,128)S(1)}, u32[]{:S(2)}) %copy-start) | copy-done | bytes 4194328
  143.3 3.9 %first_fields.1 = (f32[8,448,128]{2,1,0:T(8,128)S(1)}, f32[104,1024]{1,0:T(8,128)S(1)}, f32[104,1024]{1,0:T(8,128)S(1)}, f32[16,1024]{1,0:T(8,128)S(1)}, f32[16,1024]{1,0:T(8,128)S(1)}, /*index=5*/f32[8,128]{1,0:T(8,128)S(1)}) custom-call(s32[1]{0:T(128)} %bitcast.me_ref.place_ref, f32[13,13]{1,0:T(8,128)S(1)} %copy-done.7, f32[3,16,1024]{2,1,0:T(8,128)S(1)} %copy-done.1, ...), custom_call_target="tpu_custom_call" | custom-call | tf_op jit(solution)/shard_map/first_fields/pallas_call | solution.py:475
  147.2 1.3 copy-done.3
  148.5 1.7 collective-permute-start.19
  150.2 0.6 reduce_sum.27
  150.8 1.3 collective-permute-done.18.low_ref
  152.2 2.2 %last_fields.1 = (f32[8,64,128]{2,1,0:T(8,128)S(1)}, f32[13,8,128]{2,1,0:T(8,128)}, f32[8,128]{1,0:T(8,128)S(1)}) custom-call(s32[1]{0:T(128)} %bitcast.me_ref.place_ref, f32[3,16,1024]{2,1,0:T(8,128)S(1)} %copy-done.1, f32[104,1024]{1,0:T(8,128)S(1)} %get-tuple-element.74.later_ref, f32[104,1024]{1,0:T(8,128)S(1)} %get-tuple-element.75.next_ref, ...), custom_call_target="tpu_custom_call" | custom-call | tf_op jit(solution)/shard_map/last_fields/pallas_call | solution.py:475
  154.4 0.7 copy-done.5
  155.1 0.6 reduce_sum.28
  155.7 1.4 pad_maximum_fusion.6
  157.0 1.6 collective-permute-start.20
  158.7 0.2 collective-permute-start.22
  158.8 1.5 collective-permute-start.21
  160.3 1.4 fusion.3
  161.7 17.2 %finish_dist.1 = f32[512,8,8,128]{3,2,1,0:T(8,128)} custom-call(f32[8,1024,256]{2,1,0:T(8,128)} %carried_part.2.refs_0_, f32[8,1024,256]{2,1,0:T(8,128)} %carried_part.3.refs_1_, f32[2,1024,512]{2,1,0:T(8,128)} %copy-done, f32[8,448,128]{2,1,0:T(8,128)} %copy-done.3, f32[8,64,128]{2,1,0:T(8,128)} %copy-done.5, s32[3,512]{1,0:T(4,128)} %refs_5_.1), custom_call_target="tpu_custom_call" | custom-call | flops 2147483648 | bytes 33554432 | tf_op jit(solution)/shard_map/finish_dist/pallas_call | solution.py:696
  179.1 0.2 dynamic-slice_reduce_fusion
  179.3 0.5 sqrt.3
  (60 shorter events, 0.7 us)
Async XLA Ops:
  2.2 12.0 %copy-start.10 = (f32[8,1024]{1,0:T(8,128)S(1)}, f32[8,1024]{1,0:T(8,128)}, u32[]{:S(2)}) copy-start(f32[8,1024]{1,0:T(8,128)} %param.7) | copy-start | bytes 98308
  2.2 12.0 %copy-start.11 = (s32[8,1024]{1,0:T(8,128)S(1)}, s32[8,1024]{1,0:T(8,128)}, u32[]{:S(2)}) copy-start(s32[8,1024]{1,0:T(8,128)} %param.8) | copy-start | bytes 98308
  13.7 48.5 %collective-permute-start.2 = (f32[2,512,1024]{2,1,0:T(8,128)}, f32[2,512,1024]{2,1,0:T(8,128)}, u32[]{:S(2)}, u32[]{:S(2)}) collective-permute-start(f32[2,512,1024]{2,1,0:T(8,128)} %outflow_planes.1), channel_id=1, source_target_pairs={{0,1},{1,0},{2,3},{3,2},{4,5},{5,4},{6,7},{7,6},{8,9},{9,8},{10,11... | collective-permute-start | bytes 12582920 | tf_op jit(solution)/shard_map/ppermute | solution.py:749
  14.2 48.0 %copy-start.9 = (f32[8,1024]{1,0:T(8,128)}, f32[8,1024]{1,0:T(8,128)S(1)}, u32[]{:S(2)}) copy-start(f32[8,1024]{1,0:T(8,128)S(1)} %get-tuple-element.65.al_ref) | copy-start | bytes 98308
  14.2 4.0 %collective-permute-start.1 = (f32[3,1,1024]{2,1,0:T(1,128)S(1)}, f32[3,1,1024]{2,1,0:T(1,128)S(1)}, u32[]{:S(2)}, u32[]{:S(2)}) collective-permute-start(f32[3,1,1024]{2,1,0:T(1,128)S(1)} %get-tuple-element.90), channel_id=1, source_target_pairs={{0,1},{1,2},{2,3},{3,0},{4,5},{5,6},{6,7},{7,4},{8,9},{9,10},{10,1... | collective-permute-start | bytes 36872 | tf_op jit(solution)/shard_map/ppermute | solution.py:745
  14.3 6.5 %collective-permute-start = (f32[3,1,1024]{2,1,0:T(1,128)S(1)}, f32[3,1,1024]{2,1,0:T(1,128)S(1)}, u32[]{:S(2)}, u32[]{:S(2)}) collective-permute-start(f32[3,1,1024]{2,1,0:T(1,128)S(1)} %get-tuple-element.89), channel_id=1, source_target_pairs={{0,3},{1,0},{2,1},{3,2},{4,7},{5,4},{6,5},{7,6},{8,11},{9,8},{10,9... | collective-permute-start | bytes 36872 | tf_op jit(solution)/shard_map/ppermute | solution.py:746
  21.6 40.5 %copy-start.8 = (f32[2,512,1024]{2,1,0:T(8,128)S(1)}, f32[2,512,1024]{2,1,0:T(8,128)}, u32[]{:S(2)}) copy-start(f32[2,512,1024]{2,1,0:T(8,128)} %outflow_planes.1) | copy-start | bytes 12582916
  62.1 5.0 %copy-start.14 = (f32[576,128]{1,0:T(8,128)S(1)}, f32[576,128]{1,0:T(8,128)}, u32[]{:S(2)}) copy-start(f32[576,128]{1,0:T(8,128)} %get-tuple-element.57) | copy-start | bytes 884740
  62.1 6.5 %copy-start.13 = (f32[576,128]{1,0:T(8,128)S(1)}, f32[576,128]{1,0:T(8,128)}, u32[]{:S(2)}) copy-start(f32[576,128]{1,0:T(8,128)} %get-tuple-element.61) | copy-start | bytes 884740
  62.2 8.1 %copy-start.12 = (f32[576,128]{1,0:T(8,128)S(1)}, f32[576,128]{1,0:T(8,128)}, u32[]{:S(2)}) copy-start(f32[576,128]{1,0:T(8,128)} %get-tuple-element.62) | copy-start | bytes 884740
  64.1 50.8 %collective-permute-start.16 = (f32[2,256,1024]{2,1,0:T(8,128)S(1)}, f32[2,256,1024]{2,1,0:T(8,128)S(1)}, u32[]{:S(2)}, u32[]{:S(2)}) collective-permute-start(f32[2,256,1024]{2,1,0:T(8,128)S(1)} %dynamic-slice_select_fusion), channel_id=1, source_target_pairs={{0,2},{1,3},{2,0},{3,1},{4,6},{5,7},{6,4},{7,5},{8,10},{9,11},{10,... | collective-permute-start | bytes 6291464 | tf_op jit(solution)/shard_map/ppermute | solution.py:765
  67.1 18.6 %collective-permute-start.3 = (f32[576,128]{1,0:T(8,128)S(1)}, f32[576,128]{1,0:T(8,128)S(1)}, u32[]{:S(2)}, u32[]{:S(2)}) collective-permute-start(f32[576,128]{1,0:T(8,128)S(1)} %copy-done.14), channel_id=1, source_target_pairs={{0,4},{4,0},{8,12},{12,8},{16,20},{20,16},{24,28},{28,24},{1,5},{5... | collective-permute-start | bytes 884744 | tf_op jit(solution)/shard_map/ppermute | solution.py:775
  68.7 17.1 %collective-permute-start.4 = (f32[576,128]{1,0:T(8,128)S(1)}, f32[576,128]{1,0:T(8,128)S(1)}, u32[]{:S(2)}, u32[]{:S(2)}) collective-permute-start(f32[576,128]{1,0:T(8,128)S(1)} %copy-done.13), channel_id=1, source_target_pairs={{0,8},{4,12},{8,0},{12,4},{16,24},{20,28},{24,16},{28,20},{1,9},{5... | collective-permute-start | bytes 884744 | tf_op jit(solution)/shard_map/ppermute | solution.py:775
  70.2 15.5 %collective-permute-start.5 = (f32[576,128]{1,0:T(8,128)S(1)}, f32[576,128]{1,0:T(8,128)S(1)}, u32[]{:S(2)}, u32[]{:S(2)}) collective-permute-start(f32[576,128]{1,0:T(8,128)S(1)} %copy-done.12), channel_id=1, source_target_pairs={{0,12},{4,8},{8,4},{12,0},{16,28},{20,24},{24,20},{28,16},{1,13},{... | collective-permute-start | bytes 884744 | tf_op jit(solution)/shard_map/ppermute | solution.py:775
  70.6 15.1 %copy-start.4 = (f32[576,128]{1,0:T(8,128)S(1)}, f32[576,128]{1,0:T(8,128)}, u32[]{:S(2)}) copy-start(f32[576,128]{1,0:T(8,128)} %get-tuple-element.56.refs_0_) | copy-start | bytes 884740
  85.8 17.2 %collective-permute-start.6 = (f32[288,128]{1,0:T(8,128)S(1)}, f32[288,128]{1,0:T(8,128)S(1)}, u32[]{:S(2)}, u32[]{:S(2)}) collective-permute-start(f32[288,128]{1,0:T(8,128)S(1)} %get-tuple-element.64), channel_id=1, source_target_pairs={{0,16},{4,20},{8,24},{12,28},{16,0},{20,4},{24,8},{28,12},{1,17},{... | collective-permute-start | bytes 442376 | tf_op jit(solution)/shard_map/ppermute | solution.py:779
  88.5 25.7 %copy-start.7 = (f32[13,13]{1,0:T(8,128)S(1)}, f32[13,13]{1,0:T(8,128)}, u32[]{:S(2)}) copy-start(f32[13,13]{1,0:T(8,128)} %inv_ref.3) | copy-start | bytes 2032
  88.5 45.6 %copy-start.1 = (f32[3,16,1024]{2,1,0:T(8,128)S(1)}, f32[3,16,1024]{2,1,0:T(8,128)}, u32[]{:S(2)}) copy-start(f32[3,16,1024]{2,1,0:T(8,128)} %pad_maximum_fusion.cst_ref) | copy-start | bytes 589828
  88.5 45.6 %copy-start.2 = (f32[512,128]{1,0:T(8,128)S(1)}, f32[512,128]{1,0:T(8,128)}, u32[]{:S(2)}) copy-start(f32[512,128]{1,0:T(8,128)} %broadcast_in_dim.28.dtc_ref.sign_ref) | copy-start | bytes 786436
  88.5 45.6 %copy-start.6 = (s32[3,512]{1,0:T(4,128)S(1)}, s32[3,512]{1,0:T(4,128)}, u32[]{:S(2)}) copy-start(s32[3,512]{1,0:T(4,128)} %refs_5_.1) | copy-start | bytes 18436
  103.0 11.2 %collective-permute-start.7 = (f32[144,128]{1,0:T(8,128)S(1)}, f32[144,128]{1,0:T(8,128)S(1)}, u32[]{:S(2)}, u32[]{:S(2)}) collective-permute-start(f32[144,128]{1,0:T(8,128)S(1)} %get-tuple-element.68), channel_id=1, source_target_pairs={{0,1},{1,2},{2,3},{3,0},{4,5},{5,6},{6,7},{7,4},{8,9},{9,10},{10,1... | collective-permute-start | bytes 221192 | tf_op jit(solution)/shard_map/ppermute | solution.py:793
  103.0 11.1 %collective-permute-start.8 = (f32[144,128]{1,0:T(8,128)S(1)}, f32[144,128]{1,0:T(8,128)S(1)}, u32[]{:S(2)}, u32[]{:S(2)}) collective-permute-start(f32[144,128]{1,0:T(8,128)S(1)} %get-tuple-element.69), channel_id=1, source_target_pairs={{0,3},{1,0},{2,1},{3,2},{4,7},{5,4},{6,5},{7,6},{8,11},{9,8},{10,9... | collective-permute-start | bytes 221192 | tf_op jit(solution)/shard_map/ppermute | solution.py:794
  115.0 18.4 %collective-permute-start.17 = (f32[2,256,1024]{2,1,0:T(8,128)S(1)}, f32[2,256,1024]{2,1,0:T(8,128)S(1)}, u32[]{:S(2)}, u32[]{:S(2)}) collective-permute-start(f32[2,256,1024]{2,1,0:T(8,128)S(1)} %collective-permute-done.16.first_ref), channel_id=1, source_target_pairs={{0,1},{1,0},{2,3},{3,2},{4,5},{5,4},{6,7},{7,6},{8,9},{9,8},{10,11... | collective-permute-start | bytes 6291464 | tf_op jit(solution)/shard_map/ppermute | solution.py:800
  115.3 9.2 %collective-permute-start.12 = (f32[248,128]{1,0:T(8,128)S(1)}, f32[248,128]{1,0:T(8,128)S(1)}, u32[]{:S(2)}, u32[]{:S(2)}) collective-permute-start(f32[248,128]{1,0:T(8,128)S(1)} %local_fields.1.refs_0_), channel_id=1, source_target_pairs={{0,16},{4,20},{8,24},{12,28},{16,0},{20,4},{24,8},{28,12},{1,17},{... | collective-permute-start | bytes 380936 | tf_op jit(solution)/shard_map/ppermute | solution.py:798
  124.6 6.5 %collective-permute-start.15 = (f32[248,128]{1,0:T(8,128)S(1)}, f32[248,128]{1,0:T(8,128)S(1)}, u32[]{:S(2)}, u32[]{:S(2)}) collective-permute-start(f32[248,128]{1,0:T(8,128)S(1)} %collective-permute-done.12.refs_4_), channel_id=1, source_target_pairs={{0,12},{4,8},{8,4},{12,0},{16,28},{20,24},{24,20},{28,16},{1,13},{... | collective-permute-start | bytes 380936 | tf_op jit(solution)/shard_map/ppermute | solution.py:801
  126.2 17.0 %collective-permute-start.9 = (f32[248,128]{1,0:T(8,128)S(1)}, f32[248,128]{1,0:T(8,128)S(1)}, u32[]{:S(2)}, u32[]{:S(2)}) collective-permute-start(f32[248,128]{1,0:T(8,128)S(1)} %local_fields.1.refs_0_), channel_id=1, source_target_pairs={{0,4},{4,0},{8,12},{12,8},{16,20},{20,16},{24,28},{28,24},{1,5},{5... | collective-permute-start | bytes 380936 | tf_op jit(solution)/shard_map/ppermute | solution.py:798
  126.7 16.5 %collective-permute-start.10 = (f32[248,128]{1,0:T(8,128)S(1)}, f32[248,128]{1,0:T(8,128)S(1)}, u32[]{:S(2)}, u32[]{:S(2)}) collective-permute-start(f32[248,128]{1,0:T(8,128)S(1)} %local_fields.1.refs_0_), channel_id=1, source_target_pairs={{0,8},{4,12},{8,0},{12,4},{16,24},{20,28},{24,16},{28,20},{1,9},{5... | collective-permute-start | bytes 380936 | tf_op jit(solution)/shard_map/ppermute | solution.py:798
  128.0 15.2 %collective-permute-start.11 = (f32[248,128]{1,0:T(8,128)S(1)}, f32[248,128]{1,0:T(8,128)S(1)}, u32[]{:S(2)}, u32[]{:S(2)}) collective-permute-start(f32[248,128]{1,0:T(8,128)S(1)} %local_fields.1.refs_0_), channel_id=1, source_target_pairs={{0,12},{4,8},{8,4},{12,0},{16,28},{20,24},{24,20},{28,16},{1,13},{... | collective-permute-start | bytes 380936 | tf_op jit(solution)/shard_map/ppermute | solution.py:798
  131.0 12.2 %collective-permute-start.13 = (f32[248,128]{1,0:T(8,128)S(1)}, f32[248,128]{1,0:T(8,128)S(1)}, u32[]{:S(2)}, u32[]{:S(2)}) collective-permute-start(f32[248,128]{1,0:T(8,128)S(1)} %collective-permute-done.12.refs_4_), channel_id=1, source_target_pairs={{0,4},{4,0},{8,12},{12,8},{16,20},{20,16},{24,28},{28,24},{1,5},{5... | collective-permute-start | bytes 380936 | tf_op jit(solution)/shard_map/ppermute | solution.py:801
  133.4 9.9 %collective-permute-start.14 = (f32[248,128]{1,0:T(8,128)S(1)}, f32[248,128]{1,0:T(8,128)S(1)}, u32[]{:S(2)}, u32[]{:S(2)}) collective-permute-start(f32[248,128]{1,0:T(8,128)S(1)} %collective-permute-done.12.refs_4_), channel_id=1, source_target_pairs={{0,8},{4,12},{8,0},{12,4},{16,24},{20,28},{24,16},{28,20},{1,9},{5... | collective-permute-start | bytes 380936 | tf_op jit(solution)/shard_map/ppermute | solution.py:801
  141.3 2.0 %copy-start = (f32[2,1024,512]{2,1,0:T(8,128)}, f32[2,1024,512]{2,1,0:T(8,128)S(1)}, u32[]{:S(2)}) copy-start(f32[2,1024,512]{2,1,0:T(8,128)S(1)} %inflow_part.1.refs_2_) | copy-start | bytes 12582916
  147.2 1.3 copy-start.3
  148.5 3.7 %collective-permute-start.18 = (f32[16,1024]{1,0:T(8,128)S(1)}, f32[16,1024]{1,0:T(8,128)S(1)}, u32[]{:S(2)}, u32[]{:S(2)}) collective-permute-start(f32[16,1024]{1,0:T(8,128)S(1)} %get-tuple-element.76), channel_id=1, source_target_pairs={{0,1},{1,2},{2,3},{3,0},{4,5},{5,6},{6,7},{7,4},{8,9},{9,10},{10,1... | collective-permute-start | bytes 196616 | tf_op jit(solution)/shard_map/ppermute | solution.py:821
  148.5 3.7 %collective-permute-start.19 = (f32[16,1024]{1,0:T(8,128)S(1)}, f32[16,1024]{1,0:T(8,128)S(1)}, u32[]{:S(2)}, u32[]{:S(2)}) collective-permute-start(f32[16,1024]{1,0:T(8,128)S(1)} %get-tuple-element.77), channel_id=1, source_target_pairs={{0,3},{1,0},{2,1},{3,2},{4,7},{5,4},{6,5},{7,6},{8,11},{9,8},{10,9... | collective-permute-start | bytes 196616 | tf_op jit(solution)/shard_map/ppermute | solution.py:822
  154.4 0.7 copy-start.5
  157.0 21.8 %collective-permute-start.20 = (f32[2]{0:T(128)S(1)}, f32[2]{0:T(128)S(1)}, u32[]{:S(2)}, u32[]{:S(2)}) collective-permute-start(f32[2]{0:T(128)S(1)} %pad_maximum_fusion.6), channel_id=1, source_target_pairs={{0,1},{1,2},{2,3},{3,0},{4,5},{5,6},{6,7},{7,4},{8,9},{9,10},{10,1... | collective-permute-start | bytes 32 | tf_op jit(solution)/shard_map/ppermute | solution.py:834
  158.7 20.2 %collective-permute-start.22 = (f32[2]{0:T(128)S(1)}, f32[2]{0:T(128)S(1)}, u32[]{:S(2)}, u32[]{:S(2)}) collective-permute-start(f32[2]{0:T(128)S(1)} %pad_maximum_fusion.6), channel_id=1, source_target_pairs={{0,3},{1,0},{2,1},{3,2},{4,7},{5,4},{6,5},{7,6},{8,11},{9,8},{10,9... | collective-permute-start | bytes 32 | tf_op jit(solution)/shard_map/ppermute | solution.py:834
  158.8 20.0 %collective-permute-start.21 = (f32[2]{0:T(128)S(1)}, f32[2]{0:T(128)S(1)}, u32[]{:S(2)}, u32[]{:S(2)}) collective-permute-start(f32[2]{0:T(128)S(1)} %pad_maximum_fusion.6), channel_id=1, source_target_pairs={{0,2},{1,3},{2,0},{3,1},{4,6},{5,7},{6,4},{7,5},{8,10},{9,11},{10,... | collective-permute-start | bytes 32 | tf_op jit(solution)/shard_map/ppermute | solution.py:834

commit v3 on v2

v3 whole, which is shorter than its diff:
```python
import functools
import math

import jax
import jax.numpy as jnp
import numpy as np
from jax import lax
from jax.experimental import pallas as pl
from jax.experimental.pallas import tpu as pltpu
from jax.sharding import PartitionSpec as P

NVX = 16
NZ = 16
MOM = 13
SWEEPS = 3
LANES = 128
SUB = 8
SETS = 7
PICK = (0, 1, 2, 3, 4, 10, 11, 12)

speed_range = 4.0
time_step = 0.08
coupling = 0.5
MIB = 2**20
PIECES = 8
RUN = 16

UP, M1, DOWN, AA, PAY = 0, 40, 144, 184, 288
STILL = (0, 10, 11, 12)
MOVED, FIXED, EDGE, LATER, SQUARE, SENT = 64, 96, 128, 136, 240, 248


def functions_of(cx, cy, cz):
    square = cx * cx + cy * cy + cz * cz
    heat = square - 2.5
    one = cx * 0.0 + 1.0
    rows = [
        one, cx, cy, cz, 2.0 * square / 3.0 - 1.0, 2.0 * cx * cy, 2.0 * cx * cz, 2.0 * cy * cz,
        cx * cx - cy * cy, cy * cy - cz * cz, cx * heat, cy * heat, cz * heat,
    ]
    factor = 4.0 / 15.0
    shakhov = [
        one, 2.0 * cx, 2.0 * cy, 2.0 * cz, square - 1.5,
        factor * cx * heat, factor * cy * heat, factor * cz * heat,
    ]
    return rows, shakhov, square


def half_speeds(cx, cy, cz):
    out = []
    for c in (cx, cy, cz):
        out.append(time_step * c * (c > 0))
        out.append(-time_step * c * (c < 0))
    return out


@functools.lru_cache(None)
def stream_matrices():
    line = speed_range * (2.0 * np.arange(NVX) + 1.0 - NVX) / NVX
    cx, cy, cz = (g.reshape(-1) for g in np.meshgrid(line, line, line, indexing="ij"))
    rows, shakhov, square = functions_of(cx, cy, cz)
    weight = (2.0 * speed_range / NVX) ** 3 * math.pi ** (-1.5) * np.exp(-square)
    rows = np.stack(rows) * weight
    shakhov = np.stack(shakhov)
    speeds = half_speeds(cx, cy, cz)
    stay = 1.0 - sum(speeds)
    out = np.stack([(rows * s) @ shakhov.T for s in [stay] + speeds])
    out[np.abs(out) < 1e-13] = 0.0
    return out


def split(value):
    high = value.astype(jnp.bfloat16)
    low = (value - high.astype(jnp.float32)).astype(jnp.bfloat16)
    return high, low


def speeds_at(index):
    speed = speed_range * (2.0 * index.astype(jnp.float32) + 1.0 - NVX) / NVX
    return [time_step * speed[a : a + 1] for a in range(3)]


class Upwind:
    def __init__(self, index):
        tx, ty, tz = speeds_at(index)
        shape = (NZ, LANES)
        self.ax, self.ay, self.az = (jnp.broadcast_to(jnp.abs(t), shape) for t in (tx, ty, tz))
        self.stay = 1.0 - self.ax - self.ay - self.az
        self.px, self.py, self.pz = (jnp.broadcast_to(t, shape) > 0 for t in (tx, ty, tz))

    def across(self, rows):
        out = []
        for before, here, after in zip(rows[:-2], rows[1:-1], rows[2:]):
            in_y = jnp.where(self.py, before, after)
            in_z = jnp.where(self.pz, pltpu.roll(here, 1, axis=0), pltpu.roll(here, NZ - 1, axis=0))
            out.append(self.stay * here + self.ay * in_y + self.az * in_z)
        return out

    def stream(self, ref, x, first, count):
        mid = self.across(run_of(lambda y: ref[x + 1, rows_of(y), :], first, count))
        out = []
        for j, value in enumerate(mid):
            at = rows_of(first + j)
            out.append(value + self.ax * jnp.where(self.px, ref[x, at, :], ref[x + 2, at, :]))
        return out


def run_of(read, first, count):
    ends = [lax.rem(first + count - 1, count), lax.rem(first + RUN, count)]
    return [read(ends[0])] + [read(first + j) for j in range(RUN)] + [read(ends[1])]


def rows_of(y):
    return pl.ds(pl.multiple_of(y * NZ, NZ), NZ)


def each_run(count, body):
    @pl.loop(0, count // RUN)
    def _(i):
        body(i * RUN)


def lane_copies(ref_row, target, blocks):
    for k in range(blocks):
        at = slice(k * LANES, (k + 1) * LANES)
        target[at, :] = jnp.broadcast_to(ref_row[:, at], (LANES, LANES)).T


def roll_y(value, sign):
    cells = value.shape[1]
    return pltpu.roll(value, NZ if sign > 0 else cells - NZ, axis=1)


def roll_z(value, sign):
    cells = value.shape[1]
    zl = lax.broadcasted_iota(jnp.int32, value.shape, 1) & (NZ - 1)
    if sign > 0:
        return jnp.where(zl == 0, pltpu.roll(value, cells - (NZ - 1), axis=1), pltpu.roll(value, 1, axis=1))
    return jnp.where(zl == NZ - 1, pltpu.roll(value, NZ - 1, axis=1), pltpu.roll(value, cells - 1, axis=1))


def stream_kernel(dist_ref, index_ref, leaving_ref, read_ref, held, even, odd, done, sems, out_sems, *, vels, blocks):
    stride = blocks * SUB
    chunks = vels // LANES
    part = LANES * stride
    piece = part // PIECES
    ys = blocks * LANES // NZ

    def fetch(c):
        return [
            pltpu.make_async_copy(
                dist_ref.at[pl.ds(c * part + p * piece, piece)],
                held.at[c % 2, pl.ds(p * piece, piece)],
                sems.at[c % 2, p],
            )
            for p in range(PIECES)
        ]

    def store(c):
        return pltpu.make_async_copy(done.at[c % 2], read_ref.at[c], out_sems.at[c % 2])

    def turn(c, k):
        target = odd if c % 2 else even
        for x in range(SUB):
            value = held[c % 2, pl.ds(k * SUB + x, LANES, stride=stride), :]
            target[x + 1, pl.ds(pl.multiple_of(k * LANES, LANES), LANES), :] = value.T

    for c in range(min(2, chunks)):
        for copy in fetch(c):
            copy.start()
    empty = jnp.zeros((ys * NZ, LANES), jnp.float32)
    for ref in (even, odd):
        ref[0] = empty
        ref[SUB + 1] = empty
    for copy in fetch(0):
        copy.wait()

    @pl.loop(0, blocks)
    def _(k):
        turn(0, k)

    for c in range(chunks):
        turned = odd if c % 2 else even
        if c + 2 < chunks:
            for copy in fetch(c + 2):
                copy.start()
        if c + 1 < chunks:
            for copy in fetch(c + 1):
                copy.wait()
        if c >= 2:
            store(c - 2).wait()
        upwind = Upwind(index_ref[:, c * LANES : (c + 1) * LANES])

        @pl.loop(0, SUB)
        def _(x, upwind=upwind, c=c, turned=turned):
            if c + 1 < chunks and blocks == SUB:
                turn(c + 1, x)
            for first in range(0, ys, RUN):
                for j, value in enumerate(upwind.stream(turned, x, first, ys)):
                    done[c % 2, x, rows_of(first + j), :] = value

        if c + 1 < chunks and blocks != SUB:

            @pl.loop(0, blocks)
            def _(k, c=c):
                turn(c + 1, k)

        def edges(first, upwind=upwind, c=c, turned=turned):
            for j in range(RUN):
                at = rows_of(first + j)
                bottom, top = turned[1, at, :], turned[SUB, at, :]
                done[c % 2, SUB, at, :] = top
                done[c % 2, SUB + 1, at, :] = bottom
                leaving_ref[c, 0, at, :] = jnp.where(upwind.px, top, bottom)
                leaving_ref[c, 1, at, :] = jnp.where(upwind.px, turned[SUB - 1, at, :], turned[2, at, :])

        each_run(ys, edges)
        store(c).start()
    for c in range(max(0, chunks - 2), chunks):
        store(c).wait()


def first_stream(flat, vel_index, vels, blocks):
    cells = blocks * LANES
    anywhere = pl.BlockSpec(memory_space=pl.ANY)
    vmem = pl.BlockSpec(memory_space=pltpu.VMEM)
    return pl.pallas_call(
        functools.partial(stream_kernel, vels=vels, blocks=blocks),
        in_specs=[anywhere, vmem],
        out_specs=[vmem, anywhere],
        out_shape=[
            jax.ShapeDtypeStruct((vels // LANES, 2, cells, LANES), jnp.float32),
            jax.ShapeDtypeStruct((vels // LANES, SUB + 2, cells, LANES), jnp.float32),
        ],
        scratch_shapes=[
            pltpu.VMEM((2, LANES * blocks * SUB, LANES), jnp.float32),
            pltpu.VMEM((SUB + 2, cells, LANES), jnp.float32),
            pltpu.VMEM((SUB + 2, cells, LANES), jnp.float32),
            pltpu.VMEM((2, SUB + 2, cells, LANES), jnp.float32),
            pltpu.SemaphoreType.DMA((2, PIECES)),
            pltpu.SemaphoreType.DMA((2,)),
        ],
        compiler_params=pltpu.CompilerParams(vmem_limit_bytes=54 * MIB),
        cost_estimate=pl.CostEstimate(
            flops=20 * vels * SUB * cells, bytes_accessed=8 * vels * SUB * cells, transcendentals=0
        ),
        name="first_stream",
    )(flat, vel_index)


def moments_kernel(me_ref, read_ref, index_ref, cst_ref, *refs, vels, blocks):
    half = blocks // 2
    outs = refs[:half]
    table, wst, acc, gacc, pay = refs[half:]
    span = SETS * 16
    step = pl.program_id(0)

    @pl.when(step == 0)
    def _():
        speed = [speed_range * (2.0 * index_ref[a : a + 1, :].astype(jnp.float32) + 1.0 - NVX) / NVX for a in range(3)]
        rows, _, square = functions_of(*speed)
        weight = (2.0 * speed_range / NVX) ** 3 * math.pi ** (-1.5) * jnp.exp(-square)
        table[...] = jnp.zeros_like(table)
        for m, row in enumerate(rows):
            table[m : m + 1, :] = row * weight
        base = table[...]
        speeds = []
        for c in speed:
            speeds.append(jnp.where(c > 0, time_step * c, 0.0))
            speeds.append(jnp.where(c < 0, -time_step * c, 0.0))
        full = jnp.concatenate([base] + [base * s for s in speeds] + [jnp.zeros_like(base)], axis=0)
        for variant, factor in enumerate([None, speeds[0], speeds[1]]):
            high, low = split((full if factor is None else full * factor).T)
            wst[variant, :, 0:LANES] = high
            wst[variant, :, LANES:] = low

    wide = 2 * LANES
    at = pl.ds(pl.multiple_of(step * wide, wide), wide)
    for slot in range(SUB + 2):
        variant = max(0, slot - SUB + 1)
        high, low = split(jnp.concatenate([read_ref[g, slot] for g in range(vels // LANES)], axis=1))
        first = jnp.dot(high, wst[variant], preferred_element_type=jnp.float32)
        second = jnp.dot(low, wst[variant, :, 0:LANES], preferred_element_type=jnp.float32)
        total = (first[:, 0:LANES] + first[:, LANES:] + second).T[0:span]
        if slot < SUB:
            for j in range(2):
                acc[2 * step + j, pl.ds(slot, span, stride=SUB), :] = total[:, j * LANES : (j + 1) * LANES]
        else:
            gacc[slot - SUB, :, at] = total

    @pl.when(step == pl.num_programs(0) - 1)
    def _():
        combine_moments(me_ref, cst_ref, outs, acc, gacc, pay, blocks)


def combine_moments(me_ref, cst_ref, outs, acc, gacc, pay, blocks):
    half = blocks // 2
    al = cst_ref[0, 0:SUB, :]
    beyond = cst_ref[0, SUB : SUB + 1, :]
    below = cst_ref[0, 2 * SUB - 1 : 2 * SUB, :]
    plane = lax.broadcasted_iota(jnp.int32, al.shape, 0)

    def own(i, m):
        first = (i * 16 + m) * SUB
        return jnp.concatenate([acc[k, first : first + SUB, :] for k in range(blocks)], axis=1)

    for m in range(MOM):
        sets = [own(i, m) for i in range(SETS)]
        value = al * (sets[0] - sum(sets[1:]))
        value = value + jnp.where(plane == 0, 0.0, pltpu.roll(al * sets[1], 1, axis=0))
        value = value + jnp.where(plane == SUB - 1, 0.0, pltpu.roll(al * sets[2], SUB - 1, axis=0))
        value = value + roll_y(al * sets[3], 1) + roll_y(al * sets[4], -1)
        value = value + roll_z(al * sets[5], 1) + roll_z(al * sets[6], -1)
        for k in range(blocks):
            at = slice(k * LANES, (k + 1) * LANES)
            pay[k, M1 + m * SUB : M1 + (m + 1) * SUB, :] = sets[0][:, at]
            pay[k, AA + m * SUB : AA + (m + 1) * SUB, :] = value[:, at]

    for side, (scale, edge, toward, start) in enumerate([(beyond, SUB - 1, 1, UP), (below, 0, 2, DOWN)]):
        sets = [gacc[side, i * 16 : (i + 1) * 16, :] for i in range(SETS)]
        near = scale * (sets[0] - sum(sets[1:]))
        near = near + roll_y(scale * sets[3], 1) + roll_y(scale * sets[4], -1)
        near = near + roll_z(scale * sets[5], 1) + roll_z(scale * sets[6], -1)
        out_of = jnp.concatenate(
            [acc[k, pl.ds(toward * 16 * SUB + edge, 16, stride=SUB), :] for k in range(blocks)], axis=1
        )
        near = near + al[edge : edge + 1, :] * out_of
        far = scale * sets[toward]
        for k in range(blocks):
            at = slice(k * LANES, (k + 1) * LANES)
            for j, value in enumerate((sets[0], near, far)):
                pay[k, start + j * MOM : start + (j + 1) * MOM, :] = value[0:MOM, at]
            pay[k, start + 3 * MOM : start + 3 * MOM + 1, :] = jnp.zeros((1, LANES), jnp.float32)

    mine = me_ref[0]
    for k in range(half):
        near = jnp.bitwise_xor(mine, k)
        outs[k][0:PAY, :] = pay[near]
        outs[k][PAY:, :] = pay[jnp.bitwise_xor(near, half)]


def both_moments(place, read, vel_index, cst, vels, blocks):
    cells = blocks * LANES
    vmem = pl.BlockSpec(memory_space=pltpu.VMEM)
    span = SETS * 16
    block = pl.BlockSpec((vels // LANES, SUB + 2, 2 * LANES, LANES), lambda i: (0, 0, i, 0))
    return pl.pallas_call(
        functools.partial(moments_kernel, vels=vels, blocks=blocks),
        grid=(blocks // 2,),
        in_specs=[pl.BlockSpec(memory_space=pltpu.SMEM), block, vmem, vmem],
        out_specs=[vmem] * (blocks // 2),
        out_shape=[jax.ShapeDtypeStruct((2 * PAY, LANES), jnp.float32)] * (blocks // 2),
        scratch_shapes=[
            pltpu.VMEM((16, vels), jnp.float32),
            pltpu.VMEM((3, vels, 2 * LANES), jnp.bfloat16),
            pltpu.VMEM((blocks, span * SUB, LANES), jnp.float32),
            pltpu.VMEM((2, span, cells), jnp.float32),
            pltpu.VMEM((blocks, PAY, LANES), jnp.float32),
        ],
        compiler_params=pltpu.CompilerParams(vmem_limit_bytes=56 * MIB),
        cost_estimate=pl.CostEstimate(
            flops=2 * 336 * vels * 10 * cells, bytes_accessed=4 * vels * 10 * cells, transcendentals=0
        ),
        name="moments_of_both",
    )(place, read, vel_index, cst)


def carried_kernel(read_ref, index_ref, al_ref, *refs, blocks):
    out_ref, mid, scale = refs[-3:]
    ys = blocks * LANES // NZ

    @pl.when(pl.program_id(0) == 0)
    def _():
        for x in range(SUB):
            lane_copies(al_ref[x : x + 1, :], scale.at[x], blocks)
        empty = jnp.zeros((ys * NZ, LANES), jnp.float32)
        mid[0] = empty
        mid[SUB + 1] = empty

    upwind = Upwind(index_ref[...])

    @pl.loop(0, SUB)
    def _(x):
        def run(first):
            for j in range(RUN):
                at = rows_of(first + j)
                mid[x + 1, at, :] = scale[x, at, :] * read_ref[0, x, at, :]

        each_run(ys, run)

    @pl.loop(0, SUB)
    def _(x):
        def run(first):
            for j, value in enumerate(upwind.stream(mid, x, first, ys)):
                at = rows_of(first + j)
                out_ref[0, x, at, :] = scale[x, at, :] * value

        each_run(ys, run)


def carried(read, vel_index, al, first, count, blocks, before=None):
    groups = read.shape[0]
    cells = blocks * LANES
    start = first // LANES
    block = pl.BlockSpec((1, SUB, cells, LANES), lambda i: (i + start, 0, 0, 0))
    held = [] if before is None else [before]
    return pl.pallas_call(
        functools.partial(carried_kernel, blocks=blocks),
        grid=(count // LANES,),
        in_specs=[
            block,
            pl.BlockSpec((3, LANES), lambda i: (0, i + start)),
            pl.BlockSpec((SUB, cells), lambda i: (0, 0)),
        ]
        + [pl.BlockSpec(memory_space=pl.ANY)] * len(held),
        out_specs=block,
        out_shape=jax.ShapeDtypeStruct((groups, SUB, cells, LANES), jnp.float32),
        scratch_shapes=[
            pltpu.VMEM((SUB + 2, cells, LANES), jnp.float32),
            pltpu.VMEM((SUB, cells, LANES), jnp.float32),
        ],
        input_output_aliases={3: 0} if held else {},
        compiler_params=pltpu.CompilerParams(vmem_limit_bytes=40 * MIB),
        cost_estimate=pl.CostEstimate(flops=1, bytes_accessed=1, transcendentals=0),
        name="carried_part",
    )(read, vel_index, al, *held)


def inflow_kernel(
    core_ref, swap_ref, first_ref, first1_ref, second_ref, second1_ref, index_ref, al_ref, out_ref,
    halo, edge, scale, *, blocks
):
    core = core_ref[0]
    ys = blocks * LANES // NZ

    @pl.when(pl.program_id(0) == 0)
    def _():
        for j, x in enumerate((0, SUB - 1, 1, SUB - 2, 2 * SUB - 1, SUB)):
            lane_copies(al_ref[x : x + 1, :], scale.at[j], blocks)

    upwind = Upwind(index_ref[...])
    from_far = upwind.px == (core == 0)
    @pl.loop(0, ys // 2)
    def _(y):
        at, up = rows_of(y), rows_of(y + ys // 2)
        for depth, (one, two) in enumerate(((first_ref, second_ref), (first1_ref, second1_ref))):
            a, b = one[0, 0, at, :], two[0, 0, at, :]
            halo[depth, at, :] = jnp.where(from_far, jnp.where(core == 0, a, b), swap_ref[0, depth, at, :])
            halo[depth, up, :] = jnp.where(from_far, jnp.where(core == 0, b, a), swap_ref[0, depth, up, :])

    def scaled(pair, at):
        return jnp.where(upwind.px, scale[2 * pair, at, :], scale[2 * pair + 1, at, :])

    def start(first):
        for j in range(RUN):
            at = rows_of(first + j)
            value = scaled(0, at) * upwind.ax * halo[0, at, :]
            edge[at, :] = value
            out_ref[0, 1, at, :] = scaled(1, at) * upwind.ax * value

    each_run(ys, start)

    def run(first):
        inside = upwind.across(run_of(lambda y: edge[rows_of(y), :], first, ys))
        beyond = upwind.across(run_of(lambda y: halo[0, rows_of(y), :], first, ys))
        for j in range(RUN):
            at = rows_of(first + j)
            streamed = beyond[j] + upwind.ax * halo[1, at, :]
            out_ref[0, 0, at, :] = scaled(0, at) * (inside[j] + upwind.ax * scaled(2, at) * streamed)

    each_run(ys, run)


def inflow(core, swap, first, first1, second, second1, vel_index, al16, vels, blocks):
    cells = blocks * LANES
    narrow = pl.BlockSpec((1, 1, cells // 2, LANES), lambda i: (i, 0, 0, 0))
    return pl.pallas_call(
        functools.partial(inflow_kernel, blocks=blocks),
        grid=(vels // LANES,),
        in_specs=[
            pl.BlockSpec(memory_space=pltpu.SMEM),
            pl.BlockSpec((1, 2, cells, LANES), lambda i: (i, 0, 0, 0)),
            narrow,
            narrow,
            narrow,
            narrow,
            pl.BlockSpec((3, LANES), lambda i: (0, i)),
            pl.BlockSpec((2 * SUB, cells), lambda i: (0, 0)),
        ],
        out_specs=pl.BlockSpec((1, 2, cells, LANES), lambda i: (i, 0, 0, 0)),
        out_shape=jax.ShapeDtypeStruct((vels // LANES, 2, cells, LANES), jnp.float32),
        scratch_shapes=[
            pltpu.VMEM((2, cells, LANES), jnp.float32),
            pltpu.VMEM((cells, LANES), jnp.float32),
            pltpu.VMEM((6, cells, LANES), jnp.float32),
        ],
        compiler_params=pltpu.CompilerParams(vmem_limit_bytes=24 * MIB),
        cost_estimate=pl.CostEstimate(flops=1, bytes_accessed=1, transcendentals=0),
        name="inflow_part",
    )(core, swap, first, first1, second, second1, vel_index, al16)


def small_call(kernel, outs, name, specs, args, scratch=(), limit=16):
    vmem = pl.BlockSpec(memory_space=pltpu.VMEM)
    smem = pl.BlockSpec(memory_space=pltpu.SMEM)
    return pl.pallas_call(
        kernel,
        in_specs=[smem if s == "s" else vmem for s in specs],
        out_specs=[vmem] * len(outs),
        out_shape=[jax.ShapeDtypeStruct(o, jnp.float32) for o in outs],
        scratch_shapes=list(scratch),
        compiler_params=pltpu.CompilerParams(vmem_limit_bytes=limit * MIB),
        name=name,
    )(*args)


def pair_kernel(*refs):
    parts, (near_ref, far_ref) = refs[:-2], refs[-2:]
    value = parts[0][...]
    for part in parts[1:]:
        value = value + part[...]
    near_ref[...] = value[0:PAY]
    far_ref[...] = value[PAY:]


def total_kernel(*refs):
    parts, (all_ref, up_ref, down_ref) = refs[:-3], refs[-3:]
    value = parts[0][...]
    for part in parts[1:]:
        value = value + part[...]
    all_ref[...] = value
    up_ref[...] = value[UP:DOWN]
    down_ref[...] = value[M1:AA]


def mix(inverse, values):
    return [sum(inverse[k, j] * values[j] for j in range(MOM)) for k in range(MOM)]


def chunk_kernel(inv_ref, own_ref, low_ref, high_ref, send_ref):
    plane = lax.broadcasted_iota(jnp.int32, (SUB, LANES), 0)
    inverse = {(k, j): inv_ref[k, j] for k in range(MOM) for j in range(MOM)}
    inner, outer, later = [], [], []
    for m in range(MOM):

        def row(ref, at):
            return ref[at : at + 1, :]

        first = own_ref[M1 + m * SUB : M1 + (m + 1) * SUB, :]
        second = own_ref[AA + m * SUB : AA + (m + 1) * SUB, :]
        low = low_ref[M1 + m * SUB : M1 + (m + 1) * SUB, :]
        high = high_ref[m * SUB : (m + 1) * SUB, :]
        below = DOWN - M1 + m
        inner.append(
            first + jnp.where(plane == 0, row(low_ref, m), 0.0) + jnp.where(plane == SUB - 1, row(high_ref, below), 0.0)
        )
        outer.append(
            jnp.where(plane < SUB // 2, high, low)
            + jnp.where(plane == 0, row(own_ref, UP + m), 0.0)
            + jnp.where(plane == SUB - 1, row(own_ref, DOWN + m), 0.0)
        )
        later.append(
            second
            + jnp.where(plane == 0, row(low_ref, MOM + m), 0.0)
            + jnp.where(plane == 1, row(low_ref, 2 * MOM + m), 0.0)
            + jnp.where(plane == SUB - 1, row(high_ref, below + MOM), 0.0)
            + jnp.where(plane == SUB - 2, row(high_ref, below + 2 * MOM), 0.0)
        )
    local, around = mix(inverse, inner), mix(inverse, outer)
    for n in range(4):
        send_ref[n * 16 : n * 16 + SUB, :] = local[n + 1]
        send_ref[n * 16 + SUB : (n + 1) * 16, :] = around[n + 1]
        send_ref[MOVED + n * SUB : MOVED + (n + 1) * SUB, :] = inner[n + 1]
    for n, k in enumerate(STILL):
        send_ref[FIXED + n * SUB : FIXED + (n + 1) * SUB, :] = local[k]
        send_ref[EDGE + n : EDGE + n + 1, :] = around[k][0:1]
        send_ref[EDGE + 4 + n : EDGE + 5 + n, :] = around[k][SUB - 1 :]
    for m in range(MOM):
        send_ref[LATER + m * SUB : LATER + (m + 1) * SUB, :] = later[m]
    send_ref[SQUARE:SENT, :] = sum((local[m] - inner[m]) ** 2 for m in range(MOM) if not 1 <= m <= 4)


def sweeps(source):
    rows = source.shape[0]
    field = source
    for _ in range(SWEEPS):
        beside = pltpu.roll(field, 1, axis=0) + pltpu.roll(field, rows - 1, axis=0)
        beside = beside + roll_y(field, 1) + roll_y(field, -1) + roll_z(field, 1) + roll_z(field, -1)
        field = (source + coupling * beside) * (1.0 / (1.0 + 6.0 * coupling))
    return field


def fields_kernel(place_ref, inv_ref, cst_ref, *refs, blocks):
    parts = refs[:blocks]
    h1_ref, later_ref, next_ref, up_ref, down_ref, norm_ref, whole = refs[blocks:]
    mine = place_ref[0]
    for k in range(blocks):
        whole[jnp.bitwise_xor(mine, k)] = parts[k][...]

    def rows(first, count):
        return jnp.concatenate([whole[k, first : first + count, :] for k in range(blocks)], axis=1)

    def fold(value):
        return sum(value[:, k * LANES : (k + 1) * LANES] for k in range(blocks))

    square = sum(whole[k, SQUARE:SENT, :] for k in range(blocks))
    al = cst_ref[0, 0:SUB, :]
    edges = rows(EDGE, SUB)
    plane = lax.broadcasted_iota(jnp.int32, al.shape, 0)
    moved = []
    for n, m in enumerate(PICK):
        if 1 <= m <= 4:
            value = sweeps(rows((m - 1) * 16, 16))
            square = square + fold((value[0:SUB] - rows(MOVED + (m - 1) * SUB, SUB)) ** 2)
        else:
            k = STILL.index(m)
            around = jnp.where(
                plane == 0, edges[k : k + 1], jnp.where(plane == SUB - 1, edges[4 + k : 5 + k], 0.0)
            )
            value = jnp.concatenate([rows(FIXED + k * SUB, SUB), around], axis=0)
        given = cst_ref[1 if n in (0, 4) else 2] * value
        inside = given[0:SUB]
        shifted = [
            inside,
            pltpu.roll(given, 1, axis=0)[0:SUB],
            pltpu.roll(given, 2 * SUB - 1, axis=0)[0:SUB],
            roll_y(inside, 1),
            roll_y(inside, -1),
            roll_z(inside, 1),
            roll_z(inside, -1),
        ]
        for s in range(SETS):
            value = al * shifted[s]
            for k in range(blocks):
                first = (s * 8 + n) * SUB
                h1_ref[k, first : first + SUB, :] = value[:, k * LANES : (k + 1) * LANES]
        moved.append(shifted)
    norm_ref[...] = square

    matrices = stream_matrices()
    moments = []
    for m in range(MOM):
        value = rows(LATER + m * SUB, SUB)
        for s in range(SETS):
            for n in range(8):
                factor = float(matrices[s, m, n])
                if factor != 0.0:
                    value = value + factor * moved[n][s]
        later_ref[m * SUB : (m + 1) * SUB, :] = value
        moments.append(value)
    inverse = {(k, j): inv_ref[k, j] for k in range(MOM) for j in range(MOM)}
    for m, value in enumerate(mix(inverse, moments)):
        next_ref[m * SUB : (m + 1) * SUB, :] = value
        if 1 <= m <= 4:
            up_ref[(m - 1) * 4 : m * 4, :] = value[SUB // 2 :]
            down_ref[(m - 1) * 4 : m * 4, :] = value[: SUB // 2]


def last_kernel(
    place_ref, cst_ref, later_ref, next_ref, low_ref, high_ref, norm1_ref, h2_ref, out_ref, norm_ref, wide, *, blocks
):
    mine = place_ref[0]
    square = jnp.zeros((SUB, LANES), jnp.float32)
    for m in range(MOM):
        value = next_ref[m * SUB : (m + 1) * SUB, :]
        if 1 <= m <= 4:
            at = slice((m - 1) * 4, m * 4)
            value = sweeps(jnp.concatenate([value, high_ref[at, :], low_ref[at, :]], axis=0))[0:SUB]
        off = (value - later_ref[m * SUB : (m + 1) * SUB, :]) ** 2
        for k in range(blocks):
            wide[m, k] = value[:, k * LANES : (k + 1) * LANES]
            square = square + off[:, k * LANES : (k + 1) * LANES]
        out_ref[m] = wide[m, mine]
        if m in PICK:
            n = PICK.index(m)
            given = cst_ref[1 if n in (0, 4) else 2, 0:SUB, :] * value
            for k in range(blocks):
                h2_ref[k, n * SUB : (n + 1) * SUB, :] = given[:, k * LANES : (k + 1) * LANES]
    norm_ref[0:1, :] = jnp.sum(norm1_ref[...], axis=0, keepdims=True)
    norm_ref[1:2, :] = jnp.sum(square, axis=0, keepdims=True)


def finish_kernel(carried_ref, inflow_ref, h1_ref, h2_ref, index_ref, out_ref, rows, fields, table, *, blocks):
    group = pl.program_id(0)

    @pl.when(group == 0)
    def _():
        speed = [speed_range * (2.0 * index_ref[a : a + 1, :].astype(jnp.float32) + 1.0 - NVX) / NVX for a in range(3)]
        for n, row in enumerate(functions_of(*speed)[1]):
            table[n : n + 1, :] = row
        base = table[...]
        speeds = []
        for c in speed:
            speeds.append(jnp.where(c > 0, time_step * c, 0.0))
            speeds.append(jnp.where(c < 0, -time_step * c, 0.0))
        full = jnp.concatenate([base * (1.0 - sum(speeds))] + [base * s for s in speeds] + [base], axis=0)
        high = full.astype(jnp.bfloat16).astype(jnp.float32)
        stacked = jnp.concatenate([high, high, full - high, jnp.zeros_like(full)], axis=0).astype(jnp.bfloat16)
        for g in range(rows.shape[0]):
            rows[g] = stacked[:, g * LANES : (g + 1) * LANES]
        left = lax.broadcasted_iota(jnp.int32, (LANES, LANES), 1) < LANES // 2

        @pl.loop(0, blocks)
        def _(k):
            at = pl.ds(pl.multiple_of(k * LANES, LANES), LANES)
            for x in range(SUB):
                first = h1_ref[k, pl.ds(x, SETS * 8, stride=SUB), :]
                second = h2_ref[k, pl.ds(x, 8, stride=SUB), :]
                value = jnp.concatenate([first, second, first, second], axis=0).T
                high = value.astype(jnp.bfloat16).astype(jnp.float32)
                fields[x, at, 0:LANES] = jnp.where(left, high, value - high).astype(jnp.bfloat16)
                fields[x, at, LANES:] = jnp.where(left, high, 0.0).astype(jnp.bfloat16)

    out = out_ref.reshape(LANES * blocks * SUB, LANES)
    here = index_ref[0:1, pl.ds(pl.multiple_of(group * LANES, LANES), LANES)]
    px = here * 2 >= NVX
    for x in range(SUB):
        value = carried_ref[0, x] + jnp.dot(fields[x], rows[group], preferred_element_type=jnp.float32)
        if x in (0, 1):
            value = value + jnp.where(px, inflow_ref[0, x], 0.0)
        elif x in (SUB - 2, SUB - 1):
            value = value + jnp.where(px, 0.0, inflow_ref[0, SUB - 1 - x])
        for k in range(blocks):
            out[pl.ds(k * SUB + x, LANES, stride=blocks * SUB), :] = value[k * LANES : (k + 1) * LANES].T


def finish(carried_part, inflow_part, h1, h2, vel_index, vels, blocks):
    cells = blocks * LANES
    groups = vels // LANES
    vmem = pl.BlockSpec(memory_space=pltpu.VMEM)
    return pl.pallas_call(
        functools.partial(finish_kernel, blocks=blocks),
        grid=(groups,),
        in_specs=[
            pl.BlockSpec((1, SUB, cells, LANES), lambda g: (g, 0, 0, 0)),
            pl.BlockSpec((1, 2, cells, LANES), lambda g: (g, 0, 0, 0)),
            vmem,
            vmem,
            vmem,
        ],
        out_specs=pl.BlockSpec((LANES, blocks, SUB, LANES), lambda g: (g, 0, 0, 0)),
        out_shape=jax.ShapeDtypeStruct((vels, blocks, SUB, LANES), jnp.float32),
        scratch_shapes=[
            pltpu.VMEM((groups, 256, LANES), jnp.bfloat16),
            pltpu.VMEM((SUB, cells, 256), jnp.bfloat16),
            pltpu.VMEM((8, vels), jnp.float32),
        ],
        compiler_params=pltpu.CompilerParams(vmem_limit_bytes=36 * MIB),
        cost_estimate=pl.CostEstimate(
            flops=2 * 256 * vels * blocks * SUB * LANES, bytes_accessed=8 * vels * blocks * SUB * LANES, transcendentals=0
        ),
        name="finish_dist",
    )(carried_part, inflow_part, h1, h2, vel_index)


def ring(axis, step):
    size = lax.axis_size(axis)
    return [(i, (i + step) % size) for i in range(size)]


def shards(dist, vel_index, relax, wall_mask, macro_inverse):
    vels, width, cells = dist.shape
    blocks = cells // LANES
    peers, slabs = lax.axis_size("vel"), lax.axis_size("space")
    assert width == SUB and peers % blocks == 0 and slabs == 4 and blocks % 2 == 0
    sub = peers // blocks
    me = lax.axis_index("vel")
    place = (me // sub).astype(jnp.int32).reshape(1)
    core = (lax.axis_index("space") % 2).astype(jnp.int32).reshape(1)

    flat = dist.reshape(vels, width, blocks, LANES).transpose(0, 2, 1, 3).reshape(vels * blocks * width, LANES)
    speed = speed_range * (2.0 * vel_index.astype(jnp.float32) + 1.0 - NVX) / NVX

    wall = wall_mask > 0
    coefficients = jnp.stack(
        [
            jnp.where(wall, 0.0, 1.0 - relax),
            jnp.where(wall, 1.0, relax),
            jnp.where(wall, 0.0, relax),
        ],
        0,
    )
    from_low = lax.ppermute(coefficients[:, SUB - 1 :], "space", ring("space", 1))
    from_high = lax.ppermute(coefficients[:, :1], "space", ring("space", -1))

    leaving, read = first_stream(flat, vel_index, vels, blocks)
    (leaving, from_low, from_high) = lax.optimization_barrier((leaving, from_low, from_high))
    swap = lax.ppermute(leaving, "space", [(i, i ^ 1) for i in range(slabs)])
    cst = jnp.concatenate(
        [coefficients, from_high, jnp.zeros((3, SUB - 2, cells), jnp.float32), from_low], 1
    )

    parts = both_moments(place, read, vel_index, cst, vels, blocks)
    (swap, parts) = lax.optimization_barrier((swap, parts))

    half = cells // 2
    start = core[0] * half
    mine = lax.dynamic_slice_in_dim(leaving, start, half, 2)
    other = lax.dynamic_slice_in_dim(swap, start, half, 2)
    plus = speed[0].reshape(vels // LANES, 1, 1, LANES) > 0
    across = jnp.where(plus == (core[0] == 1), mine, other)
    (across, parts) = lax.optimization_barrier((across, parts))
    over = [(i, i ^ 2) for i in range(slabs)]
    first = [lax.ppermute(across[:, 0:1], "space", over)]

    def beside(step):
        return [(i, (i // sub ^ step) * sub + i % sub) for i in range(peers)]

    spans = [(0, vels)] if vels < 2 * LANES else [(0, vels // 2), (vels // 2, vels - vels // 2)]

    got = [parts[0]] + [lax.ppermute(parts[k], "vel", beside(k)) for k in range(1, blocks // 2)]
    carried_part = carried(read, vel_index, coefficients[0], *spans[0], blocks)
    (got[1], carried_part) = lax.optimization_barrier((got[1], carried_part))
    near, far = small_call(pair_kernel, [(PAY, LANES)] * 2, "sum_near", "v" * len(got), got)
    got = [near, lax.ppermute(far, "vel", beside(blocks // 2))]
    if len(spans) > 1:
        (al, _) = lax.optimization_barrier((coefficients[0], near))
        carried_part = carried(read, vel_index, al, *spans[1], blocks, carried_part)
        (got[1], carried_part) = lax.optimization_barrier((got[1], carried_part))
    if sub > 1:
        part = sum(got)
        got = [part]
        for k in range(1, sub):
            pairs = [(i, i // sub * sub + (i % sub + k) % sub) for i in range(peers)]
            got.append(lax.ppermute(part, "vel", pairs))
    chunk, up, down = small_call(
        total_kernel, [(PAY, LANES), (DOWN - UP, LANES), (AA - M1, LANES)], "sum_moments", "v" * len(got), got
    )
    (first[0], up, down) = lax.optimization_barrier((first[0], up, down))
    low = lax.ppermute(up, "space", ring("space", 1))
    high = lax.ppermute(down, "space", ring("space", -1))
    (send,) = small_call(
        chunk_kernel, [(SENT, LANES)], "local_fields", "svvv", (macro_inverse, chunk, low, high)
    )
    pieces = [send] + [lax.ppermute(send, "vel", beside(k)) for k in range(1, blocks // 2 + 1)]
    across1, send = lax.optimization_barrier((across[:, 1:2], send))
    first.append(lax.ppermute(across1, "space", over))
    swap_chip = [(i, i ^ 1) for i in range(slabs)]
    second = [lax.ppermute(first[0], "space", swap_chip)]
    pieces += [lax.ppermute(pieces[blocks // 2], "vel", beside(k)) for k in range(1, blocks // 2)]

    h1, later, following, up2, down2, norm1 = small_call(
        functools.partial(fields_kernel, blocks=blocks),
        [
            (blocks, SETS * 8 * SUB, LANES),
            (MOM * SUB, cells),
            (MOM * SUB, cells),
            (16, cells),
            (16, cells),
            (SUB, LANES),
        ],
        "first_fields",
        "ssv" + "v" * blocks,
        (place, macro_inverse, cst, *pieces),
        [pltpu.VMEM((blocks, SENT, LANES), jnp.float32)],
        10,
    )
    (first[1], up2) = lax.optimization_barrier((first[1], up2))
    second.append(lax.ppermute(first[1], "space", swap_chip))
    low2 = lax.ppermute(up2, "space", ring("space", 1))
    high2 = lax.ppermute(down2, "space", ring("space", -1))
    h2, owned, squares = small_call(
        functools.partial(last_kernel, blocks=blocks),
        [(blocks, 8 * SUB, LANES), (MOM, SUB, LANES), (2, LANES)],
        "last_fields",
        "svvvvvv",
        (place, cst, later, following, low2, high2, norm1),
        [pltpu.VMEM((MOM, blocks, SUB, LANES), jnp.float32)],
        10,
    )

    around = [lax.ppermute(squares, "space", ring("space", k)) for k in range(1, slabs)]
    (second[1], h2) = lax.optimization_barrier((second[1], h2))
    inflow_part = inflow(core, swap, *first, *second, vel_index, cst[0], vels, blocks)
    if sub > 1:
        owned = lax.dynamic_slice_in_dim(owned, (me % sub) * (LANES // sub), LANES // sub, 2)

    out = finish(carried_part, inflow_part, h1, h2, vel_index, vels, blocks)
    (around[0], out) = lax.optimization_barrier((around[0], out))
    slab = lax.axis_index("space")
    every = [squares] + around
    ordered = [
        functools.reduce(lambda a, k: jnp.where((slab - k) % slabs == j, every[k], a), range(1, slabs), every[0])
        for j in range(slabs)
    ]
    norms = jnp.sqrt(jnp.sum(sum(ordered), axis=1))
    out = out.transpose(0, 2, 1, 3).reshape(vels, width, cells)
    return (out, owned, norms)


def solution(mesh):
    return jax.shard_map(
        shards,
        mesh=mesh,
        in_specs=(P("vel", "space", None), P(None, "vel"), P("space", None), P("space", None), P()),
        out_specs=(P("vel", "space", None), P(None, "space", "vel"), P()),
        check_vma=False,
    )
```

time: 180 us -> 151 us (0.84)
  Pallas kernels: 113 us -> 95.6 us
  starting transfers between devices: 30.5 us -> 24.1 us
  other arithmetic: 7.67 us -> 5.25 us
    pallas_call x1, Pallas kernels: 40.5 us -> 12.6 us  [both_moments(): pl.pallas_call(functools.partial(moments_kernel, vels=vels, blocks=blocks...]
    pallas_call x3, Pallas kernels: 35.9 us -> 53.8 us  [the longest x1 27 us: first_stream(): pl.pallas_call(functools.partial(stream_kernel, vels=vels, blocks=blocks)...]
    pallas_call x2, Pallas kernels: 29.6 us -> 22.2 us  [carried(): pl.pallas_call(functools.partial(carried_kernel, blocks=blocks), grid=(co...]
    ppermute x1, waiting for transfers between devices: 9.38 us -> 2.03 us  [shards(): low = lax.ppermute(up, 'space', ring('space', 1))]
    ppermute x3, waiting for transfers between devices: 1.31 us -> 5.89 us  [shards(): lax.ppermute(pieces[blocks // 2], 'vel', beside(k))]
    ppermute x1, waiting for transfers between devices: 0.01 us -> 3.44 us  [shards(): high2 = lax.ppermute(down2, 'space', ring('space', -1))]
    another operation x3 -> x0, other arithmetic: 2.74 us -> none  [the longest x2 1.38 us: shards(): every = jnp.stack([squares] + around)]
    ppermute x4, starting transfers between devices: 6.32 us -> 3.67 us  [shards(): lax.ppermute(send, 'vel', beside(k))]
  transfers between devices with their start and end apart: 23 -> 25, of which waited for: 6 -> 10; matrix products, arithmetic and copies ran while one was open for 2% -> 1% of each run, Pallas kernels for 53% -> 63%
where the time goes in v3:
time: 151 us; the launch traced here: 150 us
  Pallas kernels  95.6 us (63%)
  starting transfers between devices  24.1 us (16%)
  waiting for transfers between devices  20.6 us (14%)
  other arithmetic  5.25 us (3%)
  local copies, waits for them, and re-layouts  3.79 us (3%)
    pallas_call x1, Pallas kernels, first_stream(): pl.pallas_call(functools.partial(stream_kernel, vels=vels, blocks=blocks)...  27 us
    pallas_call x2, Pallas kernels, carried(): pl.pallas_call(functools.partial(carried_kernel, blocks=blocks), grid=(co...  22.2 us
    pallas_call x1, Pallas kernels, finish(): pl.pallas_call(functools.partial(finish_kernel, blocks=blocks), grid=(gro...  20.1 us
    pallas_call x1, Pallas kernels, both_moments(): pl.pallas_call(functools.partial(moments_kernel, vels=vels, blocks=blocks...  12.6 us
    pallas_call x5, Pallas kernels, small_call(): pl.pallas_call(kernel, in_specs=[smem if s == 's' else vmem for s in spec...  6.99 us
    pallas_call x1, Pallas kernels, inflow(): pl.pallas_call(functools.partial(inflow_kernel, blocks=blocks), grid=(vel...  6.69 us
    ppermute x4, waiting for transfers between devices, shards(): lax.ppermute(send, 'vel', beside(k))  6.23 us
    ppermute x3, waiting for transfers between devices, shards(): lax.ppermute(pieces[blocks // 2], 'vel', beside(k))  5.89 us
  transfers between devices with their start and end apart: 25, of which 10 were waited for; matrix products, arithmetic and copies ran while one was open for 1% of the time, Pallas kernels for 63%

profile of v3, /device:TPU:0, one launch (start us, length us, event | category | flops | bytes accessed | tf_op | source)
XLA Modules:
  0.0 150.1 jit_solution(17795871433335251646)
XLA Ops:
  0.6 0.8 subtract_select_fusion
  1.4 0.8 select_bitcast_fusion.1
  2.2 0.5 collective-permute-start
  2.7 2.0 %collective-permute-start.1 = (f32[3,1,1024]{2,1,0:T(1,128)S(1)}, f32[3,1,1024]{2,1,0:T(1,128)S(1)}, u32[]{:S(2)}, u32[]{:S(2)}) collective-permute-start(f32[3,1,1024]{2,1,0:T(1,128)S(1)} %get-tuple-element.103), channel_id=1, source_target_pairs={{0,3},{1,0},{2,1},{3,2},{4,7},{5,4},{6,5},{7,6},{8,11},{9,8},{10,9... | collective-permute-start | bytes 36872 | tf_op jit(solution)/shard_map/ppermute | solution.py:784
  4.7 27.0 %first_stream.1 = (f32[4,2,1024,128]{3,2,1,0:T(8,128)}, f32[4,10,1024,128]{3,2,1,0:T(8,128)}) custom-call(f32[32768,128]{1,0:T(8,128)} %bitcast.20, s32[3,512]{1,0:T(4,128)} %index_ref.11), custom_call_target="tpu_custom_call" | custom-call | flops 83886080 | bytes 33554432 | tf_op jit(solution)/shard_map/first_stream/pallas_call | solution.py:227
  31.7 0.7 collective-permute-start.2
  32.5 0.7 compare_reduce_fusion
  33.2 0.8 pad_maximum_fusion.cst_ref
  33.9 12.6 %moments_of_both.1 = (f32[576,128]{1,0:T(8,128)}, f32[576,128]{1,0:T(8,128)}, f32[576,128]{1,0:T(8,128)}, f32[576,128]{1,0:T(8,128)}) custom-call(s32[1]{0:T(128)} %bitcast.me_ref.place_ref, f32[4,10,1024,128]{3,2,1,0:T(8,128)} %get-tuple-element.55.read_ref, s32[3,512]{1,0:T(4,128)} %index_ref.11, f32[3,16,1024]{2,1,0:T(8,128)} %pad_maximum_fusion.cst_ref), custom_call_target="tpu_custom_call" | custom-call | flops 3523215360 | bytes 20971520 | tf_op jit(solution)/shard_map/moments_of_both/pallas_call | solution.py:347
  46.6 2.1 %dynamic-slice_select_fusion = f32[4,2,512,128]{3,2,1,0:T(8,128)S(1)} fusion(f32[4,2,1024,128]{3,2,1,0:T(8,128)} %collective-permute-done.2.swap_ref, s32[]{:T(128)S(6)} %select_n.135, f32[4,2,1024,128]{3,2,1,0:T(8,128)S(1)} %copy-done.8, pred[4,128]{1,0:T(4,128)(4,1)S(1)} %bitcast.22), kind=kLoop, calls=%fused_computation | loop fusion | flops 524288 | bytes 6291972 | tf_op jit(solution)/shard_map/jit(_where)/select_n | solution.py:801
  48.8 1.7 %collective-permute-start.7 = (f32[4,1,512,128]{3,2,1,0:T(8,128)S(1)}, f32[4,1,512,128]{3,2,1,0:T(8,128)S(1)}, u32[]{:S(2)}, u32[]{:S(2)}) collective-permute-start(f32[4,1,512,128]{3,2,1,0:T(8,128)S(1)} %get-tuple-element.102), channel_id=1, source_target_pairs={{0,2},{1,3},{2,0},{3,1},{4,6},{5,7},{6,4},{7,5},{8,10},{9,11},{10,... | collective-permute-start | bytes 3145736 | tf_op jit(solution)/shard_map/ppermute | solution.py:804
  50.6 1.5 %collective-permute-start.3 = (f32[576,128]{1,0:T(8,128)S(1)}, f32[576,128]{1,0:T(8,128)S(1)}, u32[]{:S(2)}, u32[]{:S(2)}) collective-permute-start(f32[576,128]{1,0:T(8,128)S(1)} %copy-done.11), channel_id=1, source_target_pairs={{0,4},{4,0},{8,12},{12,8},{16,20},{20,16},{24,28},{28,24},{1,5},{5... | collective-permute-start | bytes 884744 | tf_op jit(solution)/shard_map/ppermute | solution.py:811
  52.1 1.6 %collective-permute-start.4 = (f32[576,128]{1,0:T(8,128)S(1)}, f32[576,128]{1,0:T(8,128)S(1)}, u32[]{:S(2)}, u32[]{:S(2)}) collective-permute-start(f32[576,128]{1,0:T(8,128)S(1)} %copy-done.10), channel_id=1, source_target_pairs={{0,8},{4,12},{8,0},{12,4},{16,24},{20,28},{24,16},{28,20},{1,9},{5... | collective-permute-start | bytes 884744 | tf_op jit(solution)/shard_map/ppermute | solution.py:811
  53.7 0.4 collective-permute-start.5
  54.1 11.0 %carried_part.2.refs_0_ = f32[4,8,1024,128]{3,2,1,0:T(8,128)} custom-call(f32[4,10,1024,128]{3,2,1,0:T(8,128)} %get-tuple-element.55.read_ref, s32[3,512]{1,0:T(4,128)S(1)} %copy-done.3, f32[8,1024]{1,0:T(8,128)S(1)} %get-tuple-element.72.al_ref), custom_call_target="tpu_custom_call" | custom-call | flops 1 | bytes 1 | tf_op jit(solution)/shard_map/carried_part/pallas_call | solution.py:407
  65.1 2.1 %collective-permute-done.5.refs_3_ = f32[576,128]{1,0:T(8,128)S(1)} collective-permute-done((f32[576,128]{1,0:T(8,128)S(1)}, f32[576,128]{1,0:T(8,128)S(1)}, u32[]{:S(2)}, u32[]{:S(2)}) %collective-permute-start.5) | collective-permute-done | bytes 294944 | tf_op jit(solution)/shard_map/ppermute | solution.py:811
  67.2 2.7 %collective-permute-start.6 = (f32[288,128]{1,0:T(8,128)S(1)}, f32[288,128]{1,0:T(8,128)S(1)}, u32[]{:S(2)}, u32[]{:S(2)}) collective-permute-start(f32[288,128]{1,0:T(8,128)S(1)} %get-tuple-element.71), channel_id=1, source_target_pairs={{0,16},{4,20},{8,24},{12,28},{16,0},{20,4},{24,8},{28,12},{1,17},{... | collective-permute-start | bytes 442376 | tf_op jit(solution)/shard_map/ppermute | solution.py:815
  69.9 11.1 %carried_part.3.carried_ref = f32[4,8,1024,128]{3,2,1,0:T(8,128)} custom-call(f32[4,10,1024,128]{3,2,1,0:T(8,128)} %get-tuple-element.55.read_ref, s32[3,512]{1,0:T(4,128)S(1)} %copy-done.3, f32[8,1024]{1,0:T(8,128)S(1)} %get-tuple-element.72.al_ref, f32[4,8,1024,128]{3,2,1,0:T(8,128)} %carried_part.2.refs_0_), custom_call_target="tpu_custom_call", output_to_operand_aliasing={{}: (3, {})} | custom-call | flops 1 | bytes 1 | tf_op jit(solution)/shard_map/carried_part/pallas_call | solution.py:407
  81.1 1.7 %collective-permute-start.9 = (f32[144,128]{1,0:T(8,128)S(1)}, f32[144,128]{1,0:T(8,128)S(1)}, u32[]{:S(2)}, u32[]{:S(2)}) collective-permute-start(f32[144,128]{1,0:T(8,128)S(1)} %get-tuple-element.80), channel_id=1, source_target_pairs={{0,3},{1,0},{2,1},{3,2},{4,7},{5,4},{6,5},{7,6},{8,11},{9,8},{10,9... | collective-permute-start | bytes 221192 | tf_op jit(solution)/shard_map/ppermute | solution.py:831
  82.9 2.0 %collective-permute-done.8.low_ref = f32[144,128]{1,0:T(8,128)S(1)} collective-permute-done((f32[144,128]{1,0:T(8,128)S(1)}, f32[144,128]{1,0:T(8,128)S(1)}, u32[]{:S(2)}, u32[]{:S(2)}) %collective-permute-start.8) | collective-permute-done | bytes 73760 | tf_op jit(solution)/shard_map/ppermute | solution.py:830
  84.9 0.8 local_fields.1.refs_0_
  85.7 0.6 collective-permute-start.17
  86.3 0.2 collective-permute-start.13
  86.5 1.7 %collective-permute-start.10 = (f32[248,128]{1,0:T(8,128)S(1)}, f32[248,128]{1,0:T(8,128)S(1)}, u32[]{:S(2)}, u32[]{:S(2)}) collective-permute-start(f32[248,128]{1,0:T(8,128)S(1)} %local_fields.1.refs_0_), channel_id=1, source_target_pairs={{0,4},{4,0},{8,12},{12,8},{16,20},{20,16},{24,28},{28,24},{1,5},{5... | collective-permute-start | bytes 380936 | tf_op jit(solution)/shard_map/ppermute | solution.py:835
  88.2 1.6 %collective-permute-start.11 = (f32[248,128]{1,0:T(8,128)S(1)}, f32[248,128]{1,0:T(8,128)S(1)}, u32[]{:S(2)}, u32[]{:S(2)}) collective-permute-start(f32[248,128]{1,0:T(8,128)S(1)} %local_fields.1.refs_0_), channel_id=1, source_target_pairs={{0,8},{4,12},{8,0},{12,4},{16,24},{20,28},{24,16},{28,20},{1,9},{5... | collective-permute-start | bytes 380936 | tf_op jit(solution)/shard_map/ppermute | solution.py:835
  89.7 0.2 collective-permute-start.12
  90.0 6.1 %collective-permute-done.13.refs_4_ = f32[248,128]{1,0:T(8,128)S(1)} collective-permute-done((f32[248,128]{1,0:T(8,128)S(1)}, f32[248,128]{1,0:T(8,128)S(1)}, u32[]{:S(2)}, u32[]{:S(2)}) %collective-permute-start.13) | collective-permute-done | bytes 127008 | tf_op jit(solution)/shard_map/ppermute | solution.py:835
  96.0 1.6 %collective-permute-start.14 = (f32[248,128]{1,0:T(8,128)S(1)}, f32[248,128]{1,0:T(8,128)S(1)}, u32[]{:S(2)}, u32[]{:S(2)}) collective-permute-start(f32[248,128]{1,0:T(8,128)S(1)} %collective-permute-done.13.refs_4_), channel_id=1, source_target_pairs={{0,4},{4,0},{8,12},{12,8},{16,20},{20,16},{24,28},{28,24},{1,5},{5... | collective-permute-start | bytes 380936 | tf_op jit(solution)/shard_map/ppermute | solution.py:840
  97.6 1.9 %collective-permute-start.16 = (f32[248,128]{1,0:T(8,128)S(1)}, f32[248,128]{1,0:T(8,128)S(1)}, u32[]{:S(2)}, u32[]{:S(2)}) collective-permute-start(f32[248,128]{1,0:T(8,128)S(1)} %collective-permute-done.13.refs_4_), channel_id=1, source_target_pairs={{0,12},{4,8},{8,4},{12,0},{16,28},{20,24},{24,20},{28,16},{1,13},{... | collective-permute-start | bytes 380936 | tf_op jit(solution)/shard_map/ppermute | solution.py:840
  99.7 3.0 %collective-permute-done.14.refs_5_ = f32[248,128]{1,0:T(8,128)S(1)} collective-permute-done((f32[248,128]{1,0:T(8,128)S(1)}, f32[248,128]{1,0:T(8,128)S(1)}, u32[]{:S(2)}, u32[]{:S(2)}) %collective-permute-start.14) | collective-permute-done | bytes 127008 | tf_op jit(solution)/shard_map/ppermute | solution.py:840
  102.7 1.1 collective-permute-done.15.refs_6_
  103.9 1.7 %collective-permute-done.16.refs_7_ = f32[248,128]{1,0:T(8,128)S(1)} collective-permute-done((f32[248,128]{1,0:T(8,128)S(1)}, f32[248,128]{1,0:T(8,128)S(1)}, u32[]{:S(2)}, u32[]{:S(2)}) %collective-permute-start.16) | collective-permute-done | bytes 127008 | tf_op jit(solution)/shard_map/ppermute | solution.py:840
  105.6 3.9 %first_fields.1 = (f32[8,448,128]{2,1,0:T(8,128)S(1)}, f32[104,1024]{1,0:T(8,128)S(1)}, f32[104,1024]{1,0:T(8,128)S(1)}, f32[16,1024]{1,0:T(8,128)S(1)}, f32[16,1024]{1,0:T(8,128)S(1)}, /*index=5*/f32[8,128]{1,0:T(8,128)S(1)}) custom-call(s32[1]{0:T(128)} %bitcast.me_ref.place_ref, f32[13,13]{1,0:T(8,128)S(1)} %copy-done.5, f32[3,16,1024]{2,1,0:T(8,128)S(1)} %copy-done, ...), custom_call_target="tpu_custom_call" | custom-call | tf_op jit(solution)/shard_map/first_fields/pallas_call | solution.py:506
  109.5 0.7 copy-done.1
  110.3 0.6 copy-done.6
  110.9 0.6 copy-done.7
  111.6 0.5 collective-permute-start.21
  112.1 0.3 collective-permute-start.19
  112.4 0.2 collective-permute-start.18
  112.6 3.4 %collective-permute-done.19.high_ref = f32[16,1024]{1,0:T(8,128)S(1)} collective-permute-done((f32[16,1024]{1,0:T(8,128)}, f32[16,1024]{1,0:T(8,128)S(1)}, u32[]{:S(2)}, u32[]{:S(2)}) %collective-permute-start.19) | collective-permute-done | bytes 65568 | tf_op jit(solution)/shard_map/ppermute | solution.py:861
  116.0 0.8 collective-permute-done.18.low_ref
  116.9 1.0 copy-done.2
  117.9 2.2 %last_fields.1 = (f32[8,64,128]{2,1,0:T(8,128)S(1)}, f32[13,8,128]{2,1,0:T(8,128)}, f32[2,128]{1,0:T(2,128)S(1)}) custom-call(s32[1]{0:T(128)} %bitcast.me_ref.place_ref, f32[3,16,1024]{2,1,0:T(8,128)S(1)} %copy-done, f32[104,1024]{1,0:T(8,128)S(1)} %get-tuple-element.81.later_ref, f32[104,1024]{1,0:T(8,128)S(1)} %copy-done.2, ...), custom_call_target="tpu_custom_call" | custom-call | tf_op jit(solution)/shard_map/last_fields/pallas_call | solution.py:506
  120.1 1.7 %collective-permute-start.23 = (f32[2,128]{1,0:T(2,128)S(1)}, f32[2,128]{1,0:T(2,128)S(1)}, u32[]{:S(2)}, u32[]{:S(2)}) collective-permute-start(f32[2,128]{1,0:T(2,128)S(1)} %get-tuple-element.88), channel_id=1, source_target_pairs={{0,3},{1,0},{2,1},{3,2},{4,7},{5,4},{6,5},{7,6},{8,11},{9,8},{10,9... | collective-permute-start | bytes 3080 | tf_op jit(solution)/shard_map/ppermute | solution.py:872
  121.8 0.7 collective-permute-start.24
  122.6 6.7 %inflow_part.1.inflow_ref = f32[4,2,1024,128]{3,2,1,0:T(8,128)S(1)} custom-call(s32[1]{0:T(128)} %bitcast.7.core_ref, f32[4,2,1024,128]{3,2,1,0:T(8,128)} %collective-permute-done.2.swap_ref, f32[4,1,512,128]{3,2,1,0:T(8,128)S(1)} %collective-permute-done.7.first_ref, f32[4,1,512,128]{3,2,1,0:T(8,128)} %collective-permute-done.17.first1_ref, ...), custom_call_target="tpu_custom_call" | custom-call | flops 1 | bytes 1 | tf_op jit(solution)/shard_map/inflow_part/pallas_call | solution.py:477
  129.3 20.1 %finish_dist.1 = f32[512,8,8,128]{3,2,1,0:T(8,128)} custom-call(f32[4,8,1024,128]{3,2,1,0:T(8,128)} %carried_part.3.carried_ref, f32[4,2,1024,128]{3,2,1,0:T(8,128)S(1)} %inflow_part.1.inflow_ref, f32[8,448,128]{2,1,0:T(8,128)S(1)} %get-tuple-element.94.h1_ref, f32[8,64,128]{2,1,0:T(8,128)S(1)} %get-tuple-element.95.h2_ref, s32[3,512]{1,0:T(4,128)S(1)} %copy-done.3), custom_call_target="tpu_custom_call" | custom-call | flops 2147483648 | bytes 33554432 | tf_op jit(solution)/shard_map/finish_dist/pallas_call | solution.py:731
  149.6 0.5 sqrt.3
  (49 shorter events, 0.8 us)
Async XLA Ops:
  2.2 29.5 %collective-permute-start = (f32[3,1,1024]{2,1,0:T(1,128)S(1)}, f32[3,1,1024]{2,1,0:T(1,128)S(1)}, u32[]{:S(2)}, u32[]{:S(2)}) collective-permute-start(f32[3,1,1024]{2,1,0:T(1,128)S(1)} %get-tuple-element.104), channel_id=1, source_target_pairs={{0,1},{1,2},{2,3},{3,0},{4,5},{5,6},{6,7},{7,4},{8,9},{9,10},{10,1... | collective-permute-start | bytes 36872 | tf_op jit(solution)/shard_map/ppermute | solution.py:783
  2.7 29.0 %collective-permute-start.1 = (f32[3,1,1024]{2,1,0:T(1,128)S(1)}, f32[3,1,1024]{2,1,0:T(1,128)S(1)}, u32[]{:S(2)}, u32[]{:S(2)}) collective-permute-start(f32[3,1,1024]{2,1,0:T(1,128)S(1)} %get-tuple-element.103), channel_id=1, source_target_pairs={{0,3},{1,0},{2,1},{3,2},{4,7},{5,4},{6,5},{7,6},{8,11},{9,8},{10,9... | collective-permute-start | bytes 36872 | tf_op jit(solution)/shard_map/ppermute | solution.py:784
  31.7 14.8 %collective-permute-start.2 = (f32[4,2,1024,128]{3,2,1,0:T(8,128)}, f32[4,2,1024,128]{3,2,1,0:T(8,128)}, u32[]{:S(2)}, u32[]{:S(2)}) collective-permute-start(f32[4,2,1024,128]{3,2,1,0:T(8,128)} %get-tuple-element.54), channel_id=1, source_target_pairs={{0,1},{1,0},{2,3},{3,2},{4,5},{5,4},{6,7},{7,6},{8,9},{9,8},{10,11... | collective-permute-start | bytes 12582920 | tf_op jit(solution)/shard_map/ppermute | solution.py:788
  33.9 12.6 %copy-start.8 = (f32[4,2,1024,128]{3,2,1,0:T(8,128)S(1)}, f32[4,2,1024,128]{3,2,1,0:T(8,128)}, u32[]{:S(2)}) copy-start(f32[4,2,1024,128]{3,2,1,0:T(8,128)} %get-tuple-element.54) | copy-start | bytes 12582916
  46.5 4.0 %copy-start.11 = (f32[576,128]{1,0:T(8,128)S(1)}, f32[576,128]{1,0:T(8,128)}, u32[]{:S(2)}) copy-start(f32[576,128]{1,0:T(8,128)} %get-tuple-element.66) | copy-start | bytes 884740
  46.6 5.5 %copy-start.10 = (f32[576,128]{1,0:T(8,128)S(1)}, f32[576,128]{1,0:T(8,128)}, u32[]{:S(2)}) copy-start(f32[576,128]{1,0:T(8,128)} %get-tuple-element.68) | copy-start | bytes 884740
  46.6 7.1 %copy-start.9 = (f32[576,128]{1,0:T(8,128)S(1)}, f32[576,128]{1,0:T(8,128)}, u32[]{:S(2)}) copy-start(f32[576,128]{1,0:T(8,128)} %get-tuple-element.69) | copy-start | bytes 884740
  46.6 7.5 %copy-start.3 = (s32[3,512]{1,0:T(4,128)S(1)}, s32[3,512]{1,0:T(4,128)}, u32[]{:S(2)}) copy-start(s32[3,512]{1,0:T(4,128)} %index_ref.11) | copy-start | bytes 18436
  48.8 18.4 %copy-start.4 = (f32[576,128]{1,0:T(8,128)S(1)}, f32[576,128]{1,0:T(8,128)}, u32[]{:S(2)}) copy-start(f32[576,128]{1,0:T(8,128)} %get-tuple-element.65.refs_0_) | copy-start | bytes 884740
  48.8 32.2 %collective-permute-start.7 = (f32[4,1,512,128]{3,2,1,0:T(8,128)S(1)}, f32[4,1,512,128]{3,2,1,0:T(8,128)S(1)}, u32[]{:S(2)}, u32[]{:S(2)}) collective-permute-start(f32[4,1,512,128]{3,2,1,0:T(8,128)S(1)} %get-tuple-element.102), channel_id=1, source_target_pairs={{0,2},{1,3},{2,0},{3,1},{4,6},{5,7},{6,4},{7,5},{8,10},{9,11},{10,... | collective-permute-start | bytes 3145736 | tf_op jit(solution)/shard_map/ppermute | solution.py:804
  50.6 14.5 %collective-permute-start.3 = (f32[576,128]{1,0:T(8,128)S(1)}, f32[576,128]{1,0:T(8,128)S(1)}, u32[]{:S(2)}, u32[]{:S(2)}) collective-permute-start(f32[576,128]{1,0:T(8,128)S(1)} %copy-done.11), channel_id=1, source_target_pairs={{0,4},{4,0},{8,12},{12,8},{16,20},{20,16},{24,28},{28,24},{1,5},{5... | collective-permute-start | bytes 884744 | tf_op jit(solution)/shard_map/ppermute | solution.py:811
  52.1 13.0 %collective-permute-start.4 = (f32[576,128]{1,0:T(8,128)S(1)}, f32[576,128]{1,0:T(8,128)S(1)}, u32[]{:S(2)}, u32[]{:S(2)}) collective-permute-start(f32[576,128]{1,0:T(8,128)S(1)} %copy-done.10), channel_id=1, source_target_pairs={{0,8},{4,12},{8,0},{12,4},{16,24},{20,28},{24,16},{28,20},{1,9},{5... | collective-permute-start | bytes 884744 | tf_op jit(solution)/shard_map/ppermute | solution.py:811
  53.7 13.5 %collective-permute-start.5 = (f32[576,128]{1,0:T(8,128)S(1)}, f32[576,128]{1,0:T(8,128)S(1)}, u32[]{:S(2)}, u32[]{:S(2)}) collective-permute-start(f32[576,128]{1,0:T(8,128)S(1)} %copy-done.9), channel_id=1, source_target_pairs={{0,12},{4,8},{8,4},{12,0},{16,28},{20,24},{24,20},{28,16},{1,13},{... | collective-permute-start | bytes 884744 | tf_op jit(solution)/shard_map/ppermute | solution.py:811
  67.2 13.8 %collective-permute-start.6 = (f32[288,128]{1,0:T(8,128)S(1)}, f32[288,128]{1,0:T(8,128)S(1)}, u32[]{:S(2)}, u32[]{:S(2)}) collective-permute-start(f32[288,128]{1,0:T(8,128)S(1)} %get-tuple-element.71), channel_id=1, source_target_pairs={{0,16},{4,20},{8,24},{12,28},{16,0},{20,4},{24,8},{28,12},{1,17},{... | collective-permute-start | bytes 442376 | tf_op jit(solution)/shard_map/ppermute | solution.py:815
  69.9 15.0 %copy-start.5 = (f32[13,13]{1,0:T(8,128)S(1)}, f32[13,13]{1,0:T(8,128)}, u32[]{:S(2)}) copy-start(f32[13,13]{1,0:T(8,128)} %inv_ref.3) | copy-start | bytes 2032
  69.9 35.7 %copy-start = (f32[3,16,1024]{2,1,0:T(8,128)S(1)}, f32[3,16,1024]{2,1,0:T(8,128)}, u32[]{:S(2)}) copy-start(f32[3,16,1024]{2,1,0:T(8,128)} %pad_maximum_fusion.cst_ref) | copy-start | bytes 589828
  81.1 3.8 %collective-permute-start.8 = (f32[144,128]{1,0:T(8,128)S(1)}, f32[144,128]{1,0:T(8,128)S(1)}, u32[]{:S(2)}, u32[]{:S(2)}) collective-permute-start(f32[144,128]{1,0:T(8,128)S(1)} %get-tuple-element.79), channel_id=1, source_target_pairs={{0,1},{1,2},{2,3},{3,0},{4,5},{5,6},{6,7},{7,4},{8,9},{9,10},{10,1... | collective-permute-start | bytes 221192 | tf_op jit(solution)/shard_map/ppermute | solution.py:830
  81.1 3.8 %collective-permute-start.9 = (f32[144,128]{1,0:T(8,128)S(1)}, f32[144,128]{1,0:T(8,128)S(1)}, u32[]{:S(2)}, u32[]{:S(2)}) collective-permute-start(f32[144,128]{1,0:T(8,128)S(1)} %get-tuple-element.80), channel_id=1, source_target_pairs={{0,3},{1,0},{2,1},{3,2},{4,7},{5,4},{6,5},{7,6},{8,11},{9,8},{10,9... | collective-permute-start | bytes 221192 | tf_op jit(solution)/shard_map/ppermute | solution.py:831
  85.7 25.9 %collective-permute-start.17 = (f32[4,1,512,128]{3,2,1,0:T(8,128)S(1)}, f32[4,1,512,128]{3,2,1,0:T(8,128)}, u32[]{:S(2)}, u32[]{:S(2)}) collective-permute-start(f32[4,1,512,128]{3,2,1,0:T(8,128)S(1)} %get-tuple-element.83), channel_id=1, source_target_pairs={{0,2},{1,3},{2,0},{3,1},{4,6},{5,7},{6,4},{7,5},{8,10},{9,11},{10,... | collective-permute-start | bytes 3145736 | tf_op jit(solution)/shard_map/ppermute | solution.py:837
  86.3 9.7 %collective-permute-start.13 = (f32[248,128]{1,0:T(8,128)S(1)}, f32[248,128]{1,0:T(8,128)S(1)}, u32[]{:S(2)}, u32[]{:S(2)}) collective-permute-start(f32[248,128]{1,0:T(8,128)S(1)} %local_fields.1.refs_0_), channel_id=1, source_target_pairs={{0,16},{4,20},{8,24},{12,28},{16,0},{20,4},{24,8},{28,12},{1,17},{... | collective-permute-start | bytes 380936 | tf_op jit(solution)/shard_map/ppermute | solution.py:835
  86.5 11.1 %collective-permute-start.10 = (f32[248,128]{1,0:T(8,128)S(1)}, f32[248,128]{1,0:T(8,128)S(1)}, u32[]{:S(2)}, u32[]{:S(2)}) collective-permute-start(f32[248,128]{1,0:T(8,128)S(1)} %local_fields.1.refs_0_), channel_id=1, source_target_pairs={{0,4},{4,0},{8,12},{12,8},{16,20},{20,16},{24,28},{28,24},{1,5},{5... | collective-permute-start | bytes 380936 | tf_op jit(solution)/shard_map/ppermute | solution.py:835
  88.2 9.5 %collective-permute-start.11 = (f32[248,128]{1,0:T(8,128)S(1)}, f32[248,128]{1,0:T(8,128)S(1)}, u32[]{:S(2)}, u32[]{:S(2)}) collective-permute-start(f32[248,128]{1,0:T(8,128)S(1)} %local_fields.1.refs_0_), channel_id=1, source_target_pairs={{0,8},{4,12},{8,0},{12,4},{16,24},{20,28},{24,16},{28,20},{1,9},{5... | collective-permute-start | bytes 380936 | tf_op jit(solution)/shard_map/ppermute | solution.py:835
  89.7 10.0 %collective-permute-start.12 = (f32[248,128]{1,0:T(8,128)S(1)}, f32[248,128]{1,0:T(8,128)S(1)}, u32[]{:S(2)}, u32[]{:S(2)}) collective-permute-start(f32[248,128]{1,0:T(8,128)S(1)} %local_fields.1.refs_0_), channel_id=1, source_target_pairs={{0,12},{4,8},{8,4},{12,0},{16,28},{20,24},{24,20},{28,16},{1,13},{... | collective-permute-start | bytes 380936 | tf_op jit(solution)/shard_map/ppermute | solution.py:835
  96.0 6.7 %collective-permute-start.14 = (f32[248,128]{1,0:T(8,128)S(1)}, f32[248,128]{1,0:T(8,128)S(1)}, u32[]{:S(2)}, u32[]{:S(2)}) collective-permute-start(f32[248,128]{1,0:T(8,128)S(1)} %collective-permute-done.13.refs_4_), channel_id=1, source_target_pairs={{0,4},{4,0},{8,12},{12,8},{16,20},{20,16},{24,28},{28,24},{1,5},{5... | collective-permute-start | bytes 380936 | tf_op jit(solution)/shard_map/ppermute | solution.py:840
  97.6 6.3 %collective-permute-start.15 = (f32[248,128]{1,0:T(8,128)S(1)}, f32[248,128]{1,0:T(8,128)S(1)}, u32[]{:S(2)}, u32[]{:S(2)}) collective-permute-start(f32[248,128]{1,0:T(8,128)S(1)} %collective-permute-done.13.refs_4_), channel_id=1, source_target_pairs={{0,8},{4,12},{8,0},{12,4},{16,24},{20,28},{24,16},{28,20},{1,9},{5... | collective-permute-start | bytes 380936 | tf_op jit(solution)/shard_map/ppermute | solution.py:840
  97.6 8.0 %collective-permute-start.16 = (f32[248,128]{1,0:T(8,128)S(1)}, f32[248,128]{1,0:T(8,128)S(1)}, u32[]{:S(2)}, u32[]{:S(2)}) collective-permute-start(f32[248,128]{1,0:T(8,128)S(1)} %collective-permute-done.13.refs_4_), channel_id=1, source_target_pairs={{0,12},{4,8},{8,4},{12,0},{16,28},{20,24},{24,20},{28,16},{1,13},{... | collective-permute-start | bytes 380936 | tf_op jit(solution)/shard_map/ppermute | solution.py:840
  109.5 0.8 copy-start.1
  110.3 0.6 copy-start.6
  110.9 0.6 copy-start.7
  111.6 11.0 %collective-permute-start.22 = (f32[4,1,512,128]{3,2,1,0:T(8,128)}, f32[4,1,512,128]{3,2,1,0:T(8,128)}, u32[]{:S(2)}, u32[]{:S(2)}) collective-permute-start(f32[4,1,512,128]{3,2,1,0:T(8,128)} %collective-permute-done.17.first1_ref), channel_id=1, source_target_pairs={{0,1},{1,0},{2,3},{3,2},{4,5},{5,4},{6,7},{7,6},{8,9},{9,8},{10,11... | collective-permute-start | bytes 3145736 | tf_op jit(solution)/shard_map/ppermute | solution.py:859
  111.6 11.0 %collective-permute-start.21 = (f32[4,1,512,128]{3,2,1,0:T(8,128)S(1)}, f32[4,1,512,128]{3,2,1,0:T(8,128)}, u32[]{:S(2)}, u32[]{:S(2)}) collective-permute-start(f32[4,1,512,128]{3,2,1,0:T(8,128)S(1)} %collective-permute-done.7.first_ref), channel_id=1, source_target_pairs={{0,1},{1,0},{2,3},{3,2},{4,5},{5,4},{6,7},{7,6},{8,9},{9,8},{10,11... | collective-permute-start | bytes 3145736 | tf_op jit(solution)/shard_map/ppermute | solution.py:839
  112.1 4.0 %collective-permute-start.19 = (f32[16,1024]{1,0:T(8,128)}, f32[16,1024]{1,0:T(8,128)S(1)}, u32[]{:S(2)}, u32[]{:S(2)}) collective-permute-start(f32[16,1024]{1,0:T(8,128)} %copy-done.7), channel_id=1, source_target_pairs={{0,3},{1,0},{2,1},{3,2},{4,7},{5,4},{6,5},{7,6},{8,11},{9,8},{10,9... | collective-permute-start | bytes 196616 | tf_op jit(solution)/shard_map/ppermute | solution.py:861
  112.4 4.5 %collective-permute-start.18 = (f32[16,1024]{1,0:T(8,128)}, f32[16,1024]{1,0:T(8,128)S(1)}, u32[]{:S(2)}, u32[]{:S(2)}) collective-permute-start(f32[16,1024]{1,0:T(8,128)} %copy-done.6), channel_id=1, source_target_pairs={{0,1},{1,2},{2,3},{3,0},{4,5},{5,6},{6,7},{7,4},{8,9},{9,10},{10,1... | collective-permute-start | bytes 196616 | tf_op jit(solution)/shard_map/ppermute | solution.py:860
  116.9 1.0 copy-start.2
  120.1 29.4 %collective-permute-start.20 = (f32[2,128]{1,0:T(2,128)S(1)}, f32[2,128]{1,0:T(2,128)S(1)}, u32[]{:S(2)}, u32[]{:S(2)}) collective-permute-start(f32[2,128]{1,0:T(2,128)S(1)} %get-tuple-element.88), channel_id=1, source_target_pairs={{0,1},{1,2},{2,3},{3,0},{4,5},{5,6},{6,7},{7,4},{8,9},{9,10},{10,1... | collective-permute-start | bytes 3080 | tf_op jit(solution)/shard_map/ppermute | solution.py:872
  120.1 29.3 %collective-permute-start.23 = (f32[2,128]{1,0:T(2,128)S(1)}, f32[2,128]{1,0:T(2,128)S(1)}, u32[]{:S(2)}, u32[]{:S(2)}) collective-permute-start(f32[2,128]{1,0:T(2,128)S(1)} %get-tuple-element.88), channel_id=1, source_target_pairs={{0,3},{1,0},{2,1},{3,2},{4,7},{5,4},{6,5},{7,6},{8,11},{9,8},{10,9... | collective-permute-start | bytes 3080 | tf_op jit(solution)/shard_map/ppermute | solution.py:872
  121.8 27.6 %collective-permute-start.24 = (f32[2,128]{1,0:T(2,128)S(1)}, f32[2,128]{1,0:T(2,128)S(1)}, u32[]{:S(2)}, u32[]{:S(2)}) collective-permute-start(f32[2,128]{1,0:T(2,128)S(1)} %get-tuple-element.88), channel_id=1, source_target_pairs={{0,2},{1,3},{2,0},{3,1},{4,6},{5,7},{6,4},{7,5},{8,10},{9,11},{10,... | collective-permute-start | bytes 3080 | tf_op jit(solution)/shard_map/ppermute | solution.py:872

commit v4 on v3

--- a/solution.py
+++ b/solution.py
@@ -209,8 +209,6 @@
             for j in range(RUN):
                 at = rows_of(first + j)
                 bottom, top = turned[1, at, :], turned[SUB, at, :]
-                done[c % 2, SUB, at, :] = top
-                done[c % 2, SUB + 1, at, :] = bottom
                 leaving_ref[c, 0, at, :] = jnp.where(upwind.px, top, bottom)
                 leaving_ref[c, 1, at, :] = jnp.where(upwind.px, turned[SUB - 1, at, :], turned[2, at, :])
 
@@ -230,13 +228,13 @@
         out_specs=[vmem, anywhere],
         out_shape=[
             jax.ShapeDtypeStruct((vels // LANES, 2, cells, LANES), jnp.float32),
-            jax.ShapeDtypeStruct((vels // LANES, SUB + 2, cells, LANES), jnp.float32),
+            jax.ShapeDtypeStruct((vels // LANES, SUB, cells, LANES), jnp.float32),
         ],
         scratch_shapes=[
             pltpu.VMEM((2, LANES * blocks * SUB, LANES), jnp.float32),
             pltpu.VMEM((SUB + 2, cells, LANES), jnp.float32),
             pltpu.VMEM((SUB + 2, cells, LANES), jnp.float32),
-            pltpu.VMEM((2, SUB + 2, cells, LANES), jnp.float32),
+            pltpu.VMEM((2, SUB, cells, LANES), jnp.float32),
             pltpu.SemaphoreType.DMA((2, PIECES)),
             pltpu.SemaphoreType.DMA((2,)),
         ],
@@ -248,7 +246,7 @@
     )(flat, vel_index)
 
 
-def moments_kernel(me_ref, read_ref, index_ref, cst_ref, *refs, vels, blocks):
+def moments_kernel(me_ref, read_ref, leaving_ref, index_ref, cst_ref, *refs, vels, blocks):
     half = blocks // 2
     outs = refs[:half]
     table, wst, acc, gacc, pay = refs[half:]
@@ -276,17 +274,20 @@
 
     wide = 2 * LANES
     at = pl.ds(pl.multiple_of(step * wide, wide), wide)
-    for slot in range(SUB + 2):
-        variant = max(0, slot - SUB + 1)
-        high, low = split(jnp.concatenate([read_ref[g, slot] for g in range(vels // LANES)], axis=1))
+    groups = range(vels // LANES)
+
+    def reduced(high, low, variant):
         first = jnp.dot(high, wst[variant], preferred_element_type=jnp.float32)
         second = jnp.dot(low, wst[variant, :, 0:LANES], preferred_element_type=jnp.float32)
-        total = (first[:, 0:LANES] + first[:, LANES:] + second).T[0:span]
-        if slot < SUB:
-            for j in range(2):
-                acc[2 * step + j, pl.ds(slot, span, stride=SUB), :] = total[:, j * LANES : (j + 1) * LANES]
-        else:
-            gacc[slot - SUB, :, at] = total
+        return (first[:, 0:LANES] + first[:, LANES:] + second).T[0:span]
+
+    for x in range(SUB):
+        total = reduced(*split(jnp.concatenate([read_ref[g, x] for g in groups], axis=1)), 0)
+        for j in range(2):
+            acc[2 * step + j, pl.ds(x, span, stride=SUB), :] = total[:, j * LANES : (j + 1) * LANES]
+    edge = split(jnp.concatenate([leaving_ref[g, 0] for g in groups], axis=1))
+    for side in range(2):
+        gacc[side, :, at] = reduced(*edge, side + 1)
 
     @pl.when(step == pl.num_programs(0) - 1)
     def _():
@@ -339,15 +340,16 @@
         outs[k][PAY:, :] = pay[jnp.bitwise_xor(near, half)]
 
 
-def both_moments(place, read, vel_index, cst, vels, blocks):
+def both_moments(place, read, leaving, vel_index, cst, vels, blocks):
     cells = blocks * LANES
     vmem = pl.BlockSpec(memory_space=pltpu.VMEM)
     span = SETS * 16
-    block = pl.BlockSpec((vels // LANES, SUB + 2, 2 * LANES, LANES), lambda i: (0, 0, i, 0))
+    block = pl.BlockSpec((vels // LANES, SUB, 2 * LANES, LANES), lambda i: (0, 0, i, 0))
+    edge = pl.BlockSpec((vels // LANES, 1, 2 * LANES, LANES), lambda i: (0, 0, i, 0))
     return pl.pallas_call(
         functools.partial(moments_kernel, vels=vels, blocks=blocks),
         grid=(blocks // 2,),
-        in_specs=[pl.BlockSpec(memory_space=pltpu.SMEM), block, vmem, vmem],
+        in_specs=[pl.BlockSpec(memory_space=pltpu.SMEM), block, edge, vmem, vmem],
         out_specs=[vmem] * (blocks // 2),
         out_shape=[jax.ShapeDtypeStruct((2 * PAY, LANES), jnp.float32)] * (blocks // 2),
         scratch_shapes=[
@@ -362,7 +364,7 @@
             flops=2 * 336 * vels * 10 * cells, bytes_accessed=4 * vels * 10 * cells, transcendentals=0
         ),
         name="moments_of_both",
-    )(place, read, vel_index, cst)
+    )(place, read, leaving, vel_index, cst)
 
 
 def carried_kernel(read_ref, index_ref, al_ref, *refs, blocks):
@@ -426,10 +428,19 @@
     )(read, vel_index, al, *held)
 
 
-def inflow_kernel(
-    core_ref, swap_ref, first_ref, first1_ref, second_ref, second1_ref, index_ref, al_ref, out_ref,
-    halo, edge, scale, *, blocks
-):
+def halo_rows(refs, core, from_far, depth, blocks, put):
+    swap_ref, first_ref, second_ref = refs
+    ys = blocks * LANES // NZ
+
+    @pl.loop(0, ys // 2)
+    def _(y):
+        at, up = rows_of(y), rows_of(y + ys // 2)
+        a, b = first_ref[0, 0, at, :], second_ref[0, 0, at, :]
+        put(at, jnp.where(from_far, jnp.where(core == 0, a, b), swap_ref[0, depth, at, :]))
+        put(up, jnp.where(from_far, jnp.where(core == 0, b, a), swap_ref[0, depth, up, :]))
+
+
+def near_kernel(core_ref, swap_ref, first_ref, second_ref, index_ref, al_ref, out_ref, halo, edge, scale, *, blocks):
     core = core_ref[0]
     ys = blocks * LANES // NZ
 
@@ -439,14 +450,11 @@
             lane_copies(al_ref[x : x + 1, :], scale.at[j], blocks)
 
     upwind = Upwind(index_ref[...])
-    from_far = upwind.px == (core == 0)
-    @pl.loop(0, ys // 2)
-    def _(y):
-        at, up = rows_of(y), rows_of(y + ys // 2)
-        for depth, (one, two) in enumerate(((first_ref, second_ref), (first1_ref, second1_ref))):
-            a, b = one[0, 0, at, :], two[0, 0, at, :]
-            halo[depth, at, :] = jnp.where(from_far, jnp.where(core == 0, a, b), swap_ref[0, depth, at, :])
-            halo[depth, up, :] = jnp.where(from_far, jnp.where(core == 0, b, a), swap_ref[0, depth, up, :])
+
+    def put(at, value):
+        halo[at, :] = value
+
+    halo_rows((swap_ref, first_ref, second_ref), core, upwind.px == (core == 0), 0, blocks, put)
 
     def scaled(pair, at):
         return jnp.where(upwind.px, scale[2 * pair, at, :], scale[2 * pair + 1, at, :])
@@ -454,7 +462,7 @@
     def start(first):
         for j in range(RUN):
             at = rows_of(first + j)
-            value = scaled(0, at) * upwind.ax * halo[0, at, :]
+            value = scaled(0, at) * upwind.ax * halo[at, :]
             edge[at, :] = value
             out_ref[0, 1, at, :] = scaled(1, at) * upwind.ax * value
 
@@ -462,42 +470,45 @@
 
     def run(first):
         inside = upwind.across(run_of(lambda y: edge[rows_of(y), :], first, ys))
-        beyond = upwind.across(run_of(lambda y: halo[0, rows_of(y), :], first, ys))
+        beyond = upwind.across(run_of(lambda y: halo[rows_of(y), :], first, ys))
         for j in range(RUN):
             at = rows_of(first + j)
-            streamed = beyond[j] + upwind.ax * halo[1, at, :]
-            out_ref[0, 0, at, :] = scaled(0, at) * (inside[j] + upwind.ax * scaled(2, at) * streamed)
+            near = scaled(0, at)
+            far = near * upwind.ax * scaled(2, at)
+            out_ref[0, 0, at, :] = near * inside[j] + far * beyond[j]
+            out_ref[0, 2, at, :] = far * upwind.ax
 
     each_run(ys, run)
 
 
-def inflow(core, swap, first, first1, second, second1, vel_index, al16, vels, blocks):
+def inflow_specs(cells):
+    narrow = pl.BlockSpec((1, 1, cells // 2, LANES), lambda i: (i, 0, 0, 0))
+    return [
+        pl.BlockSpec(memory_space=pltpu.SMEM),
+        pl.BlockSpec((1, 2, cells, LANES), lambda i: (i, 0, 0, 0)),
+        narrow,
+        narrow,
+        pl.BlockSpec((3, LANES), lambda i: (0, i)),
+    ]
+
+
+def inflow_near(core, swap, first, second, vel_index, al16, vels, blocks):
     cells = blocks * LANES
-    narrow = pl.BlockSpec((1, 1, cells // 2, LANES), lambda i: (i, 0, 0, 0))
     return pl.pallas_call(
-        functools.partial(inflow_kernel, blocks=blocks),
+        functools.partial(near_kernel, blocks=blocks),
         grid=(vels // LANES,),
-        in_specs=[
-            pl.BlockSpec(memory_space=pltpu.SMEM),
-            pl.BlockSpec((1, 2, cells, LANES), lambda i: (i, 0, 0, 0)),
-            narrow,
-            narrow,
-            narrow,
-            narrow,
-            pl.BlockSpec((3, LANES), lambda i: (0, i)),
-            pl.BlockSpec((2 * SUB, cells), lambda i: (0, 0)),
-        ],
-        out_specs=pl.BlockSpec((1, 2, cells, LANES), lambda i: (i, 0, 0, 0)),
-        out_shape=jax.ShapeDtypeStruct((vels // LANES, 2, cells, LANES), jnp.float32),
+        in_specs=inflow_specs(cells) + [pl.BlockSpec((2 * SUB, cells), lambda i: (0, 0))],
+        out_specs=pl.BlockSpec((1, 3, cells, LANES), lambda i: (i, 0, 0, 0)),
+        out_shape=pltpu.HBM((vels // LANES, 3, cells, LANES), jnp.float32),
         scratch_shapes=[
-            pltpu.VMEM((2, cells, LANES), jnp.float32),
+            pltpu.VMEM((cells, LANES), jnp.float32),
             pltpu.VMEM((cells, LANES), jnp.float32),
             pltpu.VMEM((6, cells, LANES), jnp.float32),
         ],
-        compiler_params=pltpu.CompilerParams(vmem_limit_bytes=24 * MIB),
+        compiler_params=pltpu.CompilerParams(vmem_limit_bytes=16 * MIB),
         cost_estimate=pl.CostEstimate(flops=1, bytes_accessed=1, transcendentals=0),
-        name="inflow_part",
-    )(core, swap, first, first1, second, second1, vel_index, al16)
+        name="inflow_near",
+    )(core, swap, first, second, vel_index, al16)
 
 
 def small_call(kernel, outs, name, specs, args, scratch=(), limit=16):
@@ -680,7 +691,10 @@
     norm_ref[1:2, :] = jnp.sum(square, axis=0, keepdims=True)
 
 
-def finish_kernel(carried_ref, inflow_ref, h1_ref, h2_ref, index_ref, out_ref, rows, fields, table, *, blocks):
+def finish_kernel(
+    core_ref, carried_ref, inflow_ref, swap_ref, first_ref, second_ref, h1_ref, h2_ref, index_ref, out_ref,
+    rows, fields, table, far, *, blocks
+):
     group = pl.program_id(0)
 
     @pl.when(group == 0)
@@ -714,17 +728,25 @@
     out = out_ref.reshape(LANES * blocks * SUB, LANES)
     here = index_ref[0:1, pl.ds(pl.multiple_of(group * LANES, LANES), LANES)]
     px = here * 2 >= NVX
+    core = core_ref[0]
+
+    def put(at, value):
+        far[at, :] = inflow_ref[0, 0, at, :] + inflow_ref[0, 2, at, :] * value
+
+    from_far = jnp.broadcast_to(px, (NZ, LANES)) == (core == 0)
+    halo_rows((swap_ref, first_ref, second_ref), core, from_far, 0, blocks, put)
+    inflow = (lambda: far[...], lambda: inflow_ref[0, 1])
     for x in range(SUB):
         value = carried_ref[0, x] + jnp.dot(fields[x], rows[group], preferred_element_type=jnp.float32)
         if x in (0, 1):
-            value = value + jnp.where(px, inflow_ref[0, x], 0.0)
+            value = value + jnp.where(px, inflow[x](), 0.0)
         elif x in (SUB - 2, SUB - 1):
-            value = value + jnp.where(px, 0.0, inflow_ref[0, SUB - 1 - x])
+            value = value + jnp.where(px, 0.0, inflow[SUB - 1 - x]())
         for k in range(blocks):
             out[pl.ds(k * SUB + x, LANES, stride=blocks * SUB), :] = value[k * LANES : (k + 1) * LANES].T
 
 
-def finish(carried_part, inflow_part, h1, h2, vel_index, vels, blocks):
+def finish(core, carried_part, inflow_part, swap, first, second, h1, h2, vel_index, vels, blocks):
     cells = blocks * LANES
     groups = vels // LANES
     vmem = pl.BlockSpec(memory_space=pltpu.VMEM)
@@ -732,8 +754,12 @@
         functools.partial(finish_kernel, blocks=blocks),
         grid=(groups,),
         in_specs=[
+            pl.BlockSpec(memory_space=pltpu.SMEM),
             pl.BlockSpec((1, SUB, cells, LANES), lambda g: (g, 0, 0, 0)),
-            pl.BlockSpec((1, 2, cells, LANES), lambda g: (g, 0, 0, 0)),
+            pl.BlockSpec((1, 3, cells, LANES), lambda g: (g, 0, 0, 0)),
+            pl.BlockSpec((1, 1, cells, LANES), lambda g: (g, 1, 0, 0)),
+            pl.BlockSpec((1, 1, cells // 2, LANES), lambda g: (g, 0, 0, 0)),
+            pl.BlockSpec((1, 1, cells // 2, LANES), lambda g: (g, 0, 0, 0)),
             vmem,
             vmem,
             vmem,
@@ -744,13 +770,14 @@
             pltpu.VMEM((groups, 256, LANES), jnp.bfloat16),
             pltpu.VMEM((SUB, cells, 256), jnp.bfloat16),
             pltpu.VMEM((8, vels), jnp.float32),
+            pltpu.VMEM((cells, LANES), jnp.float32),
         ],
-        compiler_params=pltpu.CompilerParams(vmem_limit_bytes=36 * MIB),
+        compiler_params=pltpu.CompilerParams(vmem_limit_bytes=40 * MIB),
         cost_estimate=pl.CostEstimate(
             flops=2 * 256 * vels * blocks * SUB * LANES, bytes_accessed=8 * vels * blocks * SUB * LANES, transcendentals=0
         ),
         name="finish_dist",
-    )(carried_part, inflow_part, h1, h2, vel_index)
+    )(core, carried_part, inflow_part, swap, first, second, h1, h2, vel_index)
 
 
 def ring(axis, step):
@@ -790,7 +817,7 @@
         [coefficients, from_high, jnp.zeros((3, SUB - 2, cells), jnp.float32), from_low], 1
     )
 
-    parts = both_moments(place, read, vel_index, cst, vels, blocks)
+    parts = both_moments(place, read, leaving, vel_index, cst, vels, blocks)
     (swap, parts) = lax.optimization_barrier((swap, parts))
 
     half = cells // 2
@@ -837,6 +864,9 @@
     first.append(lax.ppermute(across1, "space", over))
     swap_chip = [(i, i ^ 1) for i in range(slabs)]
     second = [lax.ppermute(first[0], "space", swap_chip)]
+    (second[0], send) = lax.optimization_barrier((second[0], send))
+    inflow_part = inflow_near(core, swap, first[0], second[0], vel_index, cst[0], vels, blocks)
+    (pieces[blocks // 2], inflow_part) = lax.optimization_barrier((pieces[blocks // 2], inflow_part))
     pieces += [lax.ppermute(pieces[blocks // 2], "vel", beside(k)) for k in range(1, blocks // 2)]
 
     h1, later, following, up2, down2, norm1 = small_call(
@@ -871,11 +901,12 @@
 
     around = [lax.ppermute(squares, "space", ring("space", k)) for k in range(1, slabs)]
     (second[1], h2) = lax.optimization_barrier((second[1], h2))
-    inflow_part = inflow(core, swap, *first, *second, vel_index, cst[0], vels, blocks)
     if sub > 1:
         owned = lax.dynamic_slice_in_dim(owned, (me % sub) * (LANES // sub), LANES // sub, 2)
 
-    out = finish(carried_part, inflow_part, h1, h2, vel_index, vels, blocks)
+    out = finish(
+        core, carried_part, inflow_part, swap, first[1], second[1], h1, h2, vel_index, vels, blocks
+    )
     (around[0], out) = lax.optimization_barrier((around[0], out))
     slab = lax.axis_index("space")
     every = [squares] + around

time: 151 us -> 146 us (0.967)
  waiting for transfers between devices: 20.6 us -> 13.2 us
  Pallas kernels: 95.6 us -> 99.1 us
    ppermute x4, waiting for transfers between devices: 6.23 us -> 1.24 us  [shards(): lax.ppermute(send, 'vel', beside(k))]
    ppermute x1, waiting for transfers between devices: 3.44 us -> 0.01 us  [shards(): high2 = lax.ppermute(down2, 'space', ring('space', -1))]
    pallas_call x1, Pallas kernels: 20.1 us -> 22.1 us  [finish(): pl.pallas_call(functools.partial(finish_kernel, blocks=blocks), grid=(gro...]
    unnamed x24 -> x20, local copies, waits for them, and re-layouts: 3.04 us -> 1.8 us
  transfers between devices with their start and end apart: 25 -> 25, of which waited for: 10 -> 7; matrix products, arithmetic and copies ran while one was open for 1% -> 1% of each run, Pallas kernels for 63% -> 68%
where the time goes in v4:
time: 146 us
  Pallas kernels  99.1 us (68%)
  starting transfers between devices  24.8 us (17%)
  waiting for transfers between devices  13.2 us (9%)
  other arithmetic  5.07 us (3%)
  local copies, waits for them, and re-layouts  2.54 us (2%)
    pallas_call x1, Pallas kernels, first_stream(): pl.pallas_call(functools.partial(stream_kernel, vels=vels, blocks=blocks)...  26.5 us
    pallas_call x1, Pallas kernels, finish(): pl.pallas_call(functools.partial(finish_kernel, blocks=blocks), grid=(gro...  22.1 us
    pallas_call x2, Pallas kernels, carried(): pl.pallas_call(functools.partial(carried_kernel, blocks=blocks), grid=(co...  22.1 us
    pallas_call x1, Pallas kernels, both_moments(): pl.pallas_call(functools.partial(moments_kernel, vels=vels, blocks=blocks...  12.1 us
    pallas_call x5, Pallas kernels, small_call(): pl.pallas_call(kernel, in_specs=[smem if s == 's' else vmem for s in spec...  8.49 us
    pallas_call x1, Pallas kernels, inflow_near(): pl.pallas_call(functools.partial(near_kernel, blocks=blocks), grid=(vels...  7.9 us
    ppermute x3, waiting for transfers between devices, shards(): lax.ppermute(pieces[blocks // 2], 'vel', beside(k))  5.61 us
    ppermute x4, starting transfers between devices, shards(): lax.ppermute(send, 'vel', beside(k))  3.73 us
  transfers between devices with their start and end apart: 25, of which 7 were waited for; matrix products, arithmetic and copies ran while one was open for 1% of the time, Pallas kernels for 68%

profile of v4, /device:TPU:0, one launch (start us, length us, event | category | flops | bytes accessed | tf_op | source)
XLA Modules:
  0.0 145.6 jit_solution(13112342212714169158)
XLA Ops:
  0.6 0.8 subtract_select_fusion
  1.4 0.8 select_bitcast_fusion.1
  2.2 0.5 collective-permute-start
  2.7 2.0 %collective-permute-start.1 = (f32[3,1,1024]{2,1,0:T(1,128)S(1)}, f32[3,1,1024]{2,1,0:T(1,128)S(1)}, u32[]{:S(2)}, u32[]{:S(2)}) collective-permute-start(f32[3,1,1024]{2,1,0:T(1,128)S(1)} %get-tuple-element.107), channel_id=1, source_target_pairs={{0,3},{1,0},{2,1},{3,2},{4,7},{5,4},{6,5},{7,6},{8,11},{9,8},{10,9... | collective-permute-start | bytes 36872 | tf_op jit(solution)/shard_map/ppermute | solution.py:811
  4.7 26.5 %first_stream.1 = (f32[4,2,1024,128]{3,2,1,0:T(8,128)}, f32[4,8,1024,128]{3,2,1,0:T(8,128)}) custom-call(f32[32768,128]{1,0:T(8,128)} %bitcast.20, s32[3,512]{1,0:T(4,128)} %index_ref.11), custom_call_target="tpu_custom_call" | custom-call | flops 83886080 | bytes 33554432 | tf_op jit(solution)/shard_map/first_stream/pallas_call | solution.py:225
  31.2 0.7 collective-permute-start.2
  32.0 0.7 compare_reduce_fusion
  32.7 0.8 pad_maximum_fusion.cst_ref
  33.5 12.1 %moments_of_both.1 = (f32[576,128]{1,0:T(8,128)}, f32[576,128]{1,0:T(8,128)}, f32[576,128]{1,0:T(8,128)}, f32[576,128]{1,0:T(8,128)}) custom-call(s32[1]{0:T(128)} %bitcast.me_ref.place_ref, f32[4,8,1024,128]{3,2,1,0:T(8,128)} %get-tuple-element.57.read_ref, f32[4,2,1024,128]{3,2,1,0:T(8,128)} %get-tuple-element.56.leaving_ref, s32[3,512]{1,0:T(4,128)} %index_ref.11, ...), custom_call_target="tpu_custom_call" | custom-call | flops 3523215360 | bytes 20971520 | tf_op jit(solution)/shard_map/moments_of_both/pallas_call | solution.py:349
  45.7 1.9 %dynamic-slice_select_fusion = f32[4,2,512,128]{3,2,1,0:T(8,128)S(1)} fusion(f32[4,2,1024,128]{3,2,1,0:T(8,128)} %collective-permute-done.2.swap_ref, s32[]{:T(128)S(6)} %select_n.135, f32[4,2,1024,128]{3,2,1,0:T(8,128)S(1)} %copy-done.6, pred[4,128]{1,0:T(4,128)(4,1)S(1)} %bitcast.22), kind=kLoop, calls=%fused_computation | loop fusion | flops 524288 | bytes 6291972 | tf_op jit(solution)/shard_map/jit(_where)/select_n | solution.py:828
  47.6 0.1 fusion.3
  47.7 1.7 %collective-permute-start.7 = (f32[4,1,512,128]{3,2,1,0:T(8,128)S(1)}, f32[4,1,512,128]{3,2,1,0:T(8,128)S(1)}, u32[]{:S(2)}, u32[]{:S(2)}) collective-permute-start(f32[4,1,512,128]{3,2,1,0:T(8,128)S(1)} %get-tuple-element.106), channel_id=1, source_target_pairs={{0,2},{1,3},{2,0},{3,1},{4,6},{5,7},{6,4},{7,5},{8,10},{9,11},{10,... | collective-permute-start | bytes 3145736 | tf_op jit(solution)/shard_map/ppermute | solution.py:831
  49.5 1.5 %collective-permute-start.3 = (f32[576,128]{1,0:T(8,128)S(1)}, f32[576,128]{1,0:T(8,128)S(1)}, u32[]{:S(2)}, u32[]{:S(2)}) collective-permute-start(f32[576,128]{1,0:T(8,128)S(1)} %copy-done.9), channel_id=1, source_target_pairs={{0,4},{4,0},{8,12},{12,8},{16,20},{20,16},{24,28},{28,24},{1,5},{5... | collective-permute-start | bytes 884744 | tf_op jit(solution)/shard_map/ppermute | solution.py:838
  51.0 1.6 %collective-permute-start.4 = (f32[576,128]{1,0:T(8,128)S(1)}, f32[576,128]{1,0:T(8,128)S(1)}, u32[]{:S(2)}, u32[]{:S(2)}) collective-permute-start(f32[576,128]{1,0:T(8,128)S(1)} %copy-done.8), channel_id=1, source_target_pairs={{0,8},{4,12},{8,0},{12,4},{16,24},{20,28},{24,16},{28,20},{1,9},{5... | collective-permute-start | bytes 884744 | tf_op jit(solution)/shard_map/ppermute | solution.py:838
  52.6 0.4 collective-permute-start.5
  53.0 11.1 %carried_part.2.refs_0_ = f32[4,8,1024,128]{3,2,1,0:T(8,128)} custom-call(f32[4,8,1024,128]{3,2,1,0:T(8,128)} %get-tuple-element.57.read_ref, s32[3,512]{1,0:T(4,128)S(1)} %copy-done.3, f32[8,1024]{1,0:T(8,128)S(1)} %get-tuple-element.74.al_ref), custom_call_target="tpu_custom_call" | custom-call | flops 1 | bytes 1 | tf_op jit(solution)/shard_map/carried_part/pallas_call | solution.py:409
  64.0 2.0 %collective-permute-done.5.refs_3_ = f32[576,128]{1,0:T(8,128)S(1)} collective-permute-done((f32[576,128]{1,0:T(8,128)S(1)}, f32[576,128]{1,0:T(8,128)S(1)}, u32[]{:S(2)}, u32[]{:S(2)}) %collective-permute-start.5) | collective-permute-done | bytes 294944 | tf_op jit(solution)/shard_map/ppermute | solution.py:838
  66.1 2.6 %collective-permute-start.6 = (f32[288,128]{1,0:T(8,128)S(1)}, f32[288,128]{1,0:T(8,128)S(1)}, u32[]{:S(2)}, u32[]{:S(2)}) collective-permute-start(f32[288,128]{1,0:T(8,128)S(1)} %get-tuple-element.73), channel_id=1, source_target_pairs={{0,16},{4,20},{8,24},{12,28},{16,0},{20,4},{24,8},{28,12},{1,17},{... | collective-permute-start | bytes 442376 | tf_op jit(solution)/shard_map/ppermute | solution.py:842
  68.8 11.0 %carried_part.3.carried_ref = f32[4,8,1024,128]{3,2,1,0:T(8,128)} custom-call(f32[4,8,1024,128]{3,2,1,0:T(8,128)} %get-tuple-element.57.read_ref, s32[3,512]{1,0:T(4,128)S(1)} %copy-done.3, f32[8,1024]{1,0:T(8,128)S(1)} %get-tuple-element.74.al_ref, f32[4,8,1024,128]{3,2,1,0:T(8,128)} %carried_part.2.refs_0_), custom_call_target="tpu_custom_call", output_to_operand_aliasing={{}: (3, {})} | custom-call | flops 1 | bytes 1 | tf_op jit(solution)/shard_map/carried_part/pallas_call | solution.py:409
  79.9 0.5 collective-permute-start.8
  80.4 1.3 collective-permute-start.9
  81.7 2.0 %collective-permute-done.8.low_ref = f32[144,128]{1,0:T(8,128)S(1)} collective-permute-done((f32[144,128]{1,0:T(8,128)S(1)}, f32[144,128]{1,0:T(8,128)S(1)}, u32[]{:S(2)}, u32[]{:S(2)}) %collective-permute-start.8) | collective-permute-done | bytes 73760 | tf_op jit(solution)/shard_map/ppermute | solution.py:857
  83.7 0.8 local_fields.1.refs_0_
  84.5 0.6 collective-permute-start.18
  85.1 1.5 %collective-permute-start.10 = (f32[248,128]{1,0:T(8,128)S(1)}, f32[248,128]{1,0:T(8,128)S(1)}, u32[]{:S(2)}, u32[]{:S(2)}) collective-permute-start(f32[248,128]{1,0:T(8,128)S(1)} %local_fields.1.refs_0_), channel_id=1, source_target_pairs={{0,4},{4,0},{8,12},{12,8},{16,20},{20,16},{24,28},{28,24},{1,5},{5... | collective-permute-start | bytes 380936 | tf_op jit(solution)/shard_map/ppermute | solution.py:862
  86.7 1.6 %collective-permute-start.11 = (f32[248,128]{1,0:T(8,128)S(1)}, f32[248,128]{1,0:T(8,128)S(1)}, u32[]{:S(2)}, u32[]{:S(2)}) collective-permute-start(f32[248,128]{1,0:T(8,128)S(1)} %local_fields.1.refs_0_), channel_id=1, source_target_pairs={{0,8},{4,12},{8,0},{12,4},{16,24},{20,28},{24,16},{28,20},{1,9},{5... | collective-permute-start | bytes 380936 | tf_op jit(solution)/shard_map/ppermute | solution.py:862
  88.2 0.3 collective-permute-start.13
  88.6 0.3 collective-permute-start.12
  88.9 7.9 %inflow_near.1.inflow_ref = f32[4,3,1024,128]{3,2,1,0:T(8,128)} custom-call(s32[1]{0:T(128)} %bitcast.7.core_ref, f32[4,2,1024,128]{3,2,1,0:T(8,128)} %collective-permute-done.2.swap_ref, f32[4,1,512,128]{3,2,1,0:T(8,128)S(1)} %collective-permute-done.7.first_ref, f32[4,1,512,128]{3,2,1,0:T(8,128)S(1)} %collective-permute-done.14.second_ref, ...), custom_call_target="tpu_custom_call" | custom-call | flops 1 | bytes 1 | tf_op jit(solution)/shard_map/inflow_near/pallas_call | solution.py:497
  96.8 1.2 collective-permute-done.13.refs_4_
  98.0 0.5 collective-permute-start.15
  98.6 1.5 %collective-permute-start.16 = (f32[248,128]{1,0:T(8,128)S(1)}, f32[248,128]{1,0:T(8,128)S(1)}, u32[]{:S(2)}, u32[]{:S(2)}) collective-permute-start(f32[248,128]{1,0:T(8,128)S(1)} %collective-permute-done.13.refs_4_), channel_id=1, source_target_pairs={{0,8},{4,12},{8,0},{12,4},{16,24},{20,28},{24,16},{28,20},{1,9},{5... | collective-permute-start | bytes 380936 | tf_op jit(solution)/shard_map/ppermute | solution.py:870
  100.1 1.5 %collective-permute-start.17 = (f32[248,128]{1,0:T(8,128)S(1)}, f32[248,128]{1,0:T(8,128)S(1)}, u32[]{:S(2)}, u32[]{:S(2)}) collective-permute-start(f32[248,128]{1,0:T(8,128)S(1)} %collective-permute-done.13.refs_4_), channel_id=1, source_target_pairs={{0,12},{4,8},{8,4},{12,0},{16,28},{20,24},{24,20},{28,16},{1,13},{... | collective-permute-start | bytes 380936 | tf_op jit(solution)/shard_map/ppermute | solution.py:870
  101.5 1.7 %collective-permute-done.15.refs_5_ = f32[248,128]{1,0:T(8,128)S(1)} collective-permute-done((f32[248,128]{1,0:T(8,128)S(1)}, f32[248,128]{1,0:T(8,128)S(1)}, u32[]{:S(2)}, u32[]{:S(2)}) %collective-permute-start.15) | collective-permute-done | bytes 127008 | tf_op jit(solution)/shard_map/ppermute | solution.py:870
  103.3 1.6 %collective-permute-done.16.refs_6_ = f32[248,128]{1,0:T(8,128)S(1)} collective-permute-done((f32[248,128]{1,0:T(8,128)S(1)}, f32[248,128]{1,0:T(8,128)S(1)}, u32[]{:S(2)}, u32[]{:S(2)}) %collective-permute-start.16) | collective-permute-done | bytes 127008 | tf_op jit(solution)/shard_map/ppermute | solution.py:870
  104.8 2.3 %collective-permute-done.17.refs_7_ = f32[248,128]{1,0:T(8,128)S(1)} collective-permute-done((f32[248,128]{1,0:T(8,128)S(1)}, f32[248,128]{1,0:T(8,128)S(1)}, u32[]{:S(2)}, u32[]{:S(2)}) %collective-permute-start.17) | collective-permute-done | bytes 127008 | tf_op jit(solution)/shard_map/ppermute | solution.py:870
  107.2 4.5 %first_fields.1 = (f32[8,448,128]{2,1,0:T(8,128)S(1)}, f32[104,1024]{1,0:T(8,128)S(1)}, f32[104,1024]{1,0:T(8,128)S(1)}, f32[16,1024]{1,0:T(8,128)}, f32[16,1024]{1,0:T(8,128)}, /*index=5*/f32[8,128]{1,0:T(8,128)S(1)}) custom-call(s32[1]{0:T(128)} %bitcast.me_ref.place_ref, f32[13,13]{1,0:T(8,128)S(1)} %copy-done.5, f32[3,16,1024]{2,1,0:T(8,128)S(1)} %copy-done, ...), custom_call_target="tpu_custom_call" | custom-call | tf_op jit(solution)/shard_map/first_fields/pallas_call | solution.py:517
  111.7 0.8 copy-done.1
  112.5 0.5 collective-permute-start.19
  113.0 1.2 collective-permute-start.20
  114.2 2.3 %collective-permute-done.19.low_ref = f32[16,1024]{1,0:T(8,128)} collective-permute-done((f32[16,1024]{1,0:T(8,128)}, f32[16,1024]{1,0:T(8,128)}, u32[]{:S(2)}, u32[]{:S(2)}) %collective-permute-start.19) | collective-permute-done | bytes 65568 | tf_op jit(solution)/shard_map/ppermute | solution.py:890
  116.5 1.0 copy-done.2
  117.5 3.1 %last_fields.1 = (f32[8,64,128]{2,1,0:T(8,128)S(1)}, f32[13,8,128]{2,1,0:T(8,128)}, f32[2,128]{1,0:T(2,128)S(1)}) custom-call(s32[1]{0:T(128)} %bitcast.me_ref.place_ref, f32[3,16,1024]{2,1,0:T(8,128)S(1)} %copy-done, f32[104,1024]{1,0:T(8,128)S(1)} %get-tuple-element.85.later_ref, f32[104,1024]{1,0:T(8,128)S(1)} %copy-done.2, ...), custom_call_target="tpu_custom_call" | custom-call | tf_op jit(solution)/shard_map/last_fields/pallas_call | solution.py:517
  120.5 0.7 collective-permute-start.21
  121.2 1.0 collective-permute-start.23
  122.3 0.6 collective-permute-start.24
  122.9 22.1 %finish_dist.1 = f32[512,8,8,128]{3,2,1,0:T(8,128)} custom-call(s32[1]{0:T(128)} %bitcast.7.core_ref, f32[4,8,1024,128]{3,2,1,0:T(8,128)} %carried_part.3.carried_ref, f32[4,3,1024,128]{3,2,1,0:T(8,128)} %inflow_near.1.inflow_ref, f32[4,2,1024,128]{3,2,1,0:T(8,128)} %collective-permute-done.2.swap_ref, ...), custom_call_target="tpu_custom_call" | custom-call | flops 2147483648 | bytes 33554432 | tf_op jit(solution)/shard_map/finish_dist/pallas_call | solution.py:753
  145.1 0.5 sqrt.3
  (45 shorter events, 0.5 us)
Async XLA Ops:
  2.2 29.0 %collective-permute-start = (f32[3,1,1024]{2,1,0:T(1,128)S(1)}, f32[3,1,1024]{2,1,0:T(1,128)S(1)}, u32[]{:S(2)}, u32[]{:S(2)}) collective-permute-start(f32[3,1,1024]{2,1,0:T(1,128)S(1)} %get-tuple-element.108), channel_id=1, source_target_pairs={{0,1},{1,2},{2,3},{3,0},{4,5},{5,6},{6,7},{7,4},{8,9},{9,10},{10,1... | collective-permute-start | bytes 36872 | tf_op jit(solution)/shard_map/ppermute | solution.py:810
  2.7 28.5 %collective-permute-start.1 = (f32[3,1,1024]{2,1,0:T(1,128)S(1)}, f32[3,1,1024]{2,1,0:T(1,128)S(1)}, u32[]{:S(2)}, u32[]{:S(2)}) collective-permute-start(f32[3,1,1024]{2,1,0:T(1,128)S(1)} %get-tuple-element.107), channel_id=1, source_target_pairs={{0,3},{1,0},{2,1},{3,2},{4,7},{5,4},{6,5},{7,6},{8,11},{9,8},{10,9... | collective-permute-start | bytes 36872 | tf_op jit(solution)/shard_map/ppermute | solution.py:811
  31.2 14.4 %collective-permute-start.2 = (f32[4,2,1024,128]{3,2,1,0:T(8,128)}, f32[4,2,1024,128]{3,2,1,0:T(8,128)}, u32[]{:S(2)}, u32[]{:S(2)}) collective-permute-start(f32[4,2,1024,128]{3,2,1,0:T(8,128)} %get-tuple-element.56.leaving_ref), channel_id=1, source_target_pairs={{0,1},{1,0},{2,3},{3,2},{4,5},{5,4},{6,7},{7,6},{8,9},{9,8},{10,11... | collective-permute-start | bytes 12582920 | tf_op jit(solution)/shard_map/ppermute | solution.py:815
  33.5 12.1 %copy-start.6 = (f32[4,2,1024,128]{3,2,1,0:T(8,128)S(1)}, f32[4,2,1024,128]{3,2,1,0:T(8,128)}, u32[]{:S(2)}) copy-start(f32[4,2,1024,128]{3,2,1,0:T(8,128)} %get-tuple-element.56.leaving_ref) | copy-start | bytes 12582916
  45.6 3.8 %copy-start.9 = (f32[576,128]{1,0:T(8,128)S(1)}, f32[576,128]{1,0:T(8,128)}, u32[]{:S(2)}) copy-start(f32[576,128]{1,0:T(8,128)} %get-tuple-element.68) | copy-start | bytes 884740
  45.6 5.3 %copy-start.8 = (f32[576,128]{1,0:T(8,128)S(1)}, f32[576,128]{1,0:T(8,128)}, u32[]{:S(2)}) copy-start(f32[576,128]{1,0:T(8,128)} %get-tuple-element.70) | copy-start | bytes 884740
  45.7 6.9 %copy-start.7 = (f32[576,128]{1,0:T(8,128)S(1)}, f32[576,128]{1,0:T(8,128)}, u32[]{:S(2)}) copy-start(f32[576,128]{1,0:T(8,128)} %get-tuple-element.71) | copy-start | bytes 884740
  45.7 7.3 %copy-start.3 = (s32[3,512]{1,0:T(4,128)S(1)}, s32[3,512]{1,0:T(4,128)}, u32[]{:S(2)}) copy-start(s32[3,512]{1,0:T(4,128)} %index_ref.11) | copy-start | bytes 18436
  47.7 18.4 %copy-start.4 = (f32[576,128]{1,0:T(8,128)S(1)}, f32[576,128]{1,0:T(8,128)}, u32[]{:S(2)}) copy-start(f32[576,128]{1,0:T(8,128)} %get-tuple-element.67.refs_0_) | copy-start | bytes 884740
  47.7 32.1 %collective-permute-start.7 = (f32[4,1,512,128]{3,2,1,0:T(8,128)S(1)}, f32[4,1,512,128]{3,2,1,0:T(8,128)S(1)}, u32[]{:S(2)}, u32[]{:S(2)}) collective-permute-start(f32[4,1,512,128]{3,2,1,0:T(8,128)S(1)} %get-tuple-element.106), channel_id=1, source_target_pairs={{0,2},{1,3},{2,0},{3,1},{4,6},{5,7},{6,4},{7,5},{8,10},{9,11},{10,... | collective-permute-start | bytes 3145736 | tf_op jit(solution)/shard_map/ppermute | solution.py:831
  49.5 14.6 %collective-permute-start.3 = (f32[576,128]{1,0:T(8,128)S(1)}, f32[576,128]{1,0:T(8,128)S(1)}, u32[]{:S(2)}, u32[]{:S(2)}) collective-permute-start(f32[576,128]{1,0:T(8,128)S(1)} %copy-done.9), channel_id=1, source_target_pairs={{0,4},{4,0},{8,12},{12,8},{16,20},{20,16},{24,28},{28,24},{1,5},{5... | collective-permute-start | bytes 884744 | tf_op jit(solution)/shard_map/ppermute | solution.py:838
  51.0 13.0 %collective-permute-start.4 = (f32[576,128]{1,0:T(8,128)S(1)}, f32[576,128]{1,0:T(8,128)S(1)}, u32[]{:S(2)}, u32[]{:S(2)}) collective-permute-start(f32[576,128]{1,0:T(8,128)S(1)} %copy-done.8), channel_id=1, source_target_pairs={{0,8},{4,12},{8,0},{12,4},{16,24},{20,28},{24,16},{28,20},{1,9},{5... | collective-permute-start | bytes 884744 | tf_op jit(solution)/shard_map/ppermute | solution.py:838
  52.6 13.5 %collective-permute-start.5 = (f32[576,128]{1,0:T(8,128)S(1)}, f32[576,128]{1,0:T(8,128)S(1)}, u32[]{:S(2)}, u32[]{:S(2)}) collective-permute-start(f32[576,128]{1,0:T(8,128)S(1)} %copy-done.7), channel_id=1, source_target_pairs={{0,12},{4,8},{8,4},{12,0},{16,28},{20,24},{24,20},{28,16},{1,13},{... | collective-permute-start | bytes 884744 | tf_op jit(solution)/shard_map/ppermute | solution.py:838
  66.1 13.7 %collective-permute-start.6 = (f32[288,128]{1,0:T(8,128)S(1)}, f32[288,128]{1,0:T(8,128)S(1)}, u32[]{:S(2)}, u32[]{:S(2)}) collective-permute-start(f32[288,128]{1,0:T(8,128)S(1)} %get-tuple-element.73), channel_id=1, source_target_pairs={{0,16},{4,20},{8,24},{12,28},{16,0},{20,4},{24,8},{28,12},{1,17},{... | collective-permute-start | bytes 442376 | tf_op jit(solution)/shard_map/ppermute | solution.py:842
  68.8 15.0 %copy-start.5 = (f32[13,13]{1,0:T(8,128)S(1)}, f32[13,13]{1,0:T(8,128)}, u32[]{:S(2)}) copy-start(f32[13,13]{1,0:T(8,128)} %inv_ref.3) | copy-start | bytes 2032
  68.8 19.8 %copy-start = (f32[3,16,1024]{2,1,0:T(8,128)S(1)}, f32[3,16,1024]{2,1,0:T(8,128)}, u32[]{:S(2)}) copy-start(f32[3,16,1024]{2,1,0:T(8,128)} %pad_maximum_fusion.cst_ref) | copy-start | bytes 589828
  79.8 8.8 %collective-permute-start.14 = (f32[4,1,512,128]{3,2,1,0:T(8,128)S(1)}, f32[4,1,512,128]{3,2,1,0:T(8,128)S(1)}, u32[]{:S(2)}, u32[]{:S(2)}) collective-permute-start(f32[4,1,512,128]{3,2,1,0:T(8,128)S(1)} %collective-permute-done.7.first_ref), channel_id=1, source_target_pairs={{0,1},{1,0},{2,3},{3,2},{4,5},{5,4},{6,7},{7,6},{8,9},{9,8},{10,11... | collective-permute-start | bytes 3145736 | tf_op jit(solution)/shard_map/ppermute | solution.py:866
  79.9 3.8 %collective-permute-start.8 = (f32[144,128]{1,0:T(8,128)S(1)}, f32[144,128]{1,0:T(8,128)S(1)}, u32[]{:S(2)}, u32[]{:S(2)}) collective-permute-start(f32[144,128]{1,0:T(8,128)S(1)} %get-tuple-element.81), channel_id=1, source_target_pairs={{0,1},{1,2},{2,3},{3,0},{4,5},{5,6},{6,7},{7,4},{8,9},{9,10},{10,1... | collective-permute-start | bytes 221192 | tf_op jit(solution)/shard_map/ppermute | solution.py:857
  80.4 3.3 %collective-permute-start.9 = (f32[144,128]{1,0:T(8,128)S(1)}, f32[144,128]{1,0:T(8,128)S(1)}, u32[]{:S(2)}, u32[]{:S(2)}) collective-permute-start(f32[144,128]{1,0:T(8,128)S(1)} %get-tuple-element.82), channel_id=1, source_target_pairs={{0,3},{1,0},{2,1},{3,2},{4,7},{5,4},{6,5},{7,6},{8,11},{9,8},{10,9... | collective-permute-start | bytes 221192 | tf_op jit(solution)/shard_map/ppermute | solution.py:858
  84.5 27.9 %collective-permute-start.18 = (f32[4,1,512,128]{3,2,1,0:T(8,128)S(1)}, f32[4,1,512,128]{3,2,1,0:T(8,128)S(1)}, u32[]{:S(2)}, u32[]{:S(2)}) collective-permute-start(f32[4,1,512,128]{3,2,1,0:T(8,128)S(1)} %get-tuple-element.87), channel_id=1, source_target_pairs={{0,2},{1,3},{2,0},{3,1},{4,6},{5,7},{6,4},{7,5},{8,10},{9,11},{10,... | collective-permute-start | bytes 3145736 | tf_op jit(solution)/shard_map/ppermute | solution.py:864
  85.1 13.4 %collective-permute-start.10 = (f32[248,128]{1,0:T(8,128)S(1)}, f32[248,128]{1,0:T(8,128)S(1)}, u32[]{:S(2)}, u32[]{:S(2)}) collective-permute-start(f32[248,128]{1,0:T(8,128)S(1)} %local_fields.1.refs_0_), channel_id=1, source_target_pairs={{0,4},{4,0},{8,12},{12,8},{16,20},{20,16},{24,28},{28,24},{1,5},{5... | collective-permute-start | bytes 380936 | tf_op jit(solution)/shard_map/ppermute | solution.py:862
  86.7 13.4 %collective-permute-start.11 = (f32[248,128]{1,0:T(8,128)S(1)}, f32[248,128]{1,0:T(8,128)S(1)}, u32[]{:S(2)}, u32[]{:S(2)}) collective-permute-start(f32[248,128]{1,0:T(8,128)S(1)} %local_fields.1.refs_0_), channel_id=1, source_target_pairs={{0,8},{4,12},{8,0},{12,4},{16,24},{20,28},{24,16},{28,20},{1,9},{5... | collective-permute-start | bytes 380936 | tf_op jit(solution)/shard_map/ppermute | solution.py:862
  88.2 9.8 %collective-permute-start.13 = (f32[248,128]{1,0:T(8,128)S(1)}, f32[248,128]{1,0:T(8,128)S(1)}, u32[]{:S(2)}, u32[]{:S(2)}) collective-permute-start(f32[248,128]{1,0:T(8,128)S(1)} %local_fields.1.refs_0_), channel_id=1, source_target_pairs={{0,16},{4,20},{8,24},{12,28},{16,0},{20,4},{24,8},{28,12},{1,17},{... | collective-permute-start | bytes 380936 | tf_op jit(solution)/shard_map/ppermute | solution.py:862
  88.6 12.9 %collective-permute-start.12 = (f32[248,128]{1,0:T(8,128)S(1)}, f32[248,128]{1,0:T(8,128)S(1)}, u32[]{:S(2)}, u32[]{:S(2)}) collective-permute-start(f32[248,128]{1,0:T(8,128)S(1)} %local_fields.1.refs_0_), channel_id=1, source_target_pairs={{0,12},{4,8},{8,4},{12,0},{16,28},{20,24},{24,20},{28,16},{1,13},{... | collective-permute-start | bytes 380936 | tf_op jit(solution)/shard_map/ppermute | solution.py:862
  98.0 5.2 %collective-permute-start.15 = (f32[248,128]{1,0:T(8,128)S(1)}, f32[248,128]{1,0:T(8,128)S(1)}, u32[]{:S(2)}, u32[]{:S(2)}) collective-permute-start(f32[248,128]{1,0:T(8,128)S(1)} %collective-permute-done.13.refs_4_), channel_id=1, source_target_pairs={{0,4},{4,0},{8,12},{12,8},{16,20},{20,16},{24,28},{28,24},{1,5},{5... | collective-permute-start | bytes 380936 | tf_op jit(solution)/shard_map/ppermute | solution.py:870
  98.6 6.3 %collective-permute-start.16 = (f32[248,128]{1,0:T(8,128)S(1)}, f32[248,128]{1,0:T(8,128)S(1)}, u32[]{:S(2)}, u32[]{:S(2)}) collective-permute-start(f32[248,128]{1,0:T(8,128)S(1)} %collective-permute-done.13.refs_4_), channel_id=1, source_target_pairs={{0,8},{4,12},{8,0},{12,4},{16,24},{20,28},{24,16},{28,20},{1,9},{5... | collective-permute-start | bytes 380936 | tf_op jit(solution)/shard_map/ppermute | solution.py:870
  100.1 7.1 %collective-permute-start.17 = (f32[248,128]{1,0:T(8,128)S(1)}, f32[248,128]{1,0:T(8,128)S(1)}, u32[]{:S(2)}, u32[]{:S(2)}) collective-permute-start(f32[248,128]{1,0:T(8,128)S(1)} %collective-permute-done.13.refs_4_), channel_id=1, source_target_pairs={{0,12},{4,8},{8,4},{12,0},{16,28},{20,24},{24,20},{28,16},{1,13},{... | collective-permute-start | bytes 380936 | tf_op jit(solution)/shard_map/ppermute | solution.py:870
  111.7 0.8 copy-start.1
  112.5 10.4 %collective-permute-start.22 = (f32[4,1,512,128]{3,2,1,0:T(8,128)S(1)}, f32[4,1,512,128]{3,2,1,0:T(8,128)}, u32[]{:S(2)}, u32[]{:S(2)}) collective-permute-start(f32[4,1,512,128]{3,2,1,0:T(8,128)S(1)} %collective-permute-done.18.first_ref), channel_id=1, source_target_pairs={{0,1},{1,0},{2,3},{3,2},{4,5},{5,4},{6,7},{7,6},{8,9},{9,8},{10,11... | collective-permute-start | bytes 3145736 | tf_op jit(solution)/shard_map/ppermute | solution.py:889
  112.5 4.0 %collective-permute-start.19 = (f32[16,1024]{1,0:T(8,128)}, f32[16,1024]{1,0:T(8,128)}, u32[]{:S(2)}, u32[]{:S(2)}) collective-permute-start(f32[16,1024]{1,0:T(8,128)} %get-tuple-element.89), channel_id=1, source_target_pairs={{0,1},{1,2},{2,3},{3,0},{4,5},{5,6},{6,7},{7,4},{8,9},{9,10},{10,1... | collective-permute-start | bytes 196616 | tf_op jit(solution)/shard_map/ppermute | solution.py:890
  113.0 3.5 %collective-permute-start.20 = (f32[16,1024]{1,0:T(8,128)}, f32[16,1024]{1,0:T(8,128)}, u32[]{:S(2)}, u32[]{:S(2)}) collective-permute-start(f32[16,1024]{1,0:T(8,128)} %get-tuple-element.90), channel_id=1, source_target_pairs={{0,3},{1,0},{2,1},{3,2},{4,7},{5,4},{6,5},{7,6},{8,11},{9,8},{10,9... | collective-permute-start | bytes 196616 | tf_op jit(solution)/shard_map/ppermute | solution.py:891
  116.5 1.0 copy-start.2
  120.5 24.4 %collective-permute-start.21 = (f32[2,128]{1,0:T(2,128)S(1)}, f32[2,128]{1,0:T(2,128)S(1)}, u32[]{:S(2)}, u32[]{:S(2)}) collective-permute-start(f32[2,128]{1,0:T(2,128)S(1)} %get-tuple-element.92), channel_id=1, source_target_pairs={{0,1},{1,2},{2,3},{3,0},{4,5},{5,6},{6,7},{7,4},{8,9},{9,10},{10,1... | collective-permute-start | bytes 3080 | tf_op jit(solution)/shard_map/ppermute | solution.py:902
  121.2 23.7 %collective-permute-start.23 = (f32[2,128]{1,0:T(2,128)S(1)}, f32[2,128]{1,0:T(2,128)S(1)}, u32[]{:S(2)}, u32[]{:S(2)}) collective-permute-start(f32[2,128]{1,0:T(2,128)S(1)} %get-tuple-element.92), channel_id=1, source_target_pairs={{0,3},{1,0},{2,1},{3,2},{4,7},{5,4},{6,5},{7,6},{8,11},{9,8},{10,9... | collective-permute-start | bytes 3080 | tf_op jit(solution)/shard_map/ppermute | solution.py:902
  122.3 22.7 %collective-permute-start.24 = (f32[2,128]{1,0:T(2,128)S(1)}, f32[2,128]{1,0:T(2,128)S(1)}, u32[]{:S(2)}, u32[]{:S(2)}) collective-permute-start(f32[2,128]{1,0:T(2,128)S(1)} %get-tuple-element.92), channel_id=1, source_target_pairs={{0,2},{1,3},{2,0},{3,1},{4,6},{5,7},{6,4},{7,5},{8,10},{9,11},{10,... | collective-permute-start | bytes 3080 | tf_op jit(solution)/shard_map/ppermute | solution.py:902

commit v5 on v4

--- a/solution.py
+++ b/solution.py
@@ -24,6 +24,7 @@
 MIB = 2**20
 PIECES = 8
 RUN = 16
+PAD = 8
 
 UP, M1, DOWN, AA, PAY = 0, 40, 144, 184, 288
 STILL = (0, 10, 11, 12)
@@ -142,15 +143,16 @@
 def stream_kernel(dist_ref, index_ref, leaving_ref, read_ref, held, even, odd, done, sems, out_sems, *, vels, blocks):
     stride = blocks * SUB
     chunks = vels // LANES
-    part = LANES * stride
-    piece = part // PIECES
+    piece = LANES // PIECES
+    pitch = stride + PAD
     ys = blocks * LANES // NZ
+    flat = held.reshape(2 * LANES * pitch, LANES)
 
     def fetch(c):
         return [
             pltpu.make_async_copy(
-                dist_ref.at[pl.ds(c * part + p * piece, piece)],
-                held.at[c % 2, pl.ds(p * piece, piece)],
+                dist_ref.at[pl.ds(c * LANES + p * piece, piece)],
+                held.at[c % 2, pl.ds(p * piece, piece), pl.ds(0, stride)],
                 sems.at[c % 2, p],
             )
             for p in range(PIECES)
@@ -162,7 +164,7 @@
     def turn(c, k):
         target = odd if c % 2 else even
         for x in range(SUB):
-            value = held[c % 2, pl.ds(k * SUB + x, LANES, stride=stride), :]
+            value = flat[pl.ds((c % 2) * LANES * pitch + k * SUB + x, LANES, stride=pitch), :]
             target[x + 1, pl.ds(pl.multiple_of(k * LANES, LANES), LANES), :] = value.T
 
     for c in range(min(2, chunks)):
@@ -231,7 +233,7 @@
             jax.ShapeDtypeStruct((vels // LANES, SUB, cells, LANES), jnp.float32),
         ],
         scratch_shapes=[
-            pltpu.VMEM((2, LANES * blocks * SUB, LANES), jnp.float32),
+            pltpu.VMEM((2, LANES, blocks * SUB + PAD, LANES), jnp.float32),
             pltpu.VMEM((SUB + 2, cells, LANES), jnp.float32),
             pltpu.VMEM((SUB + 2, cells, LANES), jnp.float32),
             pltpu.VMEM((2, SUB, cells, LANES), jnp.float32),
@@ -693,7 +695,7 @@
 
 def finish_kernel(
     core_ref, carried_ref, inflow_ref, swap_ref, first_ref, second_ref, h1_ref, h2_ref, index_ref, out_ref,
-    rows, fields, table, far, *, blocks
+    rows, fields, table, far, ready, sems, *, blocks
 ):
     group = pl.program_id(0)
 
@@ -725,7 +727,21 @@
                 fields[x, at, 0:LANES] = jnp.where(left, high, value - high).astype(jnp.bfloat16)
                 fields[x, at, LANES:] = jnp.where(left, high, 0.0).astype(jnp.bfloat16)
 
-    out = out_ref.reshape(LANES * blocks * SUB, LANES)
+    stride = blocks * SUB
+    pitch = stride + PAD
+    slot = lax.rem(group, 2)
+    out = ready.reshape(2 * LANES * pitch, LANES)
+
+    def store(g):
+        side = lax.rem(g, 2)
+        return pltpu.make_async_copy(
+            ready.at[side, :, pl.ds(0, stride)], out_ref.at[pl.ds(g * LANES, LANES)], sems.at[side]
+        )
+
+    @pl.when(group >= 2)
+    def _():
+        store(group - 2).wait()
+
     here = index_ref[0:1, pl.ds(pl.multiple_of(group * LANES, LANES), LANES)]
     px = here * 2 >= NVX
     core = core_ref[0]
@@ -743,7 +759,16 @@
         elif x in (SUB - 2, SUB - 1):
             value = value + jnp.where(px, 0.0, inflow[SUB - 1 - x]())
         for k in range(blocks):
-            out[pl.ds(k * SUB + x, LANES, stride=blocks * SUB), :] = value[k * LANES : (k + 1) * LANES].T
+            first = slot * (LANES * pitch) + k * SUB + x
+            out[pl.ds(first, LANES, stride=pitch), :] = value[k * LANES : (k + 1) * LANES].T
+    store(group).start()
+    last = rows.shape[0] - 1
+
+    @pl.when(group == last)
+    def _():
+        if last > 0:
+            store(group - 1).wait()
+        store(group).wait()
 
 
 def finish(core, carried_part, inflow_part, swap, first, second, h1, h2, vel_index, vels, blocks):
@@ -764,13 +789,15 @@
             vmem,
             vmem,
         ],
-        out_specs=pl.BlockSpec((LANES, blocks, SUB, LANES), lambda g: (g, 0, 0, 0)),
-        out_shape=jax.ShapeDtypeStruct((vels, blocks, SUB, LANES), jnp.float32),
+        out_specs=pl.BlockSpec(memory_space=pl.ANY),
+        out_shape=jax.ShapeDtypeStruct((vels, blocks * SUB, LANES), jnp.float32),
         scratch_shapes=[
             pltpu.VMEM((groups, 256, LANES), jnp.bfloat16),
             pltpu.VMEM((SUB, cells, 256), jnp.bfloat16),
             pltpu.VMEM((8, vels), jnp.float32),
             pltpu.VMEM((cells, LANES), jnp.float32),
+            pltpu.VMEM((2, LANES, blocks * SUB + PAD, LANES), jnp.float32),
+            pltpu.SemaphoreType.DMA((2,)),
         ],
         compiler_params=pltpu.CompilerParams(vmem_limit_bytes=40 * MIB),
         cost_estimate=pl.CostEstimate(
@@ -795,7 +822,7 @@
     place = (me // sub).astype(jnp.int32).reshape(1)
     core = (lax.axis_index("space") % 2).astype(jnp.int32).reshape(1)
 
-    flat = dist.reshape(vels, width, blocks, LANES).transpose(0, 2, 1, 3).reshape(vels * blocks * width, LANES)
+    flat = dist.reshape(vels, width, blocks, LANES).transpose(0, 2, 1, 3).reshape(vels, blocks * width, LANES)
     speed = speed_range * (2.0 * vel_index.astype(jnp.float32) + 1.0 - NVX) / NVX
 
     wall = wall_mask > 0
@@ -915,7 +942,7 @@
         for j in range(slabs)
     ]
     norms = jnp.sqrt(jnp.sum(sum(ordered), axis=1))
-    out = out.transpose(0, 2, 1, 3).reshape(vels, width, cells)
+    out = out.reshape(vels, blocks, width, LANES).transpose(0, 2, 1, 3).reshape(vels, width, cells)
     return (out, owned, norms)
 
 

time: 146 us -> 137 us (0.938)
  Pallas kernels: 99.1 us -> 89.8 us
    pallas_call x1, Pallas kernels: 26.5 us -> 21.7 us  [first_stream(): pl.pallas_call(functools.partial(stream_kernel, vels=vels, blocks=blocks)...]
    pallas_call x1, Pallas kernels: 22.1 us -> 17.5 us  [finish(): pl.pallas_call(functools.partial(finish_kernel, blocks=blocks), grid=(gro...]
  transfers between devices with their start and end apart: 25 -> 25, of which waited for: 7 -> 7; matrix products, arithmetic and copies ran while one was open for 1% -> 1% of each run, Pallas kernels for 68% -> 66%
where the time goes in v5:
time: 137 us; the launch traced here: 136 us
  Pallas kernels  89.8 us (66%)
  starting transfers between devices  24.8 us (18%)
  waiting for transfers between devices  13.2 us (10%)
  other arithmetic  5.07 us (4%)
  local copies, waits for them, and re-layouts  2.54 us (2%)
    pallas_call x2, Pallas kernels, carried(): pl.pallas_call(functools.partial(carried_kernel, blocks=blocks), grid=(co...  22.1 us
    pallas_call x1, Pallas kernels, first_stream(): pl.pallas_call(functools.partial(stream_kernel, vels=vels, blocks=blocks)...  21.7 us
    pallas_call x1, Pallas kernels, finish(): pl.pallas_call(functools.partial(finish_kernel, blocks=blocks), grid=(gro...  17.5 us
    pallas_call x1, Pallas kernels, both_moments(): pl.pallas_call(functools.partial(moments_kernel, vels=vels, blocks=blocks...  12.1 us
    pallas_call x5, Pallas kernels, small_call(): pl.pallas_call(kernel, in_specs=[smem if s == 's' else vmem for s in spec...  8.49 us
    pallas_call x1, Pallas kernels, inflow_near(): pl.pallas_call(functools.partial(near_kernel, blocks=blocks), grid=(vels...  7.9 us
    ppermute x3, waiting for transfers between devices, shards(): lax.ppermute(pieces[blocks // 2], 'vel', beside(k))  5.61 us
    ppermute x4, starting transfers between devices, shards(): lax.ppermute(send, 'vel', beside(k))  3.74 us
  transfers between devices with their start and end apart: 25, of which 7 were waited for; matrix products, arithmetic and copies ran while one was open for 1% of the time, Pallas kernels for 66%

profile of v5, /device:TPU:0, one launch (start us, length us, event | category | flops | bytes accessed | tf_op | source)
XLA Modules:
  0.0 136.2 jit_solution(5113805050415793751)
XLA Ops:
  0.6 0.8 subtract_select_fusion
  1.4 0.8 select_bitcast_fusion.1
  2.2 0.5 collective-permute-start
  2.7 2.0 %collective-permute-start.1 = (f32[3,1,1024]{2,1,0:T(1,128)S(1)}, f32[3,1,1024]{2,1,0:T(1,128)S(1)}, u32[]{:S(2)}, u32[]{:S(2)}) collective-permute-start(f32[3,1,1024]{2,1,0:T(1,128)S(1)} %get-tuple-element.107), channel_id=1, source_target_pairs={{0,3},{1,0},{2,1},{3,2},{4,7},{5,4},{6,5},{7,6},{8,11},{9,8},{10,9... | collective-permute-start | bytes 36872 | tf_op jit(solution)/shard_map/ppermute | solution.py:838
  4.7 21.7 %first_stream.1 = (f32[4,2,1024,128]{3,2,1,0:T(8,128)}, f32[4,8,1024,128]{3,2,1,0:T(8,128)}) custom-call(f32[512,64,128]{2,1,0:T(8,128)} %bitcast.22, s32[3,512]{1,0:T(4,128)} %index_ref.11), custom_call_target="tpu_custom_call" | custom-call | flops 83886080 | bytes 33554432 | tf_op jit(solution)/shard_map/first_stream/pallas_call | solution.py:227
  26.4 0.7 collective-permute-start.2
  27.1 0.7 compare_reduce_fusion
  27.9 0.8 pad_maximum_fusion.cst_ref
  28.6 12.1 %moments_of_both.1 = (f32[576,128]{1,0:T(8,128)}, f32[576,128]{1,0:T(8,128)}, f32[576,128]{1,0:T(8,128)}, f32[576,128]{1,0:T(8,128)}) custom-call(s32[1]{0:T(128)} %bitcast.me_ref.place_ref, f32[4,8,1024,128]{3,2,1,0:T(8,128)} %get-tuple-element.57.read_ref, f32[4,2,1024,128]{3,2,1,0:T(8,128)} %get-tuple-element.56.leaving_ref, s32[3,512]{1,0:T(4,128)} %index_ref.11, ...), custom_call_target="tpu_custom_call" | custom-call | flops 3523215360 | bytes 20971520 | tf_op jit(solution)/shard_map/moments_of_both/pallas_call | solution.py:351
  40.8 1.9 %dynamic-slice_select_fusion = f32[4,2,512,128]{3,2,1,0:T(8,128)S(1)} fusion(f32[4,2,1024,128]{3,2,1,0:T(8,128)} %collective-permute-done.2.swap_ref, s32[]{:T(128)S(6)} %select_n.135, f32[4,2,1024,128]{3,2,1,0:T(8,128)S(1)} %copy-done.6, pred[4,128]{1,0:T(4,128)(4,1)S(1)} %bitcast.24), kind=kLoop, calls=%fused_computation | loop fusion | flops 524288 | bytes 6291972 | tf_op jit(solution)/shard_map/jit(_where)/select_n | solution.py:855
  42.7 0.1 fusion.3
  42.9 1.7 %collective-permute-start.7 = (f32[4,1,512,128]{3,2,1,0:T(8,128)S(1)}, f32[4,1,512,128]{3,2,1,0:T(8,128)S(1)}, u32[]{:S(2)}, u32[]{:S(2)}) collective-permute-start(f32[4,1,512,128]{3,2,1,0:T(8,128)S(1)} %get-tuple-element.106), channel_id=1, source_target_pairs={{0,2},{1,3},{2,0},{3,1},{4,6},{5,7},{6,4},{7,5},{8,10},{9,11},{10,... | collective-permute-start | bytes 3145736 | tf_op jit(solution)/shard_map/ppermute | solution.py:858
  44.6 1.5 %collective-permute-start.3 = (f32[576,128]{1,0:T(8,128)S(1)}, f32[576,128]{1,0:T(8,128)S(1)}, u32[]{:S(2)}, u32[]{:S(2)}) collective-permute-start(f32[576,128]{1,0:T(8,128)S(1)} %copy-done.9), channel_id=1, source_target_pairs={{0,4},{4,0},{8,12},{12,8},{16,20},{20,16},{24,28},{28,24},{1,5},{5... | collective-permute-start | bytes 884744 | tf_op jit(solution)/shard_map/ppermute | solution.py:865
  46.1 1.6 %collective-permute-start.4 = (f32[576,128]{1,0:T(8,128)S(1)}, f32[576,128]{1,0:T(8,128)S(1)}, u32[]{:S(2)}, u32[]{:S(2)}) collective-permute-start(f32[576,128]{1,0:T(8,128)S(1)} %copy-done.8), channel_id=1, source_target_pairs={{0,8},{4,12},{8,0},{12,4},{16,24},{20,28},{24,16},{28,20},{1,9},{5... | collective-permute-start | bytes 884744 | tf_op jit(solution)/shard_map/ppermute | solution.py:865
  47.7 0.4 collective-permute-start.5
  48.1 11.1 %carried_part.2.refs_0_ = f32[4,8,1024,128]{3,2,1,0:T(8,128)} custom-call(f32[4,8,1024,128]{3,2,1,0:T(8,128)} %get-tuple-element.57.read_ref, s32[3,512]{1,0:T(4,128)S(1)} %copy-done.3, f32[8,1024]{1,0:T(8,128)S(1)} %get-tuple-element.74.al_ref), custom_call_target="tpu_custom_call" | custom-call | flops 1 | bytes 1 | tf_op jit(solution)/shard_map/carried_part/pallas_call | solution.py:411
  59.2 2.0 %collective-permute-done.5.refs_3_ = f32[576,128]{1,0:T(8,128)S(1)} collective-permute-done((f32[576,128]{1,0:T(8,128)S(1)}, f32[576,128]{1,0:T(8,128)S(1)}, u32[]{:S(2)}, u32[]{:S(2)}) %collective-permute-start.5) | collective-permute-done | bytes 294944 | tf_op jit(solution)/shard_map/ppermute | solution.py:865
  61.3 2.7 %collective-permute-start.6 = (f32[288,128]{1,0:T(8,128)S(1)}, f32[288,128]{1,0:T(8,128)S(1)}, u32[]{:S(2)}, u32[]{:S(2)}) collective-permute-start(f32[288,128]{1,0:T(8,128)S(1)} %get-tuple-element.73), channel_id=1, source_target_pairs={{0,16},{4,20},{8,24},{12,28},{16,0},{20,4},{24,8},{28,12},{1,17},{... | collective-permute-start | bytes 442376 | tf_op jit(solution)/shard_map/ppermute | solution.py:869
  63.9 11.0 %carried_part.3.carried_ref = f32[4,8,1024,128]{3,2,1,0:T(8,128)} custom-call(f32[4,8,1024,128]{3,2,1,0:T(8,128)} %get-tuple-element.57.read_ref, s32[3,512]{1,0:T(4,128)S(1)} %copy-done.3, f32[8,1024]{1,0:T(8,128)S(1)} %get-tuple-element.74.al_ref, f32[4,8,1024,128]{3,2,1,0:T(8,128)} %carried_part.2.refs_0_), custom_call_target="tpu_custom_call", output_to_operand_aliasing={{}: (3, {})} | custom-call | flops 1 | bytes 1 | tf_op jit(solution)/shard_map/carried_part/pallas_call | solution.py:411
  75.0 0.5 collective-permute-start.8
  75.5 1.3 collective-permute-start.9
  76.8 2.0 %collective-permute-done.8.low_ref = f32[144,128]{1,0:T(8,128)S(1)} collective-permute-done((f32[144,128]{1,0:T(8,128)S(1)}, f32[144,128]{1,0:T(8,128)S(1)}, u32[]{:S(2)}, u32[]{:S(2)}) %collective-permute-start.8) | collective-permute-done | bytes 73760 | tf_op jit(solution)/shard_map/ppermute | solution.py:884
  78.9 0.8 local_fields.1.refs_0_
  79.7 0.6 collective-permute-start.18
  80.3 1.5 %collective-permute-start.10 = (f32[248,128]{1,0:T(8,128)S(1)}, f32[248,128]{1,0:T(8,128)S(1)}, u32[]{:S(2)}, u32[]{:S(2)}) collective-permute-start(f32[248,128]{1,0:T(8,128)S(1)} %local_fields.1.refs_0_), channel_id=1, source_target_pairs={{0,4},{4,0},{8,12},{12,8},{16,20},{20,16},{24,28},{28,24},{1,5},{5... | collective-permute-start | bytes 380936 | tf_op jit(solution)/shard_map/ppermute | solution.py:889
  81.8 1.6 %collective-permute-start.11 = (f32[248,128]{1,0:T(8,128)S(1)}, f32[248,128]{1,0:T(8,128)S(1)}, u32[]{:S(2)}, u32[]{:S(2)}) collective-permute-start(f32[248,128]{1,0:T(8,128)S(1)} %local_fields.1.refs_0_), channel_id=1, source_target_pairs={{0,8},{4,12},{8,0},{12,4},{16,24},{20,28},{24,16},{28,20},{1,9},{5... | collective-permute-start | bytes 380936 | tf_op jit(solution)/shard_map/ppermute | solution.py:889
  83.4 0.3 collective-permute-start.13
  83.7 0.3 collective-permute-start.12
  84.0 7.9 %inflow_near.1.inflow_ref = f32[4,3,1024,128]{3,2,1,0:T(8,128)} custom-call(s32[1]{0:T(128)} %bitcast.7.core_ref, f32[4,2,1024,128]{3,2,1,0:T(8,128)} %collective-permute-done.2.swap_ref, f32[4,1,512,128]{3,2,1,0:T(8,128)S(1)} %collective-permute-done.7.first_ref, f32[4,1,512,128]{3,2,1,0:T(8,128)S(1)} %collective-permute-done.14.second_ref, ...), custom_call_target="tpu_custom_call" | custom-call | flops 1 | bytes 1 | tf_op jit(solution)/shard_map/inflow_near/pallas_call | solution.py:499
  92.0 1.2 collective-permute-done.13.refs_4_
  93.2 0.5 collective-permute-start.15
  93.7 1.5 %collective-permute-start.16 = (f32[248,128]{1,0:T(8,128)S(1)}, f32[248,128]{1,0:T(8,128)S(1)}, u32[]{:S(2)}, u32[]{:S(2)}) collective-permute-start(f32[248,128]{1,0:T(8,128)S(1)} %collective-permute-done.13.refs_4_), channel_id=1, source_target_pairs={{0,8},{4,12},{8,0},{12,4},{16,24},{20,28},{24,16},{28,20},{1,9},{5... | collective-permute-start | bytes 380936 | tf_op jit(solution)/shard_map/ppermute | solution.py:897
  95.2 1.5 %collective-permute-start.17 = (f32[248,128]{1,0:T(8,128)S(1)}, f32[248,128]{1,0:T(8,128)S(1)}, u32[]{:S(2)}, u32[]{:S(2)}) collective-permute-start(f32[248,128]{1,0:T(8,128)S(1)} %collective-permute-done.13.refs_4_), channel_id=1, source_target_pairs={{0,12},{4,8},{8,4},{12,0},{16,28},{20,24},{24,20},{28,16},{1,13},{... | collective-permute-start | bytes 380936 | tf_op jit(solution)/shard_map/ppermute | solution.py:897
  96.7 1.7 %collective-permute-done.15.refs_5_ = f32[248,128]{1,0:T(8,128)S(1)} collective-permute-done((f32[248,128]{1,0:T(8,128)S(1)}, f32[248,128]{1,0:T(8,128)S(1)}, u32[]{:S(2)}, u32[]{:S(2)}) %collective-permute-start.15) | collective-permute-done | bytes 127008 | tf_op jit(solution)/shard_map/ppermute | solution.py:897
  98.4 1.6 %collective-permute-done.16.refs_6_ = f32[248,128]{1,0:T(8,128)S(1)} collective-permute-done((f32[248,128]{1,0:T(8,128)S(1)}, f32[248,128]{1,0:T(8,128)S(1)}, u32[]{:S(2)}, u32[]{:S(2)}) %collective-permute-start.16) | collective-permute-done | bytes 127008 | tf_op jit(solution)/shard_map/ppermute | solution.py:897
  100.0 2.3 %collective-permute-done.17.refs_7_ = f32[248,128]{1,0:T(8,128)S(1)} collective-permute-done((f32[248,128]{1,0:T(8,128)S(1)}, f32[248,128]{1,0:T(8,128)S(1)}, u32[]{:S(2)}, u32[]{:S(2)}) %collective-permute-start.17) | collective-permute-done | bytes 127008 | tf_op jit(solution)/shard_map/ppermute | solution.py:897
  102.3 4.5 %first_fields.1 = (f32[8,448,128]{2,1,0:T(8,128)S(1)}, f32[104,1024]{1,0:T(8,128)S(1)}, f32[104,1024]{1,0:T(8,128)S(1)}, f32[16,1024]{1,0:T(8,128)}, f32[16,1024]{1,0:T(8,128)}, /*index=5*/f32[8,128]{1,0:T(8,128)S(1)}) custom-call(s32[1]{0:T(128)} %bitcast.me_ref.place_ref, f32[13,13]{1,0:T(8,128)S(1)} %copy-done.5, f32[3,16,1024]{2,1,0:T(8,128)S(1)} %copy-done, ...), custom_call_target="tpu_custom_call" | custom-call | tf_op jit(solution)/shard_map/first_fields/pallas_call | solution.py:519
  106.8 0.8 copy-done.1
  107.6 0.5 collective-permute-start.19
  108.1 1.2 collective-permute-start.20
  109.3 2.3 %collective-permute-done.19.low_ref = f32[16,1024]{1,0:T(8,128)} collective-permute-done((f32[16,1024]{1,0:T(8,128)}, f32[16,1024]{1,0:T(8,128)}, u32[]{:S(2)}, u32[]{:S(2)}) %collective-permute-start.19) | collective-permute-done | bytes 65568 | tf_op jit(solution)/shard_map/ppermute | solution.py:917
  111.6 1.0 copy-done.2
  112.6 3.1 %last_fields.1 = (f32[8,64,128]{2,1,0:T(8,128)S(1)}, f32[13,8,128]{2,1,0:T(8,128)}, f32[2,128]{1,0:T(2,128)S(1)}) custom-call(s32[1]{0:T(128)} %bitcast.me_ref.place_ref, f32[3,16,1024]{2,1,0:T(8,128)S(1)} %copy-done, f32[104,1024]{1,0:T(8,128)S(1)} %get-tuple-element.85.later_ref, f32[104,1024]{1,0:T(8,128)S(1)} %copy-done.2, ...), custom_call_target="tpu_custom_call" | custom-call | tf_op jit(solution)/shard_map/last_fields/pallas_call | solution.py:519
  115.7 0.7 collective-permute-start.21
  116.4 1.1 collective-permute-start.23
  117.4 0.6 collective-permute-start.24
  118.0 17.5 %finish_dist.1 = f32[512,64,128]{2,1,0:T(8,128)} custom-call(s32[1]{0:T(128)} %bitcast.7.core_ref, f32[4,8,1024,128]{3,2,1,0:T(8,128)} %carried_part.3.carried_ref, f32[4,3,1024,128]{3,2,1,0:T(8,128)} %inflow_near.1.inflow_ref, f32[4,2,1024,128]{3,2,1,0:T(8,128)} %collective-permute-done.2.swap_ref, ...), custom_call_target="tpu_custom_call" | custom-call | flops 2147483648 | bytes 33554432 | tf_op jit(solution)/shard_map/finish_dist/pallas_call | solution.py:778
  135.7 0.5 sqrt.3
  (45 shorter events, 0.5 us)
Async XLA Ops:
  2.2 24.2 %collective-permute-start = (f32[3,1,1024]{2,1,0:T(1,128)S(1)}, f32[3,1,1024]{2,1,0:T(1,128)S(1)}, u32[]{:S(2)}, u32[]{:S(2)}) collective-permute-start(f32[3,1,1024]{2,1,0:T(1,128)S(1)} %get-tuple-element.108), channel_id=1, source_target_pairs={{0,1},{1,2},{2,3},{3,0},{4,5},{5,6},{6,7},{7,4},{8,9},{9,10},{10,1... | collective-permute-start | bytes 36872 | tf_op jit(solution)/shard_map/ppermute | solution.py:837
  2.7 23.7 %collective-permute-start.1 = (f32[3,1,1024]{2,1,0:T(1,128)S(1)}, f32[3,1,1024]{2,1,0:T(1,128)S(1)}, u32[]{:S(2)}, u32[]{:S(2)}) collective-permute-start(f32[3,1,1024]{2,1,0:T(1,128)S(1)} %get-tuple-element.107), channel_id=1, source_target_pairs={{0,3},{1,0},{2,1},{3,2},{4,7},{5,4},{6,5},{7,6},{8,11},{9,8},{10,9... | collective-permute-start | bytes 36872 | tf_op jit(solution)/shard_map/ppermute | solution.py:838
  26.4 14.4 %collective-permute-start.2 = (f32[4,2,1024,128]{3,2,1,0:T(8,128)}, f32[4,2,1024,128]{3,2,1,0:T(8,128)}, u32[]{:S(2)}, u32[]{:S(2)}) collective-permute-start(f32[4,2,1024,128]{3,2,1,0:T(8,128)} %get-tuple-element.56.leaving_ref), channel_id=1, source_target_pairs={{0,1},{1,0},{2,3},{3,2},{4,5},{5,4},{6,7},{7,6},{8,9},{9,8},{10,11... | collective-permute-start | bytes 12582920 | tf_op jit(solution)/shard_map/ppermute | solution.py:842
  28.6 12.1 %copy-start.6 = (f32[4,2,1024,128]{3,2,1,0:T(8,128)S(1)}, f32[4,2,1024,128]{3,2,1,0:T(8,128)}, u32[]{:S(2)}) copy-start(f32[4,2,1024,128]{3,2,1,0:T(8,128)} %get-tuple-element.56.leaving_ref) | copy-start | bytes 12582916
  40.8 3.8 %copy-start.9 = (f32[576,128]{1,0:T(8,128)S(1)}, f32[576,128]{1,0:T(8,128)}, u32[]{:S(2)}) copy-start(f32[576,128]{1,0:T(8,128)} %get-tuple-element.68) | copy-start | bytes 884740
  40.8 5.3 %copy-start.8 = (f32[576,128]{1,0:T(8,128)S(1)}, f32[576,128]{1,0:T(8,128)}, u32[]{:S(2)}) copy-start(f32[576,128]{1,0:T(8,128)} %get-tuple-element.70) | copy-start | bytes 884740
  40.8 6.9 %copy-start.7 = (f32[576,128]{1,0:T(8,128)S(1)}, f32[576,128]{1,0:T(8,128)}, u32[]{:S(2)}) copy-start(f32[576,128]{1,0:T(8,128)} %get-tuple-element.71) | copy-start | bytes 884740
  40.8 7.3 %copy-start.3 = (s32[3,512]{1,0:T(4,128)S(1)}, s32[3,512]{1,0:T(4,128)}, u32[]{:S(2)}) copy-start(s32[3,512]{1,0:T(4,128)} %index_ref.11) | copy-start | bytes 18436
  42.9 18.4 %copy-start.4 = (f32[576,128]{1,0:T(8,128)S(1)}, f32[576,128]{1,0:T(8,128)}, u32[]{:S(2)}) copy-start(f32[576,128]{1,0:T(8,128)} %get-tuple-element.67.refs_0_) | copy-start | bytes 884740
  42.9 32.1 %collective-permute-start.7 = (f32[4,1,512,128]{3,2,1,0:T(8,128)S(1)}, f32[4,1,512,128]{3,2,1,0:T(8,128)S(1)}, u32[]{:S(2)}, u32[]{:S(2)}) collective-permute-start(f32[4,1,512,128]{3,2,1,0:T(8,128)S(1)} %get-tuple-element.106), channel_id=1, source_target_pairs={{0,2},{1,3},{2,0},{3,1},{4,6},{5,7},{6,4},{7,5},{8,10},{9,11},{10,... | collective-permute-start | bytes 3145736 | tf_op jit(solution)/shard_map/ppermute | solution.py:858
  44.6 14.6 %collective-permute-start.3 = (f32[576,128]{1,0:T(8,128)S(1)}, f32[576,128]{1,0:T(8,128)S(1)}, u32[]{:S(2)}, u32[]{:S(2)}) collective-permute-start(f32[576,128]{1,0:T(8,128)S(1)} %copy-done.9), channel_id=1, source_target_pairs={{0,4},{4,0},{8,12},{12,8},{16,20},{20,16},{24,28},{28,24},{1,5},{5... | collective-permute-start | bytes 884744 | tf_op jit(solution)/shard_map/ppermute | solution.py:865
  46.1 13.0 %collective-permute-start.4 = (f32[576,128]{1,0:T(8,128)S(1)}, f32[576,128]{1,0:T(8,128)S(1)}, u32[]{:S(2)}, u32[]{:S(2)}) collective-permute-start(f32[576,128]{1,0:T(8,128)S(1)} %copy-done.8), channel_id=1, source_target_pairs={{0,8},{4,12},{8,0},{12,4},{16,24},{20,28},{24,16},{28,20},{1,9},{5... | collective-permute-start | bytes 884744 | tf_op jit(solution)/shard_map/ppermute | solution.py:865
  47.7 13.5 %collective-permute-start.5 = (f32[576,128]{1,0:T(8,128)S(1)}, f32[576,128]{1,0:T(8,128)S(1)}, u32[]{:S(2)}, u32[]{:S(2)}) collective-permute-start(f32[576,128]{1,0:T(8,128)S(1)} %copy-done.7), channel_id=1, source_target_pairs={{0,12},{4,8},{8,4},{12,0},{16,28},{20,24},{24,20},{28,16},{1,13},{... | collective-permute-start | bytes 884744 | tf_op jit(solution)/shard_map/ppermute | solution.py:865
  61.3 13.7 %collective-permute-start.6 = (f32[288,128]{1,0:T(8,128)S(1)}, f32[288,128]{1,0:T(8,128)S(1)}, u32[]{:S(2)}, u32[]{:S(2)}) collective-permute-start(f32[288,128]{1,0:T(8,128)S(1)} %get-tuple-element.73), channel_id=1, source_target_pairs={{0,16},{4,20},{8,24},{12,28},{16,0},{20,4},{24,8},{28,12},{1,17},{... | collective-permute-start | bytes 442376 | tf_op jit(solution)/shard_map/ppermute | solution.py:869
  63.9 15.0 %copy-start.5 = (f32[13,13]{1,0:T(8,128)S(1)}, f32[13,13]{1,0:T(8,128)}, u32[]{:S(2)}) copy-start(f32[13,13]{1,0:T(8,128)} %inv_ref.3) | copy-start | bytes 2032
  63.9 19.8 %copy-start = (f32[3,16,1024]{2,1,0:T(8,128)S(1)}, f32[3,16,1024]{2,1,0:T(8,128)}, u32[]{:S(2)}) copy-start(f32[3,16,1024]{2,1,0:T(8,128)} %pad_maximum_fusion.cst_ref) | copy-start | bytes 589828
  75.0 8.8 %collective-permute-start.14 = (f32[4,1,512,128]{3,2,1,0:T(8,128)S(1)}, f32[4,1,512,128]{3,2,1,0:T(8,128)S(1)}, u32[]{:S(2)}, u32[]{:S(2)}) collective-permute-start(f32[4,1,512,128]{3,2,1,0:T(8,128)S(1)} %collective-permute-done.7.first_ref), channel_id=1, source_target_pairs={{0,1},{1,0},{2,3},{3,2},{4,5},{5,4},{6,7},{7,6},{8,9},{9,8},{10,11... | collective-permute-start | bytes 3145736 | tf_op jit(solution)/shard_map/ppermute | solution.py:893
  75.0 3.8 %collective-permute-start.8 = (f32[144,128]{1,0:T(8,128)S(1)}, f32[144,128]{1,0:T(8,128)S(1)}, u32[]{:S(2)}, u32[]{:S(2)}) collective-permute-start(f32[144,128]{1,0:T(8,128)S(1)} %get-tuple-element.81), channel_id=1, source_target_pairs={{0,1},{1,2},{2,3},{3,0},{4,5},{5,6},{6,7},{7,4},{8,9},{9,10},{10,1... | collective-permute-start | bytes 221192 | tf_op jit(solution)/shard_map/ppermute | solution.py:884
  75.5 3.3 %collective-permute-start.9 = (f32[144,128]{1,0:T(8,128)S(1)}, f32[144,128]{1,0:T(8,128)S(1)}, u32[]{:S(2)}, u32[]{:S(2)}) collective-permute-start(f32[144,128]{1,0:T(8,128)S(1)} %get-tuple-element.82), channel_id=1, source_target_pairs={{0,3},{1,0},{2,1},{3,2},{4,7},{5,4},{6,5},{7,6},{8,11},{9,8},{10,9... | collective-permute-start | bytes 221192 | tf_op jit(solution)/shard_map/ppermute | solution.py:885
  79.7 27.9 %collective-permute-start.18 = (f32[4,1,512,128]{3,2,1,0:T(8,128)S(1)}, f32[4,1,512,128]{3,2,1,0:T(8,128)S(1)}, u32[]{:S(2)}, u32[]{:S(2)}) collective-permute-start(f32[4,1,512,128]{3,2,1,0:T(8,128)S(1)} %get-tuple-element.87), channel_id=1, source_target_pairs={{0,2},{1,3},{2,0},{3,1},{4,6},{5,7},{6,4},{7,5},{8,10},{9,11},{10,... | collective-permute-start | bytes 3145736 | tf_op jit(solution)/shard_map/ppermute | solution.py:891
  80.3 13.4 %collective-permute-start.10 = (f32[248,128]{1,0:T(8,128)S(1)}, f32[248,128]{1,0:T(8,128)S(1)}, u32[]{:S(2)}, u32[]{:S(2)}) collective-permute-start(f32[248,128]{1,0:T(8,128)S(1)} %local_fields.1.refs_0_), channel_id=1, source_target_pairs={{0,4},{4,0},{8,12},{12,8},{16,20},{20,16},{24,28},{28,24},{1,5},{5... | collective-permute-start | bytes 380936 | tf_op jit(solution)/shard_map/ppermute | solution.py:889
  81.8 13.4 %collective-permute-start.11 = (f32[248,128]{1,0:T(8,128)S(1)}, f32[248,128]{1,0:T(8,128)S(1)}, u32[]{:S(2)}, u32[]{:S(2)}) collective-permute-start(f32[248,128]{1,0:T(8,128)S(1)} %local_fields.1.refs_0_), channel_id=1, source_target_pairs={{0,8},{4,12},{8,0},{12,4},{16,24},{20,28},{24,16},{28,20},{1,9},{5... | collective-permute-start | bytes 380936 | tf_op jit(solution)/shard_map/ppermute | solution.py:889
  83.4 9.8 %collective-permute-start.13 = (f32[248,128]{1,0:T(8,128)S(1)}, f32[248,128]{1,0:T(8,128)S(1)}, u32[]{:S(2)}, u32[]{:S(2)}) collective-permute-start(f32[248,128]{1,0:T(8,128)S(1)} %local_fields.1.refs_0_), channel_id=1, source_target_pairs={{0,16},{4,20},{8,24},{12,28},{16,0},{20,4},{24,8},{28,12},{1,17},{... | collective-permute-start | bytes 380936 | tf_op jit(solution)/shard_map/ppermute | solution.py:889
  83.7 12.9 %collective-permute-start.12 = (f32[248,128]{1,0:T(8,128)S(1)}, f32[248,128]{1,0:T(8,128)S(1)}, u32[]{:S(2)}, u32[]{:S(2)}) collective-permute-start(f32[248,128]{1,0:T(8,128)S(1)} %local_fields.1.refs_0_), channel_id=1, source_target_pairs={{0,12},{4,8},{8,4},{12,0},{16,28},{20,24},{24,20},{28,16},{1,13},{... | collective-permute-start | bytes 380936 | tf_op jit(solution)/shard_map/ppermute | solution.py:889
  93.2 5.2 %collective-permute-start.15 = (f32[248,128]{1,0:T(8,128)S(1)}, f32[248,128]{1,0:T(8,128)S(1)}, u32[]{:S(2)}, u32[]{:S(2)}) collective-permute-start(f32[248,128]{1,0:T(8,128)S(1)} %collective-permute-done.13.refs_4_), channel_id=1, source_target_pairs={{0,4},{4,0},{8,12},{12,8},{16,20},{20,16},{24,28},{28,24},{1,5},{5... | collective-permute-start | bytes 380936 | tf_op jit(solution)/shard_map/ppermute | solution.py:897
  93.7 6.3 %collective-permute-start.16 = (f32[248,128]{1,0:T(8,128)S(1)}, f32[248,128]{1,0:T(8,128)S(1)}, u32[]{:S(2)}, u32[]{:S(2)}) collective-permute-start(f32[248,128]{1,0:T(8,128)S(1)} %collective-permute-done.13.refs_4_), channel_id=1, source_target_pairs={{0,8},{4,12},{8,0},{12,4},{16,24},{20,28},{24,16},{28,20},{1,9},{5... | collective-permute-start | bytes 380936 | tf_op jit(solution)/shard_map/ppermute | solution.py:897
  95.2 7.1 %collective-permute-start.17 = (f32[248,128]{1,0:T(8,128)S(1)}, f32[248,128]{1,0:T(8,128)S(1)}, u32[]{:S(2)}, u32[]{:S(2)}) collective-permute-start(f32[248,128]{1,0:T(8,128)S(1)} %collective-permute-done.13.refs_4_), channel_id=1, source_target_pairs={{0,12},{4,8},{8,4},{12,0},{16,28},{20,24},{24,20},{28,16},{1,13},{... | collective-permute-start | bytes 380936 | tf_op jit(solution)/shard_map/ppermute | solution.py:897
  106.8 0.8 copy-start.1
  107.6 10.4 %collective-permute-start.22 = (f32[4,1,512,128]{3,2,1,0:T(8,128)S(1)}, f32[4,1,512,128]{3,2,1,0:T(8,128)}, u32[]{:S(2)}, u32[]{:S(2)}) collective-permute-start(f32[4,1,512,128]{3,2,1,0:T(8,128)S(1)} %collective-permute-done.18.first_ref), channel_id=1, source_target_pairs={{0,1},{1,0},{2,3},{3,2},{4,5},{5,4},{6,7},{7,6},{8,9},{9,8},{10,11... | collective-permute-start | bytes 3145736 | tf_op jit(solution)/shard_map/ppermute | solution.py:916
  107.6 4.0 %collective-permute-start.19 = (f32[16,1024]{1,0:T(8,128)}, f32[16,1024]{1,0:T(8,128)}, u32[]{:S(2)}, u32[]{:S(2)}) collective-permute-start(f32[16,1024]{1,0:T(8,128)} %get-tuple-element.89), channel_id=1, source_target_pairs={{0,1},{1,2},{2,3},{3,0},{4,5},{5,6},{6,7},{7,4},{8,9},{9,10},{10,1... | collective-permute-start | bytes 196616 | tf_op jit(solution)/shard_map/ppermute | solution.py:917
  108.1 3.5 %collective-permute-start.20 = (f32[16,1024]{1,0:T(8,128)}, f32[16,1024]{1,0:T(8,128)}, u32[]{:S(2)}, u32[]{:S(2)}) collective-permute-start(f32[16,1024]{1,0:T(8,128)} %get-tuple-element.90), channel_id=1, source_target_pairs={{0,3},{1,0},{2,1},{3,2},{4,7},{5,4},{6,5},{7,6},{8,11},{9,8},{10,9... | collective-permute-start | bytes 196616 | tf_op jit(solution)/shard_map/ppermute | solution.py:918
  111.6 1.0 copy-start.2
  115.7 19.9 %collective-permute-start.21 = (f32[2,128]{1,0:T(2,128)S(1)}, f32[2,128]{1,0:T(2,128)S(1)}, u32[]{:S(2)}, u32[]{:S(2)}) collective-permute-start(f32[2,128]{1,0:T(2,128)S(1)} %get-tuple-element.92), channel_id=1, source_target_pairs={{0,1},{1,2},{2,3},{3,0},{4,5},{5,6},{6,7},{7,4},{8,9},{9,10},{10,1... | collective-permute-start | bytes 3080 | tf_op jit(solution)/shard_map/ppermute | solution.py:929
  116.4 19.2 %collective-permute-start.23 = (f32[2,128]{1,0:T(2,128)S(1)}, f32[2,128]{1,0:T(2,128)S(1)}, u32[]{:S(2)}, u32[]{:S(2)}) collective-permute-start(f32[2,128]{1,0:T(2,128)S(1)} %get-tuple-element.92), channel_id=1, source_target_pairs={{0,3},{1,0},{2,1},{3,2},{4,7},{5,4},{6,5},{7,6},{8,11},{9,8},{10,9... | collective-permute-start | bytes 3080 | tf_op jit(solution)/shard_map/ppermute | solution.py:929
  117.4 18.1 %collective-permute-start.24 = (f32[2,128]{1,0:T(2,128)S(1)}, f32[2,128]{1,0:T(2,128)S(1)}, u32[]{:S(2)}, u32[]{:S(2)}) collective-permute-start(f32[2,128]{1,0:T(2,128)S(1)} %get-tuple-element.92), channel_id=1, source_target_pairs={{0,2},{1,3},{2,0},{3,1},{4,6},{5,7},{6,4},{7,5},{8,10},{9,11},{10,... | collective-permute-start | bytes 3080 | tf_op jit(solution)/shard_map/ppermute | solution.py:929

commit v6 on v5

--- a/solution.py
+++ b/solution.py
@@ -369,62 +369,75 @@
     )(place, read, leaving, vel_index, cst)
 
 
-def carried_kernel(read_ref, index_ref, al_ref, *refs, blocks):
-    out_ref, mid, scale = refs[-3:]
+def carried_kernel(read_ref, index_ref, al_ref, *refs, blocks, start, count):
+    out_ref, source, ready, mid, scale, in_sems, out_sems = refs[-7:]
     ys = blocks * LANES // NZ
 
-    @pl.when(pl.program_id(0) == 0)
-    def _():
+    def fetch(g, x):
+        return pltpu.make_async_copy(read_ref.at[start + g, x], source.at[g, x], in_sems.at[g, x])
+
+    def store(g, x):
+        return pltpu.make_async_copy(ready.at[g, x], out_ref.at[start + g, x], out_sems.at[g, x])
+
+    for g in range(count):
         for x in range(SUB):
-            lane_copies(al_ref[x : x + 1, :], scale.at[x], blocks)
-        empty = jnp.zeros((ys * NZ, LANES), jnp.float32)
-        mid[0] = empty
-        mid[SUB + 1] = empty
-
-    upwind = Upwind(index_ref[...])
-
-    @pl.loop(0, SUB)
-    def _(x):
-        def run(first):
-            for j in range(RUN):
-                at = rows_of(first + j)
-                mid[x + 1, at, :] = scale[x, at, :] * read_ref[0, x, at, :]
-
-        each_run(ys, run)
-
-    @pl.loop(0, SUB)
-    def _(x):
-        def run(first):
-            for j, value in enumerate(upwind.stream(mid, x, first, ys)):
-                at = rows_of(first + j)
-                out_ref[0, x, at, :] = scale[x, at, :] * value
-
-        each_run(ys, run)
-
-
-def carried(read, vel_index, al, first, count, blocks, before=None):
+            fetch(g, x).start()
+    for x in range(SUB):
+        lane_copies(al_ref[x : x + 1, :], scale.at[x], blocks)
+    empty = jnp.zeros((ys * NZ, LANES), jnp.float32)
+    mid[0] = empty
+    mid[SUB + 1] = empty
+    for g in range(count):
+        upwind = Upwind(index_ref[:, (start + g) * LANES : (start + g + 1) * LANES])
+
+        @pl.loop(0, SUB)
+        def _(x, g=g):
+            fetch(g, x).wait()
+
+            def run(first):
+                for j in range(RUN):
+                    at = rows_of(first + j)
+                    mid[x + 1, at, :] = scale[x, at, :] * source[g, x, at, :]
+
+            each_run(ys, run)
+
+        @pl.loop(0, SUB)
+        def _(x, g=g, upwind=upwind):
+            def run(first):
+                for j, value in enumerate(upwind.stream(mid, x, first, ys)):
+                    at = rows_of(first + j)
+                    ready[g, x, at, :] = scale[x, at, :] * value
+
+            each_run(ys, run)
+            store(g, x).start()
+
+    for g in range(count):
+        for x in range(SUB):
+            store(g, x).wait()
+
+
+def carried(read, vel_index, al, first, vels, blocks, before=None):
     groups = read.shape[0]
     cells = blocks * LANES
-    start = first // LANES
-    block = pl.BlockSpec((1, SUB, cells, LANES), lambda i: (i + start, 0, 0, 0))
+    count = vels // LANES
+    anywhere = pl.BlockSpec(memory_space=pl.ANY)
+    vmem = pl.BlockSpec(memory_space=pltpu.VMEM)
     held = [] if before is None else [before]
     return pl.pallas_call(
-        functools.partial(carried_kernel, blocks=blocks),
-        grid=(count // LANES,),
-        in_specs=[
-            block,
-            pl.BlockSpec((3, LANES), lambda i: (0, i + start)),
-            pl.BlockSpec((SUB, cells), lambda i: (0, 0)),
-        ]
-        + [pl.BlockSpec(memory_space=pl.ANY)] * len(held),
-        out_specs=block,
+        functools.partial(carried_kernel, blocks=blocks, start=first // LANES, count=count),
+        in_specs=[anywhere, vmem, vmem] + [anywhere] * len(held),
+        out_specs=anywhere,
         out_shape=jax.ShapeDtypeStruct((groups, SUB, cells, LANES), jnp.float32),
         scratch_shapes=[
+            pltpu.VMEM((count, SUB, cells, LANES), jnp.float32),
+            pltpu.VMEM((count, SUB, cells, LANES), jnp.float32),
             pltpu.VMEM((SUB + 2, cells, LANES), jnp.float32),
             pltpu.VMEM((SUB, cells, LANES), jnp.float32),
+            pltpu.SemaphoreType.DMA((count, SUB)),
+            pltpu.SemaphoreType.DMA((count, SUB)),
         ],
         input_output_aliases={3: 0} if held else {},
-        compiler_params=pltpu.CompilerParams(vmem_limit_bytes=40 * MIB),
+        compiler_params=pltpu.CompilerParams(vmem_limit_bytes=44 * MIB),
         cost_estimate=pl.CostEstimate(flops=1, bytes_accessed=1, transcendentals=0),
         name="carried_part",
     )(read, vel_index, al, *held)

time: 137 us -> 135 us (0.985)
  Pallas kernels: 89.8 us -> 85.4 us
  waiting for transfers between devices: 13.2 us -> 15.5 us
    pallas_call x2, Pallas kernels: 22.1 us -> 17.6 us  [carried(): pl.pallas_call(functools.partial(carried_kernel, blocks=blocks, start=fir...]
    ppermute x3, waiting for transfers between devices: 2.05 us -> 4.31 us  [shards(): lax.ppermute(parts[k], 'vel', beside(k))]
  transfers between devices with their start and end apart: 25 -> 25, of which waited for: 7 -> 7; matrix products, arithmetic and copies ran while one was open for 1% -> 1% of each run, Pallas kernels for 66% -> 64%
where the time goes in v6:
time: 135 us; the launch traced here: 134 us
  Pallas kernels  85.4 us (63%)
  starting transfers between devices  24.8 us (18%)
  waiting for transfers between devices  15.5 us (11%)
  other arithmetic  5.07 us (4%)
  local copies, waits for them, and re-layouts  2.54 us (2%)
    pallas_call x1, Pallas kernels, first_stream(): pl.pallas_call(functools.partial(stream_kernel, vels=vels, blocks=blocks)...  21.7 us
    pallas_call x2, Pallas kernels, carried(): pl.pallas_call(functools.partial(carried_kernel, blocks=blocks, start=fir...  17.6 us
    pallas_call x1, Pallas kernels, finish(): pl.pallas_call(functools.partial(finish_kernel, blocks=blocks), grid=(gro...  17.5 us
    pallas_call x1, Pallas kernels, both_moments(): pl.pallas_call(functools.partial(moments_kernel, vels=vels, blocks=blocks...  12.1 us
    pallas_call x5, Pallas kernels, small_call(): pl.pallas_call(kernel, in_specs=[smem if s == 's' else vmem for s in spec...  8.49 us
    pallas_call x1, Pallas kernels, inflow_near(): pl.pallas_call(functools.partial(near_kernel, blocks=blocks), grid=(vels...  7.9 us
    ppermute x3, waiting for transfers between devices, shards(): lax.ppermute(pieces[blocks // 2], 'vel', beside(k))  5.61 us
    ppermute x3, waiting for transfers between devices, shards(): lax.ppermute(parts[k], 'vel', beside(k))  4.31 us
  transfers between devices with their start and end apart: 25, of which 7 were waited for; matrix products, arithmetic and copies ran while one was open for 1% of the time, Pallas kernels for 64%

profile of v6, /device:TPU:0, one launch (start us, length us, event | category | flops | bytes accessed | tf_op | source)
XLA Modules:
  0.0 134.1 jit_solution(1996516781955225592)
XLA Ops:
  0.6 0.8 subtract_select_fusion
  1.4 0.8 select_bitcast_fusion.1
  2.2 0.5 collective-permute-start
  2.7 2.0 %collective-permute-start.1 = (f32[3,1,1024]{2,1,0:T(1,128)S(1)}, f32[3,1,1024]{2,1,0:T(1,128)S(1)}, u32[]{:S(2)}, u32[]{:S(2)}) collective-permute-start(f32[3,1,1024]{2,1,0:T(1,128)S(1)} %get-tuple-element.107), channel_id=1, source_target_pairs={{0,3},{1,0},{2,1},{3,2},{4,7},{5,4},{6,5},{7,6},{8,11},{9,8},{10,9... | collective-permute-start | bytes 36872 | tf_op jit(solution)/shard_map/ppermute | solution.py:851
  4.7 21.7 %first_stream.1 = (f32[4,2,1024,128]{3,2,1,0:T(8,128)}, f32[4,8,1024,128]{3,2,1,0:T(8,128)}) custom-call(f32[512,64,128]{2,1,0:T(8,128)} %bitcast.22, s32[3,512]{1,0:T(4,128)} %index_ref.11), custom_call_target="tpu_custom_call" | custom-call | flops 83886080 | bytes 33554432 | tf_op jit(solution)/shard_map/first_stream/pallas_call | solution.py:227
  26.4 0.7 collective-permute-start.2
  27.1 0.7 compare_reduce_fusion
  27.9 0.8 pad_maximum_fusion.cst_ref
  28.6 12.1 %moments_of_both.1 = (f32[576,128]{1,0:T(8,128)}, f32[576,128]{1,0:T(8,128)}, f32[576,128]{1,0:T(8,128)}, f32[576,128]{1,0:T(8,128)}) custom-call(s32[1]{0:T(128)} %bitcast.me_ref.place_ref, f32[4,8,1024,128]{3,2,1,0:T(8,128)} %get-tuple-element.57.read_ref, f32[4,2,1024,128]{3,2,1,0:T(8,128)} %get-tuple-element.56.leaving_ref, s32[3,512]{1,0:T(4,128)} %index_ref.11, ...), custom_call_target="tpu_custom_call" | custom-call | flops 3523215360 | bytes 20971520 | tf_op jit(solution)/shard_map/moments_of_both/pallas_call | solution.py:351
  40.8 1.9 %dynamic-slice_select_fusion = f32[4,2,512,128]{3,2,1,0:T(8,128)S(1)} fusion(f32[4,2,1024,128]{3,2,1,0:T(8,128)} %collective-permute-done.2.swap_ref, s32[]{:T(128)S(6)} %select_n.135, f32[4,2,1024,128]{3,2,1,0:T(8,128)S(1)} %copy-done.6, pred[4,128]{1,0:T(4,128)(4,1)S(1)} %bitcast.24), kind=kLoop, calls=%fused_computation | loop fusion | flops 524288 | bytes 6291972 | tf_op jit(solution)/shard_map/jit(_where)/select_n | solution.py:868
  42.7 0.1 fusion.3
  42.9 1.7 %collective-permute-start.7 = (f32[4,1,512,128]{3,2,1,0:T(8,128)S(1)}, f32[4,1,512,128]{3,2,1,0:T(8,128)S(1)}, u32[]{:S(2)}, u32[]{:S(2)}) collective-permute-start(f32[4,1,512,128]{3,2,1,0:T(8,128)S(1)} %get-tuple-element.106), channel_id=1, source_target_pairs={{0,2},{1,3},{2,0},{3,1},{4,6},{5,7},{6,4},{7,5},{8,10},{9,11},{10,... | collective-permute-start | bytes 3145736 | tf_op jit(solution)/shard_map/ppermute | solution.py:871
  44.6 1.5 %collective-permute-start.3 = (f32[576,128]{1,0:T(8,128)S(1)}, f32[576,128]{1,0:T(8,128)S(1)}, u32[]{:S(2)}, u32[]{:S(2)}) collective-permute-start(f32[576,128]{1,0:T(8,128)S(1)} %copy-done.9), channel_id=1, source_target_pairs={{0,4},{4,0},{8,12},{12,8},{16,20},{20,16},{24,28},{28,24},{1,5},{5... | collective-permute-start | bytes 884744 | tf_op jit(solution)/shard_map/ppermute | solution.py:878
  46.1 1.6 %collective-permute-start.4 = (f32[576,128]{1,0:T(8,128)S(1)}, f32[576,128]{1,0:T(8,128)S(1)}, u32[]{:S(2)}, u32[]{:S(2)}) collective-permute-start(f32[576,128]{1,0:T(8,128)S(1)} %copy-done.8), channel_id=1, source_target_pairs={{0,8},{4,12},{8,0},{12,4},{16,24},{20,28},{24,16},{28,20},{1,9},{5... | collective-permute-start | bytes 884744 | tf_op jit(solution)/shard_map/ppermute | solution.py:878
  47.7 0.4 collective-permute-start.5
  48.1 8.8 %carried_part.2.refs_0_ = f32[4,8,1024,128]{3,2,1,0:T(8,128)} custom-call(f32[4,8,1024,128]{3,2,1,0:T(8,128)} %get-tuple-element.57.read_ref, s32[3,512]{1,0:T(4,128)S(1)} %copy-done.3, f32[8,1024]{1,0:T(8,128)S(1)} %get-tuple-element.74.al_ref), custom_call_target="tpu_custom_call" | custom-call | flops 1 | bytes 1 | tf_op jit(solution)/shard_map/carried_part/pallas_call | solution.py:426
  56.9 4.3 %collective-permute-done.5.refs_3_ = f32[576,128]{1,0:T(8,128)S(1)} collective-permute-done((f32[576,128]{1,0:T(8,128)S(1)}, f32[576,128]{1,0:T(8,128)S(1)}, u32[]{:S(2)}, u32[]{:S(2)}) %collective-permute-start.5) | collective-permute-done | bytes 294944 | tf_op jit(solution)/shard_map/ppermute | solution.py:878
  61.3 2.7 %collective-permute-start.6 = (f32[288,128]{1,0:T(8,128)S(1)}, f32[288,128]{1,0:T(8,128)S(1)}, u32[]{:S(2)}, u32[]{:S(2)}) collective-permute-start(f32[288,128]{1,0:T(8,128)S(1)} %get-tuple-element.73), channel_id=1, source_target_pairs={{0,16},{4,20},{8,24},{12,28},{16,0},{20,4},{24,8},{28,12},{1,17},{... | collective-permute-start | bytes 442376 | tf_op jit(solution)/shard_map/ppermute | solution.py:882
  63.9 8.9 %carried_part.3.carried_ref = f32[4,8,1024,128]{3,2,1,0:T(8,128)} custom-call(f32[4,8,1024,128]{3,2,1,0:T(8,128)} %get-tuple-element.57.read_ref, s32[3,512]{1,0:T(4,128)S(1)} %copy-done.3, f32[8,1024]{1,0:T(8,128)S(1)} %get-tuple-element.74.al_ref, f32[4,8,1024,128]{3,2,1,0:T(8,128)} %carried_part.2.refs_0_), custom_call_target="tpu_custom_call", output_to_operand_aliasing={{}: (3, {})} | custom-call | flops 1 | bytes 1 | tf_op jit(solution)/shard_map/carried_part/pallas_call | solution.py:426
  72.9 0.5 collective-permute-start.8
  73.4 1.3 collective-permute-start.9
  74.7 2.0 %collective-permute-done.8.low_ref = f32[144,128]{1,0:T(8,128)S(1)} collective-permute-done((f32[144,128]{1,0:T(8,128)S(1)}, f32[144,128]{1,0:T(8,128)S(1)}, u32[]{:S(2)}, u32[]{:S(2)}) %collective-permute-start.8) | collective-permute-done | bytes 73760 | tf_op jit(solution)/shard_map/ppermute | solution.py:897
  76.8 0.8 local_fields.1.refs_0_
  77.6 0.6 collective-permute-start.18
  78.2 1.5 %collective-permute-start.10 = (f32[248,128]{1,0:T(8,128)S(1)}, f32[248,128]{1,0:T(8,128)S(1)}, u32[]{:S(2)}, u32[]{:S(2)}) collective-permute-start(f32[248,128]{1,0:T(8,128)S(1)} %local_fields.1.refs_0_), channel_id=1, source_target_pairs={{0,4},{4,0},{8,12},{12,8},{16,20},{20,16},{24,28},{28,24},{1,5},{5... | collective-permute-start | bytes 380936 | tf_op jit(solution)/shard_map/ppermute | solution.py:902
  79.7 1.6 %collective-permute-start.11 = (f32[248,128]{1,0:T(8,128)S(1)}, f32[248,128]{1,0:T(8,128)S(1)}, u32[]{:S(2)}, u32[]{:S(2)}) collective-permute-start(f32[248,128]{1,0:T(8,128)S(1)} %local_fields.1.refs_0_), channel_id=1, source_target_pairs={{0,8},{4,12},{8,0},{12,4},{16,24},{20,28},{24,16},{28,20},{1,9},{5... | collective-permute-start | bytes 380936 | tf_op jit(solution)/shard_map/ppermute | solution.py:902
  81.3 0.3 collective-permute-start.13
  81.6 0.3 collective-permute-start.12
  81.9 7.9 %inflow_near.1.inflow_ref = f32[4,3,1024,128]{3,2,1,0:T(8,128)} custom-call(s32[1]{0:T(128)} %bitcast.7.core_ref, f32[4,2,1024,128]{3,2,1,0:T(8,128)} %collective-permute-done.2.swap_ref, f32[4,1,512,128]{3,2,1,0:T(8,128)S(1)} %collective-permute-done.7.first_ref, f32[4,1,512,128]{3,2,1,0:T(8,128)S(1)} %collective-permute-done.14.second_ref, ...), custom_call_target="tpu_custom_call" | custom-call | flops 1 | bytes 1 | tf_op jit(solution)/shard_map/inflow_near/pallas_call | solution.py:512
  89.8 1.2 collective-permute-done.13.refs_4_
  91.1 0.5 collective-permute-start.15
  91.6 1.5 %collective-permute-start.16 = (f32[248,128]{1,0:T(8,128)S(1)}, f32[248,128]{1,0:T(8,128)S(1)}, u32[]{:S(2)}, u32[]{:S(2)}) collective-permute-start(f32[248,128]{1,0:T(8,128)S(1)} %collective-permute-done.13.refs_4_), channel_id=1, source_target_pairs={{0,8},{4,12},{8,0},{12,4},{16,24},{20,28},{24,16},{28,20},{1,9},{5... | collective-permute-start | bytes 380936 | tf_op jit(solution)/shard_map/ppermute | solution.py:910
  93.1 1.5 %collective-permute-start.17 = (f32[248,128]{1,0:T(8,128)S(1)}, f32[248,128]{1,0:T(8,128)S(1)}, u32[]{:S(2)}, u32[]{:S(2)}) collective-permute-start(f32[248,128]{1,0:T(8,128)S(1)} %collective-permute-done.13.refs_4_), channel_id=1, source_target_pairs={{0,12},{4,8},{8,4},{12,0},{16,28},{20,24},{24,20},{28,16},{1,13},{... | collective-permute-start | bytes 380936 | tf_op jit(solution)/shard_map/ppermute | solution.py:910
  94.6 1.7 %collective-permute-done.15.refs_5_ = f32[248,128]{1,0:T(8,128)S(1)} collective-permute-done((f32[248,128]{1,0:T(8,128)S(1)}, f32[248,128]{1,0:T(8,128)S(1)}, u32[]{:S(2)}, u32[]{:S(2)}) %collective-permute-start.15) | collective-permute-done | bytes 127008 | tf_op jit(solution)/shard_map/ppermute | solution.py:910
  96.3 1.6 %collective-permute-done.16.refs_6_ = f32[248,128]{1,0:T(8,128)S(1)} collective-permute-done((f32[248,128]{1,0:T(8,128)S(1)}, f32[248,128]{1,0:T(8,128)S(1)}, u32[]{:S(2)}, u32[]{:S(2)}) %collective-permute-start.16) | collective-permute-done | bytes 127008 | tf_op jit(solution)/shard_map/ppermute | solution.py:910
  97.9 2.3 %collective-permute-done.17.refs_7_ = f32[248,128]{1,0:T(8,128)S(1)} collective-permute-done((f32[248,128]{1,0:T(8,128)S(1)}, f32[248,128]{1,0:T(8,128)S(1)}, u32[]{:S(2)}, u32[]{:S(2)}) %collective-permute-start.17) | collective-permute-done | bytes 127008 | tf_op jit(solution)/shard_map/ppermute | solution.py:910
  100.2 4.5 %first_fields.1 = (f32[8,448,128]{2,1,0:T(8,128)S(1)}, f32[104,1024]{1,0:T(8,128)S(1)}, f32[104,1024]{1,0:T(8,128)S(1)}, f32[16,1024]{1,0:T(8,128)}, f32[16,1024]{1,0:T(8,128)}, /*index=5*/f32[8,128]{1,0:T(8,128)S(1)}) custom-call(s32[1]{0:T(128)} %bitcast.me_ref.place_ref, f32[13,13]{1,0:T(8,128)S(1)} %copy-done.5, f32[3,16,1024]{2,1,0:T(8,128)S(1)} %copy-done, ...), custom_call_target="tpu_custom_call" | custom-call | tf_op jit(solution)/shard_map/first_fields/pallas_call | solution.py:532
  104.7 0.8 copy-done.1
  105.5 0.5 collective-permute-start.19
  106.0 1.2 collective-permute-start.20
  107.2 2.3 %collective-permute-done.19.low_ref = f32[16,1024]{1,0:T(8,128)} collective-permute-done((f32[16,1024]{1,0:T(8,128)}, f32[16,1024]{1,0:T(8,128)}, u32[]{:S(2)}, u32[]{:S(2)}) %collective-permute-start.19) | collective-permute-done | bytes 65568 | tf_op jit(solution)/shard_map/ppermute | solution.py:930
  109.5 1.0 copy-done.2
  110.5 3.1 %last_fields.1 = (f32[8,64,128]{2,1,0:T(8,128)S(1)}, f32[13,8,128]{2,1,0:T(8,128)}, f32[2,128]{1,0:T(2,128)S(1)}) custom-call(s32[1]{0:T(128)} %bitcast.me_ref.place_ref, f32[3,16,1024]{2,1,0:T(8,128)S(1)} %copy-done, f32[104,1024]{1,0:T(8,128)S(1)} %get-tuple-element.85.later_ref, f32[104,1024]{1,0:T(8,128)S(1)} %copy-done.2, ...), custom_call_target="tpu_custom_call" | custom-call | tf_op jit(solution)/shard_map/last_fields/pallas_call | solution.py:532
  113.6 0.7 collective-permute-start.21
  114.3 1.1 collective-permute-start.23
  115.3 0.6 collective-permute-start.24
  115.9 17.5 %finish_dist.1 = f32[512,64,128]{2,1,0:T(8,128)} custom-call(s32[1]{0:T(128)} %bitcast.7.core_ref, f32[4,8,1024,128]{3,2,1,0:T(8,128)} %carried_part.3.carried_ref, f32[4,3,1024,128]{3,2,1,0:T(8,128)} %inflow_near.1.inflow_ref, f32[4,2,1024,128]{3,2,1,0:T(8,128)} %collective-permute-done.2.swap_ref, ...), custom_call_target="tpu_custom_call" | custom-call | flops 2147483648 | bytes 33554432 | tf_op jit(solution)/shard_map/finish_dist/pallas_call | solution.py:791
  133.6 0.5 sqrt.3
  (45 shorter events, 0.5 us)
Async XLA Ops:
  2.2 24.2 %collective-permute-start = (f32[3,1,1024]{2,1,0:T(1,128)S(1)}, f32[3,1,1024]{2,1,0:T(1,128)S(1)}, u32[]{:S(2)}, u32[]{:S(2)}) collective-permute-start(f32[3,1,1024]{2,1,0:T(1,128)S(1)} %get-tuple-element.108), channel_id=1, source_target_pairs={{0,1},{1,2},{2,3},{3,0},{4,5},{5,6},{6,7},{7,4},{8,9},{9,10},{10,1... | collective-permute-start | bytes 36872 | tf_op jit(solution)/shard_map/ppermute | solution.py:850
  2.7 23.7 %collective-permute-start.1 = (f32[3,1,1024]{2,1,0:T(1,128)S(1)}, f32[3,1,1024]{2,1,0:T(1,128)S(1)}, u32[]{:S(2)}, u32[]{:S(2)}) collective-permute-start(f32[3,1,1024]{2,1,0:T(1,128)S(1)} %get-tuple-element.107), channel_id=1, source_target_pairs={{0,3},{1,0},{2,1},{3,2},{4,7},{5,4},{6,5},{7,6},{8,11},{9,8},{10,9... | collective-permute-start | bytes 36872 | tf_op jit(solution)/shard_map/ppermute | solution.py:851
  26.4 14.4 %collective-permute-start.2 = (f32[4,2,1024,128]{3,2,1,0:T(8,128)}, f32[4,2,1024,128]{3,2,1,0:T(8,128)}, u32[]{:S(2)}, u32[]{:S(2)}) collective-permute-start(f32[4,2,1024,128]{3,2,1,0:T(8,128)} %get-tuple-element.56.leaving_ref), channel_id=1, source_target_pairs={{0,1},{1,0},{2,3},{3,2},{4,5},{5,4},{6,7},{7,6},{8,9},{9,8},{10,11... | collective-permute-start | bytes 12582920 | tf_op jit(solution)/shard_map/ppermute | solution.py:855
  28.6 12.1 %copy-start.6 = (f32[4,2,1024,128]{3,2,1,0:T(8,128)S(1)}, f32[4,2,1024,128]{3,2,1,0:T(8,128)}, u32[]{:S(2)}) copy-start(f32[4,2,1024,128]{3,2,1,0:T(8,128)} %get-tuple-element.56.leaving_ref) | copy-start | bytes 12582916
  40.8 3.8 %copy-start.9 = (f32[576,128]{1,0:T(8,128)S(1)}, f32[576,128]{1,0:T(8,128)}, u32[]{:S(2)}) copy-start(f32[576,128]{1,0:T(8,128)} %get-tuple-element.68) | copy-start | bytes 884740
  40.8 5.3 %copy-start.8 = (f32[576,128]{1,0:T(8,128)S(1)}, f32[576,128]{1,0:T(8,128)}, u32[]{:S(2)}) copy-start(f32[576,128]{1,0:T(8,128)} %get-tuple-element.70) | copy-start | bytes 884740
  40.8 6.9 %copy-start.7 = (f32[576,128]{1,0:T(8,128)S(1)}, f32[576,128]{1,0:T(8,128)}, u32[]{:S(2)}) copy-start(f32[576,128]{1,0:T(8,128)} %get-tuple-element.71) | copy-start | bytes 884740
  40.8 7.3 %copy-start.3 = (s32[3,512]{1,0:T(4,128)S(1)}, s32[3,512]{1,0:T(4,128)}, u32[]{:S(2)}) copy-start(s32[3,512]{1,0:T(4,128)} %index_ref.11) | copy-start | bytes 18436
  42.9 18.4 %copy-start.4 = (f32[576,128]{1,0:T(8,128)S(1)}, f32[576,128]{1,0:T(8,128)}, u32[]{:S(2)}) copy-start(f32[576,128]{1,0:T(8,128)} %get-tuple-element.67.refs_0_) | copy-start | bytes 884740
  42.9 30.0 %collective-permute-start.7 = (f32[4,1,512,128]{3,2,1,0:T(8,128)S(1)}, f32[4,1,512,128]{3,2,1,0:T(8,128)S(1)}, u32[]{:S(2)}, u32[]{:S(2)}) collective-permute-start(f32[4,1,512,128]{3,2,1,0:T(8,128)S(1)} %get-tuple-element.106), channel_id=1, source_target_pairs={{0,2},{1,3},{2,0},{3,1},{4,6},{5,7},{6,4},{7,5},{8,10},{9,11},{10,... | collective-permute-start | bytes 3145736 | tf_op jit(solution)/shard_map/ppermute | solution.py:871
  44.6 12.3 %collective-permute-start.3 = (f32[576,128]{1,0:T(8,128)S(1)}, f32[576,128]{1,0:T(8,128)S(1)}, u32[]{:S(2)}, u32[]{:S(2)}) collective-permute-start(f32[576,128]{1,0:T(8,128)S(1)} %copy-done.9), channel_id=1, source_target_pairs={{0,4},{4,0},{8,12},{12,8},{16,20},{20,16},{24,28},{28,24},{1,5},{5... | collective-permute-start | bytes 884744 | tf_op jit(solution)/shard_map/ppermute | solution.py:878
  46.1 10.8 %collective-permute-start.4 = (f32[576,128]{1,0:T(8,128)S(1)}, f32[576,128]{1,0:T(8,128)S(1)}, u32[]{:S(2)}, u32[]{:S(2)}) collective-permute-start(f32[576,128]{1,0:T(8,128)S(1)} %copy-done.8), channel_id=1, source_target_pairs={{0,8},{4,12},{8,0},{12,4},{16,24},{20,28},{24,16},{28,20},{1,9},{5... | collective-permute-start | bytes 884744 | tf_op jit(solution)/shard_map/ppermute | solution.py:878
  47.7 13.5 %collective-permute-start.5 = (f32[576,128]{1,0:T(8,128)S(1)}, f32[576,128]{1,0:T(8,128)S(1)}, u32[]{:S(2)}, u32[]{:S(2)}) collective-permute-start(f32[576,128]{1,0:T(8,128)S(1)} %copy-done.7), channel_id=1, source_target_pairs={{0,12},{4,8},{8,4},{12,0},{16,28},{20,24},{24,20},{28,16},{1,13},{... | collective-permute-start | bytes 884744 | tf_op jit(solution)/shard_map/ppermute | solution.py:878
  61.3 11.5 %collective-permute-start.6 = (f32[288,128]{1,0:T(8,128)S(1)}, f32[288,128]{1,0:T(8,128)S(1)}, u32[]{:S(2)}, u32[]{:S(2)}) collective-permute-start(f32[288,128]{1,0:T(8,128)S(1)} %get-tuple-element.73), channel_id=1, source_target_pairs={{0,16},{4,20},{8,24},{12,28},{16,0},{20,4},{24,8},{28,12},{1,17},{... | collective-permute-start | bytes 442376 | tf_op jit(solution)/shard_map/ppermute | solution.py:882
  63.9 12.8 %copy-start.5 = (f32[13,13]{1,0:T(8,128)S(1)}, f32[13,13]{1,0:T(8,128)}, u32[]{:S(2)}) copy-start(f32[13,13]{1,0:T(8,128)} %inv_ref.3) | copy-start | bytes 2032
  63.9 17.7 %copy-start = (f32[3,16,1024]{2,1,0:T(8,128)S(1)}, f32[3,16,1024]{2,1,0:T(8,128)}, u32[]{:S(2)}) copy-start(f32[3,16,1024]{2,1,0:T(8,128)} %pad_maximum_fusion.cst_ref) | copy-start | bytes 589828
  72.9 8.8 %collective-permute-start.14 = (f32[4,1,512,128]{3,2,1,0:T(8,128)S(1)}, f32[4,1,512,128]{3,2,1,0:T(8,128)S(1)}, u32[]{:S(2)}, u32[]{:S(2)}) collective-permute-start(f32[4,1,512,128]{3,2,1,0:T(8,128)S(1)} %collective-permute-done.7.first_ref), channel_id=1, source_target_pairs={{0,1},{1,0},{2,3},{3,2},{4,5},{5,4},{6,7},{7,6},{8,9},{9,8},{10,11... | collective-permute-start | bytes 3145736 | tf_op jit(solution)/shard_map/ppermute | solution.py:906
  72.9 3.8 %collective-permute-start.8 = (f32[144,128]{1,0:T(8,128)S(1)}, f32[144,128]{1,0:T(8,128)S(1)}, u32[]{:S(2)}, u32[]{:S(2)}) collective-permute-start(f32[144,128]{1,0:T(8,128)S(1)} %get-tuple-element.81), channel_id=1, source_target_pairs={{0,1},{1,2},{2,3},{3,0},{4,5},{5,6},{6,7},{7,4},{8,9},{9,10},{10,1... | collective-permute-start | bytes 221192 | tf_op jit(solution)/shard_map/ppermute | solution.py:897
  73.4 3.3 %collective-permute-start.9 = (f32[144,128]{1,0:T(8,128)S(1)}, f32[144,128]{1,0:T(8,128)S(1)}, u32[]{:S(2)}, u32[]{:S(2)}) collective-permute-start(f32[144,128]{1,0:T(8,128)S(1)} %get-tuple-element.82), channel_id=1, source_target_pairs={{0,3},{1,0},{2,1},{3,2},{4,7},{5,4},{6,5},{7,6},{8,11},{9,8},{10,9... | collective-permute-start | bytes 221192 | tf_op jit(solution)/shard_map/ppermute | solution.py:898
  77.6 27.9 %collective-permute-start.18 = (f32[4,1,512,128]{3,2,1,0:T(8,128)S(1)}, f32[4,1,512,128]{3,2,1,0:T(8,128)S(1)}, u32[]{:S(2)}, u32[]{:S(2)}) collective-permute-start(f32[4,1,512,128]{3,2,1,0:T(8,128)S(1)} %get-tuple-element.87), channel_id=1, source_target_pairs={{0,2},{1,3},{2,0},{3,1},{4,6},{5,7},{6,4},{7,5},{8,10},{9,11},{10,... | collective-permute-start | bytes 3145736 | tf_op jit(solution)/shard_map/ppermute | solution.py:904
  78.2 13.4 %collective-permute-start.10 = (f32[248,128]{1,0:T(8,128)S(1)}, f32[248,128]{1,0:T(8,128)S(1)}, u32[]{:S(2)}, u32[]{:S(2)}) collective-permute-start(f32[248,128]{1,0:T(8,128)S(1)} %local_fields.1.refs_0_), channel_id=1, source_target_pairs={{0,4},{4,0},{8,12},{12,8},{16,20},{20,16},{24,28},{28,24},{1,5},{5... | collective-permute-start | bytes 380936 | tf_op jit(solution)/shard_map/ppermute | solution.py:902
  79.7 13.4 %collective-permute-start.11 = (f32[248,128]{1,0:T(8,128)S(1)}, f32[248,128]{1,0:T(8,128)S(1)}, u32[]{:S(2)}, u32[]{:S(2)}) collective-permute-start(f32[248,128]{1,0:T(8,128)S(1)} %local_fields.1.refs_0_), channel_id=1, source_target_pairs={{0,8},{4,12},{8,0},{12,4},{16,24},{20,28},{24,16},{28,20},{1,9},{5... | collective-permute-start | bytes 380936 | tf_op jit(solution)/shard_map/ppermute | solution.py:902
  81.3 9.8 %collective-permute-start.13 = (f32[248,128]{1,0:T(8,128)S(1)}, f32[248,128]{1,0:T(8,128)S(1)}, u32[]{:S(2)}, u32[]{:S(2)}) collective-permute-start(f32[248,128]{1,0:T(8,128)S(1)} %local_fields.1.refs_0_), channel_id=1, source_target_pairs={{0,16},{4,20},{8,24},{12,28},{16,0},{20,4},{24,8},{28,12},{1,17},{... | collective-permute-start | bytes 380936 | tf_op jit(solution)/shard_map/ppermute | solution.py:902
  81.6 12.9 %collective-permute-start.12 = (f32[248,128]{1,0:T(8,128)S(1)}, f32[248,128]{1,0:T(8,128)S(1)}, u32[]{:S(2)}, u32[]{:S(2)}) collective-permute-start(f32[248,128]{1,0:T(8,128)S(1)} %local_fields.1.refs_0_), channel_id=1, source_target_pairs={{0,12},{4,8},{8,4},{12,0},{16,28},{20,24},{24,20},{28,16},{1,13},{... | collective-permute-start | bytes 380936 | tf_op jit(solution)/shard_map/ppermute | solution.py:902
  91.1 5.2 %collective-permute-start.15 = (f32[248,128]{1,0:T(8,128)S(1)}, f32[248,128]{1,0:T(8,128)S(1)}, u32[]{:S(2)}, u32[]{:S(2)}) collective-permute-start(f32[248,128]{1,0:T(8,128)S(1)} %collective-permute-done.13.refs_4_), channel_id=1, source_target_pairs={{0,4},{4,0},{8,12},{12,8},{16,20},{20,16},{24,28},{28,24},{1,5},{5... | collective-permute-start | bytes 380936 | tf_op jit(solution)/shard_map/ppermute | solution.py:910
  91.6 6.3 %collective-permute-start.16 = (f32[248,128]{1,0:T(8,128)S(1)}, f32[248,128]{1,0:T(8,128)S(1)}, u32[]{:S(2)}, u32[]{:S(2)}) collective-permute-start(f32[248,128]{1,0:T(8,128)S(1)} %collective-permute-done.13.refs_4_), channel_id=1, source_target_pairs={{0,8},{4,12},{8,0},{12,4},{16,24},{20,28},{24,16},{28,20},{1,9},{5... | collective-permute-start | bytes 380936 | tf_op jit(solution)/shard_map/ppermute | solution.py:910
  93.1 7.1 %collective-permute-start.17 = (f32[248,128]{1,0:T(8,128)S(1)}, f32[248,128]{1,0:T(8,128)S(1)}, u32[]{:S(2)}, u32[]{:S(2)}) collective-permute-start(f32[248,128]{1,0:T(8,128)S(1)} %collective-permute-done.13.refs_4_), channel_id=1, source_target_pairs={{0,12},{4,8},{8,4},{12,0},{16,28},{20,24},{24,20},{28,16},{1,13},{... | collective-permute-start | bytes 380936 | tf_op jit(solution)/shard_map/ppermute | solution.py:910
  104.7 0.8 copy-start.1
  105.5 10.4 %collective-permute-start.22 = (f32[4,1,512,128]{3,2,1,0:T(8,128)S(1)}, f32[4,1,512,128]{3,2,1,0:T(8,128)}, u32[]{:S(2)}, u32[]{:S(2)}) collective-permute-start(f32[4,1,512,128]{3,2,1,0:T(8,128)S(1)} %collective-permute-done.18.first_ref), channel_id=1, source_target_pairs={{0,1},{1,0},{2,3},{3,2},{4,5},{5,4},{6,7},{7,6},{8,9},{9,8},{10,11... | collective-permute-start | bytes 3145736 | tf_op jit(solution)/shard_map/ppermute | solution.py:929
  105.5 4.0 %collective-permute-start.19 = (f32[16,1024]{1,0:T(8,128)}, f32[16,1024]{1,0:T(8,128)}, u32[]{:S(2)}, u32[]{:S(2)}) collective-permute-start(f32[16,1024]{1,0:T(8,128)} %get-tuple-element.89), channel_id=1, source_target_pairs={{0,1},{1,2},{2,3},{3,0},{4,5},{5,6},{6,7},{7,4},{8,9},{9,10},{10,1... | collective-permute-start | bytes 196616 | tf_op jit(solution)/shard_map/ppermute | solution.py:930
  106.0 3.5 %collective-permute-start.20 = (f32[16,1024]{1,0:T(8,128)}, f32[16,1024]{1,0:T(8,128)}, u32[]{:S(2)}, u32[]{:S(2)}) collective-permute-start(f32[16,1024]{1,0:T(8,128)} %get-tuple-element.90), channel_id=1, source_target_pairs={{0,3},{1,0},{2,1},{3,2},{4,7},{5,4},{6,5},{7,6},{8,11},{9,8},{10,9... | collective-permute-start | bytes 196616 | tf_op jit(solution)/shard_map/ppermute | solution.py:931
  109.5 1.0 copy-start.2
  113.6 19.9 %collective-permute-start.21 = (f32[2,128]{1,0:T(2,128)S(1)}, f32[2,128]{1,0:T(2,128)S(1)}, u32[]{:S(2)}, u32[]{:S(2)}) collective-permute-start(f32[2,128]{1,0:T(2,128)S(1)} %get-tuple-element.92), channel_id=1, source_target_pairs={{0,1},{1,2},{2,3},{3,0},{4,5},{5,6},{6,7},{7,4},{8,9},{9,10},{10,1... | collective-permute-start | bytes 3080 | tf_op jit(solution)/shard_map/ppermute | solution.py:942
  114.3 19.2 %collective-permute-start.23 = (f32[2,128]{1,0:T(2,128)S(1)}, f32[2,128]{1,0:T(2,128)S(1)}, u32[]{:S(2)}, u32[]{:S(2)}) collective-permute-start(f32[2,128]{1,0:T(2,128)S(1)} %get-tuple-element.92), channel_id=1, source_target_pairs={{0,3},{1,0},{2,1},{3,2},{4,7},{5,4},{6,5},{7,6},{8,11},{9,8},{10,9... | collective-permute-start | bytes 3080 | tf_op jit(solution)/shard_map/ppermute | solution.py:942
  115.3 18.1 %collective-permute-start.24 = (f32[2,128]{1,0:T(2,128)S(1)}, f32[2,128]{1,0:T(2,128)S(1)}, u32[]{:S(2)}, u32[]{:S(2)}) collective-permute-start(f32[2,128]{1,0:T(2,128)S(1)} %get-tuple-element.92), channel_id=1, source_target_pairs={{0,2},{1,3},{2,0},{3,1},{4,6},{5,7},{6,4},{7,5},{8,10},{9,11},{10,... | collective-permute-start | bytes 3080 | tf_op jit(solution)/shard_map/ppermute | solution.py:942

commit v7 on v6

--- a/solution.py
+++ b/solution.py
@@ -873,7 +873,8 @@
     def beside(step):
         return [(i, (i // sub ^ step) * sub + i % sub) for i in range(peers)]
 
-    spans = [(0, vels)] if vels < 2 * LANES else [(0, vels // 2), (vels // 2, vels - vels // 2)]
+    most = vels // LANES * 3 // 4 * LANES
+    spans = [(0, vels)] if vels < 2 * LANES else [(0, most), (most, vels - most)]
 
     got = [parts[0]] + [lax.ppermute(parts[k], "vel", beside(k)) for k in range(1, blocks // 2)]
     carried_part = carried(read, vel_index, coefficients[0], *spans[0], blocks)

time: 135 us -> 134 us (level)
  waiting for transfers between devices: 15.5 us -> 11.3 us
  starting transfers between devices: 24.8 us -> 27 us
    ppermute x3, waiting for transfers between devices: 4.31 us -> 0.71 us  [shards(): lax.ppermute(parts[k], 'vel', beside(k))]
    ppermute x4, starting transfers between devices: 3.74 us -> 5.46 us  [shards(): lax.ppermute(send, 'vel', beside(k))]
  transfers between devices with their start and end apart: 25 -> 25, of which waited for: 7 -> 6; matrix products, arithmetic and copies ran while one was open for 1% -> 1% of each run, Pallas kernels for 64% -> 65%
where the time goes in v7:
time: 134 us; the launch traced here: 133 us
  Pallas kernels  86.5 us (65%)
  starting transfers between devices  27 us (20%)
  waiting for transfers between devices  11.3 us (8%)
  other arithmetic  5.07 us (4%)
  local copies, waits for them, and re-layouts  2.54 us (2%)
    pallas_call x1, Pallas kernels, first_stream(): pl.pallas_call(functools.partial(stream_kernel, vels=vels, blocks=blocks)...  21.7 us
    pallas_call x2, Pallas kernels, carried(): pl.pallas_call(functools.partial(carried_kernel, blocks=blocks, start=fir...  18.8 us
    pallas_call x1, Pallas kernels, finish(): pl.pallas_call(functools.partial(finish_kernel, blocks=blocks), grid=(gro...  17.5 us
    pallas_call x1, Pallas kernels, both_moments(): pl.pallas_call(functools.partial(moments_kernel, vels=vels, blocks=blocks...  12.1 us
    pallas_call x5, Pallas kernels, small_call(): pl.pallas_call(kernel, in_specs=[smem if s == 's' else vmem for s in spec...  8.49 us
    pallas_call x1, Pallas kernels, inflow_near(): pl.pallas_call(functools.partial(near_kernel, blocks=blocks), grid=(vels...  7.92 us
    ppermute x3, waiting for transfers between devices, shards(): lax.ppermute(pieces[blocks // 2], 'vel', beside(k))  6.21 us
    ppermute x4, starting transfers between devices, shards(): lax.ppermute(send, 'vel', beside(k))  5.46 us
  transfers between devices with their start and end apart: 25, of which 6 were waited for; matrix products, arithmetic and copies ran while one was open for 1% of the time, Pallas kernels for 65%

profile of v7, /device:TPU:0, one launch (start us, length us, event | category | flops | bytes accessed | tf_op | source)
XLA Modules:
  0.0 133.3 jit_solution(3705681900845472243)
XLA Ops:
  0.6 0.8 subtract_select_fusion
  1.4 0.8 select_bitcast_fusion.1
  2.2 0.5 collective-permute-start
  2.7 2.0 %collective-permute-start.1 = (f32[3,1,1024]{2,1,0:T(1,128)S(1)}, f32[3,1,1024]{2,1,0:T(1,128)S(1)}, u32[]{:S(2)}, u32[]{:S(2)}) collective-permute-start(f32[3,1,1024]{2,1,0:T(1,128)S(1)} %get-tuple-element.107), channel_id=1, source_target_pairs={{0,3},{1,0},{2,1},{3,2},{4,7},{5,4},{6,5},{7,6},{8,11},{9,8},{10,9... | collective-permute-start | bytes 36872 | tf_op jit(solution)/shard_map/ppermute | solution.py:851
  4.7 21.7 %first_stream.1 = (f32[4,2,1024,128]{3,2,1,0:T(8,128)}, f32[4,8,1024,128]{3,2,1,0:T(8,128)}) custom-call(f32[512,64,128]{2,1,0:T(8,128)} %bitcast.22, s32[3,512]{1,0:T(4,128)} %index_ref.11), custom_call_target="tpu_custom_call" | custom-call | flops 83886080 | bytes 33554432 | tf_op jit(solution)/shard_map/first_stream/pallas_call | solution.py:227
  26.4 0.7 collective-permute-start.2
  27.1 0.1 pad.4.clone
  27.1 0.7 compare_reduce_fusion
  27.9 0.8 pad_maximum_fusion.cst_ref
  28.6 12.1 %moments_of_both.1 = (f32[576,128]{1,0:T(8,128)}, f32[576,128]{1,0:T(8,128)}, f32[576,128]{1,0:T(8,128)}, f32[576,128]{1,0:T(8,128)}) custom-call(s32[1]{0:T(128)} %bitcast.me_ref.place_ref, f32[4,8,1024,128]{3,2,1,0:T(8,128)} %get-tuple-element.57.read_ref, f32[4,2,1024,128]{3,2,1,0:T(8,128)} %get-tuple-element.56.leaving_ref, s32[3,512]{1,0:T(4,128)} %index_ref.11, ...), custom_call_target="tpu_custom_call" | custom-call | flops 3523215360 | bytes 20971520 | tf_op jit(solution)/shard_map/moments_of_both/pallas_call | solution.py:351
  40.8 1.9 %dynamic-slice_select_fusion = f32[4,2,512,128]{3,2,1,0:T(8,128)S(1)} fusion(f32[4,2,1024,128]{3,2,1,0:T(8,128)} %collective-permute-done.2.swap_ref, s32[]{:T(128)S(6)} %select_n.135, f32[4,2,1024,128]{3,2,1,0:T(8,128)S(1)} %copy-done.6, pred[4,128]{1,0:T(4,128)(4,1)S(1)} %bitcast.24), kind=kLoop, calls=%fused_computation | loop fusion | flops 524288 | bytes 6291972 | tf_op jit(solution)/shard_map/jit(_where)/select_n | solution.py:868
  42.7 0.1 fusion.3
  42.9 1.7 %collective-permute-start.7 = (f32[4,1,512,128]{3,2,1,0:T(8,128)S(1)}, f32[4,1,512,128]{3,2,1,0:T(8,128)S(1)}, u32[]{:S(2)}, u32[]{:S(2)}) collective-permute-start(f32[4,1,512,128]{3,2,1,0:T(8,128)S(1)} %get-tuple-element.106), channel_id=1, source_target_pairs={{0,2},{1,3},{2,0},{3,1},{4,6},{5,7},{6,4},{7,5},{8,10},{9,11},{10,... | collective-permute-start | bytes 3145736 | tf_op jit(solution)/shard_map/ppermute | solution.py:871
  44.6 1.5 %collective-permute-start.3 = (f32[576,128]{1,0:T(8,128)S(1)}, f32[576,128]{1,0:T(8,128)S(1)}, u32[]{:S(2)}, u32[]{:S(2)}) collective-permute-start(f32[576,128]{1,0:T(8,128)S(1)} %copy-done.9), channel_id=1, source_target_pairs={{0,4},{4,0},{8,12},{12,8},{16,20},{20,16},{24,28},{28,24},{1,5},{5... | collective-permute-start | bytes 884744 | tf_op jit(solution)/shard_map/ppermute | solution.py:879
  46.1 1.6 %collective-permute-start.4 = (f32[576,128]{1,0:T(8,128)S(1)}, f32[576,128]{1,0:T(8,128)S(1)}, u32[]{:S(2)}, u32[]{:S(2)}) collective-permute-start(f32[576,128]{1,0:T(8,128)S(1)} %copy-done.8), channel_id=1, source_target_pairs={{0,8},{4,12},{8,0},{12,4},{16,24},{20,28},{24,16},{28,20},{1,9},{5... | collective-permute-start | bytes 884744 | tf_op jit(solution)/shard_map/ppermute | solution.py:879
  47.7 0.4 collective-permute-start.5
  48.1 12.4 %carried_part.2.refs_0_ = f32[4,8,1024,128]{3,2,1,0:T(8,128)} custom-call(f32[4,8,1024,128]{3,2,1,0:T(8,128)} %get-tuple-element.57.read_ref, s32[3,512]{1,0:T(4,128)S(1)} %copy-done.3, f32[8,1024]{1,0:T(8,128)S(1)} %get-tuple-element.74.al_ref), custom_call_target="tpu_custom_call" | custom-call | flops 1 | bytes 1 | tf_op jit(solution)/shard_map/carried_part/pallas_call | solution.py:426
  60.5 0.7 collective-permute-done.5.refs_3_
  61.3 2.7 %collective-permute-start.6 = (f32[288,128]{1,0:T(8,128)S(1)}, f32[288,128]{1,0:T(8,128)S(1)}, u32[]{:S(2)}, u32[]{:S(2)}) collective-permute-start(f32[288,128]{1,0:T(8,128)S(1)} %get-tuple-element.73), channel_id=1, source_target_pairs={{0,16},{4,20},{8,24},{12,28},{16,0},{20,4},{24,8},{28,12},{1,17},{... | collective-permute-start | bytes 442376 | tf_op jit(solution)/shard_map/ppermute | solution.py:883
  63.9 6.4 %carried_part.3.carried_ref = f32[4,8,1024,128]{3,2,1,0:T(8,128)} custom-call(f32[4,8,1024,128]{3,2,1,0:T(8,128)} %get-tuple-element.57.read_ref, s32[3,512]{1,0:T(4,128)S(1)} %copy-done.3, f32[8,1024]{1,0:T(8,128)S(1)} %get-tuple-element.74.al_ref, f32[4,8,1024,128]{3,2,1,0:T(8,128)} %carried_part.2.refs_0_), custom_call_target="tpu_custom_call", output_to_operand_aliasing={{}: (3, {})} | custom-call | flops 1 | bytes 1 | tf_op jit(solution)/shard_map/carried_part/pallas_call | solution.py:426
  70.4 0.1 collective-permute-start.14
  70.5 0.5 collective-permute-start.8
  71.0 1.3 collective-permute-start.9
  72.3 2.0 %collective-permute-done.8.low_ref = f32[144,128]{1,0:T(8,128)S(1)} collective-permute-done((f32[144,128]{1,0:T(8,128)S(1)}, f32[144,128]{1,0:T(8,128)S(1)}, u32[]{:S(2)}, u32[]{:S(2)}) %collective-permute-start.8) | collective-permute-done | bytes 73760 | tf_op jit(solution)/shard_map/ppermute | solution.py:898
  74.3 0.8 local_fields.1.refs_0_
  75.1 0.6 collective-permute-start.18
  75.7 1.5 %collective-permute-start.10 = (f32[248,128]{1,0:T(8,128)S(1)}, f32[248,128]{1,0:T(8,128)S(1)}, u32[]{:S(2)}, u32[]{:S(2)}) collective-permute-start(f32[248,128]{1,0:T(8,128)S(1)} %local_fields.1.refs_0_), channel_id=1, source_target_pairs={{0,4},{4,0},{8,12},{12,8},{16,20},{20,16},{24,28},{28,24},{1,5},{5... | collective-permute-start | bytes 380936 | tf_op jit(solution)/shard_map/ppermute | solution.py:903
  77.3 1.6 %collective-permute-start.11 = (f32[248,128]{1,0:T(8,128)S(1)}, f32[248,128]{1,0:T(8,128)S(1)}, u32[]{:S(2)}, u32[]{:S(2)}) collective-permute-start(f32[248,128]{1,0:T(8,128)S(1)} %local_fields.1.refs_0_), channel_id=1, source_target_pairs={{0,8},{4,12},{8,0},{12,4},{16,24},{20,28},{24,16},{28,20},{1,9},{5... | collective-permute-start | bytes 380936 | tf_op jit(solution)/shard_map/ppermute | solution.py:903
  78.8 2.3 %collective-permute-start.13 = (f32[248,128]{1,0:T(8,128)S(1)}, f32[248,128]{1,0:T(8,128)S(1)}, u32[]{:S(2)}, u32[]{:S(2)}) collective-permute-start(f32[248,128]{1,0:T(8,128)S(1)} %local_fields.1.refs_0_), channel_id=1, source_target_pairs={{0,16},{4,20},{8,24},{12,28},{16,0},{20,4},{24,8},{28,12},{1,17},{... | collective-permute-start | bytes 380936 | tf_op jit(solution)/shard_map/ppermute | solution.py:903
  81.2 7.9 %inflow_near.1.inflow_ref = f32[4,3,1024,128]{3,2,1,0:T(8,128)} custom-call(s32[1]{0:T(128)} %bitcast.7.core_ref, f32[4,2,1024,128]{3,2,1,0:T(8,128)} %collective-permute-done.2.swap_ref, f32[4,1,512,128]{3,2,1,0:T(8,128)S(1)} %collective-permute-done.7.first_ref, f32[4,1,512,128]{3,2,1,0:T(8,128)S(1)} %collective-permute-done.14.second_ref, ...), custom_call_target="tpu_custom_call" | custom-call | flops 1 | bytes 1 | tf_op jit(solution)/shard_map/inflow_near/pallas_call | solution.py:512
  89.2 1.4 %collective-permute-start.15 = (f32[248,128]{1,0:T(8,128)S(1)}, f32[248,128]{1,0:T(8,128)S(1)}, u32[]{:S(2)}, u32[]{:S(2)}) collective-permute-start(f32[248,128]{1,0:T(8,128)S(1)} %collective-permute-done.13.refs_4_), channel_id=1, source_target_pairs={{0,4},{4,0},{8,12},{12,8},{16,20},{20,16},{24,28},{28,24},{1,5},{5... | collective-permute-start | bytes 380936 | tf_op jit(solution)/shard_map/ppermute | solution.py:911
  90.6 2.0 %collective-permute-start.16 = (f32[248,128]{1,0:T(8,128)S(1)}, f32[248,128]{1,0:T(8,128)S(1)}, u32[]{:S(2)}, u32[]{:S(2)}) collective-permute-start(f32[248,128]{1,0:T(8,128)S(1)} %collective-permute-done.13.refs_4_), channel_id=1, source_target_pairs={{0,8},{4,12},{8,0},{12,4},{16,24},{20,28},{24,16},{28,20},{1,9},{5... | collective-permute-start | bytes 380936 | tf_op jit(solution)/shard_map/ppermute | solution.py:911
  92.7 2.3 %collective-permute-done.15.refs_5_ = f32[248,128]{1,0:T(8,128)S(1)} collective-permute-done((f32[248,128]{1,0:T(8,128)S(1)}, f32[248,128]{1,0:T(8,128)S(1)}, u32[]{:S(2)}, u32[]{:S(2)}) %collective-permute-start.15) | collective-permute-done | bytes 127008 | tf_op jit(solution)/shard_map/ppermute | solution.py:911
  95.0 1.9 %collective-permute-done.16.refs_6_ = f32[248,128]{1,0:T(8,128)S(1)} collective-permute-done((f32[248,128]{1,0:T(8,128)S(1)}, f32[248,128]{1,0:T(8,128)S(1)}, u32[]{:S(2)}, u32[]{:S(2)}) %collective-permute-start.16) | collective-permute-done | bytes 127008 | tf_op jit(solution)/shard_map/ppermute | solution.py:911
  96.8 2.0 %collective-permute-done.17.refs_7_ = f32[248,128]{1,0:T(8,128)S(1)} collective-permute-done((f32[248,128]{1,0:T(8,128)S(1)}, f32[248,128]{1,0:T(8,128)S(1)}, u32[]{:S(2)}, u32[]{:S(2)}) %collective-permute-start.17) | collective-permute-done | bytes 127008 | tf_op jit(solution)/shard_map/ppermute | solution.py:911
  98.9 4.5 %first_fields.1 = (f32[8,448,128]{2,1,0:T(8,128)S(1)}, f32[104,1024]{1,0:T(8,128)S(1)}, f32[104,1024]{1,0:T(8,128)S(1)}, f32[16,1024]{1,0:T(8,128)}, f32[16,1024]{1,0:T(8,128)}, /*index=5*/f32[8,128]{1,0:T(8,128)S(1)}) custom-call(s32[1]{0:T(128)} %bitcast.me_ref.place_ref, f32[13,13]{1,0:T(8,128)S(1)} %copy-done.5, f32[3,16,1024]{2,1,0:T(8,128)S(1)} %copy-done, ...), custom_call_target="tpu_custom_call" | custom-call | tf_op jit(solution)/shard_map/first_fields/pallas_call | solution.py:532
  103.4 0.8 copy-done.1
  104.2 0.5 collective-permute-start.19
  104.7 1.2 collective-permute-start.20
  105.9 2.3 %collective-permute-done.19.low_ref = f32[16,1024]{1,0:T(8,128)} collective-permute-done((f32[16,1024]{1,0:T(8,128)}, f32[16,1024]{1,0:T(8,128)}, u32[]{:S(2)}, u32[]{:S(2)}) %collective-permute-start.19) | collective-permute-done | bytes 65568 | tf_op jit(solution)/shard_map/ppermute | solution.py:931
  108.2 1.0 copy-done.2
  109.2 3.1 %last_fields.1 = (f32[8,64,128]{2,1,0:T(8,128)S(1)}, f32[13,8,128]{2,1,0:T(8,128)}, f32[2,128]{1,0:T(2,128)S(1)}) custom-call(s32[1]{0:T(128)} %bitcast.me_ref.place_ref, f32[3,16,1024]{2,1,0:T(8,128)S(1)} %copy-done, f32[104,1024]{1,0:T(8,128)S(1)} %get-tuple-element.85.later_ref, f32[104,1024]{1,0:T(8,128)S(1)} %copy-done.2, ...), custom_call_target="tpu_custom_call" | custom-call | tf_op jit(solution)/shard_map/last_fields/pallas_call | solution.py:532
  112.2 1.2 collective-permute-start.21
  113.5 0.5 collective-permute-start.23
  114.0 1.1 collective-permute-start.24
  115.1 17.5 %finish_dist.1 = f32[512,64,128]{2,1,0:T(8,128)} custom-call(s32[1]{0:T(128)} %bitcast.7.core_ref, f32[4,8,1024,128]{3,2,1,0:T(8,128)} %carried_part.3.carried_ref, f32[4,3,1024,128]{3,2,1,0:T(8,128)} %inflow_near.1.inflow_ref, f32[4,2,1024,128]{3,2,1,0:T(8,128)} %collective-permute-done.2.swap_ref, ...), custom_call_target="tpu_custom_call" | custom-call | flops 2147483648 | bytes 33554432 | tf_op jit(solution)/shard_map/finish_dist/pallas_call | solution.py:791
  132.7 0.1 add_reduce_fusion
  132.8 0.5 sqrt.3
  (45 shorter events, 0.3 us)
Async XLA Ops:
  2.2 24.2 %collective-permute-start = (f32[3,1,1024]{2,1,0:T(1,128)S(1)}, f32[3,1,1024]{2,1,0:T(1,128)S(1)}, u32[]{:S(2)}, u32[]{:S(2)}) collective-permute-start(f32[3,1,1024]{2,1,0:T(1,128)S(1)} %get-tuple-element.108), channel_id=1, source_target_pairs={{0,1},{1,2},{2,3},{3,0},{4,5},{5,6},{6,7},{7,4},{8,9},{9,10},{10,1... | collective-permute-start | bytes 36872 | tf_op jit(solution)/shard_map/ppermute | solution.py:850
  2.7 23.7 %collective-permute-start.1 = (f32[3,1,1024]{2,1,0:T(1,128)S(1)}, f32[3,1,1024]{2,1,0:T(1,128)S(1)}, u32[]{:S(2)}, u32[]{:S(2)}) collective-permute-start(f32[3,1,1024]{2,1,0:T(1,128)S(1)} %get-tuple-element.107), channel_id=1, source_target_pairs={{0,3},{1,0},{2,1},{3,2},{4,7},{5,4},{6,5},{7,6},{8,11},{9,8},{10,9... | collective-permute-start | bytes 36872 | tf_op jit(solution)/shard_map/ppermute | solution.py:851
  26.4 14.4 %collective-permute-start.2 = (f32[4,2,1024,128]{3,2,1,0:T(8,128)}, f32[4,2,1024,128]{3,2,1,0:T(8,128)}, u32[]{:S(2)}, u32[]{:S(2)}) collective-permute-start(f32[4,2,1024,128]{3,2,1,0:T(8,128)} %get-tuple-element.56.leaving_ref), channel_id=1, source_target_pairs={{0,1},{1,0},{2,3},{3,2},{4,5},{5,4},{6,7},{7,6},{8,9},{9,8},{10,11... | collective-permute-start | bytes 12582920 | tf_op jit(solution)/shard_map/ppermute | solution.py:855
  28.6 12.1 %copy-start.6 = (f32[4,2,1024,128]{3,2,1,0:T(8,128)S(1)}, f32[4,2,1024,128]{3,2,1,0:T(8,128)}, u32[]{:S(2)}) copy-start(f32[4,2,1024,128]{3,2,1,0:T(8,128)} %get-tuple-element.56.leaving_ref) | copy-start | bytes 12582916
  40.8 3.8 %copy-start.9 = (f32[576,128]{1,0:T(8,128)S(1)}, f32[576,128]{1,0:T(8,128)}, u32[]{:S(2)}) copy-start(f32[576,128]{1,0:T(8,128)} %get-tuple-element.68) | copy-start | bytes 884740
  40.8 5.3 %copy-start.8 = (f32[576,128]{1,0:T(8,128)S(1)}, f32[576,128]{1,0:T(8,128)}, u32[]{:S(2)}) copy-start(f32[576,128]{1,0:T(8,128)} %get-tuple-element.70) | copy-start | bytes 884740
  40.8 6.9 %copy-start.7 = (f32[576,128]{1,0:T(8,128)S(1)}, f32[576,128]{1,0:T(8,128)}, u32[]{:S(2)}) copy-start(f32[576,128]{1,0:T(8,128)} %get-tuple-element.71) | copy-start | bytes 884740
  40.8 7.3 %copy-start.3 = (s32[3,512]{1,0:T(4,128)S(1)}, s32[3,512]{1,0:T(4,128)}, u32[]{:S(2)}) copy-start(s32[3,512]{1,0:T(4,128)} %index_ref.11) | copy-start | bytes 18436
  42.9 18.4 %copy-start.4 = (f32[576,128]{1,0:T(8,128)S(1)}, f32[576,128]{1,0:T(8,128)}, u32[]{:S(2)}) copy-start(f32[576,128]{1,0:T(8,128)} %get-tuple-element.67.refs_0_) | copy-start | bytes 884740
  42.9 27.5 %collective-permute-start.7 = (f32[4,1,512,128]{3,2,1,0:T(8,128)S(1)}, f32[4,1,512,128]{3,2,1,0:T(8,128)S(1)}, u32[]{:S(2)}, u32[]{:S(2)}) collective-permute-start(f32[4,1,512,128]{3,2,1,0:T(8,128)S(1)} %get-tuple-element.106), channel_id=1, source_target_pairs={{0,2},{1,3},{2,0},{3,1},{4,6},{5,7},{6,4},{7,5},{8,10},{9,11},{10,... | collective-permute-start | bytes 3145736 | tf_op jit(solution)/shard_map/ppermute | solution.py:871
  44.6 15.9 %collective-permute-start.3 = (f32[576,128]{1,0:T(8,128)S(1)}, f32[576,128]{1,0:T(8,128)S(1)}, u32[]{:S(2)}, u32[]{:S(2)}) collective-permute-start(f32[576,128]{1,0:T(8,128)S(1)} %copy-done.9), channel_id=1, source_target_pairs={{0,4},{4,0},{8,12},{12,8},{16,20},{20,16},{24,28},{28,24},{1,5},{5... | collective-permute-start | bytes 884744 | tf_op jit(solution)/shard_map/ppermute | solution.py:879
  46.1 14.4 %collective-permute-start.4 = (f32[576,128]{1,0:T(8,128)S(1)}, f32[576,128]{1,0:T(8,128)S(1)}, u32[]{:S(2)}, u32[]{:S(2)}) collective-permute-start(f32[576,128]{1,0:T(8,128)S(1)} %copy-done.8), channel_id=1, source_target_pairs={{0,8},{4,12},{8,0},{12,4},{16,24},{20,28},{24,16},{28,20},{1,9},{5... | collective-permute-start | bytes 884744 | tf_op jit(solution)/shard_map/ppermute | solution.py:879
  47.7 13.5 %collective-permute-start.5 = (f32[576,128]{1,0:T(8,128)S(1)}, f32[576,128]{1,0:T(8,128)S(1)}, u32[]{:S(2)}, u32[]{:S(2)}) collective-permute-start(f32[576,128]{1,0:T(8,128)S(1)} %copy-done.7), channel_id=1, source_target_pairs={{0,12},{4,8},{8,4},{12,0},{16,28},{20,24},{24,20},{28,16},{1,13},{... | collective-permute-start | bytes 884744 | tf_op jit(solution)/shard_map/ppermute | solution.py:879
  61.3 9.1 %collective-permute-start.6 = (f32[288,128]{1,0:T(8,128)S(1)}, f32[288,128]{1,0:T(8,128)S(1)}, u32[]{:S(2)}, u32[]{:S(2)}) collective-permute-start(f32[288,128]{1,0:T(8,128)S(1)} %get-tuple-element.73), channel_id=1, source_target_pairs={{0,16},{4,20},{8,24},{12,28},{16,0},{20,4},{24,8},{28,12},{1,17},{... | collective-permute-start | bytes 442376 | tf_op jit(solution)/shard_map/ppermute | solution.py:883
  63.9 10.4 %copy-start.5 = (f32[13,13]{1,0:T(8,128)S(1)}, f32[13,13]{1,0:T(8,128)}, u32[]{:S(2)}) copy-start(f32[13,13]{1,0:T(8,128)} %inv_ref.3) | copy-start | bytes 2032
  63.9 17.2 %copy-start = (f32[3,16,1024]{2,1,0:T(8,128)S(1)}, f32[3,16,1024]{2,1,0:T(8,128)}, u32[]{:S(2)}) copy-start(f32[3,16,1024]{2,1,0:T(8,128)} %pad_maximum_fusion.cst_ref) | copy-start | bytes 589828
  70.4 10.7 %collective-permute-start.14 = (f32[4,1,512,128]{3,2,1,0:T(8,128)S(1)}, f32[4,1,512,128]{3,2,1,0:T(8,128)S(1)}, u32[]{:S(2)}, u32[]{:S(2)}) collective-permute-start(f32[4,1,512,128]{3,2,1,0:T(8,128)S(1)} %collective-permute-done.7.first_ref), channel_id=1, source_target_pairs={{0,1},{1,0},{2,3},{3,2},{4,5},{5,4},{6,7},{7,6},{8,9},{9,8},{10,11... | collective-permute-start | bytes 3145736 | tf_op jit(solution)/shard_map/ppermute | solution.py:907
  70.5 3.8 %collective-permute-start.8 = (f32[144,128]{1,0:T(8,128)S(1)}, f32[144,128]{1,0:T(8,128)S(1)}, u32[]{:S(2)}, u32[]{:S(2)}) collective-permute-start(f32[144,128]{1,0:T(8,128)S(1)} %get-tuple-element.81), channel_id=1, source_target_pairs={{0,1},{1,2},{2,3},{3,0},{4,5},{5,6},{6,7},{7,4},{8,9},{9,10},{10,1... | collective-permute-start | bytes 221192 | tf_op jit(solution)/shard_map/ppermute | solution.py:898
  71.0 3.3 %collective-permute-start.9 = (f32[144,128]{1,0:T(8,128)S(1)}, f32[144,128]{1,0:T(8,128)S(1)}, u32[]{:S(2)}, u32[]{:S(2)}) collective-permute-start(f32[144,128]{1,0:T(8,128)S(1)} %get-tuple-element.82), channel_id=1, source_target_pairs={{0,3},{1,0},{2,1},{3,2},{4,7},{5,4},{6,5},{7,6},{8,11},{9,8},{10,9... | collective-permute-start | bytes 221192 | tf_op jit(solution)/shard_map/ppermute | solution.py:899
  75.1 29.0 %collective-permute-start.18 = (f32[4,1,512,128]{3,2,1,0:T(8,128)S(1)}, f32[4,1,512,128]{3,2,1,0:T(8,128)S(1)}, u32[]{:S(2)}, u32[]{:S(2)}) collective-permute-start(f32[4,1,512,128]{3,2,1,0:T(8,128)S(1)} %get-tuple-element.87), channel_id=1, source_target_pairs={{0,2},{1,3},{2,0},{3,1},{4,6},{5,7},{6,4},{7,5},{8,10},{9,11},{10,... | collective-permute-start | bytes 3145736 | tf_op jit(solution)/shard_map/ppermute | solution.py:905
  75.7 14.9 %collective-permute-start.10 = (f32[248,128]{1,0:T(8,128)S(1)}, f32[248,128]{1,0:T(8,128)S(1)}, u32[]{:S(2)}, u32[]{:S(2)}) collective-permute-start(f32[248,128]{1,0:T(8,128)S(1)} %local_fields.1.refs_0_), channel_id=1, source_target_pairs={{0,4},{4,0},{8,12},{12,8},{16,20},{20,16},{24,28},{28,24},{1,5},{5... | collective-permute-start | bytes 380936 | tf_op jit(solution)/shard_map/ppermute | solution.py:903
  77.3 15.4 %collective-permute-start.11 = (f32[248,128]{1,0:T(8,128)S(1)}, f32[248,128]{1,0:T(8,128)S(1)}, u32[]{:S(2)}, u32[]{:S(2)}) collective-permute-start(f32[248,128]{1,0:T(8,128)S(1)} %local_fields.1.refs_0_), channel_id=1, source_target_pairs={{0,8},{4,12},{8,0},{12,4},{16,24},{20,28},{24,16},{28,20},{1,9},{5... | collective-permute-start | bytes 380936 | tf_op jit(solution)/shard_map/ppermute | solution.py:903
  78.8 10.3 %collective-permute-start.13 = (f32[248,128]{1,0:T(8,128)S(1)}, f32[248,128]{1,0:T(8,128)S(1)}, u32[]{:S(2)}, u32[]{:S(2)}) collective-permute-start(f32[248,128]{1,0:T(8,128)S(1)} %local_fields.1.refs_0_), channel_id=1, source_target_pairs={{0,16},{4,20},{8,24},{12,28},{16,0},{20,4},{24,8},{28,12},{1,17},{... | collective-permute-start | bytes 380936 | tf_op jit(solution)/shard_map/ppermute | solution.py:903
  81.2 11.5 %collective-permute-start.12 = (f32[248,128]{1,0:T(8,128)S(1)}, f32[248,128]{1,0:T(8,128)S(1)}, u32[]{:S(2)}, u32[]{:S(2)}) collective-permute-start(f32[248,128]{1,0:T(8,128)S(1)} %local_fields.1.refs_0_), channel_id=1, source_target_pairs={{0,12},{4,8},{8,4},{12,0},{16,28},{20,24},{24,20},{28,16},{1,13},{... | collective-permute-start | bytes 380936 | tf_op jit(solution)/shard_map/ppermute | solution.py:903
  89.2 5.8 %collective-permute-start.15 = (f32[248,128]{1,0:T(8,128)S(1)}, f32[248,128]{1,0:T(8,128)S(1)}, u32[]{:S(2)}, u32[]{:S(2)}) collective-permute-start(f32[248,128]{1,0:T(8,128)S(1)} %collective-permute-done.13.refs_4_), channel_id=1, source_target_pairs={{0,4},{4,0},{8,12},{12,8},{16,20},{20,16},{24,28},{28,24},{1,5},{5... | collective-permute-start | bytes 380936 | tf_op jit(solution)/shard_map/ppermute | solution.py:911
  90.6 6.2 %collective-permute-start.16 = (f32[248,128]{1,0:T(8,128)S(1)}, f32[248,128]{1,0:T(8,128)S(1)}, u32[]{:S(2)}, u32[]{:S(2)}) collective-permute-start(f32[248,128]{1,0:T(8,128)S(1)} %collective-permute-done.13.refs_4_), channel_id=1, source_target_pairs={{0,8},{4,12},{8,0},{12,4},{16,24},{20,28},{24,16},{28,20},{1,9},{5... | collective-permute-start | bytes 380936 | tf_op jit(solution)/shard_map/ppermute | solution.py:911
  92.6 6.2 %collective-permute-start.17 = (f32[248,128]{1,0:T(8,128)S(1)}, f32[248,128]{1,0:T(8,128)S(1)}, u32[]{:S(2)}, u32[]{:S(2)}) collective-permute-start(f32[248,128]{1,0:T(8,128)S(1)} %collective-permute-done.13.refs_4_), channel_id=1, source_target_pairs={{0,12},{4,8},{8,4},{12,0},{16,28},{20,24},{24,20},{28,16},{1,13},{... | collective-permute-start | bytes 380936 | tf_op jit(solution)/shard_map/ppermute | solution.py:911
  103.4 0.8 copy-start.1
  104.2 10.9 %collective-permute-start.22 = (f32[4,1,512,128]{3,2,1,0:T(8,128)S(1)}, f32[4,1,512,128]{3,2,1,0:T(8,128)}, u32[]{:S(2)}, u32[]{:S(2)}) collective-permute-start(f32[4,1,512,128]{3,2,1,0:T(8,128)S(1)} %collective-permute-done.18.first_ref), channel_id=1, source_target_pairs={{0,1},{1,0},{2,3},{3,2},{4,5},{5,4},{6,7},{7,6},{8,9},{9,8},{10,11... | collective-permute-start | bytes 3145736 | tf_op jit(solution)/shard_map/ppermute | solution.py:930
  104.2 4.0 %collective-permute-start.19 = (f32[16,1024]{1,0:T(8,128)}, f32[16,1024]{1,0:T(8,128)}, u32[]{:S(2)}, u32[]{:S(2)}) collective-permute-start(f32[16,1024]{1,0:T(8,128)} %get-tuple-element.89), channel_id=1, source_target_pairs={{0,1},{1,2},{2,3},{3,0},{4,5},{5,6},{6,7},{7,4},{8,9},{9,10},{10,1... | collective-permute-start | bytes 196616 | tf_op jit(solution)/shard_map/ppermute | solution.py:931
  104.7 3.5 %collective-permute-start.20 = (f32[16,1024]{1,0:T(8,128)}, f32[16,1024]{1,0:T(8,128)}, u32[]{:S(2)}, u32[]{:S(2)}) collective-permute-start(f32[16,1024]{1,0:T(8,128)} %get-tuple-element.90), channel_id=1, source_target_pairs={{0,3},{1,0},{2,1},{3,2},{4,7},{5,4},{6,5},{7,6},{8,11},{9,8},{10,9... | collective-permute-start | bytes 196616 | tf_op jit(solution)/shard_map/ppermute | solution.py:932
  108.2 1.0 copy-start.2
  112.2 20.4 %collective-permute-start.21 = (f32[2,128]{1,0:T(2,128)S(1)}, f32[2,128]{1,0:T(2,128)S(1)}, u32[]{:S(2)}, u32[]{:S(2)}) collective-permute-start(f32[2,128]{1,0:T(2,128)S(1)} %get-tuple-element.92), channel_id=1, source_target_pairs={{0,1},{1,2},{2,3},{3,0},{4,5},{5,6},{6,7},{7,4},{8,9},{9,10},{10,1... | collective-permute-start | bytes 3080 | tf_op jit(solution)/shard_map/ppermute | solution.py:943
  113.5 19.2 %collective-permute-start.23 = (f32[2,128]{1,0:T(2,128)S(1)}, f32[2,128]{1,0:T(2,128)S(1)}, u32[]{:S(2)}, u32[]{:S(2)}) collective-permute-start(f32[2,128]{1,0:T(2,128)S(1)} %get-tuple-element.92), channel_id=1, source_target_pairs={{0,3},{1,0},{2,1},{3,2},{4,7},{5,4},{6,5},{7,6},{8,11},{9,8},{10,9... | collective-permute-start | bytes 3080 | tf_op jit(solution)/shard_map/ppermute | solution.py:943
  114.0 18.7 %collective-permute-start.24 = (f32[2,128]{1,0:T(2,128)S(1)}, f32[2,128]{1,0:T(2,128)S(1)}, u32[]{:S(2)}, u32[]{:S(2)}) collective-permute-start(f32[2,128]{1,0:T(2,128)S(1)} %get-tuple-element.92), channel_id=1, source_target_pairs={{0,2},{1,3},{2,0},{3,1},{4,6},{5,7},{6,4},{7,5},{8,10},{9,11},{10,... | collective-permute-start | bytes 3080 | tf_op jit(solution)/shard_map/ppermute | solution.py:943
